TPU v7x, 256 devices: a whole 4x4x8 slice. The times are simulated.
256 devices in a mesh: lat: 64 (over x, y, z_lo, core), lev: 4 (over z_hi).
Axes of the slice: x: 4, y: 4, z: 8 (z_hi: 4, z_lo: 2; z = z_hi * 2 + z_lo), core: 2. Of those that a mesh axis runs over, the one named last changes fastest.
Arguments:
- zonal_wind: float32 [768, 128, 576], P('lat', 'lev'), may hold values from -3 to 3
- meridional_wind: float32 [768, 128, 576], P('lat', 'lev'), may hold values from -3 to 3
- thickness: float32 [768, 128, 576], P('lat', 'lev'), may hold values from 0.00390625 to 0.01171875
- potential_temp: float32 [768, 128, 576], P('lat', 'lev'), may hold values from 0.8 to 1.6
- surface_geo: float32 [768, 576], P('lat'), may hold values from -1.5 to 1.5
- polar_mask: int32 [768], P('lat'), may hold values from 0 to 1, as said below
- cutoff: int32 [768], P('lat'), may hold values from 1 to 143
- damping: float32 [768, 576], P('lat'), may hold values from 0.05 to 0.8
Outputs:
- zonal_next: float32 [768, 128, 576], P('lat', 'lev')
- meridional_next: float32 [768, 128, 576], P('lat', 'lev')
- thickness_next: float32 [768, 128, 576], P('lat', 'lev')
- potential_next: float32 [768, 128, 576], P('lat', 'lev')
Inputs may be any that keep to these rules, and one draw needn't show every extreme that they name: `polar_mask`: 1 exactly on the first s and the last n latitude rows and 0 elsewhere; the larger of s and n is 192, the smaller lies between 128 and 192.
All inputs are finite; a program needn't handle non-finite values.
Results may differ from a plain program's by a relative error of at most 0.0003.
Values sent between devices are 32-bit elements; how exact they have to be, the bound alone decides.
No kernel may reach another device: no remote copies, remote signals or barrier semaphores. Data moves between devices by JAX's collectives and lax.ppermute only.
A program may use at most 128 MiB of HBM per device.

v0:
```python
import math

import jax
import jax.numpy as jnp
from jax import lax
from jax.sharding import PartitionSpec as P

TOP_PRESSURE = 0.01
HYBRID_SCALE = 0.2
EXNER_POWER = 2.0 / 7.0
ZONAL_COURANT = 0.012
MERIDIONAL_COURANT = 0.012
HIGHEST = lax.Precision.HIGHEST


def extended(block, sides, width):
    for axis, dim in sides:
        count = lax.axis_size(axis)
        forward = [(i, i + 1) for i in range(count - 1)]
        backward = [(target, source) for source, target in forward]
        low = lax.ppermute(
            lax.slice_in_dim(block, block.shape[dim] - width, None, axis=dim), axis, forward
        )
        high = lax.ppermute(lax.slice_in_dim(block, 0, width, axis=dim), axis, backward)
        block = jnp.concatenate([low, block, high], axis=dim)
    return block


def shifted(array, axis, by):
    peers = lax.axis_size(axis)
    pairs = [(i, i + by) for i in range(peers) if 0 <= i + by < peers]
    return lax.ppermute(array, axis, pairs)


def fourier_basis(count):
    middle = count // 2
    points = jnp.arange(count, dtype=jnp.int32)
    column_ids = jnp.arange(count, dtype=jnp.int32)
    wave = jnp.where(column_ids <= middle, column_ids, column_ids - middle)
    phase = points[:, None] * wave[None, :] % count
    angle = 2.0 * math.pi / count * phase.astype(jnp.float32)
    edge_cols = (column_ids == 0) | (column_ids == middle)
    weight = jnp.where(edge_cols, 1.0 / math.sqrt(count), math.sqrt(2.0 / count)).astype(
        jnp.float32
    )
    basis = (
        jnp.where((column_ids <= middle)[None, :], jnp.cos(angle), jnp.sin(angle)) * weight[None, :]
    )
    return (basis, wave)


def damping_table(polar_mask, cutoff, damping, wave):
    active = (wave[None, :] >= cutoff[:, None]) & (polar_mask[:, None] != 0)
    return jnp.where(active, damping - 1.0, 0.0)


def target_interfaces(surface, count, levels):
    sigma = jnp.arange(count + 1, dtype=jnp.int32).astype(jnp.float32) / levels
    curve = sigma * sigma
    hybrid = sigma - curve
    return (
        TOP_PRESSURE
        + HYBRID_SCALE * hybrid[:, None]
        + (surface[..., None, :] - TOP_PRESSURE) * curve[:, None]
    )


def remap_column(thick_col, theta_col):
    levels = thick_col.shape[0]
    edge_ids = jnp.arange(levels + 1, dtype=jnp.int32)
    level_ids = jnp.arange(levels, dtype=jnp.int32)
    lower_tri = (edge_ids[:, None] > level_ids[None, :]).astype(jnp.float32)
    source_edges = TOP_PRESSURE + jnp.dot(lower_tri, thick_col, precision=HIGHEST)
    surface = source_edges[levels]
    target_edges = target_interfaces(surface, levels, levels)
    target_thick = target_edges[1:] - target_edges[:-1]
    exner_edges = target_edges**EXNER_POWER
    exner_mid = 0.5 * (exner_edges[:-1] + exner_edges[1:])
    block_levels = min(32, levels)
    pieces = []
    for first_level in range(0, levels, block_levels):
        upper_edge = target_edges[first_level : first_level + block_levels]
        lower_edge = target_edges[first_level + 1 : first_level + block_levels + 1]
        intersection = jnp.maximum(
            jnp.minimum(lower_edge[:, None, :], source_edges[None, 1:, :])
            - jnp.maximum(upper_edge[:, None, :], source_edges[None, :-1, :]),
            0.0,
        )
        pieces.append(jnp.sum(intersection * theta_col[None], axis=1))
    theta_remap = jnp.concatenate(pieces, 0) / target_thick
    layer_term = theta_remap * (exner_edges[1:] - exner_edges[:-1])
    strictly_below = (level_ids[None, :] > level_ids[:, None]).astype(jnp.float32)
    geo_rel = jnp.dot(strictly_below, layer_term, precision=HIGHEST) + 0.5 * layer_term
    return (target_thick, theta_remap, geo_rel, exner_mid, surface, layer_term)


def apply_filter(field, table, basis):
    spectral = jnp.einsum("alkn,nc->alkc", field, basis, precision=HIGHEST)
    return field + jnp.einsum(
        "alkc,nc->alkn", spectral * table[None, :, None, :], basis, precision=HIGHEST
    )


def maybe_filter(field, table, basis):

    def filtered(field_in):
        return apply_filter(field_in, table, basis)

    def unchanged(field_in):
        return field_in

    return lax.cond(jnp.any(table != 0.0), filtered, unchanged, field)


def body(
    zonal_wind, meridional_wind, thickness, potential_temp, surface_geo, polar_mask, cutoff, damping
):
    lat_rows, lev_levels, width = zonal_wind.shape
    lat_count = lax.axis_size("lat")
    total_rows = lat_rows * lat_count
    first_row = lax.axis_index("lat") * lat_rows
    row_ids = (first_row + jnp.arange(lat_rows + 1, dtype=jnp.int32)).astype(jnp.float32)
    faces = jnp.sin(math.pi * row_ids / total_rows)[:, None, None]
    centres = jnp.sin(math.pi * (row_ids[:-1] + 0.5) / total_rows)[:, None, None]
    heat = potential_temp * thickness
    padded = extended(jnp.stack([thickness, heat]), (("lat", 1),), 1)
    thick_pad = padded[0]
    heat_pad = padded[1]
    north_row = shifted(meridional_wind[:1], "lat", -1)
    wind_ext = jnp.concatenate([meridional_wind, north_row], 0)
    merid_mass = wind_ext * faces * 0.5 * (thick_pad[1:] + thick_pad[:-1])
    merid_heat = wind_ext * faces * 0.5 * (heat_pad[1:] + heat_pad[:-1])
    zonal_mass = zonal_wind * 0.5 * (thickness + jnp.roll(thickness, 1, axis=2))
    zonal_heat = zonal_wind * 0.5 * (heat + jnp.roll(heat, 1, axis=2))
    thick_new = (
        thickness
        - ZONAL_COURANT * (jnp.roll(zonal_mass, -1, axis=2) - zonal_mass)
        - MERIDIONAL_COURANT * (merid_mass[1:] - merid_mass[:-1]) / centres
    )
    heat_new = (
        heat
        - ZONAL_COURANT * (jnp.roll(zonal_heat, -1, axis=2) - zonal_heat)
        - MERIDIONAL_COURANT * (merid_heat[1:] - merid_heat[:-1]) / centres
    )
    theta_new = heat_new / thick_new

    def one_row(pair):
        return remap_column(pair[0], pair[1])

    thick_cols = lax.all_to_all(thick_new, "lev", split_axis=2, concat_axis=1, tiled=True)
    theta_cols = lax.all_to_all(theta_new, "lev", split_axis=2, concat_axis=1, tiled=True)
    target_thick, theta_remap, geo_rel, exner_mid, surface, layer_term = lax.map(
        one_row, (thick_cols, theta_cols)
    )
    thick_out, theta_out, geo_rel, exner_mid = (
        lax.all_to_all(target_thick, "lev", split_axis=1, concat_axis=2, tiled=True),
        lax.all_to_all(theta_remap, "lev", split_axis=1, concat_axis=2, tiled=True),
        lax.all_to_all(geo_rel, "lev", split_axis=1, concat_axis=2, tiled=True),
        lax.all_to_all(exner_mid, "lev", split_axis=1, concat_axis=2, tiled=True),
    )
    geopot = surface_geo[:, None, :] + geo_rel
    south = shifted(jnp.stack([geopot[-1:], exner_mid[-1:], theta_out[-1:]]), "lat", 1)
    geo_south = jnp.concatenate([south[0], geopot[:-1]], 0)
    exner_south = jnp.concatenate([south[1], exner_mid[:-1]], 0)
    theta_south = jnp.concatenate([south[2], theta_out[:-1]], 0)
    zonal_push = (
        geopot
        - jnp.roll(geopot, 1, axis=2)
        + 0.5
        * (theta_out + jnp.roll(theta_out, 1, axis=2))
        * (exner_mid - jnp.roll(exner_mid, 1, axis=2))
    )
    zonal_pre = zonal_wind - zonal_push
    merid_push = geopot - geo_south + 0.5 * (theta_out + theta_south) * (exner_mid - exner_south)
    meridional_pre = meridional_wind - faces[:-1] * merid_push
    basis, wave = fourier_basis(width)
    table = damping_table(polar_mask, cutoff, damping, wave)
    stacked = jnp.stack([zonal_pre, meridional_pre])
    filtered = maybe_filter(stacked, table, basis)
    return (filtered[0], filtered[1], thick_out, theta_out)


def solution(mesh):
    in_specs = (
        P("lat", "lev", None),
        P("lat", "lev", None),
        P("lat", "lev", None),
        P("lat", "lev", None),
        P("lat", None),
        P("lat"),
        P("lat"),
        P("lat", None),
    )
    out_specs = (
        P("lat", "lev", None),
        P("lat", "lev", None),
        P("lat", "lev", None),
        P("lat", "lev", None),
    )
    return jax.shard_map(body, mesh=mesh, in_specs=in_specs, out_specs=out_specs, check_vma=False)
```

profile of v0, /device:TPU:23, one launch (start us, length us, event | category | flops | bytes accessed | tf_op | source)
XLA Modules:
  0.0 463.5 jit_solution(425486635717359174)
XLA Ops:
  3.2 2.6 collective-permute-start.1
  5.7 3.4 collective-permute-start.2
  19.3 4.0 copy.140
  23.3 4.9 %reshape.78 = f32[4,1,55296]{2,1,0:T(1,128)} reshape(f32[576,12,32]{2,1,0:T(8,128)} %bitcast.118) | data formatting | bytes 1769472
  28.2 7.7 %all-to-all-start.1 = ((f32[4,1,55296]{2,1,0:T(1,128)}), f32[4,1,55296]{2,1,0:T(1,128)S(1)}, u32[]{:S(2)}, u32[]{:S(2)}) async-start(f32[4,1,55296]{2,1,0:T(1,128)} %reshape.78), calls=%async_computation.1 | async-start | bytes 1769472 | tf_op jit(solution)/shard_map/all_to_all | solution.py:151
  36.0 3.1 copy.138
  39.0 5.0 %reshape.76 = f32[4,1,55296]{2,1,0:T(1,128)} reshape(f32[576,12,32]{2,1,0:T(8,128)} %bitcast.119) | data formatting | bytes 1769472
  44.0 7.3 %all-to-all-done.1 = f32[4,1,55296]{2,1,0:T(1,128)S(1)} async-done(((f32[4,1,55296]{2,1,0:T(1,128)}), f32[4,1,55296]{2,1,0:T(1,128)S(1)}, u32[]{:S(2)}, u32[]{:S(2)}) %all-to-all-start.1) | async-done | bytes 884768 | tf_op jit(solution)/shard_map/all_to_all | solution.py:151
  51.3 5.9 %all-to-all-start = ((f32[4,1,55296]{2,1,0:T(1,128)}), f32[4,1,55296]{2,1,0:T(1,128)S(1)}, u32[]{:S(2)}, u32[]{:S(2)}) async-start(f32[4,1,55296]{2,1,0:T(1,128)} %reshape.76), calls=%async_computation | async-start | bytes 1769472 | tf_op jit(solution)/shard_map/all_to_all | solution.py:150
  57.7 3.2 reduce.9
  61.0 3.9 reshape.79
  64.9 3.4 copy.141
  69.3 3.2 reduce.8
  72.6 3.9 reshape.77
  76.5 3.4 copy.139
  79.8 162.7 %while.18 = (s32[]{:T(128)}, f32[12,128,144]{1,2,0:T(8,128)}, f32[12,128,144]{1,2,0:T(8,128)}, f32[12,128,144]{1,2,0:T(8,128)}, f32[12,128,144]{1,2,0:T(8,128)},...) while((s32[]{:T(128)}, f32[12,128,144]{1,2,0:T(8,128)}, ...), condition=%wide.region_6.7_spmd, body=%wide.region_1.6_spmd.sunk | while | flops 71311176 | bytes 3455469 | solution.py:152
  81.7 9.9 %multiply_reduce_fusion.5 = (f32[32,144]{1,0:T(8,128)S(1)}, f32[32,144]{1,0:T(8,128)S(1)}, f32[32,144]{1,0:T(8,128)S(1)}, f32[32,144]{1,0:T(8,128)S(1)}) fusion(f32[128,144]{0,1:T(8,128)S(1)} %dynamic-slice_bitcast_fusion.2, f32[128,144]{0,1:T(8,128)S(1)} %copy.179, f32[32,144]{1,0:T(8,128)S(1)} %copy.180, f32[128,144]{0,1:T(8,128)S(1)} %copy.181, ...), kind=kLoop, calls=%fused_computation.3.clone.1 | loop fusion | flops 14137344 | bytes 442368 | tf_op jit(solution)/shard_map/while/body/eval_jaxpr/reduce_sum | solution.py:89
  95.3 9.9 %multiply_reduce_fusion.5 = (f32[32,144]{1,0:T(8,128)S(1)}, f32[32,144]{1,0:T(8,128)S(1)}, f32[32,144]{1,0:T(8,128)S(1)}, f32[32,144]{1,0:T(8,128)S(1)}) fusion(f32[128,144]{0,1:T(8,128)S(1)} %dynamic-slice_bitcast_fusion.2, f32[128,144]{0,1:T(8,128)S(1)} %copy.179, f32[32,144]{1,0:T(8,128)S(1)} %copy.180, f32[128,144]{0,1:T(8,128)S(1)} %copy.181, ...), kind=kLoop, calls=%fused_computation.3.clone.1 | loop fusion | flops 14137344 | bytes 442368 | tf_op jit(solution)/shard_map/while/body/eval_jaxpr/reduce_sum | solution.py:89
  108.8 9.9 %multiply_reduce_fusion.5 = (f32[32,144]{1,0:T(8,128)S(1)}, f32[32,144]{1,0:T(8,128)S(1)}, f32[32,144]{1,0:T(8,128)S(1)}, f32[32,144]{1,0:T(8,128)S(1)}) fusion(f32[128,144]{0,1:T(8,128)S(1)} %dynamic-slice_bitcast_fusion.2, f32[128,144]{0,1:T(8,128)S(1)} %copy.179, f32[32,144]{1,0:T(8,128)S(1)} %copy.180, f32[128,144]{0,1:T(8,128)S(1)} %copy.181, ...), kind=kLoop, calls=%fused_computation.3.clone.1 | loop fusion | flops 14137344 | bytes 442368 | tf_op jit(solution)/shard_map/while/body/eval_jaxpr/reduce_sum | solution.py:89
  122.3 9.9 %multiply_reduce_fusion.5 = (f32[32,144]{1,0:T(8,128)S(1)}, f32[32,144]{1,0:T(8,128)S(1)}, f32[32,144]{1,0:T(8,128)S(1)}, f32[32,144]{1,0:T(8,128)S(1)}) fusion(f32[128,144]{0,1:T(8,128)S(1)} %dynamic-slice_bitcast_fusion.2, f32[128,144]{0,1:T(8,128)S(1)} %copy.179, f32[32,144]{1,0:T(8,128)S(1)} %copy.180, f32[128,144]{0,1:T(8,128)S(1)} %copy.181, ...), kind=kLoop, calls=%fused_computation.3.clone.1 | loop fusion | flops 14137344 | bytes 442368 | tf_op jit(solution)/shard_map/while/body/eval_jaxpr/reduce_sum | solution.py:89
  135.8 9.9 %multiply_reduce_fusion.5 = (f32[32,144]{1,0:T(8,128)S(1)}, f32[32,144]{1,0:T(8,128)S(1)}, f32[32,144]{1,0:T(8,128)S(1)}, f32[32,144]{1,0:T(8,128)S(1)}) fusion(f32[128,144]{0,1:T(8,128)S(1)} %dynamic-slice_bitcast_fusion.2, f32[128,144]{0,1:T(8,128)S(1)} %copy.179, f32[32,144]{1,0:T(8,128)S(1)} %copy.180, f32[128,144]{0,1:T(8,128)S(1)} %copy.181, ...), kind=kLoop, calls=%fused_computation.3.clone.1 | loop fusion | flops 14137344 | bytes 442368 | tf_op jit(solution)/shard_map/while/body/eval_jaxpr/reduce_sum | solution.py:89
  149.4 9.9 %multiply_reduce_fusion.5 = (f32[32,144]{1,0:T(8,128)S(1)}, f32[32,144]{1,0:T(8,128)S(1)}, f32[32,144]{1,0:T(8,128)S(1)}, f32[32,144]{1,0:T(8,128)S(1)}) fusion(f32[128,144]{0,1:T(8,128)S(1)} %dynamic-slice_bitcast_fusion.2, f32[128,144]{0,1:T(8,128)S(1)} %copy.179, f32[32,144]{1,0:T(8,128)S(1)} %copy.180, f32[128,144]{0,1:T(8,128)S(1)} %copy.181, ...), kind=kLoop, calls=%fused_computation.3.clone.1 | loop fusion | flops 14137344 | bytes 442368 | tf_op jit(solution)/shard_map/while/body/eval_jaxpr/reduce_sum | solution.py:89
  162.9 9.9 %multiply_reduce_fusion.5 = (f32[32,144]{1,0:T(8,128)S(1)}, f32[32,144]{1,0:T(8,128)S(1)}, f32[32,144]{1,0:T(8,128)S(1)}, f32[32,144]{1,0:T(8,128)S(1)}) fusion(f32[128,144]{0,1:T(8,128)S(1)} %dynamic-slice_bitcast_fusion.2, f32[128,144]{0,1:T(8,128)S(1)} %copy.179, f32[32,144]{1,0:T(8,128)S(1)} %copy.180, f32[128,144]{0,1:T(8,128)S(1)} %copy.181, ...), kind=kLoop, calls=%fused_computation.3.clone.1 | loop fusion | flops 14137344 | bytes 442368 | tf_op jit(solution)/shard_map/while/body/eval_jaxpr/reduce_sum | solution.py:89
  176.4 9.9 %multiply_reduce_fusion.5 = (f32[32,144]{1,0:T(8,128)S(1)}, f32[32,144]{1,0:T(8,128)S(1)}, f32[32,144]{1,0:T(8,128)S(1)}, f32[32,144]{1,0:T(8,128)S(1)}) fusion(f32[128,144]{0,1:T(8,128)S(1)} %dynamic-slice_bitcast_fusion.2, f32[128,144]{0,1:T(8,128)S(1)} %copy.179, f32[32,144]{1,0:T(8,128)S(1)} %copy.180, f32[128,144]{0,1:T(8,128)S(1)} %copy.181, ...), kind=kLoop, calls=%fused_computation.3.clone.1 | loop fusion | flops 14137344 | bytes 442368 | tf_op jit(solution)/shard_map/while/body/eval_jaxpr/reduce_sum | solution.py:89
  189.9 9.9 %multiply_reduce_fusion.5 = (f32[32,144]{1,0:T(8,128)S(1)}, f32[32,144]{1,0:T(8,128)S(1)}, f32[32,144]{1,0:T(8,128)S(1)}, f32[32,144]{1,0:T(8,128)S(1)}) fusion(f32[128,144]{0,1:T(8,128)S(1)} %dynamic-slice_bitcast_fusion.2, f32[128,144]{0,1:T(8,128)S(1)} %copy.179, f32[32,144]{1,0:T(8,128)S(1)} %copy.180, f32[128,144]{0,1:T(8,128)S(1)} %copy.181, ...), kind=kLoop, calls=%fused_computation.3.clone.1 | loop fusion | flops 14137344 | bytes 442368 | tf_op jit(solution)/shard_map/while/body/eval_jaxpr/reduce_sum | solution.py:89
  203.5 9.9 %multiply_reduce_fusion.5 = (f32[32,144]{1,0:T(8,128)S(1)}, f32[32,144]{1,0:T(8,128)S(1)}, f32[32,144]{1,0:T(8,128)S(1)}, f32[32,144]{1,0:T(8,128)S(1)}) fusion(f32[128,144]{0,1:T(8,128)S(1)} %dynamic-slice_bitcast_fusion.2, f32[128,144]{0,1:T(8,128)S(1)} %copy.179, f32[32,144]{1,0:T(8,128)S(1)} %copy.180, f32[128,144]{0,1:T(8,128)S(1)} %copy.181, ...), kind=kLoop, calls=%fused_computation.3.clone.1 | loop fusion | flops 14137344 | bytes 442368 | tf_op jit(solution)/shard_map/while/body/eval_jaxpr/reduce_sum | solution.py:89
  217.0 9.9 %multiply_reduce_fusion.5 = (f32[32,144]{1,0:T(8,128)S(1)}, f32[32,144]{1,0:T(8,128)S(1)}, f32[32,144]{1,0:T(8,128)S(1)}, f32[32,144]{1,0:T(8,128)S(1)}) fusion(f32[128,144]{0,1:T(8,128)S(1)} %dynamic-slice_bitcast_fusion.2, f32[128,144]{0,1:T(8,128)S(1)} %copy.179, f32[32,144]{1,0:T(8,128)S(1)} %copy.180, f32[128,144]{0,1:T(8,128)S(1)} %copy.181, ...), kind=kLoop, calls=%fused_computation.3.clone.1 | loop fusion | flops 14137344 | bytes 442368 | tf_op jit(solution)/shard_map/while/body/eval_jaxpr/reduce_sum | solution.py:89
  230.5 9.9 %multiply_reduce_fusion.5 = (f32[32,144]{1,0:T(8,128)S(1)}, f32[32,144]{1,0:T(8,128)S(1)}, f32[32,144]{1,0:T(8,128)S(1)}, f32[32,144]{1,0:T(8,128)S(1)}) fusion(f32[128,144]{0,1:T(8,128)S(1)} %dynamic-slice_bitcast_fusion.2, f32[128,144]{0,1:T(8,128)S(1)} %copy.179, f32[32,144]{1,0:T(8,128)S(1)} %copy.180, f32[128,144]{0,1:T(8,128)S(1)} %copy.181, ...), kind=kLoop, calls=%fused_computation.3.clone.1 | loop fusion | flops 14137344 | bytes 442368 | tf_op jit(solution)/shard_map/while/body/eval_jaxpr/reduce_sum | solution.py:89
  242.5 2.8 copy.143
  245.4 2.8 reshape.80
  248.2 6.1 %all-to-all-start.2 = ((f32[4,1,55296]{2,1,0:T(1,128)}), f32[4,1,55296]{2,1,0:T(1,128)S(1)}, u32[]{:S(2)}, u32[]{:S(2)}) async-start(f32[4,1,55296]{2,1,0:T(1,128)} %reshape.80), calls=%async_computation.2 | async-start | bytes 1769472 | tf_op jit(solution)/shard_map/all_to_all | solution.py:158
  254.3 2.8 copy.149
  257.2 2.8 reshape.84
  260.0 5.7 %all-to-all-done.2 = f32[4,1,55296]{2,1,0:T(1,128)S(1)} async-done(((f32[4,1,55296]{2,1,0:T(1,128)}), f32[4,1,55296]{2,1,0:T(1,128)S(1)}, u32[]{:S(2)}, u32[]{:S(2)}) %all-to-all-start.2) | async-done | bytes 884768 | tf_op jit(solution)/shard_map/all_to_all | solution.py:158
  265.7 4.2 all-to-all-start.4
  269.9 2.8 copy.146
  272.7 2.8 reshape.82
  275.6 10.8 %all-to-all-done.4 = f32[4,1,55296]{2,1,0:T(1,128)} async-done(((f32[4,1,55296]{2,1,0:T(1,128)}), f32[4,1,55296]{2,1,0:T(1,128)}, u32[]{:S(2)}, u32[]{:S(2)}) %all-to-all-start.4) | async-done | bytes 884768 | tf_op jit(solution)/shard_map/all_to_all | solution.py:159
  286.3 9.2 %all-to-all-start.3 = ((f32[4,1,55296]{2,1,0:T(1,128)}), f32[4,1,55296]{2,1,0:T(1,128)}, u32[]{:S(2)}, u32[]{:S(2)}) async-start(f32[4,1,55296]{2,1,0:T(1,128)} %reshape.82), calls=%async_computation.3 | async-start | bytes 1769472 | tf_op jit(solution)/shard_map/all_to_all | solution.py:157
  295.6 2.8 copy.156
  298.4 2.8 reshape.86
  301.3 11.2 %all-to-all-done.3 = f32[4,1,55296]{2,1,0:T(1,128)} async-done(((f32[4,1,55296]{2,1,0:T(1,128)}), f32[4,1,55296]{2,1,0:T(1,128)}, u32[]{:S(2)}, u32[]{:S(2)}) %all-to-all-start.3) | async-done | bytes 884768 | tf_op jit(solution)/shard_map/all_to_all | solution.py:157
  312.4 9.7 %all-to-all-start.5 = ((f32[4,1,55296]{2,1,0:T(1,128)}), f32[4,1,55296]{2,1,0:T(1,128)}, u32[]{:S(2)}, u32[]{:S(2)}) async-start(f32[4,1,55296]{2,1,0:T(1,128)} %reshape.86), calls=%async_computation.5 | async-start | bytes 1769472 | tf_op jit(solution)/shard_map/all_to_all | solution.py:156
  324.1 4.2 reduce.10
  328.3 2.5 reshape.81
  333.0 2.4 all_to_all.89
  335.4 5.1 %reduce.12 = f32[4,55296]{1,0:T(4,128)} reduce(f32[4,1,55296]{2,1,0:T(1,128)} %all-to-all-done.4, f32[]{:T(128)} %broadcast.216), dimensions={1}, to_apply=%all_to_all.94.reduce_sub_computation | reduce | bytes 1769476 | tf_op jit(solution)/shard_map/all_to_all | solution.py:159
  340.5 2.5 reshape.85
  345.4 5.1 %reduce.11 = f32[4,55296]{1,0:T(4,128)} reduce(f32[4,1,55296]{2,1,0:T(1,128)} %all-to-all-done.3, f32[]{:T(128)} %broadcast.216), dimensions={1}, to_apply=%all_to_all.90.reduce_sub_computation | reduce | bytes 1769476 | tf_op jit(solution)/shard_map/all_to_all | solution.py:157
  350.4 4.0 reshape.83
  354.4 2.5 copy.147
  359.2 33.1 %collective-permute-start.3 = (f32[3,1,32,576]{3,2,1,0:T(8,128)}, f32[3,1,32,576]{3,2,1,0:T(8,128)}, u32[]{:S(2)}, u32[]{:S(2)}) collective-permute-start(f32[3,1,32,576]{3,2,1,0:T(8,128)} %pad_maximum_fusion.2), channel_id=1, source_target_pairs={{0,4},{4,8},{8,12},{12,16},{16,20},{20,24},{24,28},{28,32},{32,36}... | collective-permute-start | bytes 663560 | tf_op jit(solution)/shard_map/ppermute | solution.py:32
  398.4 3.1 slice.297
  403.6 3.1 slice.300
  406.7 3.8 copy.148
  415.2 2.8 all_to_all.97
  418.8 4.2 reduce.13
  422.9 2.8 reshape.87
  425.7 3.8 copy.158
  429.4 3.2 all_to_all.101
  433.7 4.0 fusion.60
  439.0 22.8 %conditional.1 = (f32[2,12,32,576]{3,2,1,0:T(8,128)S(1)}) conditional(s32[]{:T(128)} %convert_element_type.35, f32[2,12,32,576]{3,2,1,0:T(8,128)S(1)} %pad_maximum_fusion.1, (s32[1,576]{1,0:T(1,128)S(1)}, s32[]{:T(128)}, s32[1,576]{1,0:T(1,128)S(1)}, f32[576,576]{1,0:T(8,128)S(1)}, f32[576,576]{1,0:T(8,128)S(1)}, ...), branch_computations={%region_7.8_spmd, %region_8.9_spmd} | conditional | flops 6118176256 | bytes 11549968 | solution.py:112
  439.2 10.6 %fusion.13 = f32[576,2,12,32]{0,3,2,1:T(8,128)S(1)} fusion(f32[2,12,32,576]{3,2,1,0:T(8,128)S(1)} %get-tuple-element.209, f32[576,576]{1,0:T(8,128)S(1)} %get-tuple-element.215, f32[576]{0:T(1024)S(1)} %get-tuple-element.262, pred[576]{0:T(1024)(128)(4,1)S(1)} %get-tuple-element.261), kind=kOutput, calls=%fused_computation.33 | convolution fusion | flops 3058642944 | bytes 4868928 | tf_op jit(solution)/shard_map/cond/branch_1_fun/alkn,nc->alkc/dot_general | solution.py:98
  449.9 11.7 %fusion.11 = f32[2,12,32,576]{3,2,1,0:T(8,128)S(1)} fusion(f32[2,12,32,576]{3,2,1,0:T(8,128)S(1)} %get-tuple-element.209, f32[576,2,12,32]{0,3,2,1:T(8,128)S(1)} %fusion.13, f32[576,576]{1,0:T(8,128)S(1)} %get-tuple-element.215, f32[12,576]{1,0:T(8,128)S(1)} %get-tuple-element.213, f32[576]{0:T(1024)S(1)} %get-tuple-element.263, ...), kind=kOutput, calls=%fused_computation.31 | convolution fusion | flops 3059527680 | bytes 6666048 | tf_op jit(solution)/shard_map/cond/branch_1_fun/alkc,nc->alkn/dot_general | solution.py:99
  (384 shorter events, 81.9 us)
Async XLA Ops:
  0.6 1.8 copy-start
  0.6 8.6 %copy-start.10 = (f32[12,32,576]{2,1,0:T(8,128)S(1)}, f32[12,32,576]{2,1,0:T(8,128)}, u32[]{:S(2)}) copy-start(f32[12,32,576]{2,1,0:T(8,128)} %param.13) | copy-start | bytes 2654212
  3.2 11.4 %collective-permute-start.1 = (f32[2,1,32,576]{3,2,1,0:T(8,128)}, f32[2,1,32,576]{3,2,1,0:T(8,128)S(1)}, u32[]{:S(2)}, u32[]{:S(2)}) collective-permute-start(f32[2,1,32,576]{3,2,1,0:T(8,128)} %get-tuple-element.286), channel_id=1, source_target_pairs={{4,0},{8,4},{12,8},{16,12},{20,16},{24,20},{28,24},{32,28},{36,32}... | collective-permute-start | bytes 442376 | tf_op jit(solution)/shard_map/ppermute | solution.py:24
  5.7 8.9 %collective-permute-start.2 = (f32[2,1,32,576]{3,2,1,0:T(8,128)}, f32[2,1,32,576]{3,2,1,0:T(8,128)}, u32[]{:S(2)}, u32[]{:S(2)}) collective-permute-start(f32[2,1,32,576]{3,2,1,0:T(8,128)} %get-tuple-element.287), channel_id=1, source_target_pairs={{0,4},{4,8},{8,12},{12,16},{16,20},{20,24},{24,28},{28,32},{32,36}... | collective-permute-start | bytes 442376 | tf_op jit(solution)/shard_map/ppermute | solution.py:21
  9.8 6.2 %collective-permute-start = (f32[1,32,576]{2,1,0:T(8,128)}, f32[1,32,576]{2,1,0:T(8,128)}, u32[]{:S(2)}, u32[]{:S(2)}) collective-permute-start(f32[1,32,576]{2,1,0:T(8,128)} %slice.267), channel_id=1, source_target_pairs={{4,0},{8,4},{12,8},{16,12},{20,16},{24,20},{28,24},{32,28},{36,32}... | collective-permute-start | bytes 221192 | tf_op jit(solution)/shard_map/ppermute | solution.py:32
  28.2 23.0 %all-to-all-start.1 = ((f32[4,1,55296]{2,1,0:T(1,128)}), f32[4,1,55296]{2,1,0:T(1,128)S(1)}, u32[]{:S(2)}, u32[]{:S(2)}) async-start(f32[4,1,55296]{2,1,0:T(1,128)} %reshape.78), calls=%async_computation.1 | async-start | bytes 1769472 | tf_op jit(solution)/shard_map/all_to_all | solution.py:151
  51.3 18.1 %all-to-all-start = ((f32[4,1,55296]{2,1,0:T(1,128)}), f32[4,1,55296]{2,1,0:T(1,128)S(1)}, u32[]{:S(2)}, u32[]{:S(2)}) async-start(f32[4,1,55296]{2,1,0:T(1,128)} %reshape.76), calls=%async_computation | async-start | bytes 1769472 | tf_op jit(solution)/shard_map/all_to_all | solution.py:150
  248.2 17.5 %all-to-all-start.2 = ((f32[4,1,55296]{2,1,0:T(1,128)}), f32[4,1,55296]{2,1,0:T(1,128)S(1)}, u32[]{:S(2)}, u32[]{:S(2)}) async-start(f32[4,1,55296]{2,1,0:T(1,128)} %reshape.80), calls=%async_computation.2 | async-start | bytes 1769472 | tf_op jit(solution)/shard_map/all_to_all | solution.py:158
  265.7 20.6 %all-to-all-start.4 = ((f32[4,1,55296]{2,1,0:T(1,128)}), f32[4,1,55296]{2,1,0:T(1,128)}, u32[]{:S(2)}, u32[]{:S(2)}) async-start(f32[4,1,55296]{2,1,0:T(1,128)} %reshape.84), calls=%async_computation.4 | async-start | bytes 1769472 | tf_op jit(solution)/shard_map/all_to_all | solution.py:159
  286.3 26.1 %all-to-all-start.3 = ((f32[4,1,55296]{2,1,0:T(1,128)}), f32[4,1,55296]{2,1,0:T(1,128)}, u32[]{:S(2)}, u32[]{:S(2)}) async-start(f32[4,1,55296]{2,1,0:T(1,128)} %reshape.82), calls=%async_computation.3 | async-start | bytes 1769472 | tf_op jit(solution)/shard_map/all_to_all | solution.py:157
  298.4 23.7 %copy-start.17 = (s32[12]{0:T(128)S(1)}, s32[12]{0:T(128)}, u32[]{:S(2)}) copy-start(s32[12]{0:T(128)} %param.17) | copy-start | bytes 148
  298.4 23.7 %copy-start.15 = (f32[12,576]{1,0:T(8,128)S(1)}, f32[12,576]{1,0:T(8,128)}, u32[]{:S(2)}) copy-start(f32[12,576]{1,0:T(8,128)} %param.19) | copy-start | bytes 82948
  298.4 23.7 %copy-start.16 = (s32[12]{0:T(128)S(1)}, s32[12]{0:T(128)}, u32[]{:S(2)}) copy-start(s32[12]{0:T(128)} %param.18) | copy-start | bytes 148
  312.4 106.3 %all-to-all-start.5 = ((f32[4,1,55296]{2,1,0:T(1,128)}), f32[4,1,55296]{2,1,0:T(1,128)}, u32[]{:S(2)}, u32[]{:S(2)}) async-start(f32[4,1,55296]{2,1,0:T(1,128)} %reshape.86), calls=%async_computation.5 | async-start | bytes 1769472 | tf_op jit(solution)/shard_map/all_to_all | solution.py:156
  335.4 22.9 %copy-start.4 = (f32[12,32,576]{2,1,0:T(8,128)}, f32[12,32,576]{2,1,0:T(8,128)S(1)}, u32[]{:S(2)}) copy-start(f32[12,32,576]{2,1,0:T(8,128)S(1)} %all_to_all.89) | copy-start | bytes 2654212
  344.0 1.2 copy-start.5
  354.4 3.9 copy-start.13
  356.9 1.2 copy-start.7
  358.3 35.9 %copy-start.8 = (f32[12,128,144]{2,1,0:T(8,128)S(1)}, f32[12,128,144]{2,1,0:T(8,128)}, u32[]{:S(2)}) copy-start(f32[12,128,144]{2,1,0:T(8,128)} %copy-done.7) | copy-start | bytes 2654212
  358.4 37.1 %copy-start.2 = (f32[12,32,576]{2,1,0:T(8,128)}, f32[12,32,576]{2,1,0:T(8,128)S(1)}, u32[]{:S(2)}) copy-start(f32[12,32,576]{2,1,0:T(8,128)S(1)} %broadcast_add_fusion) | copy-start | bytes 2654212
  359.2 35.2 %copy-start.6 = (f32[12,128,144]{2,1,0:T(8,128)S(1)}, f32[12,128,144]{2,1,0:T(8,128)}, u32[]{:S(2)}) copy-start(f32[12,128,144]{2,1,0:T(8,128)} %copy-done.5) | copy-start | bytes 2654212
  359.2 73.4 %collective-permute-start.3 = (f32[3,1,32,576]{3,2,1,0:T(8,128)}, f32[3,1,32,576]{3,2,1,0:T(8,128)}, u32[]{:S(2)}, u32[]{:S(2)}) collective-permute-start(f32[3,1,32,576]{3,2,1,0:T(8,128)} %pad_maximum_fusion.2), channel_id=1, source_target_pairs={{0,4},{4,8},{8,12},{12,16},{16,20},{20,24},{24,28},{28,32},{32,36}... | collective-permute-start | bytes 663560 | tf_op jit(solution)/shard_map/ppermute | solution.py:32
  412.9 20.7 %copy-start.1 = (f32[12,32,576]{2,1,0:T(8,128)}, f32[12,32,576]{2,1,0:T(8,128)S(1)}, u32[]{:S(2)}) copy-start(f32[12,32,576]{2,1,0:T(8,128)S(1)} %all_to_all.93) | copy-start | bytes 2654212
  429.4 4.2 copy-start.3
  429.4 4.2 copy-start.11
  429.4 4.2 copy-start.14
  437.7 1.4 copy-start.9
  437.7 1.4 copy-start.12
where the time goes:
time: 470 us; the launch traced here: 463 us
  other arithmetic  173 us (37%)
  local copies, waits for them, and re-layouts  131 us (28%)
  starting transfers between devices  83.8 us (18%)
  matrix products  35.6 us (8%)
  waiting for transfers between devices  35.5 us (8%)
    reduce_sum x12, other arithmetic, remap_column(): pieces.append(jnp.sum(intersection * theta_col[None], axis=1))  119 us
    unnamed x48, local copies, waits for them, and re-layouts  44.4 us
    ppermute x2, starting transfers between devices, shifted(): return lax.ppermute(array, axis, pairs)  35 us
    while x5, local copies, waits for them, and re-layouts, body(): lax.map(one_row, (thick_cols, theta_cols))  11.8 us
    dot_general x1, matrix products, apply_filter(): jnp.einsum('alkc,nc->alkn', spectral * table[None, :, None, :], basis, pr...  11.7 us
    all_to_all x1, waiting for transfers between devices, body(): lax.all_to_all(theta_remap, 'lev', split_axis=1, concat_axis=2, tiled=True)  11.2 us
    all_to_all x1, waiting for transfers between devices, body(): lax.all_to_all(exner_mid, 'lev', split_axis=1, concat_axis=2, tiled=True)  10.8 us
    dot_general x12, matrix products, remap_column(): jnp.dot(strictly_below, layer_term, precision=HIGHEST) + 0.5 * layer_term  10.7 us
  transfers between devices with their start and end apart: 10, of which 5 were waited for; matrix products, arithmetic and copies ran while one was open for 23% of the time, Pallas kernels for 0%

commit v1 on v0

v1 whole, which is shorter than its diff:
```python
import math

import jax
import jax.numpy as jnp
import numpy as np
from jax import lax
from jax.experimental import pallas as pl
from jax.experimental.pallas import tpu as pltpu
from jax.sharding import PartitionSpec as P

TOP_PRESSURE = 0.01
HYBRID_SCALE = 0.2
EXNER_POWER = 2.0 / 7.0
COURANT = 0.012
HIGHEST = lax.Precision.HIGHEST
F32 = jnp.float32
BF16 = jnp.bfloat16
VMEM = pl.BlockSpec(memory_space=pltpu.VMEM)
SMEM = pl.BlockSpec(memory_space=pltpu.SMEM)
LANES = 128
ROLL_PAD = 64


def params(mib):
    return pltpu.CompilerParams(vmem_limit_bytes=mib * 1024 * 1024)


def fourier_tables(count):
    middle = count // 2
    ids = np.arange(count)
    wave = np.where(ids <= middle, ids, ids - middle)
    angle = 2.0 * np.pi / count * (ids[:, None] * wave[None, :] % count)
    edge = (ids == 0) | (ids == middle)
    weight = np.where(edge, 1.0 / math.sqrt(count), math.sqrt(2.0 / count))
    basis = np.where((ids <= middle)[None, :], np.cos(angle), np.sin(angle)) * weight[None, :]
    basis = basis.astype(np.float32)
    high = basis.astype(jnp.bfloat16)
    low = (basis - high.astype(np.float32)).astype(jnp.bfloat16)
    return high, low, wave.astype(np.int32)


def packed_rows(rows, width):
    return rows * width // LANES


def store_packed(ref, index, value):
    rows, width = value.shape
    full = width // LANES
    for tile in range(full):
        ref[(*index, pl.ds(tile * rows, rows), slice(None))] = value[:, tile * LANES : (tile + 1) * LANES]
    if width % LANES:
        rest = value[:, full * LANES :]
        half = rows // 2
        ref[(*index, pl.ds(full * rows, half), slice(None))] = jnp.concatenate([rest[:half], rest[half:]], axis=1)


def load_tile(ref, index, rows, width, tile):
    full = width // LANES
    if tile < full:
        return ref[(*index, pl.ds(tile * rows, rows), slice(None))]
    half = rows // 2
    both = ref[(*index, pl.ds(full * rows, half), slice(None))]
    return jnp.concatenate([both[:, : LANES // 2], both[:, LANES // 2 :]], axis=0)


def tile_count(width):
    return -(-width // LANES)


def advect_kernel(offsets, rows_each, coef, zonal, merid, thick, theta, halo_s, halo_n, out):
    lat_rows, levels, width = thick.shape

    def row_of(array, halo_low, halo_high, row):
        if row < 0:
            return halo_low
        return halo_high if row >= lat_rows else array[row]

    for owner in range(lat_rows // rows_each):
        for place, offset in enumerate(offsets):
            row = owner * rows_each + offset
            t = thick[row]
            h = theta[row] * t
            t_s = halo_s[0] if row == 0 else thick[row - 1]
            h_s = halo_s[1] if row == 0 else theta[row - 1] * t_s
            last = row == lat_rows - 1
            t_n = halo_n[0] if last else thick[row + 1]
            h_n = halo_n[1] if last else theta[row + 1] * t_n
            w_n = halo_n[2] if last else merid[row + 1]
            u = zonal[row] * (0.5 * COURANT)
            w_n = w_n * coef[1, row]
            w_s = merid[row] * coef[0, row]
            for field, (x, x_s, x_n) in enumerate(((t, t_s, t_n), (h, h_s, h_n))):
                flux = u * (x + jnp.roll(x, 1, axis=1))
                new = x - (jnp.roll(flux, -1, axis=1) - flux) - (w_n * (x_n + x) - w_s * (x + x_s))
                store_packed(out, (owner, place, field), new)


def target_edges(surface, sigma):
    curve = sigma * sigma
    return TOP_PRESSURE + HYBRID_SCALE * (sigma - curve) + (surface - TOP_PRESSURE) * curve


def target_thickness(surface, first, levels):
    step = 1.0 / levels
    curve = (2.0 * first + 1.0) * (step * step)
    return HYBRID_SCALE * (step - curve) + (surface - TOP_PRESSURE) * curve


def exner(pressure):
    return jnp.exp(EXNER_POWER * jnp.log(pressure))


def remap_kernel(width, block, columns, out):
    peers, count = columns.shape[0], columns.shape[1]
    levels = peers * block
    level_r = lax.broadcasted_iota(jnp.int32, (levels, levels), 0)
    level_c = lax.broadcasted_iota(jnp.int32, (levels, levels), 1)
    running = (level_r <= level_c).astype(F32)
    below = (
        lax.broadcasted_iota(jnp.int32, (8, levels), 1)
        >= block * (1 + lax.broadcasted_iota(jnp.int32, (8, levels), 0))
    ).astype(F32)
    full = width // LANES
    data_rows = packed_rows(block, width)
    for place in range(count):
        for tile in range(tile_count(width)):
            thick = jnp.concatenate(
                [load_tile(columns, (p, place, 0), block, width, tile) for p in range(peers)], axis=0
            )
            heat = jnp.concatenate(
                [load_tile(columns, (p, place, 1), block, width, tile) for p in range(peers)], axis=0
            )
            surface_row = TOP_PRESSURE + jnp.sum(thick, axis=0, keepdims=True)
            thick = thick.T
            heat = heat.T
            cols = thick.shape[0]
            upper = TOP_PRESSURE + jnp.dot(thick, running, precision=HIGHEST, preferred_element_type=F32)
            heat_sum = jnp.dot(heat, running, precision=HIGHEST, preferred_element_type=F32)
            theta = heat / thick
            surface = upper[:, levels - 1 :]
            lane = lax.broadcasted_iota(jnp.int32, (cols, levels), 1)
            lane_f = lane.astype(F32)
            edge = target_edges(surface, (lane_f + 1.0) * (1.0 / levels))
            at = jnp.zeros((cols, levels), jnp.int32)
            step = levels // 2
            while step:
                probe = jnp.take_along_axis(upper, at + (step - 1), axis=1, mode="promise_in_bounds")
                at = jnp.where(probe < edge, at + step, at)
                step //= 2
            pick = lambda table: jnp.take_along_axis(table, at, axis=1, mode="promise_in_bounds")
            heat_to = pick(heat_sum) - pick(theta) * (pick(upper) - edge)
            heat_from = jnp.where(lane == 0, 0.0, pltpu.roll(heat_to, 1, 1))
            theta_next = (heat_to - heat_from) / target_thickness(surface, lane_f, levels)
            exner_to = exner(edge)
            exner_from = jnp.where(lane == 0, TOP_PRESSURE**EXNER_POWER, pltpu.roll(exner_to, 1, 1))
            layer = theta_next * (exner_to - exner_from)
            bases = lax.dot_general(
                below, layer, (((1,), (1,)), ((), ())), precision=HIGHEST, preferred_element_type=F32
            )
            result = theta_next.T
            for p in range(peers):
                part = result[p * block : (p + 1) * block]
                if tile < full:
                    out[p, place, pl.ds(tile * block, block), :] = part
                else:
                    half = block // 2
                    out[p, place, pl.ds(full * block, half), :] = jnp.concatenate([part[:half], part[half:]], axis=1)
                out[p, place, pl.ds(data_rows + tile, 1), pl.ds(0, cols)] = surface_row
                out[p, place, pl.ds(data_rows + 8 + tile, 1), pl.ds(0, cols)] = bases[p : p + 1]


def below_sum(layer):
    rows, width = layer.shape
    groups = rows // 8
    carry = None
    pieces = []
    sub = lax.broadcasted_iota(jnp.int32, (8, width), 0)
    for g in reversed(range(groups)):
        x = layer[g * 8 : (g + 1) * 8]
        total = x
        for step in (1, 2, 4):
            total = total + jnp.where(sub < 8 - step, pltpu.roll(total, 8 - step, 0), 0.0)
        under = total - x
        if carry is not None:
            under = under + carry
            carry = carry + total[0:1]
        else:
            carry = total[0:1]
        pieces.append(under)
    return jnp.concatenate(pieces[::-1], axis=0)


def column_state(message, index, block, width, first_level, levels, ground):
    tiles = tile_count(width)
    data_rows = packed_rows(block, width)
    theta = jnp.concatenate([load_tile(message, index, block, width, t) for t in range(tiles)], axis=1)

    def line(first):
        return jnp.concatenate(
            [message[(*index, pl.ds(first + t, 1), pl.ds(0, min(LANES, width - t * LANES)))] for t in range(tiles)],
            axis=1,
        )

    surface = line(data_rows)
    base = line(data_rows + 8)
    sub = lax.broadcasted_iota(jnp.int32, (block, width), 0).astype(F32) + first_level
    thick = target_thickness(surface, sub, levels)
    top = exner(target_edges(surface, sub * (1.0 / levels)))
    bottom_edge = exner(target_edges(surface, (first_level + block) * (1.0 / levels)))
    sub_i = lax.broadcasted_iota(jnp.int32, (block, width), 0)
    bottom = jnp.where(sub_i == block - 1, bottom_edge, pltpu.roll(top, block - 1, 0))
    layer = theta * (bottom - top)
    geopot = (ground + base) + (below_sum(layer) + 0.5 * layer)
    return theta, thick, 0.5 * (top + bottom), geopot


def push(now, before):
    theta, exner_mid, geopot = now
    theta_b, exner_b, geopot_b = before
    return (geopot - geopot_b) + 0.5 * (theta + theta_b) * (exner_mid - exner_b)


def filtered(value, table, high, low, high_t, low_t, block):
    def product(x, b_high, b_low):
        x_high = x.astype(BF16)
        x_low = (x - x_high.astype(F32)).astype(BF16)
        dot = lambda a, b: jnp.dot(a, b, preferred_element_type=F32)
        return dot(x_high, b_high) + (dot(x_low, b_high) + dot(x_high, b_low))

    spectral = product(value, high, low)
    rows, width = value.shape
    spectral = (spectral.reshape(rows // block, block, width) * table[:, None, :]).reshape(rows, width)
    return value + product(spectral, high_t, low_t)


def final_kernel(
    levels, scalars, faces, message, south, ground, south_ground, zonal, merid, table,
    high, low, high_t, low_t, zonal_out, merid_out, thick_out, theta_out, carried,
):
    lat_rows, block, width = zonal.shape
    first_level = scalars[0].astype(F32)

    def state(ref, index, ground_row):
        theta, thick, mid, geopot = column_state(ref, index, block, width, first_level, levels, ground_row)
        return theta, thick, mid, geopot

    theta, _, mid, geopot = state(south, (0,), south_ground[...])
    carried[0] = theta
    carried[1] = mid
    carried[2] = geopot

    def one_row(row, _):
        theta, thick, mid, geopot = state(message, (row,), ground[pl.ds(row, 1), :])
        theta_out[row] = theta
        thick_out[row] = thick
        now = (theta, mid, geopot)
        zonal_out[row] = zonal[row] - push(now, tuple(jnp.roll(x, 1, axis=1) for x in now))
        merid_out[row] = merid[row] - faces[row] * push(now, (carried[0], carried[1], carried[2]))
        carried[0] = theta
        carried[1] = mid
        carried[2] = geopot
        return 0

    lax.fori_loop(0, lat_rows, one_row, 0)

    @pl.when(scalars[1] != 0)
    def _():
        step = 4
        for out in (zonal_out, merid_out):
            def some_rows(i, _):
                rows = pl.ds(i * step, step)
                value = out[rows].reshape(step * block, width)
                value = filtered(value, table[i], high[...], low[...], high_t[...], low_t[...], block)
                out[rows] = value.reshape(step, block, width)
                return 0
            lax.fori_loop(0, lat_rows // step, some_rows, 0)


def body(
    zonal_wind, meridional_wind, thickness, potential_temp, surface_geo, polar_mask, cutoff, damping
):
    lat_rows, block, width = zonal_wind.shape
    lat_count = lax.axis_size("lat")
    peers = lax.axis_size("lev")
    levels = block * peers
    total_rows = lat_rows * lat_count
    first_row = lax.axis_index("lat") * lat_rows
    row_ids = (first_row + jnp.arange(lat_rows + 1, dtype=jnp.int32)).astype(F32)
    faces = jnp.sin(math.pi * row_ids / total_rows)
    centres = jnp.sin(math.pi * (row_ids[:-1] + 0.5) / total_rows)
    coef = jnp.stack([faces[:-1], faces[1:]]) * (0.5 * COURANT) / centres
    northward = [(i, i + 1) for i in range(lat_count - 1)]
    southward = [(i + 1, i) for i in range(lat_count - 1)]
    heat_first = potential_temp[0] * thickness[0]
    heat_last = potential_temp[-1] * thickness[-1]
    halo_s = lax.ppermute(jnp.stack([thickness[-1], heat_last]), "lat", northward)
    halo_n = lax.ppermute(jnp.stack([thickness[0], heat_first, meridional_wind[0]]), "lat", southward)
    south_ground = lax.ppermute(surface_geo[-1:], "lat", northward)

    rows_each = lat_rows // peers
    offsets = tuple(range(rows_each))
    data_rows = packed_rows(block, width)
    message_rows = data_rows + 16
    sent = pl.pallas_call(
        lambda *refs: advect_kernel(offsets, rows_each, *refs),
        out_shape=jax.ShapeDtypeStruct((peers, len(offsets), 2, data_rows, LANES), F32),
        in_specs=[SMEM] + [VMEM] * 6,
        out_specs=VMEM,
        compiler_params=params(32),
        name="advect",
    )(coef, zonal_wind, meridional_wind, thickness, potential_temp, halo_s, halo_n)
    columns = lax.all_to_all(sent, "lev", split_axis=0, concat_axis=0, tiled=True)
    remapped = pl.pallas_call(
        lambda *refs: remap_kernel(width, block, *refs),
        out_shape=jax.ShapeDtypeStruct((peers, len(offsets), message_rows, LANES), F32),
        in_specs=[VMEM],
        out_specs=VMEM,
        compiler_params=params(32),
        name="remap",
    )(columns)
    message = lax.all_to_all(remapped, "lev", split_axis=0, concat_axis=0, tiled=True)
    message = message.reshape(lat_rows, message_rows, LANES)
    south = lax.ppermute(message[-1:], "lat", northward)

    high, low, wave = fourier_tables(width)
    active = (jnp.asarray(wave)[None, :] >= cutoff[:, None]) & (polar_mask[:, None] != 0)
    table = jnp.where(active, damping - 1.0, 0.0).reshape(lat_rows // 4, 4, width)
    scalars = jnp.stack([lax.axis_index("lev") * block, jnp.any(polar_mask != 0).astype(jnp.int32)])
    shape = jax.ShapeDtypeStruct((lat_rows, block, width), F32)
    return pl.pallas_call(
        lambda *refs: final_kernel(levels, *refs),
        out_shape=(shape,) * 4,
        in_specs=[SMEM, SMEM] + [VMEM] * 11,
        out_specs=(VMEM,) * 4,
        scratch_shapes=[pltpu.VMEM((3, block, width), F32)],
        compiler_params=params(48),
        name="final",
    )(
        scalars, faces, message, south, surface_geo, south_ground, zonal_wind, meridional_wind, table,
        jnp.asarray(high), jnp.asarray(low), jnp.asarray(high.T), jnp.asarray(low.T),
    )


def solution(mesh):
    field = P("lat", "lev", None)
    in_specs = (field, field, field, field, P("lat", None), P("lat"), P("lat"), P("lat", None))
    return jax.shard_map(body, mesh=mesh, in_specs=in_specs, out_specs=(field,) * 4, check_vma=False)
```

time: 470 us -> 136 us (0.29)
  the two profiles are of different devices: /device:TPU:23 before, /device:TPU:14 now
where the time goes in v1:
time: 136 us; the launch traced here: 135 us
  blocking collectives  52.1 us (38%)
  waiting for transfers between devices  29 us (21%)
  Pallas kernels  26.1 us (19%)
  starting transfers between devices  13.9 us (10%)
  local copies, waits for them, and re-layouts  10 us (7%)
  other arithmetic  2.05 us (2%)
  between operations  1.48 us (1%)
    all_to_all x1, blocking collectives, body(): lax.all_to_all(sent, 'lev', split_axis=0, concat_axis=0, tiled=True)  52.1 us
    all_to_all x1, waiting for transfers between devices, body(): lax.all_to_all(remapped, 'lev', split_axis=0, concat_axis=0, tiled=True)  20.9 us
    pallas_call x1, Pallas kernels, body(): pl.pallas_call(lambda *refs: final_kernel(levels, *refs), out_shape=(shap...  12 us
    pallas_call x1, Pallas kernels, body(): pl.pallas_call(lambda *refs: remap_kernel(width, block, *refs), out_shape...  9.77 us
    unnamed x30, local copies, waits for them, and re-layouts  9.04 us
    ppermute x1, waiting for transfers between devices, body(): south = lax.ppermute(message[-1:], 'lat', northward)  4.63 us
    ppermute x1, starting transfers between devices, body(): lax.ppermute(jnp.stack([thickness[0], heat_first, meridional_wind[0]]), '...  4.54 us
    pallas_call x1, Pallas kernels, body(): pl.pallas_call(lambda *refs: advect_kernel(offsets, rows_each, *refs), ou...  4.35 us
  transfers between devices with their start and end apart: 5, of which 3 were waited for; matrix products, arithmetic and copies ran while one was open for 1% of the time, Pallas kernels for 0%

profile of v1, /device:TPU:14, one launch (start us, length us, event | category | flops | bytes accessed | tf_op | source)
XLA Modules:
  0.0 134.7 jit_solution(18349007174856913361)
XLA Ops:
  0.6 0.0 copy-start
  0.6 1.1 slice_multiply_fusion
  1.8 1.9 %collective-permute-start = (f32[2,32,576]{2,1,0:T(8,128)S(1)}, f32[2,32,576]{2,1,0:T(8,128)S(1)}, u32[]{:S(2)}, u32[]{:S(2)}) collective-permute-start(f32[2,32,576]{2,1,0:T(8,128)S(1)} %pad_maximum_fusion.1), channel_id=1, source_target_pairs={{0,4},{4,8},{8,12},{12,16},{16,20},{20,24},{24,28},{28,32},{32,36}... | collective-permute-start | bytes 442376 | tf_op jit(solution)/shard_map/ppermute | solution.py:296
  3.7 0.9 slice.39
  4.6 4.5 %collective-permute-start.1 = (f32[3,32,576]{2,1,0:T(8,128)S(1)}, f32[3,32,576]{2,1,0:T(8,128)S(1)}, u32[]{:S(2)}, u32[]{:S(2)}) collective-permute-start(f32[3,32,576]{2,1,0:T(8,128)S(1)} %pad_maximum_fusion), channel_id=1, source_target_pairs={{4,0},{8,4},{12,8},{16,12},{20,16},{24,20},{28,24},{32,28},{36,32}... | collective-permute-start | bytes 663560 | tf_op jit(solution)/shard_map/ppermute | solution.py:297
  9.3 0.1 slice_bitcast_fusion.1
  9.4 0.0 collective-permute-done.refs_5_
  9.4 3.5 %collective-permute-done.1.refs_6_ = f32[3,32,576]{2,1,0:T(8,128)S(1)} collective-permute-done((f32[3,32,576]{2,1,0:T(8,128)S(1)}, f32[3,32,576]{2,1,0:T(8,128)S(1)}, u32[]{:S(2)}, u32[]{:S(2)}) %collective-permute-start.1) | collective-permute-done | bytes 221216 | tf_op jit(solution)/shard_map/ppermute | solution.py:297
  12.9 0.0 copy-done
  12.9 0.0 copy-start.1
  12.9 1.2 copy-done.1
  14.1 0.0 copy-start.4
  14.1 1.2 copy-done.4
  15.3 0.0 copy-start.5
  15.3 1.2 copy-done.5
  16.5 4.4 %advect.1 = f32[4,3,2,144,128]{4,3,2,1,0:T(8,128)S(1)} custom-call(f32[2,12]{1,0:T(2,128)S(1)} %fusion.refs_0_, f32[12,32,576]{2,1,0:T(8,128)S(1)} %copy-done.1, f32[12,32,576]{2,1,0:T(8,128)S(1)} %copy-done, f32[12,32,576]{2,1,0:T(8,128)S(1)} %copy-done.4, f32[12,32,576]{2,1,0:T(8,128)S(1)} %copy-done.5, f32[2,32,576]{2,1,0:T(8,128)S(1)} %collective-permute-done.refs_5_, ...), custom_call_target="tpu_custom_call" | custom-call | tf_op jit(solution)/shard_map/advect/pallas_call | solution.py:304
  20.8 52.1 %all_to_all.10.refs_0_ = f32[4,3,2,144,128]{4,3,2,1,0:T(8,128)S(1)} all-to-all(f32[4,3,2,144,128]{4,3,2,1,0:T(8,128)S(1)} %advect.1), channel_id=1, replica_groups=mesh['lat'=64,'lev'=4] {'lev'}, dimensions={0} | all-to-all | bytes 3538944 | tf_op jit(solution)/shard_map/all_to_all | solution.py:312
  72.9 0.0 copy-start.10
  72.9 0.0 copy-start.14
  72.9 0.0 copy-start.11
  72.9 0.0 copy-start.12
  73.0 0.0 copy-start.13
  73.0 9.8 %remap.1 = f32[4,3,160,128]{3,2,1,0:T(8,128)S(1)} custom-call(f32[4,3,2,144,128]{4,3,2,1,0:T(8,128)S(1)} %all_to_all.10.refs_0_), custom_call_target="tpu_custom_call" | custom-call | tf_op jit(solution)/shard_map/remap/pallas_call | solution.py:313
  82.7 0.0 copy-start.3
  82.8 0.9 copy-done.3
  83.7 0.0 copy-start.2
  83.7 3.6 %all-to-all-start.1 = ((f32[4,3,160,128]{3,2,1,0:T(8,128)}), f32[4,3,160,128]{3,2,1,0:T(8,128)S(1)}, u32[]{:S(2)}, u32[]{:S(2)}) async-start(f32[4,3,160,128]{3,2,1,0:T(8,128)} %copy-done.3), calls=%async_computation.1 | async-start | bytes 1966080 | tf_op jit(solution)/shard_map/all_to_all | solution.py:321
  87.3 0.0 copy-done.10
  87.4 1.9 %collective-permute-start.3 = (f32[1,576]{1,0:T(1,128)S(1)}, f32[1,576]{1,0:T(1,128)S(1)}, u32[]{:S(2)}, u32[]{:S(2)}) collective-permute-start(f32[1,576]{1,0:T(1,128)S(1)} %slice.41), channel_id=1, source_target_pairs={{0,4},{4,8},{8,12},{12,16},{16,20},{20,24},{24,28},{28,32},{32,36}... | collective-permute-start | bytes 6920 | tf_op jit(solution)/shard_map/ppermute | solution.py:298
  89.3 0.0 copy-done.14
  89.3 0.6 broadcast_compare_fusion
  90.6 0.0 copy-done.11
  90.6 0.0 copy-done.12
  90.6 0.0 copy-done.13
  90.6 0.1 add_select_fusion
  90.7 20.9 %all-to-all-done.1 = f32[4,3,160,128]{3,2,1,0:T(8,128)S(1)} async-done(((f32[4,3,160,128]{3,2,1,0:T(8,128)}), f32[4,3,160,128]{3,2,1,0:T(8,128)S(1)}, u32[]{:S(2)}, u32[]{:S(2)}) %all-to-all-start.1) | async-done | bytes 983072 | tf_op jit(solution)/shard_map/all_to_all | solution.py:321
  111.6 1.9 %collective-permute-start.2 = (f32[1,160,128]{2,1,0:T(8,128)S(1)}, f32[1,160,128]{2,1,0:T(8,128)S(1)}, u32[]{:S(2)}, u32[]{:S(2)}) collective-permute-start(f32[1,160,128]{2,1,0:T(8,128)S(1)} %slice.42), channel_id=1, source_target_pairs={{0,4},{4,8},{8,12},{12,16},{16,20},{20,24},{24,28},{28,32},{32,36}... | collective-permute-start | bytes 245768 | tf_op jit(solution)/shard_map/ppermute | solution.py:323
  113.5 0.1 pad_add_fusion.refs_0_
  113.6 0.0 collective-permute-done.3.refs_5_
  113.7 4.6 %collective-permute-done.2.refs_3_ = f32[1,160,128]{2,1,0:T(8,128)S(1)} collective-permute-done((f32[1,160,128]{2,1,0:T(8,128)S(1)}, f32[1,160,128]{2,1,0:T(8,128)S(1)}, u32[]{:S(2)}, u32[]{:S(2)}) %collective-permute-start.2) | collective-permute-done | bytes 81952 | tf_op jit(solution)/shard_map/ppermute | solution.py:323
  118.3 0.0 copy-done.2
  118.3 0.0 copy-start.6
  118.3 1.1 copy-done.6
  119.4 0.0 copy-start.7
  119.4 1.1 copy-done.7
  120.5 0.0 copy-start.8
  120.5 1.1 copy-done.8
  121.6 0.0 copy-start.9
  121.6 1.1 copy-done.9
  122.7 12.0 %final.1 = (f32[12,32,576]{2,1,0:T(8,128)}, f32[12,32,576]{2,1,0:T(8,128)}, f32[12,32,576]{2,1,0:T(8,128)}, f32[12,32,576]{2,1,0:T(8,128)}) custom-call(s32[2]{0:T(128)S(1)} %pad_add_fusion.refs_0_, f32[13]{0:T(128)S(1)} %multiply_sine_fusion.1.refs_1_, f32[12,160,128]{2,1,0:T(8,128)S(1)} %bitcast.8, f32[1,160,128]{2,1,0:T(8,128)S(1)} %collective-permute-done.2.refs_3_, ...), custom_call_target="tpu_custom_call" | custom-call | tf_op jit(solution)/shard_map/final/pallas_call | solution.py:330
  (9 shorter events, 0.2 us)
Async XLA Ops:
  0.6 12.2 %copy-start = (f32[12,32,576]{2,1,0:T(8,128)S(1)}, f32[12,32,576]{2,1,0:T(8,128)}, u32[]{:S(2)}) copy-start(f32[12,32,576]{2,1,0:T(8,128)} %refs_7_.1) | copy-start | bytes 2654212
  1.8 7.6 %collective-permute-start = (f32[2,32,576]{2,1,0:T(8,128)S(1)}, f32[2,32,576]{2,1,0:T(8,128)S(1)}, u32[]{:S(2)}, u32[]{:S(2)}) collective-permute-start(f32[2,32,576]{2,1,0:T(8,128)S(1)} %pad_maximum_fusion.1), channel_id=1, source_target_pairs={{0,4},{4,8},{8,12},{12,16},{16,20},{20,24},{24,28},{28,32},{32,36}... | collective-permute-start | bytes 442376 | tf_op jit(solution)/shard_map/ppermute | solution.py:296
  4.6 8.2 %collective-permute-start.1 = (f32[3,32,576]{2,1,0:T(8,128)S(1)}, f32[3,32,576]{2,1,0:T(8,128)S(1)}, u32[]{:S(2)}, u32[]{:S(2)}) collective-permute-start(f32[3,32,576]{2,1,0:T(8,128)S(1)} %pad_maximum_fusion), channel_id=1, source_target_pairs={{4,0},{8,4},{12,8},{16,12},{20,16},{24,20},{28,24},{32,28},{36,32}... | collective-permute-start | bytes 663560 | tf_op jit(solution)/shard_map/ppermute | solution.py:297
  12.9 1.2 copy-start.1
  14.1 1.2 copy-start.4
  15.3 1.2 copy-start.5
  72.9 14.4 %copy-start.10 = (f32[12,576]{1,0:T(8,128)S(1)}, f32[12,576]{1,0:T(8,128)}, u32[]{:S(2)}) copy-start(f32[12,576]{1,0:T(8,128)} %refs_4_.3) | copy-start | bytes 82948
  72.9 16.4 %copy-start.14 = (s32[12]{0:T(128)S(1)}, s32[12]{0:T(128)}, u32[]{:S(2)}) copy-start(s32[12]{0:T(128)} %param.18) | copy-start | bytes 148
  72.9 17.7 %copy-start.11 = (f32[12,576]{1,0:T(8,128)S(1)}, f32[12,576]{1,0:T(8,128)}, u32[]{:S(2)}) copy-start(f32[12,576]{1,0:T(8,128)} %param.20) | copy-start | bytes 82948
  72.9 17.7 %copy-start.12 = (s32[576]{0:T(1024)S(1)}, s32[576]{0:T(1024)}, u32[]{:S(2)}) copy-start(s32[576]{0:T(1024)} %constant.46.clone) | copy-start | bytes 6916
  73.0 17.7 %copy-start.13 = (s32[12]{0:T(128)S(1)}, s32[12]{0:T(128)}, u32[]{:S(2)}) copy-start(s32[12]{0:T(128)} %param.19) | copy-start | bytes 148
  82.7 0.9 copy-start.3
  83.7 34.6 %copy-start.2 = (f32[12,32,576]{2,1,0:T(8,128)S(1)}, f32[12,32,576]{2,1,0:T(8,128)}, u32[]{:S(2)}) copy-start(f32[12,32,576]{2,1,0:T(8,128)} %refs_6_.1) | copy-start | bytes 2654212
  83.7 27.9 %all-to-all-start.1 = ((f32[4,3,160,128]{3,2,1,0:T(8,128)}), f32[4,3,160,128]{3,2,1,0:T(8,128)S(1)}, u32[]{:S(2)}, u32[]{:S(2)}) async-start(f32[4,3,160,128]{3,2,1,0:T(8,128)} %copy-done.3), calls=%async_computation.1 | async-start | bytes 1966080 | tf_op jit(solution)/shard_map/all_to_all | solution.py:321
  87.4 26.3 %collective-permute-start.3 = (f32[1,576]{1,0:T(1,128)S(1)}, f32[1,576]{1,0:T(1,128)S(1)}, u32[]{:S(2)}, u32[]{:S(2)}) collective-permute-start(f32[1,576]{1,0:T(1,128)S(1)} %slice.41), channel_id=1, source_target_pairs={{0,4},{4,8},{8,12},{12,16},{16,20},{20,24},{24,28},{28,32},{32,36}... | collective-permute-start | bytes 6920 | tf_op jit(solution)/shard_map/ppermute | solution.py:298
  111.6 6.6 %collective-permute-start.2 = (f32[1,160,128]{2,1,0:T(8,128)S(1)}, f32[1,160,128]{2,1,0:T(8,128)S(1)}, u32[]{:S(2)}, u32[]{:S(2)}) collective-permute-start(f32[1,160,128]{2,1,0:T(8,128)S(1)} %slice.42), channel_id=1, source_target_pairs={{0,4},{4,8},{8,12},{12,16},{16,20},{20,24},{24,28},{28,32},{32,36}... | collective-permute-start | bytes 245768 | tf_op jit(solution)/shard_map/ppermute | solution.py:323
  118.3 1.1 copy-start.6
  119.4 1.1 copy-start.7
  120.5 1.1 copy-start.8
  121.6 1.1 copy-start.9

commit v2 on v1

v2 whole, which is shorter than its diff:
```python
import math

import jax
import jax.numpy as jnp
import numpy as np
from jax import lax
from jax.experimental import pallas as pl
from jax.experimental.pallas import tpu as pltpu
from jax.sharding import PartitionSpec as P

TOP_PRESSURE = 0.01
HYBRID_SCALE = 0.2
EXNER_POWER = 2.0 / 7.0
COURANT = 0.012
HIGHEST = lax.Precision.HIGHEST
F32 = jnp.float32
BF16 = jnp.bfloat16
VMEM = pl.BlockSpec(memory_space=pltpu.VMEM)
SMEM = pl.BlockSpec(memory_space=pltpu.SMEM)
LANES = 128


def params(mib):
    return pltpu.CompilerParams(vmem_limit_bytes=mib * 1024 * 1024)


def fourier_tables(count):
    middle = count // 2
    ids = np.arange(count)
    wave = np.where(ids <= middle, ids, ids - middle)
    angle = 2.0 * np.pi / count * (ids[:, None] * wave[None, :] % count)
    edge = (ids == 0) | (ids == middle)
    weight = np.where(edge, 1.0 / math.sqrt(count), math.sqrt(2.0 / count))
    basis = np.where((ids <= middle)[None, :], np.cos(angle), np.sin(angle)) * weight[None, :]
    basis = basis.astype(np.float32)
    high = basis.astype(jnp.bfloat16)
    low = (basis - high.astype(np.float32)).astype(jnp.bfloat16)
    return high, low, wave.astype(np.int32)


def packed_rows(rows, width):
    return rows * width // LANES


def store_packed(ref, index, value):
    rows, width = value.shape
    full = width // LANES
    for tile in range(full):
        ref[(*index, pl.ds(tile * rows, rows), slice(None))] = value[:, tile * LANES : (tile + 1) * LANES]
    if width % LANES:
        rest = value[:, full * LANES :]
        half = rows // 2
        ref[(*index, pl.ds(full * rows, half), slice(None))] = jnp.concatenate([rest[:half], rest[half:]], axis=1)


def load_tile(ref, index, rows, width, tile):
    full = width // LANES
    if tile < full:
        return ref[(*index, pl.ds(tile * rows, rows), slice(None))]
    half = rows // 2
    both = ref[(*index, pl.ds(full * rows, half), slice(None))]
    return jnp.concatenate([both[:, : LANES // 2], both[:, LANES // 2 :]], axis=0)


def tile_count(width):
    return -(-width // LANES)


def wrapped(me, step, peers):
    other = me + step
    return jnp.where(other >= peers, other - peers, other)


def advect_row(row, coef, zonal, merid, t, h, t_s, h_s, t_n, h_n, w_n):
    u = zonal[row] * (0.5 * COURANT)
    w_n = w_n * coef[1, row]
    w_s = merid[row] * coef[0, row]
    for x, x_s, x_n in ((t, t_s, t_n), (h, h_s, h_n)):
        flux = u * (x + jnp.roll(x, 1, axis=1))
        yield x - (jnp.roll(flux, -1, axis=1) - flux) - (w_n * (x_n + x) - w_s * (x + x_s))


def advect_inner_kernel(first, rows_each, me_ref, coef, zonal, merid, thick, theta, ground, *outs):
    lat_rows, levels, _ = thick.shape
    peers = len(outs) - 2
    to_north, to_south = outs[peers:]
    for step in range(peers):
        owner = wrapped(me_ref[0], step, peers)
        for place in range(rows_each):
            row = first + owner * rows_each + place
            t, t_s, t_n = thick[row], thick[row - 1], thick[row + 1]
            h, h_s, h_n = theta[row] * t, theta[row - 1] * t_s, theta[row + 1] * t_n
            fields = advect_row(row, coef, zonal, merid, t, h, t_s, h_s, t_n, h_n, merid[row + 1])
            for field, new in enumerate(fields):
                store_packed(outs[step], (place, field), new)
    top = lat_rows - 1
    to_north[pl.ds(0, levels), :] = thick[top]
    to_north[pl.ds(levels, levels), :] = theta[top] * thick[top]
    to_north[pl.ds(2 * levels, 1), :] = ground[pl.ds(top, 1), :]
    to_south[pl.ds(0, levels), :] = thick[0]
    to_south[pl.ds(levels, levels), :] = theta[0] * thick[0]
    to_south[pl.ds(2 * levels, levels), :] = merid[0]


def advect_outer_kernel(me_ref, coef, zonal, merid, thick, theta, halo_s, halo_n, *outs):
    lat_rows, levels, _ = thick.shape
    peers = len(outs)
    top = lat_rows - 1
    for step in range(peers):
        owner = wrapped(me_ref[0], step, peers)
        is_first, is_last = owner == 0, owner == peers - 1
        row = jnp.where(is_last, top, owner)
        low, high = jnp.maximum(row - 1, 0), jnp.minimum(row + 1, top)
        t, t_s, t_n = thick[row], thick[low], thick[high]
        h, h_s, h_n = theta[row] * t, theta[low] * t_s, theta[high] * t_n
        w_n = merid[high]
        part = lambda ref, i: ref[pl.ds(i * levels, levels), :]
        t_s = jnp.where(is_first, part(halo_s, 0), t_s)
        h_s = jnp.where(is_first, part(halo_s, 1), h_s)
        t_n = jnp.where(is_last, part(halo_n, 0), t_n)
        h_n = jnp.where(is_last, part(halo_n, 1), h_n)
        w_n = jnp.where(is_last, part(halo_n, 2), w_n)
        fields = advect_row(row, coef, zonal, merid, t, h, t_s, h_s, t_n, h_n, w_n)
        for field, new in enumerate(fields):
            store_packed(outs[step], (0, field), new)


def target_edges(surface, sigma):
    curve = sigma * sigma
    return TOP_PRESSURE + HYBRID_SCALE * (sigma - curve) + (surface - TOP_PRESSURE) * curve


def target_thickness(surface, first, levels):
    step = 1.0 / levels
    curve = (2.0 * first + 1.0) * (step * step)
    return HYBRID_SCALE * (step - curve) + (surface - TOP_PRESSURE) * curve


def exner(pressure):
    return jnp.exp(EXNER_POWER * jnp.log(pressure))


def remap_kernel(width, block, me_ref, *refs):
    peers = (len(refs) - 3) // 2
    parts, outs, (gathered, spread, base_rows) = refs[:peers], refs[peers : 2 * peers], refs[2 * peers :]
    count = parts[0].shape[0]
    levels = peers * block
    level_r = lax.broadcasted_iota(jnp.int32, (levels, levels), 0)
    level_c = lax.broadcasted_iota(jnp.int32, (levels, levels), 1)
    running = (level_r <= level_c).astype(F32)
    below = (
        lax.broadcasted_iota(jnp.int32, (8, levels), 1)
        >= block * (1 + lax.broadcasted_iota(jnp.int32, (8, levels), 0))
    ).astype(F32)
    full = width // LANES
    data_rows = packed_rows(block, width)
    half = block // 2
    sources = [wrapped(me_ref[0], (peers - step) % peers, peers) for step in range(peers)]
    targets = [wrapped(me_ref[0], step, peers) for step in range(peers)]
    for place in range(count):
        for tile in range(tile_count(width)):
            cols = min(LANES, width - tile * LANES)
            slot = tile % 2

            def whole_columns(field):
                for step in range(peers):
                    at = pl.ds(pl.multiple_of(sources[step] * block, block), block)
                    gathered[slot, field, at, pl.ds(0, cols)] = load_tile(parts[step], (place, field), block, width, tile)
                return gathered[slot, field, :, pl.ds(0, cols)]

            thick = whole_columns(0)
            heat = whole_columns(1)
            surface_row = TOP_PRESSURE + jnp.sum(thick, axis=0, keepdims=True)
            thick = thick.T
            heat = heat.T
            upper = TOP_PRESSURE + jnp.dot(thick, running, precision=HIGHEST, preferred_element_type=F32)
            heat_sum = jnp.dot(heat, running, precision=HIGHEST, preferred_element_type=F32)
            theta = heat / thick
            surface = upper[:, levels - 1 :]
            lane = lax.broadcasted_iota(jnp.int32, (cols, levels), 1)
            lane_f = lane.astype(F32)
            edge = target_edges(surface, (lane_f + 1.0) * (1.0 / levels))
            at = jnp.zeros((cols, levels), jnp.int32)
            jump = levels // 2
            while jump:
                probe = jnp.take_along_axis(upper, at + (jump - 1), axis=1, mode="promise_in_bounds")
                at = jnp.where(probe < edge, at + jump, at)
                jump //= 2
            pick = lambda table: jnp.take_along_axis(table, at, axis=1, mode="promise_in_bounds")
            heat_to = pick(heat_sum) - pick(theta) * (pick(upper) - edge)
            heat_from = jnp.where(lane == 0, 0.0, pltpu.roll(heat_to, 1, 1))
            theta_next = (heat_to - heat_from) / target_thickness(surface, lane_f, levels)
            exner_to = exner(edge)
            exner_from = jnp.where(lane == 0, TOP_PRESSURE**EXNER_POWER, pltpu.roll(exner_to, 1, 1))
            layer = theta_next * (exner_to - exner_from)
            base_rows[slot, :, pl.ds(0, cols)] = lax.dot_general(
                below, layer, (((1,), (1,)), ((), ())), precision=HIGHEST, preferred_element_type=F32
            )
            spread[slot, :, pl.ds(0, cols)] = theta_next.T
            for step in range(peers):
                out = outs[step]
                start = pl.multiple_of(targets[step] * block, block)
                if tile < full:
                    out[place, pl.ds(tile * block, block), :] = spread[slot, pl.ds(start, block), :]
                else:
                    part = spread[slot, pl.ds(start, block), pl.ds(0, cols)]
                    out[place, pl.ds(full * block, half), :] = jnp.concatenate([part[:half], part[half:]], axis=1)
                out[place, pl.ds(data_rows + tile, 1), pl.ds(0, cols)] = surface_row
                out[place, pl.ds(data_rows + 8 + tile, 1), pl.ds(0, cols)] = base_rows[
                    slot, pl.ds(targets[step], 1), pl.ds(0, cols)
                ]


def below_sum(layer):
    rows, width = layer.shape
    groups = rows // 8
    carry = None
    pieces = []
    sub = lax.broadcasted_iota(jnp.int32, (8, width), 0)
    for g in reversed(range(groups)):
        x = layer[g * 8 : (g + 1) * 8]
        total = x
        for step in (1, 2, 4):
            total = total + jnp.where(sub < 8 - step, pltpu.roll(total, 8 - step, 0), 0.0)
        under = total - x
        if carry is not None:
            under = under + carry
            carry = carry + total[0:1]
        else:
            carry = total[0:1]
        pieces.append(under)
    return jnp.concatenate(pieces[::-1], axis=0)


def column_state(message, index, block, width, first_level, levels, ground):
    tiles = tile_count(width)
    data_rows = packed_rows(block, width)
    theta = jnp.concatenate([load_tile(message, index, block, width, t) for t in range(tiles)], axis=1)

    def line(first):
        return jnp.concatenate(
            [message[(*index, pl.ds(first + t, 1), pl.ds(0, min(LANES, width - t * LANES)))] for t in range(tiles)],
            axis=1,
        )

    surface = line(data_rows)
    base = line(data_rows + 8)
    sub = lax.broadcasted_iota(jnp.int32, (block, width), 0).astype(F32) + first_level
    thick = target_thickness(surface, sub, levels)
    top = exner(target_edges(surface, sub * (1.0 / levels)))
    bottom_edge = exner(target_edges(surface, (first_level + block) * (1.0 / levels)))
    sub_i = lax.broadcasted_iota(jnp.int32, (block, width), 0)
    bottom = jnp.where(sub_i == block - 1, bottom_edge, pltpu.roll(top, block - 1, 0))
    layer = theta * (bottom - top)
    geopot = (ground + base) + (below_sum(layer) + 0.5 * layer)
    return theta, thick, 0.5 * (top + bottom), geopot


def push(now, before):
    theta, exner_mid, geopot = now
    theta_b, exner_b, geopot_b = before
    return (geopot - geopot_b) + 0.5 * (theta + theta_b) * (exner_mid - exner_b)


def filtered(value, table, high, low, high_t, low_t, block):
    def product(x, b_high, b_low):
        x_high = x.astype(BF16)
        x_low = (x - x_high.astype(F32)).astype(BF16)
        dot = lambda a, b: jnp.dot(a, b, preferred_element_type=F32)
        return dot(x_high, b_high) + (dot(x_low, b_high) + dot(x_high, b_low))

    spectral = product(value, high, low)
    rows, width = value.shape
    spectral = (spectral.reshape(rows // block, block, width) * table[:, None, :]).reshape(rows, width)
    return value + product(spectral, high_t, low_t)


def gather_messages(me, parts, order):
    peers = len(parts)
    for step, part in enumerate(parts):
        owner = wrapped(me, (peers - step) % peers, peers)
        for place in range(part.shape[0]):
            order[owner * part.shape[0] + place] = part[place]


def copy_all(copies, sems):
    started = [pltpu.make_async_copy(source, target, sems.at[i]) for i, (source, target) in enumerate(copies)]
    for copy in started:
        copy.start()
    return started


def filter_rows(ref, count, table, tables, block):
    width = ref.shape[-1]
    value = ref[pl.ds(0, count)].reshape(count * block, width)
    value = filtered(value, table, *(t[...] for t in tables), block)
    ref[pl.ds(0, count)] = value.reshape(count, block, width)


def around(x):
    return jnp.roll(x, 1, axis=1)


def inner_final_kernel(
    levels, first, scalars, faces, p0, p1, p2, p3, ground, zonal, merid, table,
    high, low, high_t, low_t,
    zonal_out, merid_out, thick_out, theta_out, edge_states,
    order, zonal_s, merid_s, thick_s, theta_s, carried, sems,
):
    _, block, width = zonal.shape
    count = order.shape[0]
    level = scalars[0].astype(F32) * float(block)
    gather_messages(scalars[0], (p0, p1, p2, p3), order)

    def one_row(i, _):
        row = first + i
        theta, thick, mid, geopot = column_state(order, (i,), block, width, level, levels, ground[pl.ds(row, 1), :])
        theta_s[i] = theta
        thick_s[i] = thick
        now = (theta, mid, geopot)
        zonal_s[i] = zonal[row] - push(now, tuple(around(x) for x in now))
        before = (carried[0], carried[1], carried[2])
        merid_s[jnp.maximum(i - 1, 0)] = merid[row] - faces[row] * push(now, before)
        for field, x in enumerate(now):
            carried[field] = x

        @pl.when(i == 0)
        def _():
            for field, x in enumerate(now):
                edge_states[0, field] = x

        return 0

    carried[...] = jnp.zeros_like(carried)
    lax.fori_loop(0, count, one_row, 0)
    for field in range(3):
        edge_states[1, field] = carried[field]
    early = copy_all(
        [(theta_s, theta_out.at[pl.ds(first, count)]), (thick_s, thick_out.at[pl.ds(first, count)])],
        sems.at[pl.ds(0, 2)],
    )

    @pl.when(scalars[1] != 0)
    def _():
        tables = (high, low, high_t, low_t)
        filter_rows(zonal_s, count, table[pl.ds(first, count), :], tables, block)
        filter_rows(merid_s, count - 1, table[pl.ds(first + 1, count - 1), :], tables, block)

    late = copy_all(
        [
            (zonal_s, zonal_out.at[pl.ds(first, count)]),
            (merid_s.at[pl.ds(0, count - 1)], merid_out.at[pl.ds(first + 1, count - 1)]),
        ],
        sems.at[pl.ds(2, 2)],
    )
    for copy in early + late:
        copy.wait()


def outer_zonal_kernel(
    levels, scalars, p0, p1, p2, p3, ground, zonal, table, high, low, high_t, low_t, zonal_in, thick_in, theta_in,
    zonal_out, thick_out, theta_out, states, order, zonal_s, thick_s, theta_s, sems,
):
    del zonal_in, thick_in, theta_in
    lat_rows, block, width = zonal.shape
    count = order.shape[0]
    level = scalars[0].astype(F32) * float(block)
    gather_messages(scalars[0], (p0, p1, p2, p3), order)
    rows = [*range(count - 1), lat_rows - 1]
    for i, row in enumerate(rows):
        theta, thick, mid, geopot = column_state(order, (i,), block, width, level, levels, ground[pl.ds(row, 1), :])
        theta_s[i] = theta
        thick_s[i] = thick
        now = (theta, mid, geopot)
        zonal_s[i] = zonal[row] - push(now, tuple(around(x) for x in now))
        for field, x in enumerate(now):
            states[i, field] = x

    def out_copies(source, target):
        low = count - 1
        return [
            (source.at[pl.ds(0, low)], target.at[pl.ds(0, low)]),
            (source.at[pl.ds(low, 1)], target.at[pl.ds(lat_rows - 1, 1)]),
        ]

    early = copy_all(out_copies(theta_s, theta_out) + out_copies(thick_s, thick_out), sems.at[pl.ds(0, 4)])

    @pl.when(scalars[1] != 0)
    def _():
        picked = jnp.concatenate([table[pl.ds(0, count - 1), :], table[pl.ds(lat_rows - 1, 1), :]], axis=0)
        filter_rows(zonal_s, count, picked, (high, low, high_t, low_t), block)

    late = copy_all(out_copies(zonal_s, zonal_out), sems.at[pl.ds(4, 2)])
    for copy in early + late:
        copy.wait()


def outer_merid_kernel(
    levels, scalars, faces, south, halo_s, states, edge_states, merid, table, high, low, high_t, low_t, merid_in,
    merid_out, merid_s, sems,
):
    del merid_in
    lat_rows, block, width = merid.shape
    level = scalars[0].astype(F32) * float(block)
    outer = states.shape[0]
    theta, _, mid, geopot = column_state(
        south, (0,), block, width, level, levels, halo_s[pl.ds(2 * block, 1), :]
    )
    before = (theta, mid, geopot)
    fields = lambda ref, i: tuple(ref[i, f] for f in range(3))
    top = lat_rows - 1
    steps = [(i, fields(states, i)) for i in range(outer - 1)] + [(outer - 1, fields(edge_states, 0))]
    for row, now in steps:
        merid_s[row] = merid[row] - faces[row] * push(now, before)
        before = now
    merid_s[outer] = merid[top] - faces[top] * push(fields(states, outer - 1), fields(edge_states, 1))

    @pl.when(scalars[1] != 0)
    def _():
        picked = jnp.concatenate([table[pl.ds(0, outer), :], table[pl.ds(top, 1), :]], axis=0)
        filter_rows(merid_s, outer + 1, picked, (high, low, high_t, low_t), block)

    late = copy_all(
        [
            (merid_s.at[pl.ds(0, outer)], merid_out.at[pl.ds(0, outer)]),
            (merid_s.at[pl.ds(outer, 1)], merid_out.at[pl.ds(top, 1)]),
        ],
        sems,
    )
    for copy in late:
        copy.wait()


def exchanged(parts):
    peers = lax.axis_size("lev")
    return [parts[0]] + [
        lax.ppermute(parts[step], "lev", [(i, (i + step) % peers) for i in range(peers)]) for step in range(1, peers)
    ]


def body(
    zonal_wind, meridional_wind, thickness, potential_temp, surface_geo, polar_mask, cutoff, damping
):
    lat_rows, block, width = zonal_wind.shape
    lat_count = lax.axis_size("lat")
    peers = lax.axis_size("lev")
    levels = block * peers
    total_rows = lat_rows * lat_count
    first_row = lax.axis_index("lat") * lat_rows
    row_ids = (first_row + jnp.arange(lat_rows + 1, dtype=jnp.int32)).astype(F32)
    faces = jnp.sin(math.pi * row_ids / total_rows)
    centres = jnp.sin(math.pi * (row_ids[:-1] + 0.5) / total_rows)
    coef = jnp.stack([faces[:-1], faces[1:]]) * (0.5 * COURANT) / centres
    northward = [(i, i + 1) for i in range(lat_count - 1)]
    southward = [(i + 1, i) for i in range(lat_count - 1)]
    me = lax.axis_index("lev").astype(jnp.int32)
    scalars = jnp.stack([me, jnp.any(polar_mask != 0).astype(jnp.int32)])
    shape = lambda *dims: jax.ShapeDtypeStruct(dims, F32)

    inner_each = lat_rows // peers - 1
    inner = inner_each * peers
    first = peers - 1
    data_rows = packed_rows(block, width)
    message_rows = data_rows + 16

    *inner_sent, to_north, to_south = pl.pallas_call(
        lambda *refs: advect_inner_kernel(first, inner_each, *refs),
        out_shape=[shape(inner_each, 2, data_rows, LANES)] * peers
        + [shape(2 * block + 8, width), shape(3 * block, width)],
        in_specs=[SMEM] * 2 + [VMEM] * 5,
        out_specs=[VMEM] * (peers + 2),
        compiler_params=params(16),
        name="advect_inner",
    )(scalars, coef, zonal_wind, meridional_wind, thickness, potential_temp, surface_geo)
    inner_columns = exchanged(inner_sent)
    halo_s = lax.ppermute(to_north, "lat", northward)
    halo_n = lax.ppermute(to_south, "lat", southward)
    outer_sent = pl.pallas_call(
        advect_outer_kernel,
        out_shape=[shape(1, 2, data_rows, LANES)] * peers,
        in_specs=[SMEM] * 2 + [VMEM] * 6,
        out_specs=[VMEM] * peers,
        compiler_params=params(16),
        name="advect_outer",
    )(scalars, coef, zonal_wind, meridional_wind, thickness, potential_temp, halo_s, halo_n)
    outer_columns = exchanged(outer_sent)

    def remap(columns, each, name):
        return pl.pallas_call(
            lambda *refs: remap_kernel(width, block, *refs),
            out_shape=[shape(each, message_rows, LANES)] * peers,
            in_specs=[SMEM] + [VMEM] * peers,
            out_specs=[VMEM] * peers,
            scratch_shapes=[
                pltpu.VMEM((2, 2, levels, LANES), F32),
                pltpu.VMEM((2, levels, LANES), F32),
                pltpu.VMEM((2, 8, LANES), F32),
            ],
            compiler_params=params(16),
            name=name,
        )(scalars, *columns)

    inner_messages = exchanged(remap(inner_columns, inner_each, "remap_inner"))
    outer_messages = exchanged(remap(outer_columns, 1, "remap_outer"))

    high, low, wave = fourier_tables(width)
    active = (jnp.asarray(wave)[None, :] >= cutoff[:, None]) & (polar_mask[:, None] != 0)
    table = jnp.where(active, damping - 1.0, 0.0)
    tables = [jnp.asarray(x) for x in (high, low, np.ascontiguousarray(high.T), np.ascontiguousarray(low.T))]
    field = shape(lat_rows, block, width)
    hbm = pl.BlockSpec(memory_space=pltpu.HBM)
    rows_of = lambda n: pltpu.VMEM((n, block, width), F32)

    zonal_next, merid_next, thick_next, theta_next, edge_states = pl.pallas_call(
        lambda *refs: inner_final_kernel(levels, first, *refs),
        out_shape=[field] * 4 + [shape(2, 3, block, width)],
        in_specs=[SMEM] * 2 + [VMEM] * (peers + 8),
        out_specs=[hbm] * 4 + [VMEM],
        scratch_shapes=[pltpu.VMEM((inner, message_rows, LANES), F32)]
        + [rows_of(inner)] * 4
        + [rows_of(3), pltpu.SemaphoreType.DMA((4,))],
        compiler_params=params(24),
        name="final_inner",
    )(scalars, faces, *inner_messages, surface_geo, zonal_wind, meridional_wind, table, *tables)

    owner_of_last = peers - 1
    step_of_last = (me + peers - owner_of_last) % peers
    last_message = outer_messages[0]
    for step in range(1, peers):
        last_message = jnp.where(step_of_last == step, outer_messages[step], last_message)
    south = lax.ppermute(last_message, "lat", northward)

    outer = peers
    aliased = 2 + peers + 3 + 4 - 1
    zonal_next, thick_next, theta_next, states = pl.pallas_call(
        lambda *refs: outer_zonal_kernel(levels, *refs),
        out_shape=[field] * 3 + [shape(outer, 3, block, width)],
        in_specs=[SMEM] + [VMEM] * (peers + 7) + [hbm] * 3,
        out_specs=[hbm] * 3 + [VMEM],
        scratch_shapes=[pltpu.VMEM((outer, message_rows, LANES), F32)]
        + [rows_of(outer)] * 3
        + [pltpu.SemaphoreType.DMA((6,))],
        input_output_aliases={aliased: 0, aliased + 1: 1, aliased + 2: 2},
        compiler_params=params(16),
        name="final_outer_zonal",
    )(
        scalars, *outer_messages, surface_geo, zonal_wind, table, *tables, zonal_next, thick_next, theta_next
    )
    merid_next = pl.pallas_call(
        lambda *refs: outer_merid_kernel(levels, *refs),
        out_shape=field,
        in_specs=[SMEM] * 2 + [VMEM] * 10 + [hbm],
        out_specs=hbm,
        scratch_shapes=[rows_of(outer + 1), pltpu.SemaphoreType.DMA((2,))],
        input_output_aliases={12: 0},
        compiler_params=params(16),
        name="final_outer_merid",
    )(scalars, faces, south, halo_s, states, edge_states, meridional_wind, table, *tables, merid_next)
    return zonal_next, merid_next, thick_next, theta_next


def solution(mesh):
    field = P("lat", "lev", None)
    in_specs = (field, field, field, field, P("lat", None), P("lat"), P("lat"), P("lat", None))
    return jax.shard_map(body, mesh=mesh, in_specs=in_specs, out_specs=(field,) * 4, check_vma=False)
```

time: 136 us -> 133 us (0.978)
  the two profiles are of different devices: /device:TPU:14 before, /device:TPU:1 now
where the time goes in v2:
time: 133 us
  waiting for transfers between devices  46.9 us (35%)
  starting transfers between devices  37.9 us (28%)
  Pallas kernels  32.5 us (24%)
  local copies, waits for them, and re-layouts  11.9 us (9%)
  other arithmetic  1.82 us (1%)
  between operations  1.69 us (1%)
    ppermute x12, waiting for transfers between devices, exchanged(): lax.ppermute(parts[step], 'lev', [(i, (i + step) % peers) for i in range(...  44.4 us
    ppermute x12, starting transfers between devices, exchanged(): lax.ppermute(parts[step], 'lev', [(i, (i + step) % peers) for i in range(...  26.4 us
    pallas_call x2, Pallas kernels, remap(): pl.pallas_call(lambda *refs: remap_kernel(width, block, *refs), out_shape...  13.4 us
    unnamed x44, local copies, waits for them, and re-layouts  11.8 us
    pallas_call x1, Pallas kernels, body(): pl.pallas_call(lambda *refs: inner_final_kernel(levels, first, *refs), ou...  6.96 us
    ppermute x1, starting transfers between devices, body(): halo_n = lax.ppermute(to_south, 'lat', southward)  5.14 us
    ppermute x1, starting transfers between devices, body(): south = lax.ppermute(last_message, 'lat', northward)  4.39 us
    pallas_call x1, Pallas kernels, body(): pl.pallas_call(lambda *refs: outer_zonal_kernel(levels, *refs), out_shape...  3.83 us
  transfers between devices with their start and end apart: 15, of which 6 were waited for; matrix products, arithmetic and copies ran while one was open for 1% of the time, Pallas kernels for 18%

profile of v2, /device:TPU:1, one launch (start us, length us, event | category | flops | bytes accessed | tf_op | source)
XLA Modules:
  0.0 132.7 jit_solution(15975175446870783891)
XLA Ops:
  0.7 0.0 copy-start.21
  0.7 0.6 copy-done.21
  1.3 0.6 broadcast_compare_fusion
  2.6 0.1 slice_bitcast_fusion.1
  2.7 0.1 pad_add_fusion.refs_0_.me_ref
  2.8 0.0 copy-start
  2.8 1.2 copy-done
  4.0 1.2 copy-done.2
  5.2 1.2 copy-done.8
  6.4 1.2 copy-done.9
  7.6 0.8 copy-done.12
  8.4 3.8 %advect_inner.1 = (f32[2,2,144,128]{3,2,1,0:T(8,128)S(1)}, f32[2,2,144,128]{3,2,1,0:T(8,128)S(1)}, f32[2,2,144,128]{3,2,1,0:T(8,128)}, f32[2,2,144,128]{3,2,1,0:...) custom-call(s32[2]{0:T(128)S(1)} %pad_add_fusion.refs_0_.me_ref, f32[2,12]{1,0:T(2,128)S(1)} %fusion.refs_1_.coef, ...), custom_call_target="tpu_custom_call" | custom-call | tf_op jit(solution)/shard_map/advect_inner/pallas_call | solution.py:466
  12.2 0.7 copy-done.14
  12.9 5.1 %collective-permute-start.1 = (f32[96,576]{1,0:T(8,128)S(1)}, f32[96,576]{1,0:T(8,128)S(1)}, u32[]{:S(2)}, u32[]{:S(2)}) collective-permute-start(f32[96,576]{1,0:T(8,128)S(1)} %get-tuple-element.32), channel_id=1, source_target_pairs={{4,0},{8,4},{12,8},{16,12},{20,16},{24,20},{28,24},{32,28},{36,32}... | collective-permute-start | bytes 663560 | tf_op jit(solution)/shard_map/ppermute | solution.py:477
  18.0 1.9 %collective-permute-start = (f32[72,576]{1,0:T(8,128)S(1)}, f32[72,576]{1,0:T(8,128)S(1)}, u32[]{:S(2)}, u32[]{:S(2)}) collective-permute-start(f32[72,576]{1,0:T(8,128)S(1)} %get-tuple-element.31), channel_id=1, source_target_pairs={{0,4},{4,8},{8,12},{12,16},{16,20},{20,24},{24,28},{28,32},{32,36}... | collective-permute-start | bytes 497672 | tf_op jit(solution)/shard_map/ppermute | solution.py:476
  20.0 2.5 %collective-permute-done.halo_s.refs_3_ = f32[72,576]{1,0:T(8,128)S(1)} collective-permute-done((f32[72,576]{1,0:T(8,128)S(1)}, f32[72,576]{1,0:T(8,128)S(1)}, u32[]{:S(2)}, u32[]{:S(2)}) %collective-permute-start) | collective-permute-done | bytes 165920 | tf_op jit(solution)/shard_map/ppermute | solution.py:476
  22.4 0.0 collective-permute-done.1.halo_n
  22.4 1.7 %advect_outer.1 = (f32[1,2,144,128]{3,2,1,0:T(8,128)S(1)}, f32[1,2,144,128]{3,2,1,0:T(8,128)S(1)}, f32[1,2,144,128]{3,2,1,0:T(8,128)S(1)}, f32[1,2,144,128]{3,2,1,0:T(8,128)S(1)}) custom-call(s32[2]{0:T(128)S(1)} %pad_add_fusion.refs_0_.me_ref, f32[2,12]{1,0:T(2,128)S(1)} %fusion.refs_1_.coef, f32[12,32,576]{2,1,0:T(8,128)S(1)} %copy-done.2, ...), custom_call_target="tpu_custom_call" | custom-call | tf_op jit(solution)/shard_map/advect_outer/pallas_call | solution.py:478
  24.1 2.9 %collective-permute-start.2 = (f32[1,2,144,128]{3,2,1,0:T(8,128)S(1)}, f32[1,2,144,128]{3,2,1,0:T(8,128)S(1)}, u32[]{:S(2)}, u32[]{:S(2)}) collective-permute-start(f32[1,2,144,128]{3,2,1,0:T(8,128)S(1)} %get-tuple-element.34), channel_id=1, source_target_pairs={{0,1},{1,2},{2,3},{3,0},{4,5},{5,6},{6,7},{7,4},{8,9},{9,10},{10,1... | collective-permute-start | bytes 442376 | tf_op jit(solution)/shard_map/ppermute | solution.py:437
  27.0 3.7 %collective-permute-start.8 = (f32[2,2,144,128]{3,2,1,0:T(8,128)S(1)}, f32[2,2,144,128]{3,2,1,0:T(8,128)S(1)}, u32[]{:S(2)}, u32[]{:S(2)}) collective-permute-start(f32[2,2,144,128]{3,2,1,0:T(8,128)S(1)} %get-tuple-element.42), channel_id=1, source_target_pairs={{0,1},{1,2},{2,3},{3,0},{4,5},{5,6},{6,7},{7,4},{8,9},{9,10},{10,1... | collective-permute-start | bytes 884744 | tf_op jit(solution)/shard_map/ppermute | solution.py:437
  30.7 1.0 collective-permute-start.9
  31.7 3.5 %collective-permute-start.10 = (f32[2,2,144,128]{3,2,1,0:T(8,128)}, f32[2,2,144,128]{3,2,1,0:T(8,128)}, u32[]{:S(2)}, u32[]{:S(2)}) collective-permute-start(f32[2,2,144,128]{3,2,1,0:T(8,128)} %get-tuple-element.44), channel_id=1, source_target_pairs={{0,3},{1,0},{2,1},{3,2},{4,7},{5,4},{6,5},{7,6},{8,11},{9,8},{10,9... | collective-permute-start | bytes 884744 | tf_op jit(solution)/shard_map/ppermute | solution.py:437
  35.2 0.9 collective-permute-start.3
  36.1 0.0 collective-permute-done.2.refs_2_
  36.1 1.3 collective-permute-start.4
  37.4 18.0 %collective-permute-done.3.refs_3_ = f32[1,2,144,128]{3,2,1,0:T(8,128)S(1)} collective-permute-done((f32[1,2,144,128]{3,2,1,0:T(8,128)S(1)}, f32[1,2,144,128]{3,2,1,0:T(8,128)S(1)}, u32[]{:S(2)}, u32[]{:S(2)}) %collective-permute-start.3) | collective-permute-done | bytes 147488 | tf_op jit(solution)/shard_map/ppermute | solution.py:437
  55.3 17.7 %collective-permute-done.4.refs_4_ = f32[1,2,144,128]{3,2,1,0:T(8,128)S(1)} collective-permute-done((f32[1,2,144,128]{3,2,1,0:T(8,128)S(1)}, f32[1,2,144,128]{3,2,1,0:T(8,128)S(1)}, u32[]{:S(2)}, u32[]{:S(2)}) %collective-permute-start.4) | collective-permute-done | bytes 147488 | tf_op jit(solution)/shard_map/ppermute | solution.py:437
  73.0 5.0 %remap_outer.1 = (f32[1,160,128]{2,1,0:T(8,128)S(1)}, f32[1,160,128]{2,1,0:T(8,128)}, f32[1,160,128]{2,1,0:T(8,128)}, f32[1,160,128]{2,1,0:T(8,128)}) custom-call(s32[2]{0:T(128)S(1)} %pad_add_fusion.refs_0_.me_ref, f32[1,2,144,128]{3,2,1,0:T(8,128)S(1)} %get-tuple-element.33.refs_1_, f32[1,2,144,128]{3,2,1,0:T(8,128)S(1)} %collective-permute-done.2.refs_2_, ...), custom_call_target="tpu_custom_call" | custom-call | tf_op jit(solution)/shard_map/remap_outer/pallas_call | solution.py:489
  78.1 0.0 collective-permute-start.5
  78.1 6.3 %collective-permute-start.6 = (f32[1,160,128]{2,1,0:T(8,128)}, f32[1,160,128]{2,1,0:T(8,128)}, u32[]{:S(2)}, u32[]{:S(2)}) collective-permute-start(f32[1,160,128]{2,1,0:T(8,128)} %get-tuple-element.39), channel_id=1, source_target_pairs={{0,2},{1,3},{2,0},{3,1},{4,6},{5,7},{6,4},{7,5},{8,10},{9,11},{10,... | collective-permute-start | bytes 245768 | tf_op jit(solution)/shard_map/ppermute | solution.py:437
  84.3 0.0 collective-permute-done.8.refs_2_
  84.3 0.7 copy-done.16
  85.1 1.1 collective-permute-start.7
  86.2 0.0 collective-permute-done.9.refs_3_
  86.2 0.0 collective-permute-done.10.refs_4_
  86.2 1.0 copy-done.15
  87.2 1.0 copy-done.17
  88.1 8.3 %remap_inner.1 = (f32[2,160,128]{2,1,0:T(8,128)S(1)}, f32[2,160,128]{2,1,0:T(8,128)S(1)}, f32[2,160,128]{2,1,0:T(8,128)S(1)}, f32[2,160,128]{2,1,0:T(8,128)S(1)}) custom-call(s32[2]{0:T(128)S(1)} %pad_add_fusion.refs_0_.me_ref, f32[2,2,144,128]{3,2,1,0:T(8,128)S(1)} %copy-done.15, f32[2,2,144,128]{3,2,1,0:T(8,128)S(1)} %copy-done.17, ...), custom_call_target="tpu_custom_call" | custom-call | tf_op jit(solution)/shard_map/remap_inner/pallas_call | solution.py:489
  96.5 1.3 collective-permute-start.11
  97.7 1.0 collective-permute-start.12
  98.8 0.0 collective-permute-done.5.refs_2_
  98.8 3.5 %collective-permute-start.13 = (f32[2,160,128]{2,1,0:T(8,128)S(1)}, f32[2,160,128]{2,1,0:T(8,128)S(1)}, u32[]{:S(2)}, u32[]{:S(2)}) collective-permute-start(f32[2,160,128]{2,1,0:T(8,128)S(1)} %get-tuple-element.48), channel_id=1, source_target_pairs={{0,3},{1,0},{2,1},{3,2},{4,7},{5,4},{6,5},{7,6},{8,11},{9,8},{10,9... | collective-permute-start | bytes 491528 | tf_op jit(solution)/shard_map/ppermute | solution.py:437
  102.3 0.0 collective-permute-done.6.refs_3_
  102.3 0.0 collective-permute-done.7.refs_4_
  102.3 0.0 copy-start.19
  102.3 0.9 select_select_fusion
  103.2 0.0 copy-start.20
  103.2 4.4 %collective-permute-start.14 = (f32[1,160,128]{2,1,0:T(8,128)S(1)}, f32[1,160,128]{2,1,0:T(8,128)S(1)}, u32[]{:S(2)}, u32[]{:S(2)}) collective-permute-start(f32[1,160,128]{2,1,0:T(8,128)S(1)} %select_select_fusion), channel_id=1, source_target_pairs={{0,4},{4,8},{8,12},{12,16},{16,20},{20,24},{24,28},{28,32},{32,36}... | collective-permute-start | bytes 245768 | tf_op jit(solution)/shard_map/ppermute | solution.py:531
  107.6 0.0 copy-start.13
  107.7 0.1 add_select_fusion.refs_9_.refs_7_
  107.7 2.2 %collective-permute-done.11.refs_3_ = f32[2,160,128]{2,1,0:T(8,128)S(1)} collective-permute-done((f32[2,160,128]{2,1,0:T(8,128)S(1)}, f32[2,160,128]{2,1,0:T(8,128)S(1)}, u32[]{:S(2)}, u32[]{:S(2)}) %collective-permute-start.11) | collective-permute-done | bytes 163872 | tf_op jit(solution)/shard_map/ppermute | solution.py:437
  110.0 1.2 collective-permute-done.12.refs_4_
  111.2 5.3 %collective-permute-done.13.refs_5_ = f32[2,160,128]{2,1,0:T(8,128)S(1)} collective-permute-done((f32[2,160,128]{2,1,0:T(8,128)S(1)}, f32[2,160,128]{2,1,0:T(8,128)S(1)}, u32[]{:S(2)}, u32[]{:S(2)}) %collective-permute-start.13) | collective-permute-done | bytes 163872 | tf_op jit(solution)/shard_map/ppermute | solution.py:437
  116.5 0.0 copy-done.3
  116.5 0.0 copy-done.1
  116.5 0.0 copy-done.13
  116.5 0.0 copy-start.6
  116.5 1.1 copy-done.6
  117.6 1.1 copy-done.7
  118.8 7.0 %final_inner.1 = (f32[12,32,576]{2,1,0:T(8,128)}, f32[12,32,576]{2,1,0:T(8,128)}, f32[12,32,576]{2,1,0:T(8,128)}, f32[12,32,576]{2,1,0:T(8,128)}, f32[2,3,32,576]{3,2,1,0:T(8,128)S(1)}) custom-call(s32[2]{0:T(128)S(1)} %pad_add_fusion.refs_0_.me_ref, f32[13]{0:T(128)S(1)} %multiply_sine_fusion.1.refs_1_, f32[2,160,128]{2,1,0:T(8,128)S(1)} %get-tuple-element.45.refs_2_, ...), custom_call_target="tpu_custom_call" | custom-call | tf_op jit(solution)/shard_map/final_inner/pallas_call | solution.py:514
  125.7 0.0 copy-start.11
  125.7 3.8 %final_outer_zonal.1 = (f32[12,32,576]{2,1,0:T(8,128)}, f32[12,32,576]{2,1,0:T(8,128)}, f32[12,32,576]{2,1,0:T(8,128)}, f32[4,3,32,576]{3,2,1,0:T(8,128)S(1)}) custom-call(s32[2]{0:T(128)S(1)} %pad_add_fusion.refs_0_.me_ref, f32[1,160,128]{2,1,0:T(8,128)S(1)} %get-tuple-element.37.refs_1_, ...), custom_call_target="tpu_custom_call", output_to_operand_aliasing={{0}: (12, {}), {1}: (13, {}), {2}: (14, {})} | custom-call | tf_op jit(solution)/shard_map/final_outer_zonal/pallas_call | solution.py:535
  129.6 0.0 collective-permute-done.14.refs_2_
  129.6 3.0 %final_outer_merid.1 = f32[12,32,576]{2,1,0:T(8,128)} custom-call(s32[2]{0:T(128)S(1)} %pad_add_fusion.refs_0_.me_ref, f32[13]{0:T(128)S(1)} %multiply_sine_fusion.1.refs_1_, f32[1,160,128]{2,1,0:T(8,128)S(1)} %collective-permute-done.14.refs_2_, f32[72,576]{1,0:T(8,128)S(1)} %copy-done.11, ...), custom_call_target="tpu_custom_call", output_to_operand_aliasing={{}: (12, {})} | custom-call | tf_op jit(solution)/shard_map/final_outer_merid/pallas_call | solution.py:549
  (26 shorter events, 0.1 us)
Async XLA Ops:
  0.7 0.7 copy-start.21
  2.8 1.2 copy-start
  4.0 1.2 copy-start.2
  5.2 1.2 copy-start.8
  6.4 1.2 copy-start.9
  7.6 0.8 copy-start.12
  12.2 0.7 copy-start.14
  12.9 9.5 %collective-permute-start.1 = (f32[96,576]{1,0:T(8,128)S(1)}, f32[96,576]{1,0:T(8,128)S(1)}, u32[]{:S(2)}, u32[]{:S(2)}) collective-permute-start(f32[96,576]{1,0:T(8,128)S(1)} %get-tuple-element.32), channel_id=1, source_target_pairs={{4,0},{8,4},{12,8},{16,12},{20,16},{24,20},{28,24},{32,28},{36,32}... | collective-permute-start | bytes 663560 | tf_op jit(solution)/shard_map/ppermute | solution.py:477
  18.0 4.4 %collective-permute-start = (f32[72,576]{1,0:T(8,128)S(1)}, f32[72,576]{1,0:T(8,128)S(1)}, u32[]{:S(2)}, u32[]{:S(2)}) collective-permute-start(f32[72,576]{1,0:T(8,128)S(1)} %get-tuple-element.31), channel_id=1, source_target_pairs={{0,4},{4,8},{8,12},{12,16},{16,20},{20,24},{24,28},{28,32},{32,36}... | collective-permute-start | bytes 497672 | tf_op jit(solution)/shard_map/ppermute | solution.py:476
  22.4 1.7 %copy-start.10 = (f32[72,576]{1,0:T(8,128)}, f32[72,576]{1,0:T(8,128)S(1)}, u32[]{:S(2)}) copy-start(f32[72,576]{1,0:T(8,128)S(1)} %collective-permute-done.halo_s.refs_3_) | copy-start | bytes 497668
  22.4 94.1 %copy-start.4 = (bf16[576,576]{1,0:T(8,128)(2,1)S(1)}, bf16[576,576]{1,0:T(8,128)(2,1)}, u32[]{:S(2)}) copy-start(bf16[576,576]{1,0:T(8,128)(2,1)} %constant.64.clone.refs_10_.refs_8_) | copy-start | bytes 1990660
  22.4 94.1 %copy-start.5 = (bf16[576,576]{1,0:T(8,128)(2,1)S(1)}, bf16[576,576]{1,0:T(8,128)(2,1)}, u32[]{:S(2)}) copy-start(bf16[576,576]{1,0:T(8,128)(2,1)} %constant.65.clone.refs_11_.refs_9_) | copy-start | bytes 1990660
  24.1 12.0 %collective-permute-start.2 = (f32[1,2,144,128]{3,2,1,0:T(8,128)S(1)}, f32[1,2,144,128]{3,2,1,0:T(8,128)S(1)}, u32[]{:S(2)}, u32[]{:S(2)}) collective-permute-start(f32[1,2,144,128]{3,2,1,0:T(8,128)S(1)} %get-tuple-element.34), channel_id=1, source_target_pairs={{0,1},{1,2},{2,3},{3,0},{4,5},{5,6},{6,7},{7,4},{8,9},{9,10},{10,1... | collective-permute-start | bytes 442376 | tf_op jit(solution)/shard_map/ppermute | solution.py:437
  27.0 57.4 %collective-permute-start.8 = (f32[2,2,144,128]{3,2,1,0:T(8,128)S(1)}, f32[2,2,144,128]{3,2,1,0:T(8,128)S(1)}, u32[]{:S(2)}, u32[]{:S(2)}) collective-permute-start(f32[2,2,144,128]{3,2,1,0:T(8,128)S(1)} %get-tuple-element.42), channel_id=1, source_target_pairs={{0,1},{1,2},{2,3},{3,0},{4,5},{5,6},{6,7},{7,4},{8,9},{9,10},{10,1... | collective-permute-start | bytes 884744 | tf_op jit(solution)/shard_map/ppermute | solution.py:437
  30.7 55.5 %collective-permute-start.9 = (f32[2,2,144,128]{3,2,1,0:T(8,128)}, f32[2,2,144,128]{3,2,1,0:T(8,128)}, u32[]{:S(2)}, u32[]{:S(2)}) collective-permute-start(f32[2,2,144,128]{3,2,1,0:T(8,128)} %get-tuple-element.43), channel_id=1, source_target_pairs={{0,2},{1,3},{2,0},{3,1},{4,6},{5,7},{6,4},{7,5},{8,10},{9,11},{10,... | collective-permute-start | bytes 884744 | tf_op jit(solution)/shard_map/ppermute | solution.py:437
  31.7 54.5 %collective-permute-start.10 = (f32[2,2,144,128]{3,2,1,0:T(8,128)}, f32[2,2,144,128]{3,2,1,0:T(8,128)}, u32[]{:S(2)}, u32[]{:S(2)}) collective-permute-start(f32[2,2,144,128]{3,2,1,0:T(8,128)} %get-tuple-element.44), channel_id=1, source_target_pairs={{0,3},{1,0},{2,1},{3,2},{4,7},{5,4},{6,5},{7,6},{8,11},{9,8},{10,9... | collective-permute-start | bytes 884744 | tf_op jit(solution)/shard_map/ppermute | solution.py:437
  35.2 20.1 %collective-permute-start.3 = (f32[1,2,144,128]{3,2,1,0:T(8,128)S(1)}, f32[1,2,144,128]{3,2,1,0:T(8,128)S(1)}, u32[]{:S(2)}, u32[]{:S(2)}) collective-permute-start(f32[1,2,144,128]{3,2,1,0:T(8,128)S(1)} %get-tuple-element.35), channel_id=1, source_target_pairs={{0,2},{1,3},{2,0},{3,1},{4,6},{5,7},{6,4},{7,5},{8,10},{9,11},{10,... | collective-permute-start | bytes 442376 | tf_op jit(solution)/shard_map/ppermute | solution.py:437
  36.1 36.9 %collective-permute-start.4 = (f32[1,2,144,128]{3,2,1,0:T(8,128)S(1)}, f32[1,2,144,128]{3,2,1,0:T(8,128)S(1)}, u32[]{:S(2)}, u32[]{:S(2)}) collective-permute-start(f32[1,2,144,128]{3,2,1,0:T(8,128)S(1)} %get-tuple-element.36), channel_id=1, source_target_pairs={{0,3},{1,0},{2,1},{3,2},{4,7},{5,4},{6,5},{7,6},{8,11},{9,8},{10,9... | collective-permute-start | bytes 442376 | tf_op jit(solution)/shard_map/ppermute | solution.py:437
  73.0 43.5 %copy-start.3 = (f32[12,32,576]{2,1,0:T(8,128)S(1)}, f32[12,32,576]{2,1,0:T(8,128)}, u32[]{:S(2)}) copy-start(f32[12,32,576]{2,1,0:T(8,128)} %refs_6_.6) | copy-start | bytes 2654212
  78.1 38.4 %copy-start.1 = (f32[12,32,576]{2,1,0:T(8,128)S(1)}, f32[12,32,576]{2,1,0:T(8,128)}, u32[]{:S(2)}) copy-start(f32[12,32,576]{2,1,0:T(8,128)} %refs_6_.7) | copy-start | bytes 2654212
  78.1 20.7 %collective-permute-start.5 = (f32[1,160,128]{2,1,0:T(8,128)}, f32[1,160,128]{2,1,0:T(8,128)}, u32[]{:S(2)}, u32[]{:S(2)}) collective-permute-start(f32[1,160,128]{2,1,0:T(8,128)} %get-tuple-element.38), channel_id=1, source_target_pairs={{0,1},{1,2},{2,3},{3,0},{4,5},{5,6},{6,7},{7,4},{8,9},{9,10},{10,1... | collective-permute-start | bytes 245768 | tf_op jit(solution)/shard_map/ppermute | solution.py:437
  78.1 24.2 %collective-permute-start.6 = (f32[1,160,128]{2,1,0:T(8,128)}, f32[1,160,128]{2,1,0:T(8,128)}, u32[]{:S(2)}, u32[]{:S(2)}) collective-permute-start(f32[1,160,128]{2,1,0:T(8,128)} %get-tuple-element.39), channel_id=1, source_target_pairs={{0,2},{1,3},{2,0},{3,1},{4,6},{5,7},{6,4},{7,5},{8,10},{9,11},{10,... | collective-permute-start | bytes 245768 | tf_op jit(solution)/shard_map/ppermute | solution.py:437
  84.3 0.7 copy-start.16
  85.1 17.2 %collective-permute-start.7 = (f32[1,160,128]{2,1,0:T(8,128)}, f32[1,160,128]{2,1,0:T(8,128)}, u32[]{:S(2)}, u32[]{:S(2)}) collective-permute-start(f32[1,160,128]{2,1,0:T(8,128)} %get-tuple-element.40), channel_id=1, source_target_pairs={{0,3},{1,0},{2,1},{3,2},{4,7},{5,4},{6,5},{7,6},{8,11},{9,8},{10,9... | collective-permute-start | bytes 245768 | tf_op jit(solution)/shard_map/ppermute | solution.py:437
  86.2 1.0 copy-start.15
  87.2 1.0 copy-start.17
  96.5 13.5 %collective-permute-start.11 = (f32[2,160,128]{2,1,0:T(8,128)S(1)}, f32[2,160,128]{2,1,0:T(8,128)S(1)}, u32[]{:S(2)}, u32[]{:S(2)}) collective-permute-start(f32[2,160,128]{2,1,0:T(8,128)S(1)} %get-tuple-element.46), channel_id=1, source_target_pairs={{0,1},{1,2},{2,3},{3,0},{4,5},{5,6},{6,7},{7,4},{8,9},{9,10},{10,1... | collective-permute-start | bytes 491528 | tf_op jit(solution)/shard_map/ppermute | solution.py:437
  97.7 13.4 %collective-permute-start.12 = (f32[2,160,128]{2,1,0:T(8,128)S(1)}, f32[2,160,128]{2,1,0:T(8,128)S(1)}, u32[]{:S(2)}, u32[]{:S(2)}) collective-permute-start(f32[2,160,128]{2,1,0:T(8,128)S(1)} %get-tuple-element.47), channel_id=1, source_target_pairs={{0,2},{1,3},{2,0},{3,1},{4,6},{5,7},{6,4},{7,5},{8,10},{9,11},{10,... | collective-permute-start | bytes 491528 | tf_op jit(solution)/shard_map/ppermute | solution.py:437
  98.8 17.7 %collective-permute-start.13 = (f32[2,160,128]{2,1,0:T(8,128)S(1)}, f32[2,160,128]{2,1,0:T(8,128)S(1)}, u32[]{:S(2)}, u32[]{:S(2)}) collective-permute-start(f32[2,160,128]{2,1,0:T(8,128)S(1)} %get-tuple-element.48), channel_id=1, source_target_pairs={{0,3},{1,0},{2,1},{3,2},{4,7},{5,4},{6,5},{7,6},{8,11},{9,8},{10,9... | collective-permute-start | bytes 491528 | tf_op jit(solution)/shard_map/ppermute | solution.py:437
  102.3 5.4 %copy-start.18 = (f32[12,576]{1,0:T(8,128)S(1)}, f32[12,576]{1,0:T(8,128)}, u32[]{:S(2)}) copy-start(f32[12,576]{1,0:T(8,128)} %param.20) | copy-start | bytes 82948
  102.3 5.4 %copy-start.19 = (s32[576]{0:T(1024)S(1)}, s32[576]{0:T(1024)}, u32[]{:S(2)}) copy-start(s32[576]{0:T(1024)} %constant.63.clone) | copy-start | bytes 6916
  103.2 4.4 %copy-start.20 = (s32[12]{0:T(128)S(1)}, s32[12]{0:T(128)}, u32[]{:S(2)}) copy-start(s32[12]{0:T(128)} %param.19) | copy-start | bytes 148
  103.2 26.4 %collective-permute-start.14 = (f32[1,160,128]{2,1,0:T(8,128)S(1)}, f32[1,160,128]{2,1,0:T(8,128)S(1)}, u32[]{:S(2)}, u32[]{:S(2)}) collective-permute-start(f32[1,160,128]{2,1,0:T(8,128)S(1)} %select_select_fusion), channel_id=1, source_target_pairs={{0,4},{4,8},{8,12},{12,16},{16,20},{20,24},{24,28},{28,32},{32,36}... | collective-permute-start | bytes 245768 | tf_op jit(solution)/shard_map/ppermute | solution.py:531
  107.6 8.9 %copy-start.13 = (f32[12,576]{1,0:T(8,128)S(1)}, f32[12,576]{1,0:T(8,128)}, u32[]{:S(2)}) copy-start(f32[12,576]{1,0:T(8,128)} %refs_5_.3) | copy-start | bytes 82948
  116.5 1.1 copy-start.6
  117.6 1.1 copy-start.7
  125.7 3.9 %copy-start.11 = (f32[72,576]{1,0:T(8,128)S(1)}, f32[72,576]{1,0:T(8,128)}, u32[]{:S(2)}) copy-start(f32[72,576]{1,0:T(8,128)} %copy-done.10) | copy-start | bytes 497668

commit v3 on v2

v3 whole, which is shorter than its diff:
```python
import math

import jax
import jax.numpy as jnp
import numpy as np
from jax import lax
from jax.experimental import pallas as pl
from jax.experimental.pallas import tpu as pltpu
from jax.sharding import PartitionSpec as P

TOP_PRESSURE = 0.01
HYBRID_SCALE = 0.2
EXNER_POWER = 2.0 / 7.0
COURANT = 0.012
HIGHEST = lax.Precision.HIGHEST
F32 = jnp.float32
BF16 = jnp.bfloat16
VMEM = pl.BlockSpec(memory_space=pltpu.VMEM)
SMEM = pl.BlockSpec(memory_space=pltpu.SMEM)
LANES = 128


def params(mib):
    return pltpu.CompilerParams(vmem_limit_bytes=mib * 1024 * 1024)


def cost(microseconds):
    return pl.CostEstimate(
        flops=int(microseconds * 1.1e9), bytes_accessed=int(microseconds * 3.6e6), transcendentals=0
    )


def fourier_tables(count):
    middle = count // 2
    ids = np.arange(count)
    wave = np.where(ids <= middle, ids, ids - middle)
    angle = 2.0 * np.pi / count * (ids[:, None] * wave[None, :] % count)
    edge = (ids == 0) | (ids == middle)
    weight = np.where(edge, 1.0 / math.sqrt(count), math.sqrt(2.0 / count))
    basis = np.where((ids <= middle)[None, :], np.cos(angle), np.sin(angle)) * weight[None, :]
    basis = basis.astype(np.float32)
    high = basis.astype(jnp.bfloat16)
    low = (basis - high.astype(np.float32)).astype(jnp.bfloat16)
    return high, low, wave.astype(np.int32)


def packed_rows(rows, width):
    return rows * width // LANES


def store_packed(ref, index, value):
    rows, width = value.shape
    full = width // LANES
    for tile in range(full):
        ref[(*index, pl.ds(tile * rows, rows), slice(None))] = value[:, tile * LANES : (tile + 1) * LANES]
    if width % LANES:
        rest = value[:, full * LANES :]
        half = rows // 2
        ref[(*index, pl.ds(full * rows, half), slice(None))] = jnp.concatenate([rest[:half], rest[half:]], axis=1)


def load_tile(ref, index, rows, width, tile):
    full = width // LANES
    if tile < full:
        return ref[(*index, pl.ds(tile * rows, rows), slice(None))]
    half = rows // 2
    both = ref[(*index, pl.ds(full * rows, half), slice(None))]
    return jnp.concatenate([both[:, : LANES // 2], both[:, LANES // 2 :]], axis=0)


def tile_count(width):
    return -(-width // LANES)


def wrapped(me, step, peers):
    other = me + step
    return jnp.where(other >= peers, other - peers, other)


def advect_row(row, coef, zonal, merid, t, h, t_s, h_s, t_n, h_n, w_n):
    u = zonal * (0.5 * COURANT)
    w_n = w_n * coef[1, row]
    w_s = merid * coef[0, row]
    for x, x_s, x_n in ((t, t_s, t_n), (h, h_s, h_n)):
        flux = u * (x + jnp.roll(x, 1, axis=1))
        yield x - (jnp.roll(flux, -1, axis=1) - flux) - (w_n * (x_n + x) - w_s * (x + x_s))


def advect_inner_kernel(first, rows_each, peers, coef, *refs):
    sources, outs, held, sems = refs[:5], refs[5 : 5 + peers + 2], refs[-6:-1], refs[-1]
    for copy in copy_all(list(zip(sources, held)), sems):
        copy.wait()
    zonal, merid, thick, theta, ground = held
    lat_rows, levels, _ = thick.shape
    to_north, to_south = outs[peers:]
    me = lax.axis_index("lev")
    for step in range(peers):
        owner = wrapped(me, step, peers)
        for place in range(rows_each):
            row = first + owner * rows_each + place
            t, t_s, t_n = thick[row], thick[row - 1], thick[row + 1]
            h, h_s, h_n = theta[row] * t, theta[row - 1] * t_s, theta[row + 1] * t_n
            fields = advect_row(row, coef, zonal[row], merid[row], t, h, t_s, h_s, t_n, h_n, merid[row + 1])
            for field, new in enumerate(fields):
                store_packed(outs[step], (place, field), new)
    top = lat_rows - 1
    to_north[pl.ds(0, levels), :] = thick[top]
    to_north[pl.ds(levels, levels), :] = theta[top] * thick[top]
    to_north[pl.ds(2 * levels, 1), :] = ground[pl.ds(top, 1), :]
    to_south[pl.ds(0, levels), :] = thick[0]
    to_south[pl.ds(levels, levels), :] = theta[0] * thick[0]
    to_south[pl.ds(2 * levels, levels), :] = merid[0]


def ends_of(source, target, low, high):
    rows = source.shape[0]
    return [
        (source.at[pl.ds(0, low)], target.at[pl.ds(0, low)]),
        (source.at[pl.ds(rows - high, high)], target.at[pl.ds(low, high)]),
    ]


def advect_outer_kernel(peers, coef, *refs):
    sources, (halo_s, halo_n) = refs[:4], refs[4:6]
    outs, held, sems = refs[6 : 6 + peers], refs[-5:-1], refs[-1]
    lat_rows, levels, _ = sources[0].shape
    copies = []
    for source, target in zip(sources, held):
        copies += ends_of(source, target, peers, 2)
    for copy in copy_all(copies, sems):
        copy.wait()
    zonal, merid, thick, theta = held
    top = lat_rows - 1
    me = lax.axis_index("lev")
    for step in range(peers):
        owner = wrapped(me, step, peers)
        is_first, is_last = owner == 0, owner == peers - 1
        row = jnp.where(is_last, top, owner)
        at = jnp.where(is_last, peers + 1, owner)
        low, high = jnp.maximum(at - 1, 0), jnp.minimum(at + 1, peers + 1)
        t, t_s, t_n = thick[at], thick[low], thick[high]
        h, h_s, h_n = theta[at] * t, theta[low] * t_s, theta[high] * t_n
        part = lambda ref, i: ref[pl.ds(i * levels, levels), :]
        t_s = jnp.where(is_first, part(halo_s, 0), t_s)
        h_s = jnp.where(is_first, part(halo_s, 1), h_s)
        t_n = jnp.where(is_last, part(halo_n, 0), t_n)
        h_n = jnp.where(is_last, part(halo_n, 1), h_n)
        w_n = jnp.where(is_last, part(halo_n, 2), merid[high])
        fields = advect_row(row, coef, zonal[at], merid[at], t, h, t_s, h_s, t_n, h_n, w_n)
        for field, new in enumerate(fields):
            store_packed(outs[step], (0, field), new)


def target_edges(surface, sigma):
    curve = sigma * sigma
    return TOP_PRESSURE + HYBRID_SCALE * (sigma - curve) + (surface - TOP_PRESSURE) * curve


def target_thickness(surface, first, levels):
    step = 1.0 / levels
    curve = (2.0 * first + 1.0) * (step * step)
    return HYBRID_SCALE * (step - curve) + (surface - TOP_PRESSURE) * curve


def exner(pressure):
    return jnp.exp(EXNER_POWER * jnp.log(pressure))


def split_dot(x, ones):
    a = x.astype(BF16)
    r = x - a.astype(F32)
    b = r.astype(BF16)
    c = (r - b.astype(F32)).astype(BF16)
    dot = lambda v: jnp.dot(v, ones, preferred_element_type=F32)
    return dot(a) + (dot(b) + dot(c))

def remap_kernel(width, block, peers, *refs):
    parts = refs[:peers]
    gathered, spread, base_rows, base_s = refs[-4:]
    outs = refs[-4 - peers : -4]
    me = lax.axis_index("lev")
    count = parts[0].shape[0]
    levels = peers * block
    level_r = lax.broadcasted_iota(jnp.int32, (levels, levels), 0)
    level_c = lax.broadcasted_iota(jnp.int32, (levels, levels), 1)
    running = (level_r <= level_c).astype(F32).astype(BF16)
    below = (
        lax.broadcasted_iota(jnp.int32, (8, levels), 1)
        >= block * (1 + lax.broadcasted_iota(jnp.int32, (8, levels), 0))
    ).astype(F32)
    full = width // LANES
    data_rows = packed_rows(block, width)
    half = block // 2
    sources = [wrapped(me, (peers - step) % peers, peers) for step in range(peers)]
    targets = [wrapped(me, step, peers) for step in range(peers)]
    for place in range(count):
        for step in range(peers):
            at = pl.ds(pl.multiple_of(sources[step] * block, block), block)
            for field in range(2):
                for tile in range(tile_count(width)):
                    cols = min(LANES, width - tile * LANES)
                    gathered[place, field, at, pl.ds(tile * LANES, cols)] = load_tile(
                        parts[step], (place, field), block, width, tile)
    for place in range(count):
        cols = width
        here = pl.ds(0, cols)
        thick = gathered[place, 0, :, here]
        surface_row = TOP_PRESSURE + jnp.sum(thick, axis=0, keepdims=True)
        thick = thick.T
        heat = gathered[place, 1, :, here].T
        upper = TOP_PRESSURE + split_dot(thick, running)
        theta = heat / thick
        offset = split_dot(heat, running) - theta * upper
        surface = upper[:, levels - 1 :]
        lane = lax.broadcasted_iota(jnp.int32, (cols, levels), 1)
        lane_f = lane.astype(F32)
        edge = target_edges(surface, (lane_f + 1.0) * (1.0 / levels))
        at = jnp.zeros((cols, levels), jnp.int32)
        jump = levels // 2
        while jump:
            probe = jnp.take_along_axis(upper, at + (jump - 1), axis=1, mode="promise_in_bounds")
            at = jnp.where(probe < edge, at + jump, at)
            jump //= 2
        pick = lambda table: jnp.take_along_axis(table, at, axis=1, mode="promise_in_bounds")
        heat_to = pick(offset) + pick(theta) * edge
        heat_from = jnp.where(lane == 0, 0.0, pltpu.roll(heat_to, 1, 1))
        theta_next = (heat_to - heat_from) / target_thickness(surface, lane_f, levels)
        exner_to = exner(edge)
        exner_from = jnp.where(lane == 0, TOP_PRESSURE**EXNER_POWER, pltpu.roll(exner_to, 1, 1))
        layer = theta_next * (exner_to - exner_from)
        bases = lax.dot_general(
            below, layer, (((1,), (1,)), ((), ())), precision=HIGHEST, preferred_element_type=F32
        )
        base_s[place, :, here] = bases
        base_s[place, pl.ds(7, 1), here] = surface_row
        spread[place, :, here] = theta_next.T
    for place in range(count):
        for tile in range(tile_count(width)):
            base_rows[place, tile] = base_s[place, :, pl.ds(tile * LANES, LANES)]
        for step in range(peers):
            out = outs[step]
            start = pl.multiple_of(targets[step] * block, block)
            for tile in range(tile_count(width)):
                cols = min(LANES, width - tile * LANES)
                here = pl.ds(tile * LANES, cols)
                if tile < full:
                    out[place, pl.ds(tile * block, block), :] = spread[place, pl.ds(start, block), here]
                else:
                    part = spread[place, pl.ds(start, block), here]
                    out[place, pl.ds(full * block, half), :] = jnp.concatenate([part[:half], part[half:]], axis=1)
                out[place, pl.ds(data_rows + tile, 1), pl.ds(0, cols)] = base_rows[place, tile, pl.ds(7, 1), pl.ds(0, cols)]
                out[place, pl.ds(data_rows + 8 + tile, 1), pl.ds(0, cols)] = base_rows[place, tile, pl.ds(targets[step], 1), pl.ds(0, cols)]


def below_sum(layer):
    rows, width = layer.shape
    groups = rows // 8
    carry = None
    pieces = []
    sub = lax.broadcasted_iota(jnp.int32, (8, width), 0)
    for g in reversed(range(groups)):
        x = layer[g * 8 : (g + 1) * 8]
        total = x
        for step in (1, 2, 4):
            total = total + jnp.where(sub < 8 - step, pltpu.roll(total, 8 - step, 0), 0.0)
        under = total - x
        if carry is not None:
            under = under + carry
            carry = carry + total[0:1]
        else:
            carry = total[0:1]
        pieces.append(under)
    return jnp.concatenate(pieces[::-1], axis=0)


def column_state(message, index, block, width, first_level, levels, ground):
    tiles = tile_count(width)
    data_rows = packed_rows(block, width)
    theta = jnp.concatenate([load_tile(message, index, block, width, t) for t in range(tiles)], axis=1)

    def line(first):
        return jnp.concatenate(
            [message[(*index, pl.ds(first + t, 1), pl.ds(0, min(LANES, width - t * LANES)))] for t in range(tiles)],
            axis=1,
        )

    surface = line(data_rows)
    base = line(data_rows + 8)
    sub = lax.broadcasted_iota(jnp.int32, (block, width), 0).astype(F32) + first_level
    thick = target_thickness(surface, sub, levels)
    top = exner(target_edges(surface, sub * (1.0 / levels)))
    bottom_edge = exner(target_edges(surface, (first_level + block) * (1.0 / levels)))
    sub_i = lax.broadcasted_iota(jnp.int32, (block, width), 0)
    bottom = jnp.where(sub_i == block - 1, bottom_edge, pltpu.roll(top, block - 1, 0))
    layer = theta * (bottom - top)
    geopot = (ground + base) + (below_sum(layer) + 0.5 * layer)
    return theta, thick, 0.5 * (top + bottom), geopot


def push(now, before):
    theta, exner_mid, geopot = now
    theta_b, exner_b, geopot_b = before
    return (geopot - geopot_b) + 0.5 * (theta + theta_b) * (exner_mid - exner_b)


def filtered(value, table, high, low, high_t, low_t, block):
    def product(x, b_high, b_low):
        x_high = x.astype(BF16)
        x_low = (x - x_high.astype(F32)).astype(BF16)
        dot = lambda a, b: jnp.dot(a, b, preferred_element_type=F32)
        return dot(x_high, b_high) + (dot(x_low, b_high) + dot(x_high, b_low))

    spectral = product(value, high, low)
    rows, width = value.shape
    spectral = (spectral.reshape(rows // block, block, width) * table[:, None, :]).reshape(rows, width)
    return value + product(spectral, high_t, low_t)


def gather_messages(me, parts, order):
    peers = len(parts)
    for step, part in enumerate(parts):
        owner = wrapped(me, (peers - step) % peers, peers)
        for place in range(part.shape[0]):
            order[owner * part.shape[0] + place] = part[place]


def copy_all(copies, sems, first=0):
    started = [pltpu.make_async_copy(source, target, sems.at[first + i]) for i, (source, target) in enumerate(copies)]
    for copy in started:
        copy.start()
    return started


def wait_all(copies):
    for copy in copies:
        copy.wait()


def filter_rows(ref, count, table, tables, block):
    width = ref.shape[-1]
    value = ref[pl.ds(0, count)].reshape(count * block, width)
    value = filtered(value, table, *(t[...] for t in tables), block)
    ref[pl.ds(0, count)] = value.reshape(count, block, width)


def around(x):
    return jnp.roll(x, 1, axis=1)


def inner_final_kernel(
    levels, first, flag, faces, p0, p1, p2, p3, ground, table, zonal_h, merid_h, t0, t1, t2, t3, after,
    zonal_out, merid_out, thick_out, theta_out, edge_states,
    order, zonal, merid, zonal_s, merid_s, thick_s, theta_s, carried, b0, b1, b2, b3, sems,
):
    del after
    count, _, _ = zonal.shape
    _, block, width = zonal_h.shape
    inner = pl.ds(first, count)
    winds = copy_all([(zonal_h.at[inner], zonal), (merid_h.at[inner], merid)], sems)
    tables = (b0, b1, b2, b3)
    basis = copy_all(list(zip((t0, t1, t2, t3), tables)), sems, 2)
    me = lax.axis_index("lev")
    level = (me * block).astype(F32)
    gather_messages(me, (p0, p1, p2, p3), order)
    carried[...] = jnp.zeros_like(carried)
    wait_all(winds)

    def one_row(i, _):
        row = first + i
        theta, thick, mid, geopot = column_state(order, (i,), block, width, level, levels, ground[pl.ds(row, 1), :])
        theta_s[i] = theta
        thick_s[i] = thick
        now = (theta, mid, geopot)
        zonal_s[i] = zonal[i] - push(now, tuple(around(x) for x in now))
        before = (carried[0], carried[1], carried[2])
        merid_s[jnp.maximum(i - 1, 0)] = merid[i] - faces[row] * push(now, before)
        for field, x in enumerate(now):
            carried[field] = x

        @pl.when(i == 0)
        def _():
            for field, x in enumerate(now):
                edge_states[0, field] = x

        return 0

    lax.fori_loop(0, count, one_row, 0)
    for field in range(3):
        edge_states[1, field] = carried[field]
    early = copy_all([(theta_s, theta_out.at[inner]), (thick_s, thick_out.at[inner])], sems, 6)
    wait_all(basis)

    @pl.when(flag[0] != 0)
    def _():
        filter_rows(zonal_s, count, table[pl.ds(first, count), :], tables, block)
        filter_rows(merid_s, count - 1, table[pl.ds(first + 1, count - 1), :], tables, block)

    late = copy_all(
        [
            (zonal_s, zonal_out.at[inner]),
            (merid_s.at[pl.ds(0, count - 1)], merid_out.at[pl.ds(first + 1, count - 1)]),
        ],
        sems,
        8,
    )
    wait_all(early + late)


def rows_back(source, target, low):
    rows = target.shape[0]
    return [
        (source.at[pl.ds(0, low)], target.at[pl.ds(0, low)]),
        (source.at[pl.ds(low, 1)], target.at[pl.ds(rows - 1, 1)]),
    ]


def outer_zonal_kernel(
    levels, flag, p0, p1, p2, p3, ground, table, zonal_h, t0, t1, t2, t3, zonal_in, thick_in, theta_in,
    zonal_out, thick_out, theta_out, states,
    order, zonal, zonal_s, thick_s, theta_s, b0, b1, b2, b3, sems,
):
    del zonal_in, thick_in, theta_in
    lat_rows, block, width = zonal_h.shape
    count = order.shape[0]
    winds = copy_all(ends_of(zonal_h, zonal, count - 1, 1), sems)
    tables = (b0, b1, b2, b3)
    basis = copy_all(list(zip((t0, t1, t2, t3), tables)), sems, 2)
    me = lax.axis_index("lev")
    level = (me * block).astype(F32)
    gather_messages(me, (p0, p1, p2, p3), order)
    wait_all(winds)
    rows = [*range(count - 1), lat_rows - 1]
    for i, row in enumerate(rows):
        theta, thick, mid, geopot = column_state(order, (i,), block, width, level, levels, ground[pl.ds(row, 1), :])
        theta_s[i] = theta
        thick_s[i] = thick
        now = (theta, mid, geopot)
        zonal_s[i] = zonal[i] - push(now, tuple(around(x) for x in now))
        for field, x in enumerate(now):
            states[i, field] = x
    early = copy_all(rows_back(theta_s, theta_out, count - 1) + rows_back(thick_s, thick_out, count - 1), sems, 6)
    wait_all(basis)

    @pl.when(flag[0] != 0)
    def _():
        picked = jnp.concatenate([table[pl.ds(0, count - 1), :], table[pl.ds(lat_rows - 1, 1), :]], axis=0)
        filter_rows(zonal_s, count, picked, tables, block)

    late = copy_all(rows_back(zonal_s, zonal_out, count - 1), sems, 10)
    wait_all(early + late)


def outer_merid_kernel(
    levels, flag, faces, south, halo_s, states, edge_states, table, merid_h, t0, t1, t2, t3, merid_in,
    merid_out, merid, merid_s, b0, b1, b2, b3, sems,
):
    del merid_in
    lat_rows, block, width = merid_h.shape
    outer = states.shape[0]
    winds = copy_all(ends_of(merid_h, merid, outer, 1), sems)
    tables = (b0, b1, b2, b3)
    basis = copy_all(list(zip((t0, t1, t2, t3), tables)), sems, 2)
    level = (lax.axis_index("lev") * block).astype(F32)
    theta, _, mid, geopot = column_state(south, (0,), block, width, level, levels, halo_s[pl.ds(2 * block, 1), :])
    before = (theta, mid, geopot)
    fields = lambda ref, i: tuple(ref[i, f] for f in range(3))
    top = lat_rows - 1
    steps = [(i, fields(states, i)) for i in range(outer - 1)] + [(outer - 1, fields(edge_states, 0))]
    wait_all(winds)
    for row, now in steps:
        merid_s[row] = merid[row] - faces[row] * push(now, before)
        before = now
    merid_s[outer] = merid[outer] - faces[top] * push(fields(states, outer - 1), fields(edge_states, 1))
    wait_all(basis)

    @pl.when(flag[0] != 0)
    def _():
        picked = jnp.concatenate([table[pl.ds(0, outer), :], table[pl.ds(top, 1), :]], axis=0)
        filter_rows(merid_s, outer + 1, picked, tables, block)

    wait_all(copy_all(rows_back(merid_s, merid_out, outer), sems, 6))


def exchanged(parts):
    peers = lax.axis_size("lev")
    return [parts[0]] + [
        lax.ppermute(parts[step], "lev", [(i, (i + step) % peers) for i in range(peers)]) for step in range(1, peers)
    ]


def body(
    zonal_wind, meridional_wind, thickness, potential_temp, surface_geo, polar_mask, cutoff, damping
):
    lat_rows, block, width = zonal_wind.shape
    lat_count = lax.axis_size("lat")
    peers = lax.axis_size("lev")
    levels = block * peers
    total_rows = lat_rows * lat_count
    first_row = lax.axis_index("lat") * lat_rows
    row_ids = (first_row + jnp.arange(lat_rows + 1, dtype=jnp.int32)).astype(F32)
    faces = jnp.sin(math.pi * row_ids / total_rows)
    centres = jnp.sin(math.pi * (row_ids[:-1] + 0.5) / total_rows)
    coef = jnp.stack([faces[:-1], faces[1:]]) * (0.5 * COURANT) / centres
    northward = [(i, i + 1) for i in range(lat_count - 1)]
    southward = [(i + 1, i) for i in range(lat_count - 1)]
    flag = jnp.any(polar_mask != 0).astype(jnp.int32).reshape(1)
    shape = lambda *dims: jax.ShapeDtypeStruct(dims, F32)
    hbm = pl.BlockSpec(memory_space=pltpu.HBM)
    rows_of = lambda n: pltpu.VMEM((n, block, width), F32)
    dma = lambda n: pltpu.SemaphoreType.DMA((n,))

    inner_each = lat_rows // peers - 1
    inner = inner_each * peers
    outer, first = peers, peers - 1
    data_rows = packed_rows(block, width)
    message_rows = data_rows + 16
    stay = lambda *arrays: [pltpu.with_memory_space_constraint(x, pltpu.HBM) for x in arrays]
    winds_and_state = stay(zonal_wind, meridional_wind, thickness, potential_temp)
    ground_h, zonal_h, merid_h = stay(surface_geo, zonal_wind, meridional_wind)

    *inner_sent, to_north, to_south = pl.pallas_call(
        lambda *refs: advect_inner_kernel(first, inner_each, peers, *refs),
        out_shape=[shape(inner_each, 2, data_rows, LANES)] * peers
        + [shape(2 * block + 8, width), shape(3 * block, width)],
        in_specs=[SMEM] + [hbm] * 5,
        out_specs=[VMEM] * (peers + 2),
        scratch_shapes=[rows_of(lat_rows)] * 4 + [pltpu.VMEM((lat_rows, width), F32), dma(5)],
        compiler_params=params(12),
        cost_estimate=cost(5),
        name="advect_inner",
    )(coef, *winds_and_state, ground_h)
    inner_columns = exchanged(inner_sent)
    halo_s = lax.ppermute(to_north, "lat", northward)
    halo_n = lax.ppermute(to_south, "lat", southward)
    outer_sent = pl.pallas_call(
        lambda *refs: advect_outer_kernel(peers, *refs),
        out_shape=[shape(1, 2, data_rows, LANES)] * peers,
        in_specs=[SMEM] + [hbm] * 4 + [VMEM] * 2,
        out_specs=[VMEM] * peers,
        scratch_shapes=[rows_of(peers + 2)] * 4 + [dma(8)],
        compiler_params=params(12),
        cost_estimate=cost(3),
        name="advect_outer",
    )(coef, *winds_and_state, halo_s, halo_n)
    outer_columns = exchanged(outer_sent)

    def remap(columns, each, name, after):
        lanes = tile_count(width) * LANES
        return pl.pallas_call(
            lambda *refs: remap_kernel(width, block, peers, *refs),
            out_shape=[shape(each, message_rows, LANES)] * peers,
            in_specs=[VMEM] * peers + [pl.BlockSpec(memory_space=pl.ANY)] * len(after),
            out_specs=[VMEM] * peers,
            scratch_shapes=[
                pltpu.VMEM((each, 2, levels, lanes), F32),
                pltpu.VMEM((each, levels, lanes), F32),
                pltpu.VMEM((each, tile_count(width), 8, LANES), F32),
                pltpu.VMEM((each, 8, lanes), F32),
            ],
            compiler_params=params(12),
            cost_estimate=cost(1 + 3 * each),
            name=name,
        )(*columns, *after)

    inner_remapped = remap(inner_columns, inner_each, "remap_inner", [])
    inner_messages = exchanged(inner_remapped)
    outer_remapped = remap(outer_columns, 1, "remap_outer", inner_messages[1:2])
    outer_messages = exchanged(outer_remapped)

    high, low, wave = fourier_tables(width)
    active = (jnp.asarray(wave)[None, :] >= cutoff[:, None]) & (polar_mask[:, None] != 0)
    table = jnp.where(active, damping - 1.0, 0.0)
    tables = stay(*(jnp.asarray(x) for x in (high, low, np.ascontiguousarray(high.T), np.ascontiguousarray(low.T))))
    basis_scratch = [pltpu.VMEM((width, width), BF16)] * 4
    field = shape(lat_rows, block, width)

    zonal_next, merid_next, thick_next, theta_next, edge_states = pl.pallas_call(
        lambda *refs: inner_final_kernel(levels, first, *refs),
        out_shape=[field] * 4 + [shape(2, 3, block, width)],
        in_specs=[SMEM] * 2 + [VMEM] * (peers + 2) + [hbm] * 6 + [pl.BlockSpec(memory_space=pl.ANY)],
        out_specs=[hbm] * 4 + [VMEM],
        scratch_shapes=[pltpu.VMEM((inner, message_rows, LANES), F32)]
        + [rows_of(inner)] * 6
        + [rows_of(3), *basis_scratch, dma(10)],
        compiler_params=params(20),
        cost_estimate=cost(8),
        name="final_inner",
    )(
        flag, faces, *inner_messages, surface_geo, table, zonal_h, merid_h, *tables, outer_remapped[0]
    )

    edge_states, *outer_messages = lax.optimization_barrier((edge_states, *outer_messages))
    step_of_last = (lax.axis_index("lev") + 1) % peers
    last_message = outer_messages[0]
    for step in range(1, peers):
        last_message = jnp.where(step_of_last == step, outer_messages[step], last_message)
    south = lax.ppermute(last_message, "lat", northward)

    zonal_next, thick_next, theta_next, states = pl.pallas_call(
        lambda *refs: outer_zonal_kernel(levels, *refs),
        out_shape=[field] * 3 + [shape(outer, 3, block, width)],
        in_specs=[SMEM] + [VMEM] * (peers + 2) + [hbm] * 8,
        out_specs=[hbm] * 3 + [VMEM],
        scratch_shapes=[pltpu.VMEM((outer, message_rows, LANES), F32)]
        + [rows_of(outer)] * 4
        + [*basis_scratch, dma(12)],
        input_output_aliases={peers + 8: 0, peers + 9: 1, peers + 10: 2},
        compiler_params=params(16),
        cost_estimate=cost(4),
        name="final_outer_zonal",
    )(
        flag, *outer_messages, surface_geo, table, zonal_h, *tables, zonal_next, thick_next, theta_next
    )
    merid_next = pl.pallas_call(
        lambda *refs: outer_merid_kernel(levels, *refs),
        out_shape=field,
        in_specs=[SMEM] * 2 + [VMEM] * 5 + [hbm] * 6,
        out_specs=hbm,
        scratch_shapes=[rows_of(outer + 1)] * 2 + [*basis_scratch, dma(8)],
        input_output_aliases={12: 0},
        compiler_params=params(16),
        cost_estimate=cost(3),
        name="final_outer_merid",
    )(flag, faces, south, halo_s, states, edge_states, table, merid_h, *tables, merid_next)
    return zonal_next, merid_next, thick_next, theta_next


def solution(mesh):
    field = P("lat", "lev", None)
    in_specs = (field, field, field, field, P("lat", None), P("lat"), P("lat"), P("lat", None))
    return jax.shard_map(body, mesh=mesh, in_specs=in_specs, out_specs=(field,) * 4, check_vma=False)
```

time: 133 us -> 111 us (0.83)
  the two profiles are of different devices: /device:TPU:1 before, /device:TPU:23 now
where the time goes in v3:
time: 111 us; the launch traced here: 110 us
  starting transfers between devices  47.5 us (43%)
  Pallas kernels  33.4 us (30%)
  waiting for transfers between devices  26.2 us (24%)
  between operations  1.64 us (1%)
    ppermute x12, starting transfers between devices, exchanged(): lax.ppermute(parts[step], 'lev', [(i, (i + step) % peers) for i in range(...  29.2 us
    ppermute x1, starting transfers between devices, body(): south = lax.ppermute(last_message, 'lat', northward)  12.3 us
    ppermute x1, waiting for transfers between devices, body(): halo_n = lax.ppermute(to_south, 'lat', southward)  11.6 us
    ppermute x1, waiting for transfers between devices, body(): halo_s = lax.ppermute(to_north, 'lat', northward)  9.52 us
    pallas_call x2, Pallas kernels, remap(): pl.pallas_call(lambda *refs: remap_kernel(width, block, peers, *refs), ou...  8.33 us
    pallas_call x1, Pallas kernels, body(): pl.pallas_call(lambda *refs: inner_final_kernel(levels, first, *refs), ou...  8.2 us
    ppermute x12, waiting for transfers between devices, exchanged(): lax.ppermute(parts[step], 'lev', [(i, (i + step) % peers) for i in range(...  5.11 us
    pallas_call x1, Pallas kernels, body(): pl.pallas_call(lambda *refs: advect_inner_kernel(first, inner_each, peers...  5.1 us
  transfers between devices with their start and end apart: 15, of which 4 were waited for; matrix products, arithmetic and copies ran while one was open for 1% of the time, Pallas kernels for 21%

profile of v3, /device:TPU:23, one launch (start us, length us, event | category | flops | bytes accessed | tf_op | source)
XLA Modules:
  0.0 110.3 jit_solution(1535009598216273169)
XLA Ops:
  0.7 0.1 slice_bitcast_fusion.1
  0.8 5.1 %advect_inner.1 = (f32[2,2,144,128]{3,2,1,0:T(8,128)S(1)}, f32[2,2,144,128]{3,2,1,0:T(8,128)S(1)}, f32[2,2,144,128]{3,2,1,0:T(8,128)S(1)}, f32[2,2,144,128]{3,2,...) custom-call(f32[2,12]{1,0:T(2,128)S(1)} %fusion.refs_0_, f32[12,32,576]{2,1,0:T(8,128)} %refs_7_.2, ...), custom_call_target="tpu_custom_call" | custom-call | flops 5500000256 | bytes 18000000 | tf_op jit(solution)/shard_map/advect_inner/pallas_call | solution.py:521
  5.9 3.1 %collective-permute-start = (f32[2,2,144,128]{3,2,1,0:T(8,128)S(1)}, f32[2,2,144,128]{3,2,1,0:T(8,128)S(1)}, u32[]{:S(2)}, u32[]{:S(2)}) collective-permute-start(f32[2,2,144,128]{3,2,1,0:T(8,128)S(1)} %get-tuple-element.37), channel_id=1, source_target_pairs={{0,1},{1,2},{2,3},{3,0},{4,5},{5,6},{6,7},{7,4},{8,9},{9,10},{10,1... | collective-permute-start | bytes 884744 | tf_op jit(solution)/shard_map/ppermute | solution.py:487
  9.0 5.1 %collective-permute-start.1 = (f32[2,2,144,128]{3,2,1,0:T(8,128)S(1)}, f32[2,2,144,128]{3,2,1,0:T(8,128)S(1)}, u32[]{:S(2)}, u32[]{:S(2)}) collective-permute-start(f32[2,2,144,128]{3,2,1,0:T(8,128)S(1)} %get-tuple-element.38), channel_id=1, source_target_pairs={{0,2},{1,3},{2,0},{3,1},{4,6},{5,7},{6,4},{7,5},{8,10},{9,11},{10,... | collective-permute-start | bytes 884744 | tf_op jit(solution)/shard_map/ppermute | solution.py:487
  14.1 2.4 %collective-permute-start.2 = (f32[2,2,144,128]{3,2,1,0:T(8,128)S(1)}, f32[2,2,144,128]{3,2,1,0:T(8,128)S(1)}, u32[]{:S(2)}, u32[]{:S(2)}) collective-permute-start(f32[2,2,144,128]{3,2,1,0:T(8,128)S(1)} %get-tuple-element.39), channel_id=1, source_target_pairs={{0,3},{1,0},{2,1},{3,2},{4,7},{5,4},{6,5},{7,6},{8,11},{9,8},{10,9... | collective-permute-start | bytes 884744 | tf_op jit(solution)/shard_map/ppermute | solution.py:487
  16.5 4.0 %collective-permute-start.6 = (f32[72,576]{1,0:T(8,128)S(1)}, f32[72,576]{1,0:T(8,128)S(1)}, u32[]{:S(2)}, u32[]{:S(2)}) collective-permute-start(f32[72,576]{1,0:T(8,128)S(1)} %get-tuple-element.44), channel_id=1, source_target_pairs={{0,4},{4,8},{8,12},{12,16},{16,20},{20,24},{24,28},{28,32},{32,36}... | collective-permute-start | bytes 497672 | tf_op jit(solution)/shard_map/ppermute | solution.py:533
  20.5 1.9 %collective-permute-start.7 = (f32[96,576]{1,0:T(8,128)S(1)}, f32[96,576]{1,0:T(8,128)S(1)}, u32[]{:S(2)}, u32[]{:S(2)}) collective-permute-start(f32[96,576]{1,0:T(8,128)S(1)} %get-tuple-element.45), channel_id=1, source_target_pairs={{4,0},{8,4},{12,8},{16,12},{20,16},{24,20},{28,24},{32,28},{36,32}... | collective-permute-start | bytes 663560 | tf_op jit(solution)/shard_map/ppermute | solution.py:534
  22.5 0.0 copy-start.4
  22.5 0.6 copy-done.4
  23.1 0.6 broadcast_compare_fusion
  24.4 9.5 %collective-permute-done.6.refs_5_.refs_3_ = f32[72,576]{1,0:T(8,128)S(1)} collective-permute-done((f32[72,576]{1,0:T(8,128)S(1)}, f32[72,576]{1,0:T(8,128)S(1)}, u32[]{:S(2)}, u32[]{:S(2)}) %collective-permute-start.6) | collective-permute-done | bytes 165920 | tf_op jit(solution)/shard_map/ppermute | solution.py:533
  33.9 11.6 %collective-permute-done.7.refs_6_ = f32[96,576]{1,0:T(8,128)S(1)} collective-permute-done((f32[96,576]{1,0:T(8,128)S(1)}, f32[96,576]{1,0:T(8,128)S(1)}, u32[]{:S(2)}, u32[]{:S(2)}) %collective-permute-start.7) | collective-permute-done | bytes 221216 | tf_op jit(solution)/shard_map/ppermute | solution.py:534
  45.5 3.2 %advect_outer.1 = (f32[1,2,144,128]{3,2,1,0:T(8,128)S(1)}, f32[1,2,144,128]{3,2,1,0:T(8,128)S(1)}, f32[1,2,144,128]{3,2,1,0:T(8,128)S(1)}, f32[1,2,144,128]{3,2,1,0:T(8,128)S(1)}) custom-call(f32[2,12]{1,0:T(2,128)S(1)} %fusion.refs_0_, f32[12,32,576]{2,1,0:T(8,128)} %refs_7_.2, f32[12,32,576]{2,1,0:T(8,128)} %refs_7_.3, f32[12,32,576]{2,1,0:T(8,128)} %refs_3_.3, ...), custom_call_target="tpu_custom_call" | custom-call | flops 3300000000 | bytes 10800000 | tf_op jit(solution)/shard_map/advect_outer/pallas_call | solution.py:535
  48.7 0.4 collective-permute-start.8
  49.1 4.4 %collective-permute-start.9 = (f32[1,2,144,128]{3,2,1,0:T(8,128)S(1)}, f32[1,2,144,128]{3,2,1,0:T(8,128)S(1)}, u32[]{:S(2)}, u32[]{:S(2)}) collective-permute-start(f32[1,2,144,128]{3,2,1,0:T(8,128)S(1)} %get-tuple-element.48), channel_id=1, source_target_pairs={{0,2},{1,3},{2,0},{3,1},{4,6},{5,7},{6,4},{7,5},{8,10},{9,11},{10,... | collective-permute-start | bytes 442376 | tf_op jit(solution)/shard_map/ppermute | solution.py:487
  53.5 0.0 collective-permute-done.refs_1_
  53.5 0.2 collective-permute-start.10
  53.7 0.0 collective-permute-done.1.refs_2_
  53.7 0.0 collective-permute-done.2.refs_3_
  53.7 0.0 copy-start.1
  53.7 0.0 copy-start.2
  53.7 5.6 %remap_inner.1 = (f32[2,160,128]{2,1,0:T(8,128)S(1)}, f32[2,160,128]{2,1,0:T(8,128)S(1)}, f32[2,160,128]{2,1,0:T(8,128)S(1)}, f32[2,160,128]{2,1,0:T(8,128)S(1)}) custom-call(f32[2,2,144,128]{3,2,1,0:T(8,128)S(1)} %get-tuple-element.36.refs_0_, f32[2,2,144,128]{3,2,1,0:T(8,128)S(1)} %collective-permute-done.refs_1_, ...), custom_call_target="tpu_custom_call" | custom-call | flops 7699999744 | bytes 25200000 | tf_op jit(solution)/shard_map/remap_inner/pallas_call | solution.py:549
  59.3 0.0 copy-start.3
  59.4 2.4 %collective-permute-start.3 = (f32[2,160,128]{2,1,0:T(8,128)S(1)}, f32[2,160,128]{2,1,0:T(8,128)S(1)}, u32[]{:S(2)}, u32[]{:S(2)}) collective-permute-start(f32[2,160,128]{2,1,0:T(8,128)S(1)} %get-tuple-element.41), channel_id=1, source_target_pairs={{0,1},{1,2},{2,3},{3,0},{4,5},{5,6},{6,7},{7,4},{8,9},{9,10},{10,1... | collective-permute-start | bytes 491528 | tf_op jit(solution)/shard_map/ppermute | solution.py:487
  61.8 0.0 copy-done.1
  61.8 0.0 copy-done.2
  61.8 0.0 copy-done.3
  61.8 0.1 add_select_fusion.refs_7_.refs_6_
  61.9 2.3 %collective-permute-start.4 = (f32[2,160,128]{2,1,0:T(8,128)S(1)}, f32[2,160,128]{2,1,0:T(8,128)S(1)}, u32[]{:S(2)}, u32[]{:S(2)}) collective-permute-start(f32[2,160,128]{2,1,0:T(8,128)S(1)} %get-tuple-element.42), channel_id=1, source_target_pairs={{0,2},{1,3},{2,0},{3,1},{4,6},{5,7},{6,4},{7,5},{8,10},{9,11},{10,... | collective-permute-start | bytes 491528 | tf_op jit(solution)/shard_map/ppermute | solution.py:487
  64.2 0.0 collective-permute-done.8.refs_1_
  64.2 3.2 %collective-permute-start.5 = (f32[2,160,128]{2,1,0:T(8,128)S(1)}, f32[2,160,128]{2,1,0:T(8,128)S(1)}, u32[]{:S(2)}, u32[]{:S(2)}) collective-permute-start(f32[2,160,128]{2,1,0:T(8,128)S(1)} %get-tuple-element.43), channel_id=1, source_target_pairs={{0,3},{1,0},{2,1},{3,2},{4,7},{5,4},{6,5},{7,6},{8,11},{9,8},{10,9... | collective-permute-start | bytes 491528 | tf_op jit(solution)/shard_map/ppermute | solution.py:487
  67.4 0.0 collective-permute-done.9.refs_2_
  67.4 0.0 collective-permute-done.10.refs_3_
  67.4 1.9 %collective-permute-done.3.refs_4_.refs_3_ = f32[2,160,128]{2,1,0:T(8,128)S(1)} collective-permute-done((f32[2,160,128]{2,1,0:T(8,128)S(1)}, f32[2,160,128]{2,1,0:T(8,128)S(1)}, u32[]{:S(2)}, u32[]{:S(2)}) %collective-permute-start.3) | collective-permute-done | bytes 163872 | tf_op jit(solution)/shard_map/ppermute | solution.py:487
  69.3 0.0 copy-start
  69.3 2.7 %remap_outer.1 = (f32[1,160,128]{2,1,0:T(8,128)S(1)}, f32[1,160,128]{2,1,0:T(8,128)S(1)}, f32[1,160,128]{2,1,0:T(8,128)S(1)}, f32[1,160,128]{2,1,0:T(8,128)S(1)}) custom-call(f32[1,2,144,128]{3,2,1,0:T(8,128)S(1)} %get-tuple-element.46.refs_0_, f32[1,2,144,128]{3,2,1,0:T(8,128)S(1)} %collective-permute-done.8.refs_1_, ...), custom_call_target="tpu_custom_call" | custom-call | flops 4400000000 | bytes 14400000 | tf_op jit(solution)/shard_map/remap_outer/pallas_call | solution.py:549
  72.0 0.1 collective-permute-start.11
  72.1 4.5 %collective-permute-start.12 = (f32[1,160,128]{2,1,0:T(8,128)S(1)}, f32[1,160,128]{2,1,0:T(8,128)S(1)}, u32[]{:S(2)}, u32[]{:S(2)}) collective-permute-start(f32[1,160,128]{2,1,0:T(8,128)S(1)} %get-tuple-element.53), channel_id=1, source_target_pairs={{0,2},{1,3},{2,0},{3,1},{4,6},{5,7},{6,4},{7,5},{8,10},{9,11},{10,... | collective-permute-start | bytes 245768 | tf_op jit(solution)/shard_map/ppermute | solution.py:487
  76.6 1.1 %collective-permute-start.13 = (f32[1,160,128]{2,1,0:T(8,128)S(1)}, f32[1,160,128]{2,1,0:T(8,128)S(1)}, u32[]{:S(2)}, u32[]{:S(2)}) collective-permute-start(f32[1,160,128]{2,1,0:T(8,128)S(1)} %get-tuple-element.54), channel_id=1, source_target_pairs={{0,3},{1,0},{2,1},{3,2},{4,7},{5,4},{6,5},{7,6},{8,11},{9,8},{10,9... | collective-permute-start | bytes 245768 | tf_op jit(solution)/shard_map/ppermute | solution.py:487
  77.7 0.0 collective-permute-done.4.refs_4_
  77.7 3.2 %collective-permute-done.5.refs_5_ = f32[2,160,128]{2,1,0:T(8,128)S(1)} collective-permute-done((f32[2,160,128]{2,1,0:T(8,128)S(1)}, f32[2,160,128]{2,1,0:T(8,128)S(1)}, u32[]{:S(2)}, u32[]{:S(2)}) %collective-permute-start.5) | collective-permute-done | bytes 163872 | tf_op jit(solution)/shard_map/ppermute | solution.py:487
  80.9 0.0 copy-done
  80.9 8.2 %final_inner.1 = (f32[12,32,576]{2,1,0:T(8,128)}, f32[12,32,576]{2,1,0:T(8,128)}, f32[12,32,576]{2,1,0:T(8,128)}, f32[12,32,576]{2,1,0:T(8,128)}, f32[2,3,32,576]{3,2,1,0:T(8,128)S(1)}) custom-call(s32[1]{0:T(128)} %bitcast.refs_0_, f32[13]{0:T(128)S(1)} %multiply_sine_fusion.1.refs_1_, f32[2,160,128]{2,1,0:T(8,128)S(1)} %get-tuple-element.40.refs_2_, ...), custom_call_target="tpu_custom_call" | custom-call | flops 8800000000 | bytes 28800000 | tf_op jit(solution)/shard_map/final_inner/pallas_call | solution.py:577
  89.1 0.0 collective-permute-done.11.refs_2_
  89.1 0.0 collective-permute-done.12.refs_3_
  89.2 0.0 collective-permute-done.13.refs_4_
  89.2 12.3 %collective-permute-start.14 = (f32[1,160,128]{2,1,0:T(8,128)S(1)}, f32[1,160,128]{2,1,0:T(8,128)S(1)}, u32[]{:S(2)}, u32[]{:S(2)}) collective-permute-start(f32[1,160,128]{2,1,0:T(8,128)S(1)} %select_select_fusion), channel_id=1, source_target_pairs={{0,4},{4,8},{8,12},{12,16},{16,20},{20,24},{24,28},{28,32},{32,36}... | collective-permute-start | bytes 245768 | tf_op jit(solution)/shard_map/ppermute | solution.py:597
  101.5 3.9 %final_outer_zonal.1 = (f32[12,32,576]{2,1,0:T(8,128)}, f32[12,32,576]{2,1,0:T(8,128)}, f32[12,32,576]{2,1,0:T(8,128)}, f32[4,3,32,576]{3,2,1,0:T(8,128)S(1)}) custom-call(s32[1]{0:T(128)} %bitcast.refs_0_, f32[1,160,128]{2,1,0:T(8,128)S(1)} %get-tuple-element.55.refs_14_.refs_1_, ...), custom_call_target="tpu_custom_call", output_to_operand_aliasing={{0}: (12, {}), {1}: (13, {}), {2}: (14, {})} | custom-call | flops 4400000000 | bytes 14400000 | tf_op jit(solution)/shard_map/final_outer_zonal/pallas_call | solution.py:599
  105.5 0.0 collective-permute-done.14.refs_2_
  105.5 4.6 %final_outer_merid.1 = f32[12,32,576]{2,1,0:T(8,128)} custom-call(s32[1]{0:T(128)} %bitcast.refs_0_, f32[13]{0:T(128)S(1)} %multiply_sine_fusion.1.refs_1_, f32[1,160,128]{2,1,0:T(8,128)S(1)} %collective-permute-done.14.refs_2_, f32[72,576]{1,0:T(8,128)S(1)} %collective-permute-done.6.refs_5_.refs_3_, ...), custom_call_target="tpu_custom_call", output_to_operand_aliasing={{}: (12, {})} | custom-call | flops 3300000000 | bytes 10800000 | tf_op jit(solution)/shard_map/final_outer_merid/pallas_call | solution.py:614
  (5 shorter events, 0.1 us)
Async XLA Ops:
  5.9 47.6 %collective-permute-start = (f32[2,2,144,128]{3,2,1,0:T(8,128)S(1)}, f32[2,2,144,128]{3,2,1,0:T(8,128)S(1)}, u32[]{:S(2)}, u32[]{:S(2)}) collective-permute-start(f32[2,2,144,128]{3,2,1,0:T(8,128)S(1)} %get-tuple-element.37), channel_id=1, source_target_pairs={{0,1},{1,2},{2,3},{3,0},{4,5},{5,6},{6,7},{7,4},{8,9},{9,10},{10,1... | collective-permute-start | bytes 884744 | tf_op jit(solution)/shard_map/ppermute | solution.py:487
  9.0 44.7 %collective-permute-start.1 = (f32[2,2,144,128]{3,2,1,0:T(8,128)S(1)}, f32[2,2,144,128]{3,2,1,0:T(8,128)S(1)}, u32[]{:S(2)}, u32[]{:S(2)}) collective-permute-start(f32[2,2,144,128]{3,2,1,0:T(8,128)S(1)} %get-tuple-element.38), channel_id=1, source_target_pairs={{0,2},{1,3},{2,0},{3,1},{4,6},{5,7},{6,4},{7,5},{8,10},{9,11},{10,... | collective-permute-start | bytes 884744 | tf_op jit(solution)/shard_map/ppermute | solution.py:487
  14.1 39.6 %collective-permute-start.2 = (f32[2,2,144,128]{3,2,1,0:T(8,128)S(1)}, f32[2,2,144,128]{3,2,1,0:T(8,128)S(1)}, u32[]{:S(2)}, u32[]{:S(2)}) collective-permute-start(f32[2,2,144,128]{3,2,1,0:T(8,128)S(1)} %get-tuple-element.39), channel_id=1, source_target_pairs={{0,3},{1,0},{2,1},{3,2},{4,7},{5,4},{6,5},{7,6},{8,11},{9,8},{10,9... | collective-permute-start | bytes 884744 | tf_op jit(solution)/shard_map/ppermute | solution.py:487
  16.5 17.5 %collective-permute-start.6 = (f32[72,576]{1,0:T(8,128)S(1)}, f32[72,576]{1,0:T(8,128)S(1)}, u32[]{:S(2)}, u32[]{:S(2)}) collective-permute-start(f32[72,576]{1,0:T(8,128)S(1)} %get-tuple-element.44), channel_id=1, source_target_pairs={{0,4},{4,8},{8,12},{12,16},{16,20},{20,24},{24,28},{28,32},{32,36}... | collective-permute-start | bytes 497672 | tf_op jit(solution)/shard_map/ppermute | solution.py:533
  20.5 25.0 %collective-permute-start.7 = (f32[96,576]{1,0:T(8,128)S(1)}, f32[96,576]{1,0:T(8,128)S(1)}, u32[]{:S(2)}, u32[]{:S(2)}) collective-permute-start(f32[96,576]{1,0:T(8,128)S(1)} %get-tuple-element.45), channel_id=1, source_target_pairs={{4,0},{8,4},{12,8},{16,12},{20,16},{24,20},{28,24},{32,28},{36,32}... | collective-permute-start | bytes 663560 | tf_op jit(solution)/shard_map/ppermute | solution.py:534
  22.5 0.7 copy-start.4
  48.7 15.5 %collective-permute-start.8 = (f32[1,2,144,128]{3,2,1,0:T(8,128)S(1)}, f32[1,2,144,128]{3,2,1,0:T(8,128)S(1)}, u32[]{:S(2)}, u32[]{:S(2)}) collective-permute-start(f32[1,2,144,128]{3,2,1,0:T(8,128)S(1)} %get-tuple-element.47), channel_id=1, source_target_pairs={{0,1},{1,2},{2,3},{3,0},{4,5},{5,6},{6,7},{7,4},{8,9},{9,10},{10,1... | collective-permute-start | bytes 442376 | tf_op jit(solution)/shard_map/ppermute | solution.py:487
  49.1 18.3 %collective-permute-start.9 = (f32[1,2,144,128]{3,2,1,0:T(8,128)S(1)}, f32[1,2,144,128]{3,2,1,0:T(8,128)S(1)}, u32[]{:S(2)}, u32[]{:S(2)}) collective-permute-start(f32[1,2,144,128]{3,2,1,0:T(8,128)S(1)} %get-tuple-element.48), channel_id=1, source_target_pairs={{0,2},{1,3},{2,0},{3,1},{4,6},{5,7},{6,4},{7,5},{8,10},{9,11},{10,... | collective-permute-start | bytes 442376 | tf_op jit(solution)/shard_map/ppermute | solution.py:487
  53.5 13.9 %collective-permute-start.10 = (f32[1,2,144,128]{3,2,1,0:T(8,128)S(1)}, f32[1,2,144,128]{3,2,1,0:T(8,128)S(1)}, u32[]{:S(2)}, u32[]{:S(2)}) collective-permute-start(f32[1,2,144,128]{3,2,1,0:T(8,128)S(1)} %get-tuple-element.49), channel_id=1, source_target_pairs={{0,3},{1,0},{2,1},{3,2},{4,7},{5,4},{6,5},{7,6},{8,11},{9,8},{10,9... | collective-permute-start | bytes 442376 | tf_op jit(solution)/shard_map/ppermute | solution.py:487
  53.7 8.1 %copy-start.1 = (f32[12,576]{1,0:T(8,128)S(1)}, f32[12,576]{1,0:T(8,128)}, u32[]{:S(2)}) copy-start(f32[12,576]{1,0:T(8,128)} %param.20) | copy-start | bytes 82948
  53.7 8.1 %copy-start.2 = (s32[576]{0:T(1024)S(1)}, s32[576]{0:T(1024)}, u32[]{:S(2)}) copy-start(s32[576]{0:T(1024)} %constant.61.clone) | copy-start | bytes 6916
  59.3 2.5 %copy-start.3 = (s32[12]{0:T(128)S(1)}, s32[12]{0:T(128)}, u32[]{:S(2)}) copy-start(s32[12]{0:T(128)} %param.19) | copy-start | bytes 148
  59.4 9.9 %collective-permute-start.3 = (f32[2,160,128]{2,1,0:T(8,128)S(1)}, f32[2,160,128]{2,1,0:T(8,128)S(1)}, u32[]{:S(2)}, u32[]{:S(2)}) collective-permute-start(f32[2,160,128]{2,1,0:T(8,128)S(1)} %get-tuple-element.41), channel_id=1, source_target_pairs={{0,1},{1,2},{2,3},{3,0},{4,5},{5,6},{6,7},{7,4},{8,9},{9,10},{10,1... | collective-permute-start | bytes 491528 | tf_op jit(solution)/shard_map/ppermute | solution.py:487
  61.9 15.8 %collective-permute-start.4 = (f32[2,160,128]{2,1,0:T(8,128)S(1)}, f32[2,160,128]{2,1,0:T(8,128)S(1)}, u32[]{:S(2)}, u32[]{:S(2)}) collective-permute-start(f32[2,160,128]{2,1,0:T(8,128)S(1)} %get-tuple-element.42), channel_id=1, source_target_pairs={{0,2},{1,3},{2,0},{3,1},{4,6},{5,7},{6,4},{7,5},{8,10},{9,11},{10,... | collective-permute-start | bytes 491528 | tf_op jit(solution)/shard_map/ppermute | solution.py:487
  64.2 16.7 %collective-permute-start.5 = (f32[2,160,128]{2,1,0:T(8,128)S(1)}, f32[2,160,128]{2,1,0:T(8,128)S(1)}, u32[]{:S(2)}, u32[]{:S(2)}) collective-permute-start(f32[2,160,128]{2,1,0:T(8,128)S(1)} %get-tuple-element.43), channel_id=1, source_target_pairs={{0,3},{1,0},{2,1},{3,2},{4,7},{5,4},{6,5},{7,6},{8,11},{9,8},{10,9... | collective-permute-start | bytes 491528 | tf_op jit(solution)/shard_map/ppermute | solution.py:487
  69.3 11.7 %copy-start = (f32[12,576]{1,0:T(8,128)S(1)}, f32[12,576]{1,0:T(8,128)}, u32[]{:S(2)}) copy-start(f32[12,576]{1,0:T(8,128)} %refs_5_.3) | copy-start | bytes 82948
  72.0 17.2 %collective-permute-start.11 = (f32[1,160,128]{2,1,0:T(8,128)S(1)}, f32[1,160,128]{2,1,0:T(8,128)S(1)}, u32[]{:S(2)}, u32[]{:S(2)}) collective-permute-start(f32[1,160,128]{2,1,0:T(8,128)S(1)} %get-tuple-element.52), channel_id=1, source_target_pairs={{0,1},{1,2},{2,3},{3,0},{4,5},{5,6},{6,7},{7,4},{8,9},{9,10},{10,1... | collective-permute-start | bytes 245768 | tf_op jit(solution)/shard_map/ppermute | solution.py:487
  72.1 17.1 %collective-permute-start.12 = (f32[1,160,128]{2,1,0:T(8,128)S(1)}, f32[1,160,128]{2,1,0:T(8,128)S(1)}, u32[]{:S(2)}, u32[]{:S(2)}) collective-permute-start(f32[1,160,128]{2,1,0:T(8,128)S(1)} %get-tuple-element.53), channel_id=1, source_target_pairs={{0,2},{1,3},{2,0},{3,1},{4,6},{5,7},{6,4},{7,5},{8,10},{9,11},{10,... | collective-permute-start | bytes 245768 | tf_op jit(solution)/shard_map/ppermute | solution.py:487
  76.6 12.6 %collective-permute-start.13 = (f32[1,160,128]{2,1,0:T(8,128)S(1)}, f32[1,160,128]{2,1,0:T(8,128)S(1)}, u32[]{:S(2)}, u32[]{:S(2)}) collective-permute-start(f32[1,160,128]{2,1,0:T(8,128)S(1)} %get-tuple-element.54), channel_id=1, source_target_pairs={{0,3},{1,0},{2,1},{3,2},{4,7},{5,4},{6,5},{7,6},{8,11},{9,8},{10,9... | collective-permute-start | bytes 245768 | tf_op jit(solution)/shard_map/ppermute | solution.py:487
  89.2 16.3 %collective-permute-start.14 = (f32[1,160,128]{2,1,0:T(8,128)S(1)}, f32[1,160,128]{2,1,0:T(8,128)S(1)}, u32[]{:S(2)}, u32[]{:S(2)}) collective-permute-start(f32[1,160,128]{2,1,0:T(8,128)S(1)} %select_select_fusion), channel_id=1, source_target_pairs={{0,4},{4,8},{8,12},{12,16},{16,20},{20,24},{24,28},{28,32},{32,36}... | collective-permute-start | bytes 245768 | tf_op jit(solution)/shard_map/ppermute | solution.py:597

commit v4 on v3

--- a/solution.py
+++ b/solution.py
@@ -86,69 +86,62 @@
         yield x - (jnp.roll(flux, -1, axis=1) - flux) - (w_n * (x_n + x) - w_s * (x + x_s))
 
 
-def advect_inner_kernel(first, rows_each, peers, coef, *refs):
-    sources, outs, held, sems = refs[:5], refs[5 : 5 + peers + 2], refs[-6:-1], refs[-1]
-    for copy in copy_all(list(zip(sources, held)), sems):
-        copy.wait()
-    zonal, merid, thick, theta, ground = held
+def edges_kernel(merid, thick, theta, ground, to_north, to_south, thick_s, theta_s, merid_s, ground_s, sems):
     lat_rows, levels, _ = thick.shape
-    to_north, to_south = outs[peers:]
-    me = lax.axis_index("lev")
-    for step in range(peers):
-        owner = wrapped(me, step, peers)
-        for place in range(rows_each):
-            row = first + owner * rows_each + place
-            t, t_s, t_n = thick[row], thick[row - 1], thick[row + 1]
-            h, h_s, h_n = theta[row] * t, theta[row - 1] * t_s, theta[row + 1] * t_n
-            fields = advect_row(row, coef, zonal[row], merid[row], t, h, t_s, h_s, t_n, h_n, merid[row + 1])
-            for field, new in enumerate(fields):
-                store_packed(outs[step], (place, field), new)
     top = lat_rows - 1
-    to_north[pl.ds(0, levels), :] = thick[top]
-    to_north[pl.ds(levels, levels), :] = theta[top] * thick[top]
-    to_north[pl.ds(2 * levels, 1), :] = ground[pl.ds(top, 1), :]
-    to_south[pl.ds(0, levels), :] = thick[0]
-    to_south[pl.ds(levels, levels), :] = theta[0] * thick[0]
-    to_south[pl.ds(2 * levels, levels), :] = merid[0]
-
-
-def ends_of(source, target, low, high):
-    rows = source.shape[0]
-    return [
-        (source.at[pl.ds(0, low)], target.at[pl.ds(0, low)]),
-        (source.at[pl.ds(rows - high, high)], target.at[pl.ds(low, high)]),
-    ]
-
-
-def advect_outer_kernel(peers, coef, *refs):
-    sources, (halo_s, halo_n) = refs[:4], refs[4:6]
-    outs, held, sems = refs[6 : 6 + peers], refs[-5:-1], refs[-1]
-    lat_rows, levels, _ = sources[0].shape
     copies = []
-    for source, target in zip(sources, held):
-        copies += ends_of(source, target, peers, 2)
-    for copy in copy_all(copies, sems):
-        copy.wait()
-    zonal, merid, thick, theta = held
+    for source, target in ((thick, thick_s), (theta, theta_s)):
+        copies += [(source.at[pl.ds(0, 1)], target.at[pl.ds(0, 1)]), (source.at[pl.ds(top, 1)], target.at[pl.ds(1, 1)])]
+    wait_all(copy_all([*copies, (merid.at[pl.ds(0, 1)], merid_s), (ground, ground_s)], sems))
+    to_north[pl.ds(0, levels), :] = thick_s[1]
+    to_north[pl.ds(levels, levels), :] = theta_s[1] * thick_s[1]
+    to_north[pl.ds(2 * levels, 1), :] = ground_s[pl.ds(top, 1), :]
+    to_south[pl.ds(0, levels), :] = thick_s[0]
+    to_south[pl.ds(levels, levels), :] = theta_s[0] * thick_s[0]
+    to_south[pl.ds(2 * levels, levels), :] = merid_s[0]
+
+
+def advect_kernel(first, rows_each, peers, coef, halo, *refs):
+    fields, outs, held, sems = refs[:4], refs[4 : 4 + peers], refs[4 + peers : -1], refs[-1]
+    lat_rows, levels, _ = fields[0].shape
     top = lat_rows - 1
     me = lax.axis_index("lev")
+    part = lambda i: halo[pl.ds(i * levels, levels), :]
+    owned = [first + wrapped(me, step, peers) * rows_each for step in range(peers)]
+    reach = ((0, rows_each), (0, rows_each + 1), (1, rows_each + 2), (1, rows_each + 2))
+    starts = [[jnp.clip(row - before, 0, lat_rows - count) for before, count in reach] for row in owned]
+    arriving = [
+        copy_all(
+            [
+                (field.at[pl.ds(start, count)], target.at[step])
+                for field, target, start, (_, count) in zip(fields, held, starts[step], reach)
+            ],
+            sems,
+            4 * step,
+        )
+        for step in range(peers)
+    ]
     for step in range(peers):
-        owner = wrapped(me, step, peers)
-        is_first, is_last = owner == 0, owner == peers - 1
-        row = jnp.where(is_last, top, owner)
-        at = jnp.where(is_last, peers + 1, owner)
-        low, high = jnp.maximum(at - 1, 0), jnp.minimum(at + 1, peers + 1)
-        t, t_s, t_n = thick[at], thick[low], thick[high]
-        h, h_s, h_n = theta[at] * t, theta[low] * t_s, theta[high] * t_n
-        part = lambda ref, i: ref[pl.ds(i * levels, levels), :]
-        t_s = jnp.where(is_first, part(halo_s, 0), t_s)
-        h_s = jnp.where(is_first, part(halo_s, 1), h_s)
-        t_n = jnp.where(is_last, part(halo_n, 0), t_n)
-        h_n = jnp.where(is_last, part(halo_n, 1), h_n)
-        w_n = jnp.where(is_last, part(halo_n, 2), merid[high])
-        fields = advect_row(row, coef, zonal[at], merid[at], t, h, t_s, h_s, t_n, h_n, w_n)
-        for field, new in enumerate(fields):
-            store_packed(outs[step], (0, field), new)
+        wait_all(arriving[step])
+        zonal, merid, thick, theta = (ref.at[step] for ref in held)
+        z_at, w_at, t_at, _ = (owned[step] - start for start in starts[step])
+        for place in range(rows_each):
+            row = owned[step] + place
+            at = t_at + place
+            low, high = jnp.maximum(at - 1, 0), jnp.minimum(at + 1, rows_each + 1)
+            t, t_s, t_n = thick[at], thick[low], thick[high]
+            h, h_s, h_n = theta[at] * t, theta[low] * t_s, theta[high] * t_n
+            w, w_n = merid[w_at + place], merid[jnp.minimum(w_at + place + 1, rows_each)]
+            if first == 0 and place == 0:
+                t_s = jnp.where(row == 0, part(0), t_s)
+                h_s = jnp.where(row == 0, part(1), h_s)
+            if first + peers * rows_each == lat_rows and place == rows_each - 1:
+                t_n = jnp.where(row == top, part(0), t_n)
+                h_n = jnp.where(row == top, part(1), h_n)
+                w_n = jnp.where(row == top, part(2), w_n)
+            fields_new = advect_row(row, coef, zonal[z_at + place], w, t, h, t_s, h_s, t_n, h_n, w_n)
+            for field, new in enumerate(fields_new):
+                store_packed(outs[step], (place, field), new)
 
 
 def target_edges(surface, sigma):
@@ -347,23 +340,19 @@
     return jnp.roll(x, 1, axis=1)
 
 
-def inner_final_kernel(
-    levels, first, flag, faces, p0, p1, p2, p3, ground, table, zonal_h, merid_h, t0, t1, t2, t3, after,
-    zonal_out, merid_out, thick_out, theta_out, edge_states,
-    order, zonal, merid, zonal_s, merid_s, thick_s, theta_s, carried, b0, b1, b2, b3, sems,
+def upper_final_kernel(
+    levels, first, flag, faces, p0, p1, p2, p3, ground, table, zonal, merid, b0, b1, b2, b3, after,
+    zonal_out, merid_out, thick_out, theta_out, edge_state,
+    order, zonal_s, merid_s, thick_s, theta_s, carried, sems,
 ):
     del after
-    count, _, _ = zonal.shape
-    _, block, width = zonal_h.shape
-    inner = pl.ds(first, count)
-    winds = copy_all([(zonal_h.at[inner], zonal), (merid_h.at[inner], merid)], sems)
-    tables = (b0, b1, b2, b3)
-    basis = copy_all(list(zip((t0, t1, t2, t3), tables)), sems, 2)
+    lat_rows, block, width = zonal.shape
+    count = lat_rows - first
+    rows = pl.ds(first, count)
     me = lax.axis_index("lev")
     level = (me * block).astype(F32)
     gather_messages(me, (p0, p1, p2, p3), order)
     carried[...] = jnp.zeros_like(carried)
-    wait_all(winds)
 
     def one_row(i, _):
         row = first + i
@@ -371,114 +360,81 @@
         theta_s[i] = theta
         thick_s[i] = thick
         now = (theta, mid, geopot)
-        zonal_s[i] = zonal[i] - push(now, tuple(around(x) for x in now))
+        zonal_s[i] = zonal[row] - push(now, tuple(around(x) for x in now))
         before = (carried[0], carried[1], carried[2])
-        merid_s[jnp.maximum(i - 1, 0)] = merid[i] - faces[row] * push(now, before)
+        merid_s[jnp.maximum(i - 1, 0)] = merid[row] - faces[row] * push(now, before)
         for field, x in enumerate(now):
             carried[field] = x
 
         @pl.when(i == 0)
         def _():
             for field, x in enumerate(now):
-                edge_states[0, field] = x
+                edge_state[field] = x
 
         return 0
 
     lax.fori_loop(0, count, one_row, 0)
-    for field in range(3):
-        edge_states[1, field] = carried[field]
-    early = copy_all([(theta_s, theta_out.at[inner]), (thick_s, thick_out.at[inner])], sems, 6)
-    wait_all(basis)
+    early = copy_all([(theta_s, theta_out.at[rows]), (thick_s, thick_out.at[rows])], sems)
 
     @pl.when(flag[0] != 0)
     def _():
-        filter_rows(zonal_s, count, table[pl.ds(first, count), :], tables, block)
+        tables = (b0, b1, b2, b3)
+        filter_rows(zonal_s, count, table[rows, :], tables, block)
         filter_rows(merid_s, count - 1, table[pl.ds(first + 1, count - 1), :], tables, block)
 
     late = copy_all(
         [
-            (zonal_s, zonal_out.at[inner]),
+            (zonal_s, zonal_out.at[rows]),
             (merid_s.at[pl.ds(0, count - 1)], merid_out.at[pl.ds(first + 1, count - 1)]),
         ],
         sems,
-        8,
+        2,
     )
     wait_all(early + late)
 
 
-def rows_back(source, target, low):
-    rows = target.shape[0]
-    return [
-        (source.at[pl.ds(0, low)], target.at[pl.ds(0, low)]),
-        (source.at[pl.ds(low, 1)], target.at[pl.ds(rows - 1, 1)]),
-    ]
-
-
-def outer_zonal_kernel(
-    levels, flag, p0, p1, p2, p3, ground, table, zonal_h, t0, t1, t2, t3, zonal_in, thick_in, theta_in,
-    zonal_out, thick_out, theta_out, states,
-    order, zonal, zonal_s, thick_s, theta_s, b0, b1, b2, b3, sems,
+def lower_final_kernel(
+    levels, flag, faces, south, halo_s, edge_state, p0, p1, p2, p3, ground, table, zonal, merid, b0, b1, b2, b3,
+    zonal_in, merid_in, thick_in, theta_in,
+    zonal_out, merid_out, thick_out, theta_out,
+    order, winds_s, thick_s, theta_s, sems,
 ):
-    del zonal_in, thick_in, theta_in
-    lat_rows, block, width = zonal_h.shape
+    del zonal_in, merid_in, thick_in, theta_in
     count = order.shape[0]
-    winds = copy_all(ends_of(zonal_h, zonal, count - 1, 1), sems)
-    tables = (b0, b1, b2, b3)
-    basis = copy_all(list(zip((t0, t1, t2, t3), tables)), sems, 2)
+    _, block, width = zonal.shape
     me = lax.axis_index("lev")
     level = (me * block).astype(F32)
     gather_messages(me, (p0, p1, p2, p3), order)
-    wait_all(winds)
-    rows = [*range(count - 1), lat_rows - 1]
-    for i, row in enumerate(rows):
-        theta, thick, mid, geopot = column_state(order, (i,), block, width, level, levels, ground[pl.ds(row, 1), :])
-        theta_s[i] = theta
-        thick_s[i] = thick
+    state = lambda ref, i, line: column_state(ref, (i,), block, width, level, levels, line)
+    theta, _, mid, geopot = state(south, 0, halo_s[pl.ds(2 * block, 1), :])
+    before = (theta, mid, geopot)
+    for row in range(count):
+        theta, thick, mid, geopot = state(order, row, ground[pl.ds(row, 1), :])
+        theta_s[row] = theta
+        thick_s[row] = thick
         now = (theta, mid, geopot)
-        zonal_s[i] = zonal[i] - push(now, tuple(around(x) for x in now))
-        for field, x in enumerate(now):
-            states[i, field] = x
-    early = copy_all(rows_back(theta_s, theta_out, count - 1) + rows_back(thick_s, thick_out, count - 1), sems, 6)
-    wait_all(basis)
+        winds_s[row] = zonal[row] - push(now, tuple(around(x) for x in now))
+        winds_s[count + row] = merid[row] - faces[row] * push(now, before)
+        before = now
+    now = tuple(edge_state[field] for field in range(3))
+    winds_s[2 * count] = merid[count] - faces[count] * push(now, before)
+    rows = pl.ds(0, count)
+    early = copy_all([(theta_s, theta_out.at[rows]), (thick_s, thick_out.at[rows])], sems)
 
     @pl.when(flag[0] != 0)
     def _():
-        picked = jnp.concatenate([table[pl.ds(0, count - 1), :], table[pl.ds(lat_rows - 1, 1), :]], axis=0)
-        filter_rows(zonal_s, count, picked, tables, block)
-
-    late = copy_all(rows_back(zonal_s, zonal_out, count - 1), sems, 10)
+        picked = jnp.concatenate([table[rows, :], table[pl.ds(0, count + 1), :]], axis=0)
+        filter_rows(winds_s, 2 * count + 1, picked, (b0, b1, b2, b3), block)
+
+    late = copy_all(
+        [
+            (winds_s.at[rows], zonal_out.at[rows]),
+            (winds_s.at[pl.ds(count, count + 1)], merid_out.at[pl.ds(0, count + 1)]),
+        ],
+        sems,
+        2,
+    )
     wait_all(early + late)
-
-
-def outer_merid_kernel(
-    levels, flag, faces, south, halo_s, states, edge_states, table, merid_h, t0, t1, t2, t3, merid_in,
-    merid_out, merid, merid_s, b0, b1, b2, b3, sems,
-):
-    del merid_in
-    lat_rows, block, width = merid_h.shape
-    outer = states.shape[0]
-    winds = copy_all(ends_of(merid_h, merid, outer, 1), sems)
-    tables = (b0, b1, b2, b3)
-    basis = copy_all(list(zip((t0, t1, t2, t3), tables)), sems, 2)
-    level = (lax.axis_index("lev") * block).astype(F32)
-    theta, _, mid, geopot = column_state(south, (0,), block, width, level, levels, halo_s[pl.ds(2 * block, 1), :])
-    before = (theta, mid, geopot)
-    fields = lambda ref, i: tuple(ref[i, f] for f in range(3))
-    top = lat_rows - 1
-    steps = [(i, fields(states, i)) for i in range(outer - 1)] + [(outer - 1, fields(edge_states, 0))]
-    wait_all(winds)
-    for row, now in steps:
-        merid_s[row] = merid[row] - faces[row] * push(now, before)
-        before = now
-    merid_s[outer] = merid[outer] - faces[top] * push(fields(states, outer - 1), fields(edge_states, 1))
-    wait_all(basis)
-
-    @pl.when(flag[0] != 0)
-    def _():
-        picked = jnp.concatenate([table[pl.ds(0, outer), :], table[pl.ds(top, 1), :]], axis=0)
-        filter_rows(merid_s, outer + 1, picked, tables, block)
-
-    wait_all(copy_all(rows_back(merid_s, merid_out, outer), sems, 6))
 
 
 def exchanged(parts):
@@ -509,40 +465,46 @@
     rows_of = lambda n: pltpu.VMEM((n, block, width), F32)
     dma = lambda n: pltpu.SemaphoreType.DMA((n,))
 
-    inner_each = lat_rows // peers - 1
-    inner = inner_each * peers
-    outer, first = peers, peers - 1
+    lower_each = 1
+    upper_each = lat_rows // peers - lower_each
+    first = lower_each * peers
+    upper = lat_rows - first
     data_rows = packed_rows(block, width)
     message_rows = data_rows + 16
     stay = lambda *arrays: [pltpu.with_memory_space_constraint(x, pltpu.HBM) for x in arrays]
-    winds_and_state = stay(zonal_wind, meridional_wind, thickness, potential_temp)
-    ground_h, zonal_h, merid_h = stay(surface_geo, zonal_wind, meridional_wind)
-
-    *inner_sent, to_north, to_south = pl.pallas_call(
-        lambda *refs: advect_inner_kernel(first, inner_each, peers, *refs),
-        out_shape=[shape(inner_each, 2, data_rows, LANES)] * peers
-        + [shape(2 * block + 8, width), shape(3 * block, width)],
-        in_specs=[SMEM] + [hbm] * 5,
-        out_specs=[VMEM] * (peers + 2),
-        scratch_shapes=[rows_of(lat_rows)] * 4 + [pltpu.VMEM((lat_rows, width), F32), dma(5)],
-        compiler_params=params(12),
-        cost_estimate=cost(5),
-        name="advect_inner",
-    )(coef, *winds_and_state, ground_h)
-    inner_columns = exchanged(inner_sent)
+    field = shape(lat_rows, block, width)
+
+    fields = stay(zonal_wind, meridional_wind, thickness, potential_temp)
+    to_north, to_south = pl.pallas_call(
+        edges_kernel,
+        out_shape=[shape(2 * block + 8, width), shape(3 * block, width)],
+        in_specs=[hbm] * 4,
+        out_specs=[VMEM] * 2,
+        scratch_shapes=[rows_of(2), rows_of(2), rows_of(1), pltpu.VMEM((lat_rows, width), F32), dma(6)],
+        compiler_params=params(8),
+        cost_estimate=cost(1),
+        name="edges",
+    )(*fields[1:], *stay(surface_geo))
+    halo_n = lax.ppermute(to_south, "lat", southward)
     halo_s = lax.ppermute(to_north, "lat", northward)
-    halo_n = lax.ppermute(to_south, "lat", southward)
-    outer_sent = pl.pallas_call(
-        lambda *refs: advect_outer_kernel(peers, *refs),
-        out_shape=[shape(1, 2, data_rows, LANES)] * peers,
-        in_specs=[SMEM] + [hbm] * 4 + [VMEM] * 2,
-        out_specs=[VMEM] * peers,
-        scratch_shapes=[rows_of(peers + 2)] * 4 + [dma(8)],
-        compiler_params=params(12),
-        cost_estimate=cost(3),
-        name="advect_outer",
-    )(coef, *winds_and_state, halo_s, halo_n)
-    outer_columns = exchanged(outer_sent)
+
+    def advect(start, each, halo, name):
+        return pl.pallas_call(
+            lambda *refs: advect_kernel(start, each, peers, *refs),
+            out_shape=[shape(each, 2, data_rows, LANES)] * peers,
+            in_specs=[SMEM, VMEM] + [hbm] * 4,
+            out_specs=[VMEM] * peers,
+            scratch_shapes=[
+                pltpu.VMEM((peers, each + extra, block, width), F32) for extra in (0, 1, 2, 2)
+            ]
+            + [dma(4 * peers)],
+            compiler_params=params(12),
+            cost_estimate=cost(1 + 2 * each),
+            name=name,
+        )(coef, halo, *fields)
+
+    upper_columns = exchanged(advect(first, upper_each, halo_n, "advect_upper"))
+    lower_columns = exchanged(advect(0, lower_each, halo_s, "advect_lower"))
 
     def remap(columns, each, name, after):
         lanes = tile_count(width) * LANES
@@ -562,67 +524,54 @@
             name=name,
         )(*columns, *after)
 
-    inner_remapped = remap(inner_columns, inner_each, "remap_inner", [])
-    inner_messages = exchanged(inner_remapped)
-    outer_remapped = remap(outer_columns, 1, "remap_outer", inner_messages[1:2])
-    outer_messages = exchanged(outer_remapped)
+    upper_remapped = remap(upper_columns, upper_each, "remap_upper", lower_columns[:1])
+    upper_messages = exchanged(upper_remapped)
+    lower_remapped = remap(lower_columns, lower_each, "remap_lower", upper_messages[1:2])
+    lower_messages = exchanged(lower_remapped)
+    step_of_last = (lax.axis_index("lev") + 1) % peers
+    _, *candidates = lax.optimization_barrier((lower_remapped[0], *upper_messages))
+    last_message = candidates[0][-1:]
+    for step in range(1, peers):
+        last_message = jnp.where(step_of_last == step, candidates[step][-1:], last_message)
+    south = lax.ppermute(last_message, "lat", northward)
 
     high, low, wave = fourier_tables(width)
     active = (jnp.asarray(wave)[None, :] >= cutoff[:, None]) & (polar_mask[:, None] != 0)
     table = jnp.where(active, damping - 1.0, 0.0)
-    tables = stay(*(jnp.asarray(x) for x in (high, low, np.ascontiguousarray(high.T), np.ascontiguousarray(low.T))))
-    basis_scratch = [pltpu.VMEM((width, width), BF16)] * 4
-    field = shape(lat_rows, block, width)
-
-    zonal_next, merid_next, thick_next, theta_next, edge_states = pl.pallas_call(
-        lambda *refs: inner_final_kernel(levels, first, *refs),
-        out_shape=[field] * 4 + [shape(2, 3, block, width)],
-        in_specs=[SMEM] * 2 + [VMEM] * (peers + 2) + [hbm] * 6 + [pl.BlockSpec(memory_space=pl.ANY)],
+    tables = [jnp.asarray(x) for x in (high, low, np.ascontiguousarray(high.T), np.ascontiguousarray(low.T))]
+
+    *partial, edge_state = pl.pallas_call(
+        lambda *refs: upper_final_kernel(levels, first, *refs),
+        out_shape=[field] * 4 + [shape(3, block, width)],
+        in_specs=[SMEM] * 2 + [VMEM] * (peers + 8) + [pl.BlockSpec(memory_space=pl.ANY)],
         out_specs=[hbm] * 4 + [VMEM],
-        scratch_shapes=[pltpu.VMEM((inner, message_rows, LANES), F32)]
-        + [rows_of(inner)] * 6
-        + [rows_of(3), *basis_scratch, dma(10)],
-        compiler_params=params(20),
-        cost_estimate=cost(8),
-        name="final_inner",
+        scratch_shapes=[pltpu.VMEM((upper, message_rows, LANES), F32)]
+        + [rows_of(upper)] * 4
+        + [rows_of(3), dma(4)],
+        compiler_params=params(18),
+        cost_estimate=cost(7),
+        name="final_upper",
     )(
-        flag, faces, *inner_messages, surface_geo, table, zonal_h, merid_h, *tables, outer_remapped[0]
+        flag, faces, *upper_messages, surface_geo, table, zonal_wind, meridional_wind, *tables, lower_remapped[0]
     )
-
-    edge_states, *outer_messages = lax.optimization_barrier((edge_states, *outer_messages))
-    step_of_last = (lax.axis_index("lev") + 1) % peers
-    last_message = outer_messages[0]
-    for step in range(1, peers):
-        last_message = jnp.where(step_of_last == step, outer_messages[step], last_message)
-    south = lax.ppermute(last_message, "lat", northward)
-
-    zonal_next, thick_next, theta_next, states = pl.pallas_call(
-        lambda *refs: outer_zonal_kernel(levels, *refs),
-        out_shape=[field] * 3 + [shape(outer, 3, block, width)],
-        in_specs=[SMEM] + [VMEM] * (peers + 2) + [hbm] * 8,
-        out_specs=[hbm] * 3 + [VMEM],
-        scratch_shapes=[pltpu.VMEM((outer, message_rows, LANES), F32)]
-        + [rows_of(outer)] * 4
-        + [*basis_scratch, dma(12)],
-        input_output_aliases={peers + 8: 0, peers + 9: 1, peers + 10: 2},
-        compiler_params=params(16),
-        cost_estimate=cost(4),
-        name="final_outer_zonal",
-    )(
-        flag, *outer_messages, surface_geo, table, zonal_h, *tables, zonal_next, thick_next, theta_next
+    edge_state, *lower_messages = lax.optimization_barrier((edge_state, *lower_messages))
+    return tuple(
+        pl.pallas_call(
+            lambda *refs: lower_final_kernel(levels, *refs),
+            out_shape=[field] * 4,
+            in_specs=[SMEM] * 2 + [VMEM] * (peers + 11) + [hbm] * 4,
+            out_specs=[hbm] * 4,
+            scratch_shapes=[pltpu.VMEM((first, message_rows, LANES), F32)]
+            + [rows_of(2 * first + 1), rows_of(first), rows_of(first), dma(4)],
+            input_output_aliases={peers + 13 + i: i for i in range(4)},
+            compiler_params=params(16),
+            cost_estimate=cost(6),
+            name="final_lower",
+        )(
+            flag, faces, south, halo_s, edge_state, *lower_messages, surface_geo, table, zonal_wind, meridional_wind, *tables,
+            *partial,
+        )
     )
-    merid_next = pl.pallas_call(
-        lambda *refs: outer_merid_kernel(levels, *refs),
-        out_shape=field,
-        in_specs=[SMEM] * 2 + [VMEM] * 5 + [hbm] * 6,
-        out_specs=hbm,
-        scratch_shapes=[rows_of(outer + 1)] * 2 + [*basis_scratch, dma(8)],
-        input_output_aliases={12: 0},
-        compiler_params=params(16),
-        cost_estimate=cost(3),
-        name="final_outer_merid",
-    )(flag, faces, south, halo_s, states, edge_states, table, merid_h, *tables, merid_next)
-    return zonal_next, merid_next, thick_next, theta_next
 
 
 def solution(mesh):

time: 111 us -> 108 us (0.973)
  the two profiles are of different devices: /device:TPU:23 before, /device:TPU:41 now
where the time goes in v4:
time: 108 us
  starting transfers between devices  59.8 us (55%)
  Pallas kernels  27.7 us (26%)
  waiting for transfers between devices  16.7 us (15%)
  between operations  1.71 us (2%)
    ppermute x12, starting transfers between devices, exchanged(): lax.ppermute(parts[step], 'lev', [(i, (i + step) % peers) for i in range(...  32.9 us
    ppermute x1, starting transfers between devices, body(): south = lax.ppermute(last_message, 'lat', northward)  21.6 us
    ppermute x12, waiting for transfers between devices, exchanged(): lax.ppermute(parts[step], 'lev', [(i, (i + step) % peers) for i in range(...  12.3 us
    pallas_call x2, Pallas kernels, remap(): pl.pallas_call(lambda *refs: remap_kernel(width, block, peers, *refs), ou...  8.32 us
    pallas_call x1, Pallas kernels, body(): pl.pallas_call(lambda *refs: upper_final_kernel(levels, first, *refs), ou...  7.01 us
    pallas_call x2, Pallas kernels, advect(): pl.pallas_call(lambda *refs: advect_kernel(start, each, peers, *refs), ou...  6.78 us
    pallas_call x1, Pallas kernels, body(): pl.pallas_call(lambda *refs: lower_final_kernel(levels, *refs), out_shape...  4.43 us
    ppermute x1, waiting for transfers between devices, body(): halo_n = lax.ppermute(to_south, 'lat', southward)  4.4 us
  transfers between devices with their start and end apart: 15, of which 5 were waited for; matrix products, arithmetic and copies ran while one was open for 1% of the time, Pallas kernels for 21%

profile of v4, /device:TPU:41, one launch (start us, length us, event | category | flops | bytes accessed | tf_op | source)
XLA Modules:
  0.0 107.5 jit_solution(2159802375979749410)
XLA Ops:
  0.6 1.1 %edges.1 = (f32[72,576]{1,0:T(8,128)S(1)}, f32[96,576]{1,0:T(8,128)S(1)}) custom-call(f32[12,32,576]{2,1,0:T(8,128)} %refs_12_.2, f32[12,32,576]{2,1,0:T(8,128)} %refs_4_.3, f32[12,32,576]{2,1,0:T(8,128)} %refs_5_.3, f32[12,576]{1,0:T(8,128)} %refs_9_.3), custom_call_target="tpu_custom_call" | custom-call | flops 1100000000 | bytes 3600000 | tf_op jit(solution)/shard_map/edges/pallas_call | solution.py:478
  1.8 3.3 %collective-permute-start = (f32[72,576]{1,0:T(8,128)S(1)}, f32[72,576]{1,0:T(8,128)S(1)}, u32[]{:S(2)}, u32[]{:S(2)}) collective-permute-start(f32[72,576]{1,0:T(8,128)S(1)} %get-tuple-element.36), channel_id=1, source_target_pairs={{0,4},{4,8},{8,12},{12,16},{16,20},{20,24},{24,28},{28,32},{32,36}... | collective-permute-start | bytes 497672 | tf_op jit(solution)/shard_map/ppermute | solution.py:489
  5.1 1.9 %collective-permute-start.4 = (f32[96,576]{1,0:T(8,128)S(1)}, f32[96,576]{1,0:T(8,128)S(1)}, u32[]{:S(2)}, u32[]{:S(2)}) collective-permute-start(f32[96,576]{1,0:T(8,128)S(1)} %get-tuple-element.41), channel_id=1, source_target_pairs={{4,0},{8,4},{12,8},{16,12},{20,16},{24,20},{28,24},{32,28},{36,32}... | collective-permute-start | bytes 663560 | tf_op jit(solution)/shard_map/ppermute | solution.py:488
  7.1 0.0 copy-start.10
  7.2 0.1 slice_bitcast_fusion.1
  7.2 0.6 copy-done.10
  7.8 0.6 broadcast_compare_fusion
  9.1 4.4 %collective-permute-done.4.refs_1_ = f32[96,576]{1,0:T(8,128)S(1)} collective-permute-done((f32[96,576]{1,0:T(8,128)S(1)}, f32[96,576]{1,0:T(8,128)S(1)}, u32[]{:S(2)}, u32[]{:S(2)}) %collective-permute-start.4) | collective-permute-done | bytes 221216 | tf_op jit(solution)/shard_map/ppermute | solution.py:488
  13.5 3.5 %advect_upper.1 = (f32[2,2,144,128]{3,2,1,0:T(8,128)S(1)}, f32[2,2,144,128]{3,2,1,0:T(8,128)S(1)}, f32[2,2,144,128]{3,2,1,0:T(8,128)S(1)}, f32[2,2,144,128]{3,2,1,0:T(8,128)S(1)}) custom-call(f32[2,12]{1,0:T(2,128)S(1)} %fusion.refs_0_, f32[96,576]{1,0:T(8,128)S(1)} %collective-permute-done.4.refs_1_, f32[12,32,576]{2,1,0:T(8,128)} %refs_11_.2, ...), custom_call_target="tpu_custom_call" | custom-call | flops 5500000256 | bytes 18000000 | tf_op jit(solution)/shard_map/advect_upper/pallas_call | solution.py:492
  17.0 3.1 %collective-permute-start.5 = (f32[2,2,144,128]{3,2,1,0:T(8,128)S(1)}, f32[2,2,144,128]{3,2,1,0:T(8,128)S(1)}, u32[]{:S(2)}, u32[]{:S(2)}) collective-permute-start(f32[2,2,144,128]{3,2,1,0:T(8,128)S(1)} %get-tuple-element.43), channel_id=1, source_target_pairs={{0,1},{1,2},{2,3},{3,0},{4,5},{5,6},{6,7},{7,4},{8,9},{9,10},{10,1... | collective-permute-start | bytes 884744 | tf_op jit(solution)/shard_map/ppermute | solution.py:443
  20.1 5.1 %collective-permute-start.6 = (f32[2,2,144,128]{3,2,1,0:T(8,128)S(1)}, f32[2,2,144,128]{3,2,1,0:T(8,128)S(1)}, u32[]{:S(2)}, u32[]{:S(2)}) collective-permute-start(f32[2,2,144,128]{3,2,1,0:T(8,128)S(1)} %get-tuple-element.44), channel_id=1, source_target_pairs={{0,2},{1,3},{2,0},{3,1},{4,6},{5,7},{6,4},{7,5},{8,10},{9,11},{10,... | collective-permute-start | bytes 884744 | tf_op jit(solution)/shard_map/ppermute | solution.py:443
  25.2 2.4 %collective-permute-start.7 = (f32[2,2,144,128]{3,2,1,0:T(8,128)S(1)}, f32[2,2,144,128]{3,2,1,0:T(8,128)S(1)}, u32[]{:S(2)}, u32[]{:S(2)}) collective-permute-start(f32[2,2,144,128]{3,2,1,0:T(8,128)S(1)} %get-tuple-element.45), channel_id=1, source_target_pairs={{0,3},{1,0},{2,1},{3,2},{4,7},{5,4},{6,5},{7,6},{8,11},{9,8},{10,9... | collective-permute-start | bytes 884744 | tf_op jit(solution)/shard_map/ppermute | solution.py:443
  27.6 0.0 collective-permute-done.refs_1_.refs_3_
  27.6 3.3 %advect_lower.1 = (f32[1,2,144,128]{3,2,1,0:T(8,128)S(1)}, f32[1,2,144,128]{3,2,1,0:T(8,128)S(1)}, f32[1,2,144,128]{3,2,1,0:T(8,128)S(1)}, f32[1,2,144,128]{3,2,1,0:T(8,128)S(1)}) custom-call(f32[2,12]{1,0:T(2,128)S(1)} %fusion.refs_0_, f32[72,576]{1,0:T(8,128)S(1)} %collective-permute-done.refs_1_.refs_3_, f32[12,32,576]{2,1,0:T(8,128)} %refs_11_.2, ...), custom_call_target="tpu_custom_call" | custom-call | flops 3300000000 | bytes 10800000 | tf_op jit(solution)/shard_map/advect_lower/pallas_call | solution.py:492
  30.9 0.1 collective-permute-start.1
  31.0 1.8 %collective-permute-start.2 = (f32[1,2,144,128]{3,2,1,0:T(8,128)S(1)}, f32[1,2,144,128]{3,2,1,0:T(8,128)S(1)}, u32[]{:S(2)}, u32[]{:S(2)}) collective-permute-start(f32[1,2,144,128]{3,2,1,0:T(8,128)S(1)} %get-tuple-element.39), channel_id=1, source_target_pairs={{0,2},{1,3},{2,0},{3,1},{4,6},{5,7},{6,4},{7,5},{8,10},{9,11},{10,... | collective-permute-start | bytes 442376 | tf_op jit(solution)/shard_map/ppermute | solution.py:443
  32.8 0.5 collective-permute-done.5.refs_1_
  33.3 4.9 %collective-permute-start.3 = (f32[1,2,144,128]{3,2,1,0:T(8,128)S(1)}, f32[1,2,144,128]{3,2,1,0:T(8,128)S(1)}, u32[]{:S(2)}, u32[]{:S(2)}) collective-permute-start(f32[1,2,144,128]{3,2,1,0:T(8,128)S(1)} %get-tuple-element.40), channel_id=1, source_target_pairs={{0,3},{1,0},{2,1},{3,2},{4,7},{5,4},{6,5},{7,6},{8,11},{9,8},{10,9... | collective-permute-start | bytes 442376 | tf_op jit(solution)/shard_map/ppermute | solution.py:443
  38.1 0.0 collective-permute-done.6.refs_2_
  38.1 9.2 %collective-permute-done.7.refs_3_ = f32[2,2,144,128]{3,2,1,0:T(8,128)S(1)} collective-permute-done((f32[2,2,144,128]{3,2,1,0:T(8,128)S(1)}, f32[2,2,144,128]{3,2,1,0:T(8,128)S(1)}, u32[]{:S(2)}, u32[]{:S(2)}) %collective-permute-start.7) | collective-permute-done | bytes 294944 | tf_op jit(solution)/shard_map/ppermute | solution.py:443
  47.3 0.0 copy-start.7
  47.4 0.0 copy-start.8
  47.4 5.6 %remap_upper.1 = (f32[2,160,128]{2,1,0:T(8,128)S(1)}, f32[2,160,128]{2,1,0:T(8,128)S(1)}, f32[2,160,128]{2,1,0:T(8,128)S(1)}, f32[2,160,128]{2,1,0:T(8,128)S(1)}) custom-call(f32[2,2,144,128]{3,2,1,0:T(8,128)S(1)} %get-tuple-element.42.refs_0_, f32[2,2,144,128]{3,2,1,0:T(8,128)S(1)} %collective-permute-done.5.refs_1_, ...), custom_call_target="tpu_custom_call" | custom-call | flops 7699999744 | bytes 25200000 | tf_op jit(solution)/shard_map/remap_upper/pallas_call | solution.py:511
  53.0 0.0 copy-start.9
  53.0 0.5 collective-permute-start.8
  53.5 0.0 copy-done.7
  53.5 0.0 copy-done.8
  53.5 0.2 copy-done.9
  53.6 0.1 add_select_fusion.refs_7_.refs_10_
  53.7 5.0 %collective-permute-start.9 = (f32[2,160,128]{2,1,0:T(8,128)S(1)}, f32[2,160,128]{2,1,0:T(8,128)S(1)}, u32[]{:S(2)}, u32[]{:S(2)}) collective-permute-start(f32[2,160,128]{2,1,0:T(8,128)S(1)} %get-tuple-element.49), channel_id=1, source_target_pairs={{0,2},{1,3},{2,0},{3,1},{4,6},{5,7},{6,4},{7,5},{8,10},{9,11},{10,... | collective-permute-start | bytes 491528 | tf_op jit(solution)/shard_map/ppermute | solution.py:443
  58.7 0.0 collective-permute-done.1.refs_1_
  58.7 0.0 copy-start
  58.7 0.0 copy-start.1
  58.7 0.0 copy-start.3
  58.7 0.0 copy-start.4
  58.7 0.0 copy-start.5
  58.7 0.0 copy-start.6
  58.7 3.3 %collective-permute-start.10 = (f32[2,160,128]{2,1,0:T(8,128)S(1)}, f32[2,160,128]{2,1,0:T(8,128)S(1)}, u32[]{:S(2)}, u32[]{:S(2)}) collective-permute-start(f32[2,160,128]{2,1,0:T(8,128)S(1)} %get-tuple-element.50), channel_id=1, source_target_pairs={{0,3},{1,0},{2,1},{3,2},{4,7},{5,4},{6,5},{7,6},{8,11},{9,8},{10,9... | collective-permute-start | bytes 491528 | tf_op jit(solution)/shard_map/ppermute | solution.py:443
  62.0 0.0 collective-permute-done.2.refs_2_
  62.0 0.0 collective-permute-done.3.refs_3_
  62.0 2.4 %collective-permute-done.8.refs_4_.refs_3_ = f32[2,160,128]{2,1,0:T(8,128)S(1)} collective-permute-done((f32[2,160,128]{2,1,0:T(8,128)S(1)}, f32[2,160,128]{2,1,0:T(8,128)S(1)}, u32[]{:S(2)}, u32[]{:S(2)}) %collective-permute-start.8) | collective-permute-done | bytes 163872 | tf_op jit(solution)/shard_map/ppermute | solution.py:443
  64.5 2.7 %remap_lower.1 = (f32[1,160,128]{2,1,0:T(8,128)S(1)}, f32[1,160,128]{2,1,0:T(8,128)S(1)}, f32[1,160,128]{2,1,0:T(8,128)S(1)}, f32[1,160,128]{2,1,0:T(8,128)S(1)}) custom-call(f32[1,2,144,128]{3,2,1,0:T(8,128)S(1)} %get-tuple-element.37.refs_4_.refs_0_, f32[1,2,144,128]{3,2,1,0:T(8,128)S(1)} %collective-permute-done.1.refs_1_, ...), custom_call_target="tpu_custom_call" | custom-call | flops 4400000000 | bytes 14400000 | tf_op jit(solution)/shard_map/remap_lower/pallas_call | solution.py:511
  67.2 0.1 collective-permute-start.12
  67.3 3.2 %collective-permute-start.13 = (f32[1,160,128]{2,1,0:T(8,128)S(1)}, f32[1,160,128]{2,1,0:T(8,128)S(1)}, u32[]{:S(2)}, u32[]{:S(2)}) collective-permute-start(f32[1,160,128]{2,1,0:T(8,128)S(1)} %get-tuple-element.57), channel_id=1, source_target_pairs={{0,2},{1,3},{2,0},{3,1},{4,6},{5,7},{6,4},{7,5},{8,10},{9,11},{10,... | collective-permute-start | bytes 245768 | tf_op jit(solution)/shard_map/ppermute | solution.py:443
  70.6 3.5 %collective-permute-start.14 = (f32[1,160,128]{2,1,0:T(8,128)S(1)}, f32[1,160,128]{2,1,0:T(8,128)S(1)}, u32[]{:S(2)}, u32[]{:S(2)}) collective-permute-start(f32[1,160,128]{2,1,0:T(8,128)S(1)} %get-tuple-element.58), channel_id=1, source_target_pairs={{0,3},{1,0},{2,1},{3,2},{4,7},{5,4},{6,5},{7,6},{8,11},{9,8},{10,9... | collective-permute-start | bytes 245768 | tf_op jit(solution)/shard_map/ppermute | solution.py:443
  74.0 0.0 collective-permute-done.9.refs_4_
  74.0 0.1 collective-permute-done.10.refs_5_
  74.1 0.0 copy-start.2
  74.1 21.6 %collective-permute-start.11 = (f32[1,160,128]{2,1,0:T(8,128)S(1)}, f32[1,160,128]{2,1,0:T(8,128)S(1)}, u32[]{:S(2)}, u32[]{:S(2)}) collective-permute-start(f32[1,160,128]{2,1,0:T(8,128)S(1)} %select_select_fusion), channel_id=1, source_target_pairs={{0,4},{4,8},{8,12},{12,16},{16,20},{20,24},{24,28},{28,32},{32,36}... | collective-permute-start | bytes 245768 | tf_op jit(solution)/shard_map/ppermute | solution.py:536
  95.8 0.0 copy-done
  95.8 0.0 copy-done.1
  95.8 0.0 copy-done.3
  95.8 0.0 copy-done.4
  95.8 0.0 copy-done.5
  95.8 0.0 copy-done.6
  95.8 0.0 copy-done.2
  95.9 7.0 %final_upper.1 = (f32[12,32,576]{2,1,0:T(8,128)}, f32[12,32,576]{2,1,0:T(8,128)}, f32[12,32,576]{2,1,0:T(8,128)}, f32[12,32,576]{2,1,0:T(8,128)}, f32[3,32,576]{2,1,0:T(8,128)S(1)}) custom-call(s32[1]{0:T(128)} %bitcast.refs_0_, f32[13]{0:T(128)S(1)} %multiply_sine_fusion.1.refs_1_, f32[2,160,128]{2,1,0:T(8,128)S(1)} %get-tuple-element.54.refs_2_, ...), custom_call_target="tpu_custom_call" | custom-call | flops 7699999744 | bytes 25200000 | tf_op jit(solution)/shard_map/final_upper/pallas_call | solution.py:543
  102.9 0.0 collective-permute-done.12.refs_6_
  102.9 0.0 collective-permute-done.13.refs_7_
  102.9 0.0 collective-permute-done.14.refs_8_
  102.9 0.0 collective-permute-done.11.refs_2_
  102.9 4.4 %final_lower.1 = (f32[12,32,576]{2,1,0:T(8,128)}, f32[12,32,576]{2,1,0:T(8,128)}, f32[12,32,576]{2,1,0:T(8,128)}, f32[12,32,576]{2,1,0:T(8,128)}) custom-call(s32[1]{0:T(128)} %bitcast.refs_0_, f32[13]{0:T(128)S(1)} %multiply_sine_fusion.1.refs_1_, ...), custom_call_target="tpu_custom_call", output_to_operand_aliasing={{0}: (17, {}), {1}: (18, {}), {2}: (19, {}), {3}: (20, {})} | custom-call | flops 6600000000 | bytes 21600000 | tf_op jit(solution)/shard_map/final_lower/pallas_call | solution.py:559
  (5 shorter events, 0.1 us)
Async XLA Ops:
  1.8 25.8 %collective-permute-start = (f32[72,576]{1,0:T(8,128)S(1)}, f32[72,576]{1,0:T(8,128)S(1)}, u32[]{:S(2)}, u32[]{:S(2)}) collective-permute-start(f32[72,576]{1,0:T(8,128)S(1)} %get-tuple-element.36), channel_id=1, source_target_pairs={{0,4},{4,8},{8,12},{12,16},{16,20},{20,24},{24,28},{28,32},{32,36}... | collective-permute-start | bytes 497672 | tf_op jit(solution)/shard_map/ppermute | solution.py:489
  5.1 8.4 %collective-permute-start.4 = (f32[96,576]{1,0:T(8,128)S(1)}, f32[96,576]{1,0:T(8,128)S(1)}, u32[]{:S(2)}, u32[]{:S(2)}) collective-permute-start(f32[96,576]{1,0:T(8,128)S(1)} %get-tuple-element.41), channel_id=1, source_target_pairs={{4,0},{8,4},{12,8},{16,12},{20,16},{24,20},{28,24},{32,28},{36,32}... | collective-permute-start | bytes 663560 | tf_op jit(solution)/shard_map/ppermute | solution.py:488
  7.1 0.7 copy-start.10
  17.0 16.2 %collective-permute-start.5 = (f32[2,2,144,128]{3,2,1,0:T(8,128)S(1)}, f32[2,2,144,128]{3,2,1,0:T(8,128)S(1)}, u32[]{:S(2)}, u32[]{:S(2)}) collective-permute-start(f32[2,2,144,128]{3,2,1,0:T(8,128)S(1)} %get-tuple-element.43), channel_id=1, source_target_pairs={{0,1},{1,2},{2,3},{3,0},{4,5},{5,6},{6,7},{7,4},{8,9},{9,10},{10,1... | collective-permute-start | bytes 884744 | tf_op jit(solution)/shard_map/ppermute | solution.py:443
  20.1 18.1 %collective-permute-start.6 = (f32[2,2,144,128]{3,2,1,0:T(8,128)S(1)}, f32[2,2,144,128]{3,2,1,0:T(8,128)S(1)}, u32[]{:S(2)}, u32[]{:S(2)}) collective-permute-start(f32[2,2,144,128]{3,2,1,0:T(8,128)S(1)} %get-tuple-element.44), channel_id=1, source_target_pairs={{0,2},{1,3},{2,0},{3,1},{4,6},{5,7},{6,4},{7,5},{8,10},{9,11},{10,... | collective-permute-start | bytes 884744 | tf_op jit(solution)/shard_map/ppermute | solution.py:443
  25.2 22.2 %collective-permute-start.7 = (f32[2,2,144,128]{3,2,1,0:T(8,128)S(1)}, f32[2,2,144,128]{3,2,1,0:T(8,128)S(1)}, u32[]{:S(2)}, u32[]{:S(2)}) collective-permute-start(f32[2,2,144,128]{3,2,1,0:T(8,128)S(1)} %get-tuple-element.45), channel_id=1, source_target_pairs={{0,3},{1,0},{2,1},{3,2},{4,7},{5,4},{6,5},{7,6},{8,11},{9,8},{10,9... | collective-permute-start | bytes 884744 | tf_op jit(solution)/shard_map/ppermute | solution.py:443
  30.9 27.8 %collective-permute-start.1 = (f32[1,2,144,128]{3,2,1,0:T(8,128)S(1)}, f32[1,2,144,128]{3,2,1,0:T(8,128)S(1)}, u32[]{:S(2)}, u32[]{:S(2)}) collective-permute-start(f32[1,2,144,128]{3,2,1,0:T(8,128)S(1)} %get-tuple-element.38), channel_id=1, source_target_pairs={{0,1},{1,2},{2,3},{3,0},{4,5},{5,6},{6,7},{7,4},{8,9},{9,10},{10,1... | collective-permute-start | bytes 442376 | tf_op jit(solution)/shard_map/ppermute | solution.py:443
  31.0 31.1 %collective-permute-start.2 = (f32[1,2,144,128]{3,2,1,0:T(8,128)S(1)}, f32[1,2,144,128]{3,2,1,0:T(8,128)S(1)}, u32[]{:S(2)}, u32[]{:S(2)}) collective-permute-start(f32[1,2,144,128]{3,2,1,0:T(8,128)S(1)} %get-tuple-element.39), channel_id=1, source_target_pairs={{0,2},{1,3},{2,0},{3,1},{4,6},{5,7},{6,4},{7,5},{8,10},{9,11},{10,... | collective-permute-start | bytes 442376 | tf_op jit(solution)/shard_map/ppermute | solution.py:443
  33.3 28.8 %collective-permute-start.3 = (f32[1,2,144,128]{3,2,1,0:T(8,128)S(1)}, f32[1,2,144,128]{3,2,1,0:T(8,128)S(1)}, u32[]{:S(2)}, u32[]{:S(2)}) collective-permute-start(f32[1,2,144,128]{3,2,1,0:T(8,128)S(1)} %get-tuple-element.40), channel_id=1, source_target_pairs={{0,3},{1,0},{2,1},{3,2},{4,7},{5,4},{6,5},{7,6},{8,11},{9,8},{10,9... | collective-permute-start | bytes 442376 | tf_op jit(solution)/shard_map/ppermute | solution.py:443
  47.3 6.1 %copy-start.7 = (f32[12,576]{1,0:T(8,128)S(1)}, f32[12,576]{1,0:T(8,128)}, u32[]{:S(2)}) copy-start(f32[12,576]{1,0:T(8,128)} %param.20) | copy-start | bytes 82948
  47.4 6.1 %copy-start.8 = (s32[576]{0:T(1024)S(1)}, s32[576]{0:T(1024)}, u32[]{:S(2)}) copy-start(s32[576]{0:T(1024)} %constant.61.clone) | copy-start | bytes 6916
  53.0 0.7 copy-start.9
  53.0 11.5 %collective-permute-start.8 = (f32[2,160,128]{2,1,0:T(8,128)S(1)}, f32[2,160,128]{2,1,0:T(8,128)S(1)}, u32[]{:S(2)}, u32[]{:S(2)}) collective-permute-start(f32[2,160,128]{2,1,0:T(8,128)S(1)} %get-tuple-element.46), channel_id=1, source_target_pairs={{0,1},{1,2},{2,3},{3,0},{4,5},{5,6},{6,7},{7,4},{8,9},{9,10},{10,1... | collective-permute-start | bytes 491528 | tf_op jit(solution)/shard_map/ppermute | solution.py:443
  53.7 20.3 %collective-permute-start.9 = (f32[2,160,128]{2,1,0:T(8,128)S(1)}, f32[2,160,128]{2,1,0:T(8,128)S(1)}, u32[]{:S(2)}, u32[]{:S(2)}) collective-permute-start(f32[2,160,128]{2,1,0:T(8,128)S(1)} %get-tuple-element.49), channel_id=1, source_target_pairs={{0,2},{1,3},{2,0},{3,1},{4,6},{5,7},{6,4},{7,5},{8,10},{9,11},{10,... | collective-permute-start | bytes 491528 | tf_op jit(solution)/shard_map/ppermute | solution.py:443
  58.7 37.1 %copy-start = (f32[12,32,576]{2,1,0:T(8,128)S(1)}, f32[12,32,576]{2,1,0:T(8,128)}, u32[]{:S(2)}) copy-start(f32[12,32,576]{2,1,0:T(8,128)} %refs_12_.2) | copy-start | bytes 2654212
  58.7 37.1 %copy-start.1 = (f32[12,32,576]{2,1,0:T(8,128)S(1)}, f32[12,32,576]{2,1,0:T(8,128)}, u32[]{:S(2)}) copy-start(f32[12,32,576]{2,1,0:T(8,128)} %refs_11_.2) | copy-start | bytes 2654212
  58.7 37.1 %copy-start.3 = (bf16[576,576]{1,0:T(8,128)(2,1)S(1)}, bf16[576,576]{1,0:T(8,128)(2,1)}, u32[]{:S(2)}) copy-start(bf16[576,576]{1,0:T(8,128)(2,1)} %constant.65.clone.refs_13_.refs_16_) | copy-start | bytes 1990660
  58.7 37.1 %copy-start.4 = (bf16[576,576]{1,0:T(8,128)(2,1)S(1)}, bf16[576,576]{1,0:T(8,128)(2,1)}, u32[]{:S(2)}) copy-start(bf16[576,576]{1,0:T(8,128)(2,1)} %constant.64.clone.refs_12_.refs_15_) | copy-start | bytes 1990660
  58.7 37.1 %copy-start.5 = (bf16[576,576]{1,0:T(8,128)(2,1)S(1)}, bf16[576,576]{1,0:T(8,128)(2,1)}, u32[]{:S(2)}) copy-start(bf16[576,576]{1,0:T(8,128)(2,1)} %constant.63.clone.refs_11_.refs_14_) | copy-start | bytes 1990660
  58.7 37.1 %copy-start.6 = (bf16[576,576]{1,0:T(8,128)(2,1)S(1)}, bf16[576,576]{1,0:T(8,128)(2,1)}, u32[]{:S(2)}) copy-start(bf16[576,576]{1,0:T(8,128)(2,1)} %constant.62.clone.refs_10_.refs_13_) | copy-start | bytes 1990660
  58.7 15.4 %collective-permute-start.10 = (f32[2,160,128]{2,1,0:T(8,128)S(1)}, f32[2,160,128]{2,1,0:T(8,128)S(1)}, u32[]{:S(2)}, u32[]{:S(2)}) collective-permute-start(f32[2,160,128]{2,1,0:T(8,128)S(1)} %get-tuple-element.50), channel_id=1, source_target_pairs={{0,3},{1,0},{2,1},{3,2},{4,7},{5,4},{6,5},{7,6},{8,11},{9,8},{10,9... | collective-permute-start | bytes 491528 | tf_op jit(solution)/shard_map/ppermute | solution.py:443
  67.2 35.7 %collective-permute-start.12 = (f32[1,160,128]{2,1,0:T(8,128)S(1)}, f32[1,160,128]{2,1,0:T(8,128)S(1)}, u32[]{:S(2)}, u32[]{:S(2)}) collective-permute-start(f32[1,160,128]{2,1,0:T(8,128)S(1)} %get-tuple-element.56), channel_id=1, source_target_pairs={{0,1},{1,2},{2,3},{3,0},{4,5},{5,6},{6,7},{7,4},{8,9},{9,10},{10,1... | collective-permute-start | bytes 245768 | tf_op jit(solution)/shard_map/ppermute | solution.py:443
  67.3 35.6 %collective-permute-start.13 = (f32[1,160,128]{2,1,0:T(8,128)S(1)}, f32[1,160,128]{2,1,0:T(8,128)S(1)}, u32[]{:S(2)}, u32[]{:S(2)}) collective-permute-start(f32[1,160,128]{2,1,0:T(8,128)S(1)} %get-tuple-element.57), channel_id=1, source_target_pairs={{0,2},{1,3},{2,0},{3,1},{4,6},{5,7},{6,4},{7,5},{8,10},{9,11},{10,... | collective-permute-start | bytes 245768 | tf_op jit(solution)/shard_map/ppermute | solution.py:443
  70.6 32.3 %collective-permute-start.14 = (f32[1,160,128]{2,1,0:T(8,128)S(1)}, f32[1,160,128]{2,1,0:T(8,128)S(1)}, u32[]{:S(2)}, u32[]{:S(2)}) collective-permute-start(f32[1,160,128]{2,1,0:T(8,128)S(1)} %get-tuple-element.58), channel_id=1, source_target_pairs={{0,3},{1,0},{2,1},{3,2},{4,7},{5,4},{6,5},{7,6},{8,11},{9,8},{10,9... | collective-permute-start | bytes 245768 | tf_op jit(solution)/shard_map/ppermute | solution.py:443
  74.1 21.7 %copy-start.2 = (f32[12,576]{1,0:T(8,128)S(1)}, f32[12,576]{1,0:T(8,128)}, u32[]{:S(2)}) copy-start(f32[12,576]{1,0:T(8,128)} %refs_9_.3) | copy-start | bytes 82948
  74.1 28.8 %collective-permute-start.11 = (f32[1,160,128]{2,1,0:T(8,128)S(1)}, f32[1,160,128]{2,1,0:T(8,128)S(1)}, u32[]{:S(2)}, u32[]{:S(2)}) collective-permute-start(f32[1,160,128]{2,1,0:T(8,128)S(1)} %select_select_fusion), channel_id=1, source_target_pairs={{0,4},{4,8},{8,12},{12,16},{16,20},{20,24},{24,28},{28,32},{32,36}... | collective-permute-start | bytes 245768 | tf_op jit(solution)/shard_map/ppermute | solution.py:536

commit v5 on v4

--- a/solution.py
+++ b/solution.py
@@ -504,7 +504,10 @@
         )(coef, halo, *fields)
 
     upper_columns = exchanged(advect(first, upper_each, halo_n, "advect_upper"))
-    lower_columns = exchanged(advect(0, lower_each, halo_s, "advect_lower"))
+    lower_sent = advect(0, lower_each, halo_s, "advect_lower")
+    settled = lax.optimization_barrier((*upper_columns, *lower_sent))
+    upper_columns, lower_sent = settled[:peers], settled[peers:]
+    lower_columns = exchanged(lower_sent)
 
     def remap(columns, each, name, after):
         lanes = tile_count(width) * LANES

time: 108 us -> 109 us (level)
  the two profiles are of different devices: /device:TPU:41 before, /device:TPU:1 now
where the time goes in v5:
time: 109 us; the launch traced here: 108 us
  starting transfers between devices  52.8 us (48%)
  Pallas kernels  27.7 us (25%)
  waiting for transfers between devices  24.6 us (23%)
  between operations  1.71 us (2%)
    ppermute x12, starting transfers between devices, exchanged(): lax.ppermute(parts[step], 'lev', [(i, (i + step) % peers) for i in range(...  30.1 us
    ppermute x12, waiting for transfers between devices, exchanged(): lax.ppermute(parts[step], 'lev', [(i, (i + step) % peers) for i in range(...  21.1 us
    ppermute x1, starting transfers between devices, body(): south = lax.ppermute(last_message, 'lat', northward)  15.9 us
    pallas_call x2, Pallas kernels, remap(): pl.pallas_call(lambda *refs: remap_kernel(width, block, peers, *refs), ou...  8.32 us
    pallas_call x1, Pallas kernels, body(): pl.pallas_call(lambda *refs: upper_final_kernel(levels, first, *refs), ou...  7.01 us
    pallas_call x2, Pallas kernels, advect(): pl.pallas_call(lambda *refs: advect_kernel(start, each, peers, *refs), ou...  6.78 us
    ppermute x1, starting transfers between devices, body(): halo_s = lax.ppermute(to_north, 'lat', northward)  4.94 us
    pallas_call x1, Pallas kernels, body(): pl.pallas_call(lambda *refs: lower_final_kernel(levels, *refs), out_shape...  4.43 us
  transfers between devices with their start and end apart: 15, of which 6 were waited for; matrix products, arithmetic and copies ran while one was open for 1% of the time, Pallas kernels for 20%

profile of v5, /device:TPU:1, one launch (start us, length us, event | category | flops | bytes accessed | tf_op | source)
XLA Modules:
  0.0 108.4 jit_solution(9513437995833915652)
XLA Ops:
  0.6 1.1 %edges.1 = (f32[72,576]{1,0:T(8,128)S(1)}, f32[96,576]{1,0:T(8,128)S(1)}) custom-call(f32[12,32,576]{2,1,0:T(8,128)} %refs_12_.2, f32[12,32,576]{2,1,0:T(8,128)} %refs_4_.3, f32[12,32,576]{2,1,0:T(8,128)} %refs_5_.3, f32[12,576]{1,0:T(8,128)} %refs_9_.3), custom_call_target="tpu_custom_call" | custom-call | flops 1100000000 | bytes 3600000 | tf_op jit(solution)/shard_map/edges/pallas_call | solution.py:478
  1.8 4.9 %collective-permute-start.4 = (f32[72,576]{1,0:T(8,128)S(1)}, f32[72,576]{1,0:T(8,128)S(1)}, u32[]{:S(2)}, u32[]{:S(2)}) collective-permute-start(f32[72,576]{1,0:T(8,128)S(1)} %get-tuple-element.49), channel_id=1, source_target_pairs={{0,4},{4,8},{8,12},{12,16},{16,20},{20,24},{24,28},{28,32},{32,36}... | collective-permute-start | bytes 497672 | tf_op jit(solution)/shard_map/ppermute | solution.py:489
  6.7 1.9 %collective-permute-start = (f32[96,576]{1,0:T(8,128)S(1)}, f32[96,576]{1,0:T(8,128)S(1)}, u32[]{:S(2)}, u32[]{:S(2)}) collective-permute-start(f32[96,576]{1,0:T(8,128)S(1)} %get-tuple-element.44), channel_id=1, source_target_pairs={{4,0},{8,4},{12,8},{16,12},{20,16},{24,20},{28,24},{32,28},{36,32}... | collective-permute-start | bytes 663560 | tf_op jit(solution)/shard_map/ppermute | solution.py:488
  8.8 0.0 copy-start.10
  8.8 0.1 slice_bitcast_fusion.1
  8.8 0.6 copy-done.10
  9.4 0.6 broadcast_compare_fusion
  10.7 3.5 %collective-permute-done.refs_1_ = f32[96,576]{1,0:T(8,128)S(1)} collective-permute-done((f32[96,576]{1,0:T(8,128)S(1)}, f32[96,576]{1,0:T(8,128)S(1)}, u32[]{:S(2)}, u32[]{:S(2)}) %collective-permute-start) | collective-permute-done | bytes 221216 | tf_op jit(solution)/shard_map/ppermute | solution.py:488
  14.2 3.5 %advect_upper.1 = (f32[2,2,144,128]{3,2,1,0:T(8,128)S(1)}, f32[2,2,144,128]{3,2,1,0:T(8,128)S(1)}, f32[2,2,144,128]{3,2,1,0:T(8,128)S(1)}, f32[2,2,144,128]{3,2,1,0:T(8,128)S(1)}) custom-call(f32[2,12]{1,0:T(2,128)S(1)} %fusion.refs_0_, f32[96,576]{1,0:T(8,128)S(1)} %collective-permute-done.refs_1_, f32[12,32,576]{2,1,0:T(8,128)} %refs_11_.2, ...), custom_call_target="tpu_custom_call" | custom-call | flops 5500000256 | bytes 18000000 | tf_op jit(solution)/shard_map/advect_upper/pallas_call | solution.py:492
  17.7 3.1 %collective-permute-start.1 = (f32[2,2,144,128]{3,2,1,0:T(8,128)S(1)}, f32[2,2,144,128]{3,2,1,0:T(8,128)S(1)}, u32[]{:S(2)}, u32[]{:S(2)}) collective-permute-start(f32[2,2,144,128]{3,2,1,0:T(8,128)S(1)} %get-tuple-element.46), channel_id=1, source_target_pairs={{0,1},{1,2},{2,3},{3,0},{4,5},{5,6},{6,7},{7,4},{8,9},{9,10},{10,1... | collective-permute-start | bytes 884744 | tf_op jit(solution)/shard_map/ppermute | solution.py:443
  20.8 4.2 %collective-permute-start.2 = (f32[2,2,144,128]{3,2,1,0:T(8,128)S(1)}, f32[2,2,144,128]{3,2,1,0:T(8,128)S(1)}, u32[]{:S(2)}, u32[]{:S(2)}) collective-permute-start(f32[2,2,144,128]{3,2,1,0:T(8,128)S(1)} %get-tuple-element.47), channel_id=1, source_target_pairs={{0,2},{1,3},{2,0},{3,1},{4,6},{5,7},{6,4},{7,5},{8,10},{9,11},{10,... | collective-permute-start | bytes 884744 | tf_op jit(solution)/shard_map/ppermute | solution.py:443
  25.0 2.4 %collective-permute-start.3 = (f32[2,2,144,128]{3,2,1,0:T(8,128)S(1)}, f32[2,2,144,128]{3,2,1,0:T(8,128)S(1)}, u32[]{:S(2)}, u32[]{:S(2)}) collective-permute-start(f32[2,2,144,128]{3,2,1,0:T(8,128)S(1)} %get-tuple-element.48), channel_id=1, source_target_pairs={{0,3},{1,0},{2,1},{3,2},{4,7},{5,4},{6,5},{7,6},{8,11},{9,8},{10,9... | collective-permute-start | bytes 884744 | tf_op jit(solution)/shard_map/ppermute | solution.py:443
  27.4 0.0 collective-permute-done.4.refs_1_.refs_3_
  27.4 3.3 %advect_lower.1 = (f32[1,2,144,128]{3,2,1,0:T(8,128)S(1)}, f32[1,2,144,128]{3,2,1,0:T(8,128)S(1)}, f32[1,2,144,128]{3,2,1,0:T(8,128)S(1)}, f32[1,2,144,128]{3,2,1,0:T(8,128)S(1)}) custom-call(f32[2,12]{1,0:T(2,128)S(1)} %fusion.refs_0_, f32[72,576]{1,0:T(8,128)S(1)} %collective-permute-done.4.refs_1_.refs_3_, f32[12,32,576]{2,1,0:T(8,128)} %refs_11_.2, ...), custom_call_target="tpu_custom_call" | custom-call | flops 3300000000 | bytes 10800000 | tf_op jit(solution)/shard_map/advect_lower/pallas_call | solution.py:492
  30.7 3.5 %collective-permute-done.1.refs_1_ = f32[2,2,144,128]{3,2,1,0:T(8,128)S(1)} collective-permute-done((f32[2,2,144,128]{3,2,1,0:T(8,128)S(1)}, f32[2,2,144,128]{3,2,1,0:T(8,128)S(1)}, u32[]{:S(2)}, u32[]{:S(2)}) %collective-permute-start.1) | collective-permute-done | bytes 294944 | tf_op jit(solution)/shard_map/ppermute | solution.py:443
  34.2 5.6 %collective-permute-done.2.refs_2_ = f32[2,2,144,128]{3,2,1,0:T(8,128)S(1)} collective-permute-done((f32[2,2,144,128]{3,2,1,0:T(8,128)S(1)}, f32[2,2,144,128]{3,2,1,0:T(8,128)S(1)}, u32[]{:S(2)}, u32[]{:S(2)}) %collective-permute-start.2) | collective-permute-done | bytes 294944 | tf_op jit(solution)/shard_map/ppermute | solution.py:443
  39.8 10.3 %collective-permute-done.3.refs_3_ = f32[2,2,144,128]{3,2,1,0:T(8,128)S(1)} collective-permute-done((f32[2,2,144,128]{3,2,1,0:T(8,128)S(1)}, f32[2,2,144,128]{3,2,1,0:T(8,128)S(1)}, u32[]{:S(2)}, u32[]{:S(2)}) %collective-permute-start.3) | collective-permute-done | bytes 294944 | tf_op jit(solution)/shard_map/ppermute | solution.py:443
  50.2 0.0 copy-start.7
  50.2 0.0 collective-permute-start.5
  50.2 6.1 %collective-permute-start.6 = (f32[1,2,144,128]{3,2,1,0:T(8,128)S(1)}, f32[1,2,144,128]{3,2,1,0:T(8,128)S(1)}, u32[]{:S(2)}, u32[]{:S(2)}) collective-permute-start(f32[1,2,144,128]{3,2,1,0:T(8,128)S(1)} %get-tuple-element.56), channel_id=1, source_target_pairs={{0,2},{1,3},{2,0},{3,1},{4,6},{5,7},{6,4},{7,5},{8,10},{9,11},{10,... | collective-permute-start | bytes 442376 | tf_op jit(solution)/shard_map/ppermute | solution.py:443
  56.3 0.0 collective-permute-start.7
  56.3 0.0 copy-start.8
  56.3 5.6 %remap_upper.1 = (f32[2,160,128]{2,1,0:T(8,128)S(1)}, f32[2,160,128]{2,1,0:T(8,128)S(1)}, f32[2,160,128]{2,1,0:T(8,128)S(1)}, f32[2,160,128]{2,1,0:T(8,128)S(1)}) custom-call(f32[2,2,144,128]{3,2,1,0:T(8,128)S(1)} %get-tuple-element.58.refs_0_, f32[2,2,144,128]{3,2,1,0:T(8,128)S(1)} %collective-permute-done.1.refs_1_, ...), custom_call_target="tpu_custom_call" | custom-call | flops 7699999744 | bytes 25200000 | tf_op jit(solution)/shard_map/remap_upper/pallas_call | solution.py:514
  61.9 0.0 copy-start.9
  61.9 2.6 %collective-permute-start.8 = (f32[2,160,128]{2,1,0:T(8,128)S(1)}, f32[2,160,128]{2,1,0:T(8,128)S(1)}, u32[]{:S(2)}, u32[]{:S(2)}) collective-permute-start(f32[2,160,128]{2,1,0:T(8,128)S(1)} %get-tuple-element.62), channel_id=1, source_target_pairs={{0,1},{1,2},{2,3},{3,0},{4,5},{5,6},{6,7},{7,4},{8,9},{9,10},{10,1... | collective-permute-start | bytes 491528 | tf_op jit(solution)/shard_map/ppermute | solution.py:443
  64.5 0.0 copy-done.7
  64.5 0.0 copy-done.8
  64.5 0.0 copy-done.9
  64.5 0.1 add_select_fusion.refs_7_.refs_10_
  64.6 1.4 %collective-permute-start.9 = (f32[2,160,128]{2,1,0:T(8,128)S(1)}, f32[2,160,128]{2,1,0:T(8,128)S(1)}, u32[]{:S(2)}, u32[]{:S(2)}) collective-permute-start(f32[2,160,128]{2,1,0:T(8,128)S(1)} %get-tuple-element.65), channel_id=1, source_target_pairs={{0,2},{1,3},{2,0},{3,1},{4,6},{5,7},{6,4},{7,5},{8,10},{9,11},{10,... | collective-permute-start | bytes 491528 | tf_op jit(solution)/shard_map/ppermute | solution.py:443
  66.0 0.0 collective-permute-done.5.refs_1_
  66.0 0.0 copy-start
  66.0 0.0 copy-start.1
  66.0 0.0 copy-start.3
  66.0 0.0 copy-start.4
  66.0 0.0 copy-start.5
  66.0 0.0 copy-start.6
  66.0 3.3 %collective-permute-start.10 = (f32[2,160,128]{2,1,0:T(8,128)S(1)}, f32[2,160,128]{2,1,0:T(8,128)S(1)}, u32[]{:S(2)}, u32[]{:S(2)}) collective-permute-start(f32[2,160,128]{2,1,0:T(8,128)S(1)} %get-tuple-element.66), channel_id=1, source_target_pairs={{0,3},{1,0},{2,1},{3,2},{4,7},{5,4},{6,5},{7,6},{8,11},{9,8},{10,9... | collective-permute-start | bytes 491528 | tf_op jit(solution)/shard_map/ppermute | solution.py:443
  69.3 0.0 collective-permute-done.6.refs_2_
  69.3 1.1 collective-permute-done.7.refs_3_
  70.4 0.6 collective-permute-done.8.refs_4_.refs_3_
  70.9 2.7 %remap_lower.1 = (f32[1,160,128]{2,1,0:T(8,128)S(1)}, f32[1,160,128]{2,1,0:T(8,128)S(1)}, f32[1,160,128]{2,1,0:T(8,128)S(1)}, f32[1,160,128]{2,1,0:T(8,128)S(1)}) custom-call(f32[1,2,144,128]{3,2,1,0:T(8,128)S(1)} %get-tuple-element.54.refs_4_.refs_0_, f32[1,2,144,128]{3,2,1,0:T(8,128)S(1)} %collective-permute-done.5.refs_1_, ...), custom_call_target="tpu_custom_call" | custom-call | flops 4400000000 | bytes 14400000 | tf_op jit(solution)/shard_map/remap_lower/pallas_call | solution.py:514
  73.7 2.1 %collective-permute-start.12 = (f32[1,160,128]{2,1,0:T(8,128)S(1)}, f32[1,160,128]{2,1,0:T(8,128)S(1)}, u32[]{:S(2)}, u32[]{:S(2)}) collective-permute-start(f32[1,160,128]{2,1,0:T(8,128)S(1)} %get-tuple-element.72), channel_id=1, source_target_pairs={{0,1},{1,2},{2,3},{3,0},{4,5},{5,6},{6,7},{7,4},{8,9},{9,10},{10,1... | collective-permute-start | bytes 245768 | tf_op jit(solution)/shard_map/ppermute | solution.py:443
  75.8 2.3 %collective-permute-start.13 = (f32[1,160,128]{2,1,0:T(8,128)S(1)}, f32[1,160,128]{2,1,0:T(8,128)S(1)}, u32[]{:S(2)}, u32[]{:S(2)}) collective-permute-start(f32[1,160,128]{2,1,0:T(8,128)S(1)} %get-tuple-element.73), channel_id=1, source_target_pairs={{0,2},{1,3},{2,0},{3,1},{4,6},{5,7},{6,4},{7,5},{8,10},{9,11},{10,... | collective-permute-start | bytes 245768 | tf_op jit(solution)/shard_map/ppermute | solution.py:443
  78.0 2.7 %collective-permute-start.14 = (f32[1,160,128]{2,1,0:T(8,128)S(1)}, f32[1,160,128]{2,1,0:T(8,128)S(1)}, u32[]{:S(2)}, u32[]{:S(2)}) collective-permute-start(f32[1,160,128]{2,1,0:T(8,128)S(1)} %get-tuple-element.74), channel_id=1, source_target_pairs={{0,3},{1,0},{2,1},{3,2},{4,7},{5,4},{6,5},{7,6},{8,11},{9,8},{10,9... | collective-permute-start | bytes 245768 | tf_op jit(solution)/shard_map/ppermute | solution.py:443
  80.7 0.0 collective-permute-done.9.refs_4_
  80.7 0.0 collective-permute-done.10.refs_5_
  80.7 0.0 copy-start.2
  80.8 15.9 %collective-permute-start.11 = (f32[1,160,128]{2,1,0:T(8,128)S(1)}, f32[1,160,128]{2,1,0:T(8,128)S(1)}, u32[]{:S(2)}, u32[]{:S(2)}) collective-permute-start(f32[1,160,128]{2,1,0:T(8,128)S(1)} %select_select_fusion), channel_id=1, source_target_pairs={{0,4},{4,8},{8,12},{12,16},{16,20},{20,24},{24,28},{28,32},{32,36}... | collective-permute-start | bytes 245768 | tf_op jit(solution)/shard_map/ppermute | solution.py:539
  96.7 0.0 copy-done
  96.7 0.0 copy-done.1
  96.7 0.0 copy-done.3
  96.7 0.0 copy-done.4
  96.7 0.0 copy-done.5
  96.7 0.0 copy-done.6
  96.7 0.0 copy-done.2
  96.7 7.0 %final_upper.1 = (f32[12,32,576]{2,1,0:T(8,128)}, f32[12,32,576]{2,1,0:T(8,128)}, f32[12,32,576]{2,1,0:T(8,128)}, f32[12,32,576]{2,1,0:T(8,128)}, f32[3,32,576]{2,1,0:T(8,128)S(1)}) custom-call(s32[1]{0:T(128)} %bitcast.refs_0_, f32[13]{0:T(128)S(1)} %multiply_sine_fusion.1.refs_1_, f32[2,160,128]{2,1,0:T(8,128)S(1)} %get-tuple-element.70.refs_2_, ...), custom_call_target="tpu_custom_call" | custom-call | flops 7699999744 | bytes 25200000 | tf_op jit(solution)/shard_map/final_upper/pallas_call | solution.py:546
  103.8 0.0 collective-permute-done.12.refs_6_
  103.8 0.0 collective-permute-done.13.refs_7_
  103.8 0.0 collective-permute-done.14.refs_8_
  103.8 0.0 collective-permute-done.11.refs_2_
  103.8 4.4 %final_lower.1 = (f32[12,32,576]{2,1,0:T(8,128)}, f32[12,32,576]{2,1,0:T(8,128)}, f32[12,32,576]{2,1,0:T(8,128)}, f32[12,32,576]{2,1,0:T(8,128)}) custom-call(s32[1]{0:T(128)} %bitcast.refs_0_, f32[13]{0:T(128)S(1)} %multiply_sine_fusion.1.refs_1_, ...), custom_call_target="tpu_custom_call", output_to_operand_aliasing={{0}: (17, {}), {1}: (18, {}), {2}: (19, {}), {3}: (20, {})} | custom-call | flops 6600000000 | bytes 21600000 | tf_op jit(solution)/shard_map/final_lower/pallas_call | solution.py:562
  (5 shorter events, 0.1 us)
Async XLA Ops:
  1.8 25.6 %collective-permute-start.4 = (f32[72,576]{1,0:T(8,128)S(1)}, f32[72,576]{1,0:T(8,128)S(1)}, u32[]{:S(2)}, u32[]{:S(2)}) collective-permute-start(f32[72,576]{1,0:T(8,128)S(1)} %get-tuple-element.49), channel_id=1, source_target_pairs={{0,4},{4,8},{8,12},{12,16},{16,20},{20,24},{24,28},{28,32},{32,36}... | collective-permute-start | bytes 497672 | tf_op jit(solution)/shard_map/ppermute | solution.py:489
  6.7 7.5 %collective-permute-start = (f32[96,576]{1,0:T(8,128)S(1)}, f32[96,576]{1,0:T(8,128)S(1)}, u32[]{:S(2)}, u32[]{:S(2)}) collective-permute-start(f32[96,576]{1,0:T(8,128)S(1)} %get-tuple-element.44), channel_id=1, source_target_pairs={{4,0},{8,4},{12,8},{16,12},{20,16},{24,20},{28,24},{32,28},{36,32}... | collective-permute-start | bytes 663560 | tf_op jit(solution)/shard_map/ppermute | solution.py:488
  8.8 0.7 copy-start.10
  17.7 16.5 %collective-permute-start.1 = (f32[2,2,144,128]{3,2,1,0:T(8,128)S(1)}, f32[2,2,144,128]{3,2,1,0:T(8,128)S(1)}, u32[]{:S(2)}, u32[]{:S(2)}) collective-permute-start(f32[2,2,144,128]{3,2,1,0:T(8,128)S(1)} %get-tuple-element.46), channel_id=1, source_target_pairs={{0,1},{1,2},{2,3},{3,0},{4,5},{5,6},{6,7},{7,4},{8,9},{9,10},{10,1... | collective-permute-start | bytes 884744 | tf_op jit(solution)/shard_map/ppermute | solution.py:443
  20.8 19.0 %collective-permute-start.2 = (f32[2,2,144,128]{3,2,1,0:T(8,128)S(1)}, f32[2,2,144,128]{3,2,1,0:T(8,128)S(1)}, u32[]{:S(2)}, u32[]{:S(2)}) collective-permute-start(f32[2,2,144,128]{3,2,1,0:T(8,128)S(1)} %get-tuple-element.47), channel_id=1, source_target_pairs={{0,2},{1,3},{2,0},{3,1},{4,6},{5,7},{6,4},{7,5},{8,10},{9,11},{10,... | collective-permute-start | bytes 884744 | tf_op jit(solution)/shard_map/ppermute | solution.py:443
  25.0 25.1 %collective-permute-start.3 = (f32[2,2,144,128]{3,2,1,0:T(8,128)S(1)}, f32[2,2,144,128]{3,2,1,0:T(8,128)S(1)}, u32[]{:S(2)}, u32[]{:S(2)}) collective-permute-start(f32[2,2,144,128]{3,2,1,0:T(8,128)S(1)} %get-tuple-element.48), channel_id=1, source_target_pairs={{0,3},{1,0},{2,1},{3,2},{4,7},{5,4},{6,5},{7,6},{8,11},{9,8},{10,9... | collective-permute-start | bytes 884744 | tf_op jit(solution)/shard_map/ppermute | solution.py:443
  50.2 14.4 %copy-start.7 = (f32[12,576]{1,0:T(8,128)S(1)}, f32[12,576]{1,0:T(8,128)}, u32[]{:S(2)}) copy-start(f32[12,576]{1,0:T(8,128)} %param.20) | copy-start | bytes 82948
  50.2 15.8 %collective-permute-start.5 = (f32[1,2,144,128]{3,2,1,0:T(8,128)S(1)}, f32[1,2,144,128]{3,2,1,0:T(8,128)S(1)}, u32[]{:S(2)}, u32[]{:S(2)}) collective-permute-start(f32[1,2,144,128]{3,2,1,0:T(8,128)S(1)} %get-tuple-element.55), channel_id=1, source_target_pairs={{0,1},{1,2},{2,3},{3,0},{4,5},{5,6},{6,7},{7,4},{8,9},{9,10},{10,1... | collective-permute-start | bytes 442376 | tf_op jit(solution)/shard_map/ppermute | solution.py:443
  50.2 19.1 %collective-permute-start.6 = (f32[1,2,144,128]{3,2,1,0:T(8,128)S(1)}, f32[1,2,144,128]{3,2,1,0:T(8,128)S(1)}, u32[]{:S(2)}, u32[]{:S(2)}) collective-permute-start(f32[1,2,144,128]{3,2,1,0:T(8,128)S(1)} %get-tuple-element.56), channel_id=1, source_target_pairs={{0,2},{1,3},{2,0},{3,1},{4,6},{5,7},{6,4},{7,5},{8,10},{9,11},{10,... | collective-permute-start | bytes 442376 | tf_op jit(solution)/shard_map/ppermute | solution.py:443
  56.3 14.1 %collective-permute-start.7 = (f32[1,2,144,128]{3,2,1,0:T(8,128)S(1)}, f32[1,2,144,128]{3,2,1,0:T(8,128)S(1)}, u32[]{:S(2)}, u32[]{:S(2)}) collective-permute-start(f32[1,2,144,128]{3,2,1,0:T(8,128)S(1)} %get-tuple-element.57), channel_id=1, source_target_pairs={{0,3},{1,0},{2,1},{3,2},{4,7},{5,4},{6,5},{7,6},{8,11},{9,8},{10,9... | collective-permute-start | bytes 442376 | tf_op jit(solution)/shard_map/ppermute | solution.py:443
  56.3 8.3 %copy-start.8 = (s32[576]{0:T(1024)S(1)}, s32[576]{0:T(1024)}, u32[]{:S(2)}) copy-start(s32[576]{0:T(1024)} %constant.61.clone) | copy-start | bytes 6916
  61.9 2.6 %copy-start.9 = (s32[12]{0:T(128)S(1)}, s32[12]{0:T(128)}, u32[]{:S(2)}) copy-start(s32[12]{0:T(128)} %param.19) | copy-start | bytes 148
  61.9 9.1 %collective-permute-start.8 = (f32[2,160,128]{2,1,0:T(8,128)S(1)}, f32[2,160,128]{2,1,0:T(8,128)S(1)}, u32[]{:S(2)}, u32[]{:S(2)}) collective-permute-start(f32[2,160,128]{2,1,0:T(8,128)S(1)} %get-tuple-element.62), channel_id=1, source_target_pairs={{0,1},{1,2},{2,3},{3,0},{4,5},{5,6},{6,7},{7,4},{8,9},{9,10},{10,1... | collective-permute-start | bytes 491528 | tf_op jit(solution)/shard_map/ppermute | solution.py:443
  64.6 16.1 %collective-permute-start.9 = (f32[2,160,128]{2,1,0:T(8,128)S(1)}, f32[2,160,128]{2,1,0:T(8,128)S(1)}, u32[]{:S(2)}, u32[]{:S(2)}) collective-permute-start(f32[2,160,128]{2,1,0:T(8,128)S(1)} %get-tuple-element.65), channel_id=1, source_target_pairs={{0,2},{1,3},{2,0},{3,1},{4,6},{5,7},{6,4},{7,5},{8,10},{9,11},{10,... | collective-permute-start | bytes 491528 | tf_op jit(solution)/shard_map/ppermute | solution.py:443
  66.0 30.7 %copy-start = (f32[12,32,576]{2,1,0:T(8,128)S(1)}, f32[12,32,576]{2,1,0:T(8,128)}, u32[]{:S(2)}) copy-start(f32[12,32,576]{2,1,0:T(8,128)} %refs_12_.2) | copy-start | bytes 2654212
  66.0 30.7 %copy-start.1 = (f32[12,32,576]{2,1,0:T(8,128)S(1)}, f32[12,32,576]{2,1,0:T(8,128)}, u32[]{:S(2)}) copy-start(f32[12,32,576]{2,1,0:T(8,128)} %refs_11_.2) | copy-start | bytes 2654212
  66.0 30.7 %copy-start.3 = (bf16[576,576]{1,0:T(8,128)(2,1)S(1)}, bf16[576,576]{1,0:T(8,128)(2,1)}, u32[]{:S(2)}) copy-start(bf16[576,576]{1,0:T(8,128)(2,1)} %constant.65.clone.refs_13_.refs_16_) | copy-start | bytes 1990660
  66.0 30.7 %copy-start.4 = (bf16[576,576]{1,0:T(8,128)(2,1)S(1)}, bf16[576,576]{1,0:T(8,128)(2,1)}, u32[]{:S(2)}) copy-start(bf16[576,576]{1,0:T(8,128)(2,1)} %constant.64.clone.refs_12_.refs_15_) | copy-start | bytes 1990660
  66.0 30.7 %copy-start.5 = (bf16[576,576]{1,0:T(8,128)(2,1)S(1)}, bf16[576,576]{1,0:T(8,128)(2,1)}, u32[]{:S(2)}) copy-start(bf16[576,576]{1,0:T(8,128)(2,1)} %constant.63.clone.refs_11_.refs_14_) | copy-start | bytes 1990660
  66.0 30.7 %copy-start.6 = (bf16[576,576]{1,0:T(8,128)(2,1)S(1)}, bf16[576,576]{1,0:T(8,128)(2,1)}, u32[]{:S(2)}) copy-start(bf16[576,576]{1,0:T(8,128)(2,1)} %constant.62.clone.refs_10_.refs_13_) | copy-start | bytes 1990660
  66.0 14.7 %collective-permute-start.10 = (f32[2,160,128]{2,1,0:T(8,128)S(1)}, f32[2,160,128]{2,1,0:T(8,128)S(1)}, u32[]{:S(2)}, u32[]{:S(2)}) collective-permute-start(f32[2,160,128]{2,1,0:T(8,128)S(1)} %get-tuple-element.66), channel_id=1, source_target_pairs={{0,3},{1,0},{2,1},{3,2},{4,7},{5,4},{6,5},{7,6},{8,11},{9,8},{10,9... | collective-permute-start | bytes 491528 | tf_op jit(solution)/shard_map/ppermute | solution.py:443
  73.7 30.1 %collective-permute-start.12 = (f32[1,160,128]{2,1,0:T(8,128)S(1)}, f32[1,160,128]{2,1,0:T(8,128)S(1)}, u32[]{:S(2)}, u32[]{:S(2)}) collective-permute-start(f32[1,160,128]{2,1,0:T(8,128)S(1)} %get-tuple-element.72), channel_id=1, source_target_pairs={{0,1},{1,2},{2,3},{3,0},{4,5},{5,6},{6,7},{7,4},{8,9},{9,10},{10,1... | collective-permute-start | bytes 245768 | tf_op jit(solution)/shard_map/ppermute | solution.py:443
  75.8 28.0 %collective-permute-start.13 = (f32[1,160,128]{2,1,0:T(8,128)S(1)}, f32[1,160,128]{2,1,0:T(8,128)S(1)}, u32[]{:S(2)}, u32[]{:S(2)}) collective-permute-start(f32[1,160,128]{2,1,0:T(8,128)S(1)} %get-tuple-element.73), channel_id=1, source_target_pairs={{0,2},{1,3},{2,0},{3,1},{4,6},{5,7},{6,4},{7,5},{8,10},{9,11},{10,... | collective-permute-start | bytes 245768 | tf_op jit(solution)/shard_map/ppermute | solution.py:443
  78.0 25.8 %collective-permute-start.14 = (f32[1,160,128]{2,1,0:T(8,128)S(1)}, f32[1,160,128]{2,1,0:T(8,128)S(1)}, u32[]{:S(2)}, u32[]{:S(2)}) collective-permute-start(f32[1,160,128]{2,1,0:T(8,128)S(1)} %get-tuple-element.74), channel_id=1, source_target_pairs={{0,3},{1,0},{2,1},{3,2},{4,7},{5,4},{6,5},{7,6},{8,11},{9,8},{10,9... | collective-permute-start | bytes 245768 | tf_op jit(solution)/shard_map/ppermute | solution.py:443
  80.7 16.0 %copy-start.2 = (f32[12,576]{1,0:T(8,128)S(1)}, f32[12,576]{1,0:T(8,128)}, u32[]{:S(2)}) copy-start(f32[12,576]{1,0:T(8,128)} %refs_9_.3) | copy-start | bytes 82948
  80.8 23.0 %collective-permute-start.11 = (f32[1,160,128]{2,1,0:T(8,128)S(1)}, f32[1,160,128]{2,1,0:T(8,128)S(1)}, u32[]{:S(2)}, u32[]{:S(2)}) collective-permute-start(f32[1,160,128]{2,1,0:T(8,128)S(1)} %select_select_fusion), channel_id=1, source_target_pairs={{0,4},{4,8},{8,12},{12,16},{16,20},{20,24},{24,28},{28,32},{32,36}... | collective-permute-start | bytes 245768 | tf_op jit(solution)/shard_map/ppermute | solution.py:539

commit v6 on v5

--- a/solution.py
+++ b/solution.py
@@ -523,13 +523,13 @@
                 pltpu.VMEM((each, 8, lanes), F32),
             ],
             compiler_params=params(12),
-            cost_estimate=cost(1 + 3 * each),
+            cost_estimate=cost(3 * each - 2.8),
             name=name,
         )(*columns, *after)
 
     upper_remapped = remap(upper_columns, upper_each, "remap_upper", lower_columns[:1])
     upper_messages = exchanged(upper_remapped)
-    lower_remapped = remap(lower_columns, lower_each, "remap_lower", upper_messages[1:2])
+    lower_remapped = remap(lower_columns, lower_each, "remap_lower", upper_remapped[:1])
     lower_messages = exchanged(lower_remapped)
     step_of_last = (lax.axis_index("lev") + 1) % peers
     _, *candidates = lax.optimization_barrier((lower_remapped[0], *upper_messages))

time: 109 us -> 102 us (0.936)
  starting transfers between devices: 52.8 us -> 45.4 us
    ppermute x1, starting transfers between devices: 15.9 us -> 9.3 us  [body(): south = lax.ppermute(last_message, 'lat', northward)]
  transfers between devices with their start and end apart: 15 -> 15, of which waited for: 6 -> 5; matrix products, arithmetic and copies ran while one was open for 1% -> 1% of each run, Pallas kernels for 20% -> 22%
where the time goes in v6:
time: 102 us; the launch traced here: 101 us
  starting transfers between devices  45.4 us (45%)
  Pallas kernels  27.7 us (27%)
  waiting for transfers between devices  24.2 us (24%)
  between operations  1.72 us (2%)
    ppermute x12, starting transfers between devices, exchanged(): lax.ppermute(parts[step], 'lev', [(i, (i + step) % peers) for i in range(...  29.2 us
    ppermute x12, waiting for transfers between devices, exchanged(): lax.ppermute(parts[step], 'lev', [(i, (i + step) % peers) for i in range(...  20.7 us
    ppermute x1, starting transfers between devices, body(): south = lax.ppermute(last_message, 'lat', northward)  9.3 us
    pallas_call x2, Pallas kernels, remap(): pl.pallas_call(lambda *refs: remap_kernel(width, block, peers, *refs), ou...  8.33 us
    pallas_call x1, Pallas kernels, body(): pl.pallas_call(lambda *refs: upper_final_kernel(levels, first, *refs), ou...  7.01 us
    pallas_call x2, Pallas kernels, advect(): pl.pallas_call(lambda *refs: advect_kernel(start, each, peers, *refs), ou...  6.78 us
    ppermute x1, starting transfers between devices, body(): halo_s = lax.ppermute(to_north, 'lat', northward)  4.94 us
    pallas_call x1, Pallas kernels, body(): pl.pallas_call(lambda *refs: lower_final_kernel(levels, *refs), out_shape...  4.43 us
  transfers between devices with their start and end apart: 15, of which 5 were waited for; matrix products, arithmetic and copies ran while one was open for 1% of the time, Pallas kernels for 22%

profile of v6, /device:TPU:1, one launch (start us, length us, event | category | flops | bytes accessed | tf_op | source)
XLA Modules:
  0.0 100.5 jit_solution(17126624923566809558)
XLA Ops:
  0.6 1.1 %edges.1 = (f32[72,576]{1,0:T(8,128)S(1)}, f32[96,576]{1,0:T(8,128)S(1)}) custom-call(f32[12,32,576]{2,1,0:T(8,128)} %refs_12_.2, f32[12,32,576]{2,1,0:T(8,128)} %refs_4_.3, f32[12,32,576]{2,1,0:T(8,128)} %refs_5_.3, f32[12,576]{1,0:T(8,128)} %refs_9_.3), custom_call_target="tpu_custom_call" | custom-call | flops 1100000000 | bytes 3600000 | tf_op jit(solution)/shard_map/edges/pallas_call | solution.py:478
  1.8 4.9 %collective-permute-start.4 = (f32[72,576]{1,0:T(8,128)S(1)}, f32[72,576]{1,0:T(8,128)S(1)}, u32[]{:S(2)}, u32[]{:S(2)}) collective-permute-start(f32[72,576]{1,0:T(8,128)S(1)} %get-tuple-element.49), channel_id=1, source_target_pairs={{0,4},{4,8},{8,12},{12,16},{16,20},{20,24},{24,28},{28,32},{32,36}... | collective-permute-start | bytes 497672 | tf_op jit(solution)/shard_map/ppermute | solution.py:489
  6.7 1.9 %collective-permute-start = (f32[96,576]{1,0:T(8,128)S(1)}, f32[96,576]{1,0:T(8,128)S(1)}, u32[]{:S(2)}, u32[]{:S(2)}) collective-permute-start(f32[96,576]{1,0:T(8,128)S(1)} %get-tuple-element.44), channel_id=1, source_target_pairs={{4,0},{8,4},{12,8},{16,12},{20,16},{24,20},{28,24},{32,28},{36,32}... | collective-permute-start | bytes 663560 | tf_op jit(solution)/shard_map/ppermute | solution.py:488
  8.8 0.0 copy-start.10
  8.8 0.1 slice_bitcast_fusion.1
  8.8 0.6 copy-done.10
  9.4 0.6 broadcast_compare_fusion
  10.7 3.5 %collective-permute-done.refs_1_ = f32[96,576]{1,0:T(8,128)S(1)} collective-permute-done((f32[96,576]{1,0:T(8,128)S(1)}, f32[96,576]{1,0:T(8,128)S(1)}, u32[]{:S(2)}, u32[]{:S(2)}) %collective-permute-start) | collective-permute-done | bytes 221216 | tf_op jit(solution)/shard_map/ppermute | solution.py:488
  14.2 3.5 %advect_upper.1 = (f32[2,2,144,128]{3,2,1,0:T(8,128)S(1)}, f32[2,2,144,128]{3,2,1,0:T(8,128)S(1)}, f32[2,2,144,128]{3,2,1,0:T(8,128)S(1)}, f32[2,2,144,128]{3,2,1,0:T(8,128)S(1)}) custom-call(f32[2,12]{1,0:T(2,128)S(1)} %fusion.refs_0_, f32[96,576]{1,0:T(8,128)S(1)} %collective-permute-done.refs_1_, f32[12,32,576]{2,1,0:T(8,128)} %refs_11_.2, ...), custom_call_target="tpu_custom_call" | custom-call | flops 5500000256 | bytes 18000000 | tf_op jit(solution)/shard_map/advect_upper/pallas_call | solution.py:492
  17.7 3.1 %collective-permute-start.1 = (f32[2,2,144,128]{3,2,1,0:T(8,128)S(1)}, f32[2,2,144,128]{3,2,1,0:T(8,128)S(1)}, u32[]{:S(2)}, u32[]{:S(2)}) collective-permute-start(f32[2,2,144,128]{3,2,1,0:T(8,128)S(1)} %get-tuple-element.46), channel_id=1, source_target_pairs={{0,1},{1,2},{2,3},{3,0},{4,5},{5,6},{6,7},{7,4},{8,9},{9,10},{10,1... | collective-permute-start | bytes 884744 | tf_op jit(solution)/shard_map/ppermute | solution.py:443
  20.8 4.2 %collective-permute-start.2 = (f32[2,2,144,128]{3,2,1,0:T(8,128)S(1)}, f32[2,2,144,128]{3,2,1,0:T(8,128)S(1)}, u32[]{:S(2)}, u32[]{:S(2)}) collective-permute-start(f32[2,2,144,128]{3,2,1,0:T(8,128)S(1)} %get-tuple-element.47), channel_id=1, source_target_pairs={{0,2},{1,3},{2,0},{3,1},{4,6},{5,7},{6,4},{7,5},{8,10},{9,11},{10,... | collective-permute-start | bytes 884744 | tf_op jit(solution)/shard_map/ppermute | solution.py:443
  25.0 2.4 %collective-permute-start.3 = (f32[2,2,144,128]{3,2,1,0:T(8,128)S(1)}, f32[2,2,144,128]{3,2,1,0:T(8,128)S(1)}, u32[]{:S(2)}, u32[]{:S(2)}) collective-permute-start(f32[2,2,144,128]{3,2,1,0:T(8,128)S(1)} %get-tuple-element.48), channel_id=1, source_target_pairs={{0,3},{1,0},{2,1},{3,2},{4,7},{5,4},{6,5},{7,6},{8,11},{9,8},{10,9... | collective-permute-start | bytes 884744 | tf_op jit(solution)/shard_map/ppermute | solution.py:443
  27.4 0.0 collective-permute-done.4.refs_1_.refs_3_
  27.4 3.3 %advect_lower.1 = (f32[1,2,144,128]{3,2,1,0:T(8,128)S(1)}, f32[1,2,144,128]{3,2,1,0:T(8,128)S(1)}, f32[1,2,144,128]{3,2,1,0:T(8,128)S(1)}, f32[1,2,144,128]{3,2,1,0:T(8,128)S(1)}) custom-call(f32[2,12]{1,0:T(2,128)S(1)} %fusion.refs_0_, f32[72,576]{1,0:T(8,128)S(1)} %collective-permute-done.4.refs_1_.refs_3_, f32[12,32,576]{2,1,0:T(8,128)} %refs_11_.2, ...), custom_call_target="tpu_custom_call" | custom-call | flops 3300000000 | bytes 10800000 | tf_op jit(solution)/shard_map/advect_lower/pallas_call | solution.py:492
  30.7 3.5 %collective-permute-done.1.refs_1_ = f32[2,2,144,128]{3,2,1,0:T(8,128)S(1)} collective-permute-done((f32[2,2,144,128]{3,2,1,0:T(8,128)S(1)}, f32[2,2,144,128]{3,2,1,0:T(8,128)S(1)}, u32[]{:S(2)}, u32[]{:S(2)}) %collective-permute-start.1) | collective-permute-done | bytes 294944 | tf_op jit(solution)/shard_map/ppermute | solution.py:443
  34.2 5.6 %collective-permute-done.2.refs_2_ = f32[2,2,144,128]{3,2,1,0:T(8,128)S(1)} collective-permute-done((f32[2,2,144,128]{3,2,1,0:T(8,128)S(1)}, f32[2,2,144,128]{3,2,1,0:T(8,128)S(1)}, u32[]{:S(2)}, u32[]{:S(2)}) %collective-permute-start.2) | collective-permute-done | bytes 294944 | tf_op jit(solution)/shard_map/ppermute | solution.py:443
  39.8 10.3 %collective-permute-done.3.refs_3_ = f32[2,2,144,128]{3,2,1,0:T(8,128)S(1)} collective-permute-done((f32[2,2,144,128]{3,2,1,0:T(8,128)S(1)}, f32[2,2,144,128]{3,2,1,0:T(8,128)S(1)}, u32[]{:S(2)}, u32[]{:S(2)}) %collective-permute-start.3) | collective-permute-done | bytes 294944 | tf_op jit(solution)/shard_map/ppermute | solution.py:443
  50.2 0.0 copy-start.7
  50.2 0.0 collective-permute-start.5
  50.2 6.1 %collective-permute-start.6 = (f32[1,2,144,128]{3,2,1,0:T(8,128)S(1)}, f32[1,2,144,128]{3,2,1,0:T(8,128)S(1)}, u32[]{:S(2)}, u32[]{:S(2)}) collective-permute-start(f32[1,2,144,128]{3,2,1,0:T(8,128)S(1)} %get-tuple-element.56), channel_id=1, source_target_pairs={{0,2},{1,3},{2,0},{3,1},{4,6},{5,7},{6,4},{7,5},{8,10},{9,11},{10,... | collective-permute-start | bytes 442376 | tf_op jit(solution)/shard_map/ppermute | solution.py:443
  56.3 0.0 collective-permute-start.7
  56.3 0.0 copy-start.8
  56.3 0.0 copy-start.9
  56.3 0.0 copy-start.1
  56.3 0.0 copy-start.3
  56.3 0.0 copy-start.4
  56.3 0.0 copy-start.5
  56.3 0.0 copy-start.6
  56.3 5.6 %remap_upper.1 = (f32[2,160,128]{2,1,0:T(8,128)S(1)}, f32[2,160,128]{2,1,0:T(8,128)S(1)}, f32[2,160,128]{2,1,0:T(8,128)S(1)}, f32[2,160,128]{2,1,0:T(8,128)S(1)}) custom-call(f32[2,2,144,128]{3,2,1,0:T(8,128)S(1)} %get-tuple-element.58.refs_0_, f32[2,2,144,128]{3,2,1,0:T(8,128)S(1)} %collective-permute-done.1.refs_1_, ...), custom_call_target="tpu_custom_call" | custom-call | flops 3520000000 | bytes 11520000 | tf_op jit(solution)/shard_map/remap_upper/pallas_call | solution.py:514
  61.9 0.0 copy-start
  62.0 2.6 %collective-permute-start.8 = (f32[2,160,128]{2,1,0:T(8,128)S(1)}, f32[2,160,128]{2,1,0:T(8,128)S(1)}, u32[]{:S(2)}, u32[]{:S(2)}) collective-permute-start(f32[2,160,128]{2,1,0:T(8,128)S(1)} %get-tuple-element.64), channel_id=1, source_target_pairs={{0,1},{1,2},{2,3},{3,0},{4,5},{5,6},{6,7},{7,4},{8,9},{9,10},{10,1... | collective-permute-start | bytes 491528 | tf_op jit(solution)/shard_map/ppermute | solution.py:443
  64.6 1.0 %collective-permute-start.9 = (f32[2,160,128]{2,1,0:T(8,128)S(1)}, f32[2,160,128]{2,1,0:T(8,128)S(1)}, u32[]{:S(2)}, u32[]{:S(2)}) collective-permute-start(f32[2,160,128]{2,1,0:T(8,128)S(1)} %get-tuple-element.65), channel_id=1, source_target_pairs={{0,2},{1,3},{2,0},{3,1},{4,6},{5,7},{6,4},{7,5},{8,10},{9,11},{10,... | collective-permute-start | bytes 491528 | tf_op jit(solution)/shard_map/ppermute | solution.py:443
  65.6 0.0 collective-permute-done.5.refs_1_
  65.6 3.5 %collective-permute-start.10 = (f32[2,160,128]{2,1,0:T(8,128)S(1)}, f32[2,160,128]{2,1,0:T(8,128)S(1)}, u32[]{:S(2)}, u32[]{:S(2)}) collective-permute-start(f32[2,160,128]{2,1,0:T(8,128)S(1)} %get-tuple-element.66), channel_id=1, source_target_pairs={{0,3},{1,0},{2,1},{3,2},{4,7},{5,4},{6,5},{7,6},{8,11},{9,8},{10,9... | collective-permute-start | bytes 491528 | tf_op jit(solution)/shard_map/ppermute | solution.py:443
  69.1 0.0 copy-done.7
  69.1 0.0 copy-done.8
  69.1 0.0 copy-done.9
  69.1 0.1 add_select_fusion.refs_7_.refs_10_
  69.2 0.0 collective-permute-done.6.refs_2_
  69.2 1.2 %collective-permute-done.7.refs_3_ = f32[1,2,144,128]{3,2,1,0:T(8,128)S(1)} collective-permute-done((f32[1,2,144,128]{3,2,1,0:T(8,128)S(1)}, f32[1,2,144,128]{3,2,1,0:T(8,128)S(1)}, u32[]{:S(2)}, u32[]{:S(2)}) %collective-permute-start.7) | collective-permute-done | bytes 147488 | tf_op jit(solution)/shard_map/ppermute | solution.py:443
  70.4 2.7 %remap_lower.1 = (f32[1,160,128]{2,1,0:T(8,128)S(1)}, f32[1,160,128]{2,1,0:T(8,128)S(1)}, f32[1,160,128]{2,1,0:T(8,128)S(1)}, f32[1,160,128]{2,1,0:T(8,128)S(1)}) custom-call(f32[1,2,144,128]{3,2,1,0:T(8,128)S(1)} %get-tuple-element.54.refs_4_.refs_0_, f32[1,2,144,128]{3,2,1,0:T(8,128)S(1)} %collective-permute-done.5.refs_1_, ...), custom_call_target="tpu_custom_call" | custom-call | flops 220000000 | bytes 720000 | tf_op jit(solution)/shard_map/remap_lower/pallas_call | solution.py:514
  73.1 2.9 %collective-permute-start.12 = (f32[1,160,128]{2,1,0:T(8,128)S(1)}, f32[1,160,128]{2,1,0:T(8,128)S(1)}, u32[]{:S(2)}, u32[]{:S(2)}) collective-permute-start(f32[1,160,128]{2,1,0:T(8,128)S(1)} %get-tuple-element.72), channel_id=1, source_target_pairs={{0,1},{1,2},{2,3},{3,0},{4,5},{5,6},{6,7},{7,4},{8,9},{9,10},{10,1... | collective-permute-start | bytes 245768 | tf_op jit(solution)/shard_map/ppermute | solution.py:443
  76.0 1.8 %collective-permute-start.13 = (f32[1,160,128]{2,1,0:T(8,128)S(1)}, f32[1,160,128]{2,1,0:T(8,128)S(1)}, u32[]{:S(2)}, u32[]{:S(2)}) collective-permute-start(f32[1,160,128]{2,1,0:T(8,128)S(1)} %get-tuple-element.73), channel_id=1, source_target_pairs={{0,2},{1,3},{2,0},{3,1},{4,6},{5,7},{6,4},{7,5},{8,10},{9,11},{10,... | collective-permute-start | bytes 245768 | tf_op jit(solution)/shard_map/ppermute | solution.py:443
  77.8 0.0 collective-permute-done.8.refs_3_
  77.8 1.6 %collective-permute-start.14 = (f32[1,160,128]{2,1,0:T(8,128)S(1)}, f32[1,160,128]{2,1,0:T(8,128)S(1)}, u32[]{:S(2)}, u32[]{:S(2)}) collective-permute-start(f32[1,160,128]{2,1,0:T(8,128)S(1)} %get-tuple-element.74), channel_id=1, source_target_pairs={{0,3},{1,0},{2,1},{3,2},{4,7},{5,4},{6,5},{7,6},{8,11},{9,8},{10,9... | collective-permute-start | bytes 245768 | tf_op jit(solution)/shard_map/ppermute | solution.py:443
  79.4 0.0 collective-permute-done.9.refs_4_
  79.4 0.0 collective-permute-done.10.refs_5_
  79.4 0.0 copy-start.2
  79.5 9.3 %collective-permute-start.11 = (f32[1,160,128]{2,1,0:T(8,128)S(1)}, f32[1,160,128]{2,1,0:T(8,128)S(1)}, u32[]{:S(2)}, u32[]{:S(2)}) collective-permute-start(f32[1,160,128]{2,1,0:T(8,128)S(1)} %select_select_fusion), channel_id=1, source_target_pairs={{0,4},{4,8},{8,12},{12,16},{16,20},{20,24},{24,28},{28,32},{32,36}... | collective-permute-start | bytes 245768 | tf_op jit(solution)/shard_map/ppermute | solution.py:539
  88.8 0.0 copy-done.1
  88.8 0.0 copy-done.3
  88.8 0.0 copy-done.4
  88.8 0.0 copy-done.5
  88.8 0.0 copy-done.6
  88.8 0.0 copy-done
  88.8 0.0 copy-done.2
  88.9 7.0 %final_upper.1 = (f32[12,32,576]{2,1,0:T(8,128)}, f32[12,32,576]{2,1,0:T(8,128)}, f32[12,32,576]{2,1,0:T(8,128)}, f32[12,32,576]{2,1,0:T(8,128)}, f32[3,32,576]{2,1,0:T(8,128)S(1)}) custom-call(s32[1]{0:T(128)} %bitcast.refs_0_, f32[13]{0:T(128)S(1)} %multiply_sine_fusion.1.refs_1_, f32[2,160,128]{2,1,0:T(8,128)S(1)} %get-tuple-element.70.refs_4_.refs_2_, ...), custom_call_target="tpu_custom_call" | custom-call | flops 7699999744 | bytes 25200000 | tf_op jit(solution)/shard_map/final_upper/pallas_call | solution.py:546
  95.9 0.0 collective-permute-done.12.refs_6_
  95.9 0.0 collective-permute-done.13.refs_7_
  95.9 0.0 collective-permute-done.14.refs_8_
  95.9 0.0 collective-permute-done.11.refs_2_
  95.9 4.4 %final_lower.1 = (f32[12,32,576]{2,1,0:T(8,128)}, f32[12,32,576]{2,1,0:T(8,128)}, f32[12,32,576]{2,1,0:T(8,128)}, f32[12,32,576]{2,1,0:T(8,128)}) custom-call(s32[1]{0:T(128)} %bitcast.refs_0_, f32[13]{0:T(128)S(1)} %multiply_sine_fusion.1.refs_1_, ...), custom_call_target="tpu_custom_call", output_to_operand_aliasing={{0}: (17, {}), {1}: (18, {}), {2}: (19, {}), {3}: (20, {})} | custom-call | flops 6600000000 | bytes 21600000 | tf_op jit(solution)/shard_map/final_lower/pallas_call | solution.py:562
  (5 shorter events, 0.1 us)
Async XLA Ops:
  1.8 25.6 %collective-permute-start.4 = (f32[72,576]{1,0:T(8,128)S(1)}, f32[72,576]{1,0:T(8,128)S(1)}, u32[]{:S(2)}, u32[]{:S(2)}) collective-permute-start(f32[72,576]{1,0:T(8,128)S(1)} %get-tuple-element.49), channel_id=1, source_target_pairs={{0,4},{4,8},{8,12},{12,16},{16,20},{20,24},{24,28},{28,32},{32,36}... | collective-permute-start | bytes 497672 | tf_op jit(solution)/shard_map/ppermute | solution.py:489
  6.7 7.5 %collective-permute-start = (f32[96,576]{1,0:T(8,128)S(1)}, f32[96,576]{1,0:T(8,128)S(1)}, u32[]{:S(2)}, u32[]{:S(2)}) collective-permute-start(f32[96,576]{1,0:T(8,128)S(1)} %get-tuple-element.44), channel_id=1, source_target_pairs={{4,0},{8,4},{12,8},{16,12},{20,16},{24,20},{28,24},{32,28},{36,32}... | collective-permute-start | bytes 663560 | tf_op jit(solution)/shard_map/ppermute | solution.py:488
  8.8 0.7 copy-start.10
  17.7 16.5 %collective-permute-start.1 = (f32[2,2,144,128]{3,2,1,0:T(8,128)S(1)}, f32[2,2,144,128]{3,2,1,0:T(8,128)S(1)}, u32[]{:S(2)}, u32[]{:S(2)}) collective-permute-start(f32[2,2,144,128]{3,2,1,0:T(8,128)S(1)} %get-tuple-element.46), channel_id=1, source_target_pairs={{0,1},{1,2},{2,3},{3,0},{4,5},{5,6},{6,7},{7,4},{8,9},{9,10},{10,1... | collective-permute-start | bytes 884744 | tf_op jit(solution)/shard_map/ppermute | solution.py:443
  20.8 19.0 %collective-permute-start.2 = (f32[2,2,144,128]{3,2,1,0:T(8,128)S(1)}, f32[2,2,144,128]{3,2,1,0:T(8,128)S(1)}, u32[]{:S(2)}, u32[]{:S(2)}) collective-permute-start(f32[2,2,144,128]{3,2,1,0:T(8,128)S(1)} %get-tuple-element.47), channel_id=1, source_target_pairs={{0,2},{1,3},{2,0},{3,1},{4,6},{5,7},{6,4},{7,5},{8,10},{9,11},{10,... | collective-permute-start | bytes 884744 | tf_op jit(solution)/shard_map/ppermute | solution.py:443
  25.0 25.1 %collective-permute-start.3 = (f32[2,2,144,128]{3,2,1,0:T(8,128)S(1)}, f32[2,2,144,128]{3,2,1,0:T(8,128)S(1)}, u32[]{:S(2)}, u32[]{:S(2)}) collective-permute-start(f32[2,2,144,128]{3,2,1,0:T(8,128)S(1)} %get-tuple-element.48), channel_id=1, source_target_pairs={{0,3},{1,0},{2,1},{3,2},{4,7},{5,4},{6,5},{7,6},{8,11},{9,8},{10,9... | collective-permute-start | bytes 884744 | tf_op jit(solution)/shard_map/ppermute | solution.py:443
  50.2 18.9 %copy-start.7 = (f32[12,576]{1,0:T(8,128)S(1)}, f32[12,576]{1,0:T(8,128)}, u32[]{:S(2)}) copy-start(f32[12,576]{1,0:T(8,128)} %param.20) | copy-start | bytes 82948
  50.2 15.4 %collective-permute-start.5 = (f32[1,2,144,128]{3,2,1,0:T(8,128)S(1)}, f32[1,2,144,128]{3,2,1,0:T(8,128)S(1)}, u32[]{:S(2)}, u32[]{:S(2)}) collective-permute-start(f32[1,2,144,128]{3,2,1,0:T(8,128)S(1)} %get-tuple-element.55), channel_id=1, source_target_pairs={{0,1},{1,2},{2,3},{3,0},{4,5},{5,6},{6,7},{7,4},{8,9},{9,10},{10,1... | collective-permute-start | bytes 442376 | tf_op jit(solution)/shard_map/ppermute | solution.py:443
  50.2 19.0 %collective-permute-start.6 = (f32[1,2,144,128]{3,2,1,0:T(8,128)S(1)}, f32[1,2,144,128]{3,2,1,0:T(8,128)S(1)}, u32[]{:S(2)}, u32[]{:S(2)}) collective-permute-start(f32[1,2,144,128]{3,2,1,0:T(8,128)S(1)} %get-tuple-element.56), channel_id=1, source_target_pairs={{0,2},{1,3},{2,0},{3,1},{4,6},{5,7},{6,4},{7,5},{8,10},{9,11},{10,... | collective-permute-start | bytes 442376 | tf_op jit(solution)/shard_map/ppermute | solution.py:443
  56.3 14.1 %collective-permute-start.7 = (f32[1,2,144,128]{3,2,1,0:T(8,128)S(1)}, f32[1,2,144,128]{3,2,1,0:T(8,128)S(1)}, u32[]{:S(2)}, u32[]{:S(2)}) collective-permute-start(f32[1,2,144,128]{3,2,1,0:T(8,128)S(1)} %get-tuple-element.57), channel_id=1, source_target_pairs={{0,3},{1,0},{2,1},{3,2},{4,7},{5,4},{6,5},{7,6},{8,11},{9,8},{10,9... | collective-permute-start | bytes 442376 | tf_op jit(solution)/shard_map/ppermute | solution.py:443
  56.3 12.8 %copy-start.8 = (s32[576]{0:T(1024)S(1)}, s32[576]{0:T(1024)}, u32[]{:S(2)}) copy-start(s32[576]{0:T(1024)} %constant.61.clone) | copy-start | bytes 6916
  56.3 12.8 %copy-start.9 = (s32[12]{0:T(128)S(1)}, s32[12]{0:T(128)}, u32[]{:S(2)}) copy-start(s32[12]{0:T(128)} %param.19) | copy-start | bytes 148
  56.3 32.5 %copy-start.1 = (f32[12,32,576]{2,1,0:T(8,128)S(1)}, f32[12,32,576]{2,1,0:T(8,128)}, u32[]{:S(2)}) copy-start(f32[12,32,576]{2,1,0:T(8,128)} %refs_11_.2) | copy-start | bytes 2654212
  56.3 32.5 %copy-start.3 = (bf16[576,576]{1,0:T(8,128)(2,1)S(1)}, bf16[576,576]{1,0:T(8,128)(2,1)}, u32[]{:S(2)}) copy-start(bf16[576,576]{1,0:T(8,128)(2,1)} %constant.65.clone.refs_13_.refs_16_) | copy-start | bytes 1990660
  56.3 32.5 %copy-start.4 = (bf16[576,576]{1,0:T(8,128)(2,1)S(1)}, bf16[576,576]{1,0:T(8,128)(2,1)}, u32[]{:S(2)}) copy-start(bf16[576,576]{1,0:T(8,128)(2,1)} %constant.64.clone.refs_12_.refs_15_) | copy-start | bytes 1990660
  56.3 32.5 %copy-start.5 = (bf16[576,576]{1,0:T(8,128)(2,1)S(1)}, bf16[576,576]{1,0:T(8,128)(2,1)}, u32[]{:S(2)}) copy-start(bf16[576,576]{1,0:T(8,128)(2,1)} %constant.63.clone.refs_11_.refs_14_) | copy-start | bytes 1990660
  56.3 32.5 %copy-start.6 = (bf16[576,576]{1,0:T(8,128)(2,1)S(1)}, bf16[576,576]{1,0:T(8,128)(2,1)}, u32[]{:S(2)}) copy-start(bf16[576,576]{1,0:T(8,128)(2,1)} %constant.62.clone.refs_10_.refs_13_) | copy-start | bytes 1990660
  61.9 26.9 %copy-start = (f32[12,32,576]{2,1,0:T(8,128)S(1)}, f32[12,32,576]{2,1,0:T(8,128)}, u32[]{:S(2)}) copy-start(f32[12,32,576]{2,1,0:T(8,128)} %refs_12_.2) | copy-start | bytes 2654212
  62.0 15.9 %collective-permute-start.8 = (f32[2,160,128]{2,1,0:T(8,128)S(1)}, f32[2,160,128]{2,1,0:T(8,128)S(1)}, u32[]{:S(2)}, u32[]{:S(2)}) collective-permute-start(f32[2,160,128]{2,1,0:T(8,128)S(1)} %get-tuple-element.64), channel_id=1, source_target_pairs={{0,1},{1,2},{2,3},{3,0},{4,5},{5,6},{6,7},{7,4},{8,9},{9,10},{10,1... | collective-permute-start | bytes 491528 | tf_op jit(solution)/shard_map/ppermute | solution.py:443
  64.6 14.9 %collective-permute-start.9 = (f32[2,160,128]{2,1,0:T(8,128)S(1)}, f32[2,160,128]{2,1,0:T(8,128)S(1)}, u32[]{:S(2)}, u32[]{:S(2)}) collective-permute-start(f32[2,160,128]{2,1,0:T(8,128)S(1)} %get-tuple-element.65), channel_id=1, source_target_pairs={{0,2},{1,3},{2,0},{3,1},{4,6},{5,7},{6,4},{7,5},{8,10},{9,11},{10,... | collective-permute-start | bytes 491528 | tf_op jit(solution)/shard_map/ppermute | solution.py:443
  65.6 13.8 %collective-permute-start.10 = (f32[2,160,128]{2,1,0:T(8,128)S(1)}, f32[2,160,128]{2,1,0:T(8,128)S(1)}, u32[]{:S(2)}, u32[]{:S(2)}) collective-permute-start(f32[2,160,128]{2,1,0:T(8,128)S(1)} %get-tuple-element.66), channel_id=1, source_target_pairs={{0,3},{1,0},{2,1},{3,2},{4,7},{5,4},{6,5},{7,6},{8,11},{9,8},{10,9... | collective-permute-start | bytes 491528 | tf_op jit(solution)/shard_map/ppermute | solution.py:443
  73.1 22.8 %collective-permute-start.12 = (f32[1,160,128]{2,1,0:T(8,128)S(1)}, f32[1,160,128]{2,1,0:T(8,128)S(1)}, u32[]{:S(2)}, u32[]{:S(2)}) collective-permute-start(f32[1,160,128]{2,1,0:T(8,128)S(1)} %get-tuple-element.72), channel_id=1, source_target_pairs={{0,1},{1,2},{2,3},{3,0},{4,5},{5,6},{6,7},{7,4},{8,9},{9,10},{10,1... | collective-permute-start | bytes 245768 | tf_op jit(solution)/shard_map/ppermute | solution.py:443
  76.0 19.8 %collective-permute-start.13 = (f32[1,160,128]{2,1,0:T(8,128)S(1)}, f32[1,160,128]{2,1,0:T(8,128)S(1)}, u32[]{:S(2)}, u32[]{:S(2)}) collective-permute-start(f32[1,160,128]{2,1,0:T(8,128)S(1)} %get-tuple-element.73), channel_id=1, source_target_pairs={{0,2},{1,3},{2,0},{3,1},{4,6},{5,7},{6,4},{7,5},{8,10},{9,11},{10,... | collective-permute-start | bytes 245768 | tf_op jit(solution)/shard_map/ppermute | solution.py:443
  77.8 18.1 %collective-permute-start.14 = (f32[1,160,128]{2,1,0:T(8,128)S(1)}, f32[1,160,128]{2,1,0:T(8,128)S(1)}, u32[]{:S(2)}, u32[]{:S(2)}) collective-permute-start(f32[1,160,128]{2,1,0:T(8,128)S(1)} %get-tuple-element.74), channel_id=1, source_target_pairs={{0,3},{1,0},{2,1},{3,2},{4,7},{5,4},{6,5},{7,6},{8,11},{9,8},{10,9... | collective-permute-start | bytes 245768 | tf_op jit(solution)/shard_map/ppermute | solution.py:443
  79.4 9.4 %copy-start.2 = (f32[12,576]{1,0:T(8,128)S(1)}, f32[12,576]{1,0:T(8,128)}, u32[]{:S(2)}) copy-start(f32[12,576]{1,0:T(8,128)} %refs_9_.3) | copy-start | bytes 82948
  79.5 16.4 %collective-permute-start.11 = (f32[1,160,128]{2,1,0:T(8,128)S(1)}, f32[1,160,128]{2,1,0:T(8,128)S(1)}, u32[]{:S(2)}, u32[]{:S(2)}) collective-permute-start(f32[1,160,128]{2,1,0:T(8,128)S(1)} %select_select_fusion), channel_id=1, source_target_pairs={{0,4},{4,8},{8,12},{12,16},{16,20},{20,24},{24,28},{28,32},{32,36}... | collective-permute-start | bytes 245768 | tf_op jit(solution)/shard_map/ppermute | solution.py:539

commit v7 on v6

--- a/solution.py
+++ b/solution.py
@@ -380,16 +380,15 @@
     def _():
         tables = (b0, b1, b2, b3)
         filter_rows(zonal_s, count, table[rows, :], tables, block)
+
+    early += copy_all([(zonal_s, zonal_out.at[rows])], sems, 2)
+
+    @pl.when(flag[0] != 0)
+    def _():
+        tables = (b0, b1, b2, b3)
         filter_rows(merid_s, count - 1, table[pl.ds(first + 1, count - 1), :], tables, block)
 
-    late = copy_all(
-        [
-            (zonal_s, zonal_out.at[rows]),
-            (merid_s.at[pl.ds(0, count - 1)], merid_out.at[pl.ds(first + 1, count - 1)]),
-        ],
-        sems,
-        2,
-    )
+    late = copy_all([(merid_s.at[pl.ds(0, count - 1)], merid_out.at[pl.ds(first + 1, count - 1)])], sems, 3)
     wait_all(early + late)
 
 
@@ -505,8 +504,7 @@
 
     upper_columns = exchanged(advect(first, upper_each, halo_n, "advect_upper"))
     lower_sent = advect(0, lower_each, halo_s, "advect_lower")
-    settled = lax.optimization_barrier((*upper_columns, *lower_sent))
-    upper_columns, lower_sent = settled[:peers], settled[peers:]
+    upper_columns[1], *lower_sent = lax.optimization_barrier((upper_columns[1], *lower_sent))
     lower_columns = exchanged(lower_sent)
 
     def remap(columns, each, name, after):

time: 102 us -> 103 us (level)
  starting transfers between devices: 45.4 us -> 56.6 us
  waiting for transfers between devices: 24.2 us -> 14.9 us
    ppermute x12, waiting for transfers between devices: 20.7 us -> 11.4 us  [exchanged(): lax.ppermute(parts[step], 'lev', [(i, (i + step) % peers) for i in range(...]
    ppermute x12, starting transfers between devices: 29.2 us -> 35.7 us  [exchanged(): lax.ppermute(parts[step], 'lev', [(i, (i + step) % peers) for i in range(...]
    ppermute x1, starting transfers between devices: 9.3 us -> 14 us  [body(): south = lax.ppermute(last_message, 'lat', northward)]
  transfers between devices with their start and end apart: 15 -> 15, of which waited for: 5 -> 6; matrix products, arithmetic and copies ran while one was open for 1% -> 1% of each run, Pallas kernels for 22% -> 21%
where the time goes in v7:
time: 103 us; the launch traced here: 102 us
  starting transfers between devices  56.6 us (55%)
  Pallas kernels  27.5 us (27%)
  waiting for transfers between devices  14.9 us (14%)
  between operations  1.74 us (2%)
    ppermute x12, starting transfers between devices, exchanged(): lax.ppermute(parts[step], 'lev', [(i, (i + step) % peers) for i in range(...  35.7 us
    ppermute x1, starting transfers between devices, body(): south = lax.ppermute(last_message, 'lat', northward)  14 us
    ppermute x12, waiting for transfers between devices, exchanged(): lax.ppermute(parts[step], 'lev', [(i, (i + step) % peers) for i in range(...  11.4 us
    pallas_call x2, Pallas kernels, remap(): pl.pallas_call(lambda *refs: remap_kernel(width, block, peers, *refs), ou...  8.33 us
    pallas_call x1, Pallas kernels, body(): pl.pallas_call(lambda *refs: upper_final_kernel(levels, first, *refs), ou...  6.87 us
    pallas_call x2, Pallas kernels, advect(): pl.pallas_call(lambda *refs: advect_kernel(start, each, peers, *refs), ou...  6.78 us
    ppermute x1, starting transfers between devices, body(): halo_s = lax.ppermute(to_north, 'lat', northward)  4.94 us
    pallas_call x1, Pallas kernels, body(): pl.pallas_call(lambda *refs: lower_final_kernel(levels, *refs), out_shape...  4.43 us
  transfers between devices with their start and end apart: 15, of which 6 were waited for; matrix products, arithmetic and copies ran while one was open for 1% of the time, Pallas kernels for 21%

profile of v7, /device:TPU:1, one launch (start us, length us, event | category | flops | bytes accessed | tf_op | source)
XLA Modules:
  0.0 102.3 jit_solution(3594038806646582700)
XLA Ops:
  0.6 1.1 %edges.1 = (f32[72,576]{1,0:T(8,128)S(1)}, f32[96,576]{1,0:T(8,128)S(1)}) custom-call(f32[12,32,576]{2,1,0:T(8,128)} %refs_12_.2, f32[12,32,576]{2,1,0:T(8,128)} %refs_4_.3, f32[12,32,576]{2,1,0:T(8,128)} %refs_5_.3, f32[12,576]{1,0:T(8,128)} %refs_9_.3), custom_call_target="tpu_custom_call" | custom-call | flops 1100000000 | bytes 3600000 | tf_op jit(solution)/shard_map/edges/pallas_call | solution.py:477
  1.8 4.9 %collective-permute-start.2 = (f32[72,576]{1,0:T(8,128)S(1)}, f32[72,576]{1,0:T(8,128)S(1)}, u32[]{:S(2)}, u32[]{:S(2)}) collective-permute-start(f32[72,576]{1,0:T(8,128)S(1)} %get-tuple-element.43), channel_id=1, source_target_pairs={{0,4},{4,8},{8,12},{12,16},{16,20},{20,24},{24,28},{28,32},{32,36}... | collective-permute-start | bytes 497672 | tf_op jit(solution)/shard_map/ppermute | solution.py:488
  6.7 1.9 %collective-permute-start = (f32[96,576]{1,0:T(8,128)S(1)}, f32[96,576]{1,0:T(8,128)S(1)}, u32[]{:S(2)}, u32[]{:S(2)}) collective-permute-start(f32[96,576]{1,0:T(8,128)S(1)} %get-tuple-element.41), channel_id=1, source_target_pairs={{4,0},{8,4},{12,8},{16,12},{20,16},{24,20},{28,24},{32,28},{36,32}... | collective-permute-start | bytes 663560 | tf_op jit(solution)/shard_map/ppermute | solution.py:487
  8.8 0.0 copy-start.10
  8.8 0.1 slice_bitcast_fusion.1
  8.8 0.6 copy-done.10
  9.4 0.6 broadcast_compare_fusion
  10.7 3.5 %collective-permute-done.refs_1_ = f32[96,576]{1,0:T(8,128)S(1)} collective-permute-done((f32[96,576]{1,0:T(8,128)S(1)}, f32[96,576]{1,0:T(8,128)S(1)}, u32[]{:S(2)}, u32[]{:S(2)}) %collective-permute-start) | collective-permute-done | bytes 221216 | tf_op jit(solution)/shard_map/ppermute | solution.py:487
  14.2 3.5 %advect_upper.1 = (f32[2,2,144,128]{3,2,1,0:T(8,128)S(1)}, f32[2,2,144,128]{3,2,1,0:T(8,128)S(1)}, f32[2,2,144,128]{3,2,1,0:T(8,128)S(1)}, f32[2,2,144,128]{3,2,1,0:T(8,128)S(1)}) custom-call(f32[2,12]{1,0:T(2,128)S(1)} %fusion.refs_0_, f32[96,576]{1,0:T(8,128)S(1)} %collective-permute-done.refs_1_, f32[12,32,576]{2,1,0:T(8,128)} %refs_11_.2, ...), custom_call_target="tpu_custom_call" | custom-call | flops 5500000256 | bytes 18000000 | tf_op jit(solution)/shard_map/advect_upper/pallas_call | solution.py:491
  17.7 3.1 %collective-permute-start.1 = (f32[2,2,144,128]{3,2,1,0:T(8,128)S(1)}, f32[2,2,144,128]{3,2,1,0:T(8,128)S(1)}, u32[]{:S(2)}, u32[]{:S(2)}) collective-permute-start(f32[2,2,144,128]{3,2,1,0:T(8,128)S(1)} %get-tuple-element.42), channel_id=1, source_target_pairs={{0,1},{1,2},{2,3},{3,0},{4,5},{5,6},{6,7},{7,4},{8,9},{9,10},{10,1... | collective-permute-start | bytes 884744 | tf_op jit(solution)/shard_map/ppermute | solution.py:442
  20.8 4.2 %collective-permute-start.6 = (f32[2,2,144,128]{3,2,1,0:T(8,128)S(1)}, f32[2,2,144,128]{3,2,1,0:T(8,128)S(1)}, u32[]{:S(2)}, u32[]{:S(2)}) collective-permute-start(f32[2,2,144,128]{3,2,1,0:T(8,128)S(1)} %get-tuple-element.54), channel_id=1, source_target_pairs={{0,2},{1,3},{2,0},{3,1},{4,6},{5,7},{6,4},{7,5},{8,10},{9,11},{10,... | collective-permute-start | bytes 884744 | tf_op jit(solution)/shard_map/ppermute | solution.py:442
  25.0 2.4 %collective-permute-start.7 = (f32[2,2,144,128]{3,2,1,0:T(8,128)S(1)}, f32[2,2,144,128]{3,2,1,0:T(8,128)S(1)}, u32[]{:S(2)}, u32[]{:S(2)}) collective-permute-start(f32[2,2,144,128]{3,2,1,0:T(8,128)S(1)} %get-tuple-element.55), channel_id=1, source_target_pairs={{0,3},{1,0},{2,1},{3,2},{4,7},{5,4},{6,5},{7,6},{8,11},{9,8},{10,9... | collective-permute-start | bytes 884744 | tf_op jit(solution)/shard_map/ppermute | solution.py:442
  27.4 0.0 collective-permute-done.2.refs_1_.refs_3_
  27.4 3.3 %advect_lower.1 = (f32[1,2,144,128]{3,2,1,0:T(8,128)S(1)}, f32[1,2,144,128]{3,2,1,0:T(8,128)S(1)}, f32[1,2,144,128]{3,2,1,0:T(8,128)S(1)}, f32[1,2,144,128]{3,2,1,0:T(8,128)S(1)}) custom-call(f32[2,12]{1,0:T(2,128)S(1)} %fusion.refs_0_, f32[72,576]{1,0:T(8,128)S(1)} %collective-permute-done.2.refs_1_.refs_3_, f32[12,32,576]{2,1,0:T(8,128)} %refs_11_.2, ...), custom_call_target="tpu_custom_call" | custom-call | flops 3300000000 | bytes 10800000 | tf_op jit(solution)/shard_map/advect_lower/pallas_call | solution.py:491
  30.7 3.5 %collective-permute-done.1.refs_1_ = f32[2,2,144,128]{3,2,1,0:T(8,128)S(1)} collective-permute-done((f32[2,2,144,128]{3,2,1,0:T(8,128)S(1)}, f32[2,2,144,128]{3,2,1,0:T(8,128)S(1)}, u32[]{:S(2)}, u32[]{:S(2)}) %collective-permute-start.1) | collective-permute-done | bytes 294944 | tf_op jit(solution)/shard_map/ppermute | solution.py:442
  34.2 3.0 %collective-permute-start.3 = (f32[1,2,144,128]{3,2,1,0:T(8,128)S(1)}, f32[1,2,144,128]{3,2,1,0:T(8,128)S(1)}, u32[]{:S(2)}, u32[]{:S(2)}) collective-permute-start(f32[1,2,144,128]{3,2,1,0:T(8,128)S(1)} %get-tuple-element.49), channel_id=1, source_target_pairs={{0,1},{1,2},{2,3},{3,0},{4,5},{5,6},{6,7},{7,4},{8,9},{9,10},{10,1... | collective-permute-start | bytes 442376 | tf_op jit(solution)/shard_map/ppermute | solution.py:442
  37.3 4.0 %collective-permute-start.4 = (f32[1,2,144,128]{3,2,1,0:T(8,128)S(1)}, f32[1,2,144,128]{3,2,1,0:T(8,128)S(1)}, u32[]{:S(2)}, u32[]{:S(2)}) collective-permute-start(f32[1,2,144,128]{3,2,1,0:T(8,128)S(1)} %get-tuple-element.50), channel_id=1, source_target_pairs={{0,2},{1,3},{2,0},{3,1},{4,6},{5,7},{6,4},{7,5},{8,10},{9,11},{10,... | collective-permute-start | bytes 442376 | tf_op jit(solution)/shard_map/ppermute | solution.py:442
  41.2 3.6 %collective-permute-start.5 = (f32[1,2,144,128]{3,2,1,0:T(8,128)S(1)}, f32[1,2,144,128]{3,2,1,0:T(8,128)S(1)}, u32[]{:S(2)}, u32[]{:S(2)}) collective-permute-start(f32[1,2,144,128]{3,2,1,0:T(8,128)S(1)} %get-tuple-element.51), channel_id=1, source_target_pairs={{0,3},{1,0},{2,1},{3,2},{4,7},{5,4},{6,5},{7,6},{8,11},{9,8},{10,9... | collective-permute-start | bytes 442376 | tf_op jit(solution)/shard_map/ppermute | solution.py:442
  44.8 1.3 %collective-permute-done.6.refs_2_ = f32[2,2,144,128]{3,2,1,0:T(8,128)S(1)} collective-permute-done((f32[2,2,144,128]{3,2,1,0:T(8,128)S(1)}, f32[2,2,144,128]{3,2,1,0:T(8,128)S(1)}, u32[]{:S(2)}, u32[]{:S(2)}) %collective-permute-start.6) | collective-permute-done | bytes 294944 | tf_op jit(solution)/shard_map/ppermute | solution.py:442
  46.1 4.2 %collective-permute-done.7.refs_3_ = f32[2,2,144,128]{3,2,1,0:T(8,128)S(1)} collective-permute-done((f32[2,2,144,128]{3,2,1,0:T(8,128)S(1)}, f32[2,2,144,128]{3,2,1,0:T(8,128)S(1)}, u32[]{:S(2)}, u32[]{:S(2)}) %collective-permute-start.7) | collective-permute-done | bytes 294944 | tf_op jit(solution)/shard_map/ppermute | solution.py:442
  50.3 0.0 copy-start.7
  50.3 0.0 copy-start.8
  50.3 0.0 copy-start.9
  50.3 0.0 copy-start.1
  50.3 0.0 copy-start.3
  50.3 0.0 copy-start.4
  50.3 0.0 copy-start.5
  50.3 0.0 copy-start.6
  50.3 5.6 %remap_upper.1 = (f32[2,160,128]{2,1,0:T(8,128)S(1)}, f32[2,160,128]{2,1,0:T(8,128)S(1)}, f32[2,160,128]{2,1,0:T(8,128)S(1)}, f32[2,160,128]{2,1,0:T(8,128)S(1)}) custom-call(f32[2,2,144,128]{3,2,1,0:T(8,128)S(1)} %get-tuple-element.52.refs_0_, f32[2,2,144,128]{3,2,1,0:T(8,128)S(1)} %collective-permute-done.1.refs_1_, ...), custom_call_target="tpu_custom_call" | custom-call | flops 3520000000 | bytes 11520000 | tf_op jit(solution)/shard_map/remap_upper/pallas_call | solution.py:512
  56.0 0.0 copy-start
  56.0 0.3 collective-permute-start.8
  56.2 6.5 %collective-permute-start.9 = (f32[2,160,128]{2,1,0:T(8,128)S(1)}, f32[2,160,128]{2,1,0:T(8,128)S(1)}, u32[]{:S(2)}, u32[]{:S(2)}) collective-permute-start(f32[2,160,128]{2,1,0:T(8,128)S(1)} %get-tuple-element.59), channel_id=1, source_target_pairs={{0,2},{1,3},{2,0},{3,1},{4,6},{5,7},{6,4},{7,5},{8,10},{9,11},{10,... | collective-permute-start | bytes 491528 | tf_op jit(solution)/shard_map/ppermute | solution.py:442
  62.8 0.0 collective-permute-done.3.refs_1_
  62.8 0.0 collective-permute-start.10
  62.8 0.0 copy-done.7
  62.8 0.0 copy-done.8
  62.8 0.0 copy-done.9
  62.8 0.1 add_select_fusion.refs_7_.refs_10_
  62.9 0.0 collective-permute-done.4.refs_2_
  62.9 0.0 collective-permute-done.5.refs_3_
  62.9 2.7 %remap_lower.1 = (f32[1,160,128]{2,1,0:T(8,128)S(1)}, f32[1,160,128]{2,1,0:T(8,128)S(1)}, f32[1,160,128]{2,1,0:T(8,128)S(1)}, f32[1,160,128]{2,1,0:T(8,128)S(1)}) custom-call(f32[1,2,144,128]{3,2,1,0:T(8,128)S(1)} %get-tuple-element.48.refs_4_.refs_0_, f32[1,2,144,128]{3,2,1,0:T(8,128)S(1)} %collective-permute-done.3.refs_1_, ...), custom_call_target="tpu_custom_call" | custom-call | flops 220000000 | bytes 720000 | tf_op jit(solution)/shard_map/remap_lower/pallas_call | solution.py:512
  65.6 2.4 %collective-permute-start.12 = (f32[1,160,128]{2,1,0:T(8,128)S(1)}, f32[1,160,128]{2,1,0:T(8,128)S(1)}, u32[]{:S(2)}, u32[]{:S(2)}) collective-permute-start(f32[1,160,128]{2,1,0:T(8,128)S(1)} %get-tuple-element.66), channel_id=1, source_target_pairs={{0,1},{1,2},{2,3},{3,0},{4,5},{5,6},{6,7},{7,4},{8,9},{9,10},{10,1... | collective-permute-start | bytes 245768 | tf_op jit(solution)/shard_map/ppermute | solution.py:442
  68.0 2.0 %collective-permute-start.13 = (f32[1,160,128]{2,1,0:T(8,128)S(1)}, f32[1,160,128]{2,1,0:T(8,128)S(1)}, u32[]{:S(2)}, u32[]{:S(2)}) collective-permute-start(f32[1,160,128]{2,1,0:T(8,128)S(1)} %get-tuple-element.67), channel_id=1, source_target_pairs={{0,2},{1,3},{2,0},{3,1},{4,6},{5,7},{6,4},{7,5},{8,10},{9,11},{10,... | collective-permute-start | bytes 245768 | tf_op jit(solution)/shard_map/ppermute | solution.py:442
  70.1 0.0 collective-permute-done.8.refs_3_
  70.1 4.2 %collective-permute-start.14 = (f32[1,160,128]{2,1,0:T(8,128)S(1)}, f32[1,160,128]{2,1,0:T(8,128)S(1)}, u32[]{:S(2)}, u32[]{:S(2)}) collective-permute-start(f32[1,160,128]{2,1,0:T(8,128)S(1)} %get-tuple-element.68), channel_id=1, source_target_pairs={{0,3},{1,0},{2,1},{3,2},{4,7},{5,4},{6,5},{7,6},{8,11},{9,8},{10,9... | collective-permute-start | bytes 245768 | tf_op jit(solution)/shard_map/ppermute | solution.py:442
  74.3 1.5 %collective-permute-done.9.refs_4_ = f32[2,160,128]{2,1,0:T(8,128)S(1)} collective-permute-done((f32[2,160,128]{2,1,0:T(8,128)S(1)}, f32[2,160,128]{2,1,0:T(8,128)S(1)}, u32[]{:S(2)}, u32[]{:S(2)}) %collective-permute-start.9) | collective-permute-done | bytes 163872 | tf_op jit(solution)/shard_map/ppermute | solution.py:442
  75.8 0.8 collective-permute-done.10.refs_5_
  76.6 0.0 copy-start.2
  76.7 14.0 %collective-permute-start.11 = (f32[1,160,128]{2,1,0:T(8,128)S(1)}, f32[1,160,128]{2,1,0:T(8,128)S(1)}, u32[]{:S(2)}, u32[]{:S(2)}) collective-permute-start(f32[1,160,128]{2,1,0:T(8,128)S(1)} %select_select_fusion), channel_id=1, source_target_pairs={{0,4},{4,8},{8,12},{12,16},{16,20},{20,24},{24,28},{28,32},{32,36}... | collective-permute-start | bytes 245768 | tf_op jit(solution)/shard_map/ppermute | solution.py:537
  90.7 0.0 copy-done.1
  90.7 0.0 copy-done.3
  90.7 0.0 copy-done.4
  90.7 0.0 copy-done.5
  90.8 0.0 copy-done.6
  90.8 0.0 copy-done
  90.8 0.0 copy-done.2
  90.8 6.9 %final_upper.1 = (f32[12,32,576]{2,1,0:T(8,128)}, f32[12,32,576]{2,1,0:T(8,128)}, f32[12,32,576]{2,1,0:T(8,128)}, f32[12,32,576]{2,1,0:T(8,128)}, f32[3,32,576]{2,1,0:T(8,128)S(1)}) custom-call(s32[1]{0:T(128)} %bitcast.refs_0_, f32[13]{0:T(128)S(1)} %multiply_sine_fusion.1.refs_1_, f32[2,160,128]{2,1,0:T(8,128)S(1)} %get-tuple-element.64.refs_4_.refs_2_, ...), custom_call_target="tpu_custom_call" | custom-call | flops 7699999744 | bytes 25200000 | tf_op jit(solution)/shard_map/final_upper/pallas_call | solution.py:544
  97.7 0.0 collective-permute-done.12.refs_6_
  97.7 0.0 collective-permute-done.13.refs_7_
  97.7 0.0 collective-permute-done.14.refs_8_
  97.7 0.0 collective-permute-done.11.refs_2_
  97.7 4.4 %final_lower.1 = (f32[12,32,576]{2,1,0:T(8,128)}, f32[12,32,576]{2,1,0:T(8,128)}, f32[12,32,576]{2,1,0:T(8,128)}, f32[12,32,576]{2,1,0:T(8,128)}) custom-call(s32[1]{0:T(128)} %bitcast.refs_0_, f32[13]{0:T(128)S(1)} %multiply_sine_fusion.1.refs_1_, ...), custom_call_target="tpu_custom_call", output_to_operand_aliasing={{0}: (17, {}), {1}: (18, {}), {2}: (19, {}), {3}: (20, {})} | custom-call | flops 6600000000 | bytes 21600000 | tf_op jit(solution)/shard_map/final_lower/pallas_call | solution.py:560
  (5 shorter events, 0.1 us)
Async XLA Ops:
  1.8 25.6 %collective-permute-start.2 = (f32[72,576]{1,0:T(8,128)S(1)}, f32[72,576]{1,0:T(8,128)S(1)}, u32[]{:S(2)}, u32[]{:S(2)}) collective-permute-start(f32[72,576]{1,0:T(8,128)S(1)} %get-tuple-element.43), channel_id=1, source_target_pairs={{0,4},{4,8},{8,12},{12,16},{16,20},{20,24},{24,28},{28,32},{32,36}... | collective-permute-start | bytes 497672 | tf_op jit(solution)/shard_map/ppermute | solution.py:488
  6.7 7.5 %collective-permute-start = (f32[96,576]{1,0:T(8,128)S(1)}, f32[96,576]{1,0:T(8,128)S(1)}, u32[]{:S(2)}, u32[]{:S(2)}) collective-permute-start(f32[96,576]{1,0:T(8,128)S(1)} %get-tuple-element.41), channel_id=1, source_target_pairs={{4,0},{8,4},{12,8},{16,12},{20,16},{24,20},{28,24},{32,28},{36,32}... | collective-permute-start | bytes 663560 | tf_op jit(solution)/shard_map/ppermute | solution.py:487
  8.8 0.7 copy-start.10
  17.7 16.5 %collective-permute-start.1 = (f32[2,2,144,128]{3,2,1,0:T(8,128)S(1)}, f32[2,2,144,128]{3,2,1,0:T(8,128)S(1)}, u32[]{:S(2)}, u32[]{:S(2)}) collective-permute-start(f32[2,2,144,128]{3,2,1,0:T(8,128)S(1)} %get-tuple-element.42), channel_id=1, source_target_pairs={{0,1},{1,2},{2,3},{3,0},{4,5},{5,6},{6,7},{7,4},{8,9},{9,10},{10,1... | collective-permute-start | bytes 884744 | tf_op jit(solution)/shard_map/ppermute | solution.py:442
  20.8 25.3 %collective-permute-start.6 = (f32[2,2,144,128]{3,2,1,0:T(8,128)S(1)}, f32[2,2,144,128]{3,2,1,0:T(8,128)S(1)}, u32[]{:S(2)}, u32[]{:S(2)}) collective-permute-start(f32[2,2,144,128]{3,2,1,0:T(8,128)S(1)} %get-tuple-element.54), channel_id=1, source_target_pairs={{0,2},{1,3},{2,0},{3,1},{4,6},{5,7},{6,4},{7,5},{8,10},{9,11},{10,... | collective-permute-start | bytes 884744 | tf_op jit(solution)/shard_map/ppermute | solution.py:442
  25.0 25.3 %collective-permute-start.7 = (f32[2,2,144,128]{3,2,1,0:T(8,128)S(1)}, f32[2,2,144,128]{3,2,1,0:T(8,128)S(1)}, u32[]{:S(2)}, u32[]{:S(2)}) collective-permute-start(f32[2,2,144,128]{3,2,1,0:T(8,128)S(1)} %get-tuple-element.55), channel_id=1, source_target_pairs={{0,3},{1,0},{2,1},{3,2},{4,7},{5,4},{6,5},{7,6},{8,11},{9,8},{10,9... | collective-permute-start | bytes 884744 | tf_op jit(solution)/shard_map/ppermute | solution.py:442
  34.2 28.5 %collective-permute-start.3 = (f32[1,2,144,128]{3,2,1,0:T(8,128)S(1)}, f32[1,2,144,128]{3,2,1,0:T(8,128)S(1)}, u32[]{:S(2)}, u32[]{:S(2)}) collective-permute-start(f32[1,2,144,128]{3,2,1,0:T(8,128)S(1)} %get-tuple-element.49), channel_id=1, source_target_pairs={{0,1},{1,2},{2,3},{3,0},{4,5},{5,6},{6,7},{7,4},{8,9},{9,10},{10,1... | collective-permute-start | bytes 442376 | tf_op jit(solution)/shard_map/ppermute | solution.py:442
  37.3 25.6 %collective-permute-start.4 = (f32[1,2,144,128]{3,2,1,0:T(8,128)S(1)}, f32[1,2,144,128]{3,2,1,0:T(8,128)S(1)}, u32[]{:S(2)}, u32[]{:S(2)}) collective-permute-start(f32[1,2,144,128]{3,2,1,0:T(8,128)S(1)} %get-tuple-element.50), channel_id=1, source_target_pairs={{0,2},{1,3},{2,0},{3,1},{4,6},{5,7},{6,4},{7,5},{8,10},{9,11},{10,... | collective-permute-start | bytes 442376 | tf_op jit(solution)/shard_map/ppermute | solution.py:442
  41.2 21.7 %collective-permute-start.5 = (f32[1,2,144,128]{3,2,1,0:T(8,128)S(1)}, f32[1,2,144,128]{3,2,1,0:T(8,128)S(1)}, u32[]{:S(2)}, u32[]{:S(2)}) collective-permute-start(f32[1,2,144,128]{3,2,1,0:T(8,128)S(1)} %get-tuple-element.51), channel_id=1, source_target_pairs={{0,3},{1,0},{2,1},{3,2},{4,7},{5,4},{6,5},{7,6},{8,11},{9,8},{10,9... | collective-permute-start | bytes 442376 | tf_op jit(solution)/shard_map/ppermute | solution.py:442
  50.3 12.5 %copy-start.7 = (f32[12,576]{1,0:T(8,128)S(1)}, f32[12,576]{1,0:T(8,128)}, u32[]{:S(2)}) copy-start(f32[12,576]{1,0:T(8,128)} %param.20) | copy-start | bytes 82948
  50.3 12.5 %copy-start.8 = (s32[576]{0:T(1024)S(1)}, s32[576]{0:T(1024)}, u32[]{:S(2)}) copy-start(s32[576]{0:T(1024)} %constant.61.clone) | copy-start | bytes 6916
  50.3 12.5 %copy-start.9 = (s32[12]{0:T(128)S(1)}, s32[12]{0:T(128)}, u32[]{:S(2)}) copy-start(s32[12]{0:T(128)} %param.19) | copy-start | bytes 148
  50.3 40.4 %copy-start.1 = (f32[12,32,576]{2,1,0:T(8,128)S(1)}, f32[12,32,576]{2,1,0:T(8,128)}, u32[]{:S(2)}) copy-start(f32[12,32,576]{2,1,0:T(8,128)} %refs_11_.2) | copy-start | bytes 2654212
  50.3 40.4 %copy-start.3 = (bf16[576,576]{1,0:T(8,128)(2,1)S(1)}, bf16[576,576]{1,0:T(8,128)(2,1)}, u32[]{:S(2)}) copy-start(bf16[576,576]{1,0:T(8,128)(2,1)} %constant.65.clone.refs_13_.refs_16_) | copy-start | bytes 1990660
  50.3 40.4 %copy-start.4 = (bf16[576,576]{1,0:T(8,128)(2,1)S(1)}, bf16[576,576]{1,0:T(8,128)(2,1)}, u32[]{:S(2)}) copy-start(bf16[576,576]{1,0:T(8,128)(2,1)} %constant.64.clone.refs_12_.refs_15_) | copy-start | bytes 1990660
  50.3 40.4 %copy-start.5 = (bf16[576,576]{1,0:T(8,128)(2,1)S(1)}, bf16[576,576]{1,0:T(8,128)(2,1)}, u32[]{:S(2)}) copy-start(bf16[576,576]{1,0:T(8,128)(2,1)} %constant.63.clone.refs_11_.refs_14_) | copy-start | bytes 1990660
  50.3 40.4 %copy-start.6 = (bf16[576,576]{1,0:T(8,128)(2,1)S(1)}, bf16[576,576]{1,0:T(8,128)(2,1)}, u32[]{:S(2)}) copy-start(bf16[576,576]{1,0:T(8,128)(2,1)} %constant.62.clone.refs_10_.refs_13_) | copy-start | bytes 1990660
  56.0 34.8 %copy-start = (f32[12,32,576]{2,1,0:T(8,128)S(1)}, f32[12,32,576]{2,1,0:T(8,128)}, u32[]{:S(2)}) copy-start(f32[12,32,576]{2,1,0:T(8,128)} %refs_12_.2) | copy-start | bytes 2654212
  56.0 14.1 %collective-permute-start.8 = (f32[2,160,128]{2,1,0:T(8,128)S(1)}, f32[2,160,128]{2,1,0:T(8,128)S(1)}, u32[]{:S(2)}, u32[]{:S(2)}) collective-permute-start(f32[2,160,128]{2,1,0:T(8,128)S(1)} %get-tuple-element.58), channel_id=1, source_target_pairs={{0,1},{1,2},{2,3},{3,0},{4,5},{5,6},{6,7},{7,4},{8,9},{9,10},{10,1... | collective-permute-start | bytes 491528 | tf_op jit(solution)/shard_map/ppermute | solution.py:442
  56.2 19.6 %collective-permute-start.9 = (f32[2,160,128]{2,1,0:T(8,128)S(1)}, f32[2,160,128]{2,1,0:T(8,128)S(1)}, u32[]{:S(2)}, u32[]{:S(2)}) collective-permute-start(f32[2,160,128]{2,1,0:T(8,128)S(1)} %get-tuple-element.59), channel_id=1, source_target_pairs={{0,2},{1,3},{2,0},{3,1},{4,6},{5,7},{6,4},{7,5},{8,10},{9,11},{10,... | collective-permute-start | bytes 491528 | tf_op jit(solution)/shard_map/ppermute | solution.py:442
  62.8 13.9 %collective-permute-start.10 = (f32[2,160,128]{2,1,0:T(8,128)S(1)}, f32[2,160,128]{2,1,0:T(8,128)S(1)}, u32[]{:S(2)}, u32[]{:S(2)}) collective-permute-start(f32[2,160,128]{2,1,0:T(8,128)S(1)} %get-tuple-element.60), channel_id=1, source_target_pairs={{0,3},{1,0},{2,1},{3,2},{4,7},{5,4},{6,5},{7,6},{8,11},{9,8},{10,9... | collective-permute-start | bytes 491528 | tf_op jit(solution)/shard_map/ppermute | solution.py:442
  65.6 32.1 %collective-permute-start.12 = (f32[1,160,128]{2,1,0:T(8,128)S(1)}, f32[1,160,128]{2,1,0:T(8,128)S(1)}, u32[]{:S(2)}, u32[]{:S(2)}) collective-permute-start(f32[1,160,128]{2,1,0:T(8,128)S(1)} %get-tuple-element.66), channel_id=1, source_target_pairs={{0,1},{1,2},{2,3},{3,0},{4,5},{5,6},{6,7},{7,4},{8,9},{9,10},{10,1... | collective-permute-start | bytes 245768 | tf_op jit(solution)/shard_map/ppermute | solution.py:442
  68.0 29.6 %collective-permute-start.13 = (f32[1,160,128]{2,1,0:T(8,128)S(1)}, f32[1,160,128]{2,1,0:T(8,128)S(1)}, u32[]{:S(2)}, u32[]{:S(2)}) collective-permute-start(f32[1,160,128]{2,1,0:T(8,128)S(1)} %get-tuple-element.67), channel_id=1, source_target_pairs={{0,2},{1,3},{2,0},{3,1},{4,6},{5,7},{6,4},{7,5},{8,10},{9,11},{10,... | collective-permute-start | bytes 245768 | tf_op jit(solution)/shard_map/ppermute | solution.py:442
  70.1 27.6 %collective-permute-start.14 = (f32[1,160,128]{2,1,0:T(8,128)S(1)}, f32[1,160,128]{2,1,0:T(8,128)S(1)}, u32[]{:S(2)}, u32[]{:S(2)}) collective-permute-start(f32[1,160,128]{2,1,0:T(8,128)S(1)} %get-tuple-element.68), channel_id=1, source_target_pairs={{0,3},{1,0},{2,1},{3,2},{4,7},{5,4},{6,5},{7,6},{8,11},{9,8},{10,9... | collective-permute-start | bytes 245768 | tf_op jit(solution)/shard_map/ppermute | solution.py:442
  76.6 14.1 %copy-start.2 = (f32[12,576]{1,0:T(8,128)S(1)}, f32[12,576]{1,0:T(8,128)}, u32[]{:S(2)}) copy-start(f32[12,576]{1,0:T(8,128)} %refs_9_.3) | copy-start | bytes 82948
  76.7 21.0 %collective-permute-start.11 = (f32[1,160,128]{2,1,0:T(8,128)S(1)}, f32[1,160,128]{2,1,0:T(8,128)S(1)}, u32[]{:S(2)}, u32[]{:S(2)}) collective-permute-start(f32[1,160,128]{2,1,0:T(8,128)S(1)} %select_select_fusion), channel_id=1, source_target_pairs={{0,4},{4,8},{8,12},{12,16},{16,20},{20,24},{24,28},{28,32},{32,36}... | collective-permute-start | bytes 245768 | tf_op jit(solution)/shard_map/ppermute | solution.py:537

commit v8 on v7

--- a/solution.py
+++ b/solution.py
@@ -504,7 +504,8 @@
 
     upper_columns = exchanged(advect(first, upper_each, halo_n, "advect_upper"))
     lower_sent = advect(0, lower_each, halo_s, "advect_lower")
-    upper_columns[1], *lower_sent = lax.optimization_barrier((upper_columns[1], *lower_sent))
+    far = peers // 2
+    upper_columns[far], *lower_sent = lax.optimization_barrier((upper_columns[far], *lower_sent))
     lower_columns = exchanged(lower_sent)
 
     def remap(columns, each, name, after):

time: 103 us -> 104 us (level)
  the two profiles are of different devices: /device:TPU:1 before, /device:TPU:111 now
where the time goes in v8:
time: 104 us
  starting transfers between devices  45.2 us (43%)
  waiting for transfers between devices  28 us (27%)
  Pallas kernels  27.2 us (26%)
  between operations  1.73 us (2%)
    ppermute x12, starting transfers between devices, exchanged(): lax.ppermute(parts[step], 'lev', [(i, (i + step) % peers) for i in range(...  28.7 us
    ppermute x12, waiting for transfers between devices, exchanged(): lax.ppermute(parts[step], 'lev', [(i, (i + step) % peers) for i in range(...  23.6 us
    ppermute x1, starting transfers between devices, body(): south = lax.ppermute(last_message, 'lat', northward)  11.2 us
    pallas_call x2, Pallas kernels, remap(): pl.pallas_call(lambda *refs: remap_kernel(width, block, peers, *refs), ou...  8.33 us
    pallas_call x1, Pallas kernels, body(): pl.pallas_call(lambda *refs: upper_final_kernel(levels, first, *refs), ou...  6.87 us
    pallas_call x2, Pallas kernels, advect(): pl.pallas_call(lambda *refs: advect_kernel(start, each, peers, *refs), ou...  6.4 us
    pallas_call x1, Pallas kernels, body(): pl.pallas_call(lambda *refs: lower_final_kernel(levels, *refs), out_shape...  4.43 us
    ppermute x1, waiting for transfers between devices, body(): halo_n = lax.ppermute(to_south, 'lat', southward)  4.4 us
  transfers between devices with their start and end apart: 15, of which 5 were waited for; matrix products, arithmetic and copies ran while one was open for 1% of the time, Pallas kernels for 21%

profile of v8, /device:TPU:111, one launch (start us, length us, event | category | flops | bytes accessed | tf_op | source)
XLA Modules:
  0.0 103.6 jit_solution(10331910925640992497)
XLA Ops:
  0.6 1.1 %edges.1 = (f32[72,576]{1,0:T(8,128)S(1)}, f32[96,576]{1,0:T(8,128)S(1)}) custom-call(f32[12,32,576]{2,1,0:T(8,128)} %refs_12_.2, f32[12,32,576]{2,1,0:T(8,128)} %refs_4_.3, f32[12,32,576]{2,1,0:T(8,128)} %refs_5_.3, f32[12,576]{1,0:T(8,128)} %refs_9_.3), custom_call_target="tpu_custom_call" | custom-call | flops 1100000000 | bytes 3600000 | tf_op jit(solution)/shard_map/edges/pallas_call | solution.py:477
  1.8 3.3 %collective-permute-start.2 = (f32[72,576]{1,0:T(8,128)S(1)}, f32[72,576]{1,0:T(8,128)S(1)}, u32[]{:S(2)}, u32[]{:S(2)}) collective-permute-start(f32[72,576]{1,0:T(8,128)S(1)} %get-tuple-element.43), channel_id=1, source_target_pairs={{0,4},{4,8},{8,12},{12,16},{16,20},{20,24},{24,28},{28,32},{32,36}... | collective-permute-start | bytes 497672 | tf_op jit(solution)/shard_map/ppermute | solution.py:488
  5.1 1.9 %collective-permute-start = (f32[96,576]{1,0:T(8,128)S(1)}, f32[96,576]{1,0:T(8,128)S(1)}, u32[]{:S(2)}, u32[]{:S(2)}) collective-permute-start(f32[96,576]{1,0:T(8,128)S(1)} %get-tuple-element.41), channel_id=1, source_target_pairs={{4,0},{8,4},{12,8},{16,12},{20,16},{24,20},{28,24},{32,28},{36,32}... | collective-permute-start | bytes 663560 | tf_op jit(solution)/shard_map/ppermute | solution.py:487
  7.1 0.0 copy-start.10
  7.2 0.1 slice_bitcast_fusion.1
  7.2 0.6 copy-done.10
  7.8 0.6 broadcast_compare_fusion
  9.1 4.4 %collective-permute-done.refs_1_ = f32[96,576]{1,0:T(8,128)S(1)} collective-permute-done((f32[96,576]{1,0:T(8,128)S(1)}, f32[96,576]{1,0:T(8,128)S(1)}, u32[]{:S(2)}, u32[]{:S(2)}) %collective-permute-start) | collective-permute-done | bytes 221216 | tf_op jit(solution)/shard_map/ppermute | solution.py:487
  13.5 3.5 %advect_upper.1 = (f32[2,2,144,128]{3,2,1,0:T(8,128)S(1)}, f32[2,2,144,128]{3,2,1,0:T(8,128)S(1)}, f32[2,2,144,128]{3,2,1,0:T(8,128)S(1)}, f32[2,2,144,128]{3,2,1,0:T(8,128)S(1)}) custom-call(f32[2,12]{1,0:T(2,128)S(1)} %fusion.refs_0_, f32[96,576]{1,0:T(8,128)S(1)} %collective-permute-done.refs_1_, f32[12,32,576]{2,1,0:T(8,128)} %refs_11_.2, ...), custom_call_target="tpu_custom_call" | custom-call | flops 5500000256 | bytes 18000000 | tf_op jit(solution)/shard_map/advect_upper/pallas_call | solution.py:491
  17.0 5.2 %collective-permute-start.1 = (f32[2,2,144,128]{3,2,1,0:T(8,128)S(1)}, f32[2,2,144,128]{3,2,1,0:T(8,128)S(1)}, u32[]{:S(2)}, u32[]{:S(2)}) collective-permute-start(f32[2,2,144,128]{3,2,1,0:T(8,128)S(1)} %get-tuple-element.42), channel_id=1, source_target_pairs={{0,2},{1,3},{2,0},{3,1},{4,6},{5,7},{6,4},{7,5},{8,10},{9,11},{10,... | collective-permute-start | bytes 884744 | tf_op jit(solution)/shard_map/ppermute | solution.py:442
  22.2 0.0 collective-permute-start.6
  22.2 2.4 %collective-permute-start.7 = (f32[2,2,144,128]{3,2,1,0:T(8,128)S(1)}, f32[2,2,144,128]{3,2,1,0:T(8,128)S(1)}, u32[]{:S(2)}, u32[]{:S(2)}) collective-permute-start(f32[2,2,144,128]{3,2,1,0:T(8,128)S(1)} %get-tuple-element.55), channel_id=1, source_target_pairs={{0,3},{1,0},{2,1},{3,2},{4,7},{5,4},{6,5},{7,6},{8,11},{9,8},{10,9... | collective-permute-start | bytes 884744 | tf_op jit(solution)/shard_map/ppermute | solution.py:442
  24.6 0.0 collective-permute-done.2.refs_1_.refs_3_
  24.6 2.9 %advect_lower.1 = (f32[1,2,144,128]{3,2,1,0:T(8,128)S(1)}, f32[1,2,144,128]{3,2,1,0:T(8,128)S(1)}, f32[1,2,144,128]{3,2,1,0:T(8,128)S(1)}, f32[1,2,144,128]{3,2,1,0:T(8,128)S(1)}) custom-call(f32[2,12]{1,0:T(2,128)S(1)} %fusion.refs_0_, f32[72,576]{1,0:T(8,128)S(1)} %collective-permute-done.2.refs_1_.refs_3_, f32[12,32,576]{2,1,0:T(8,128)} %refs_11_.2, ...), custom_call_target="tpu_custom_call" | custom-call | flops 3300000000 | bytes 10800000 | tf_op jit(solution)/shard_map/advect_lower/pallas_call | solution.py:491
  27.5 6.2 %collective-permute-done.1.refs_2_ = f32[2,2,144,128]{3,2,1,0:T(8,128)S(1)} collective-permute-done((f32[2,2,144,128]{3,2,1,0:T(8,128)S(1)}, f32[2,2,144,128]{3,2,1,0:T(8,128)S(1)}, u32[]{:S(2)}, u32[]{:S(2)}) %collective-permute-start.1) | collective-permute-done | bytes 294944 | tf_op jit(solution)/shard_map/ppermute | solution.py:442
  33.7 6.6 %collective-permute-start.3 = (f32[1,2,144,128]{3,2,1,0:T(8,128)S(1)}, f32[1,2,144,128]{3,2,1,0:T(8,128)S(1)}, u32[]{:S(2)}, u32[]{:S(2)}) collective-permute-start(f32[1,2,144,128]{3,2,1,0:T(8,128)S(1)} %get-tuple-element.49), channel_id=1, source_target_pairs={{0,1},{1,2},{2,3},{3,0},{4,5},{5,6},{6,7},{7,4},{8,9},{9,10},{10,1... | collective-permute-start | bytes 442376 | tf_op jit(solution)/shard_map/ppermute | solution.py:442
  40.2 0.2 collective-permute-start.4
  40.4 1.9 %collective-permute-start.5 = (f32[1,2,144,128]{3,2,1,0:T(8,128)S(1)}, f32[1,2,144,128]{3,2,1,0:T(8,128)S(1)}, u32[]{:S(2)}, u32[]{:S(2)}) collective-permute-start(f32[1,2,144,128]{3,2,1,0:T(8,128)S(1)} %get-tuple-element.51), channel_id=1, source_target_pairs={{0,3},{1,0},{2,1},{3,2},{4,7},{5,4},{6,5},{7,6},{8,11},{9,8},{10,9... | collective-permute-start | bytes 442376 | tf_op jit(solution)/shard_map/ppermute | solution.py:442
  42.3 13.2 %collective-permute-done.6.refs_1_ = f32[2,2,144,128]{3,2,1,0:T(8,128)S(1)} collective-permute-done((f32[2,2,144,128]{3,2,1,0:T(8,128)S(1)}, f32[2,2,144,128]{3,2,1,0:T(8,128)S(1)}, u32[]{:S(2)}, u32[]{:S(2)}) %collective-permute-start.6) | collective-permute-done | bytes 294944 | tf_op jit(solution)/shard_map/ppermute | solution.py:442
  55.5 0.0 collective-permute-done.7.refs_3_
  55.5 0.0 copy-start.7
  55.5 0.0 copy-start.8
  55.5 0.0 copy-start.9
  55.5 0.0 copy-start.1
  55.5 0.0 copy-start.3
  55.6 0.0 copy-start.4
  55.6 0.0 copy-start.5
  55.6 0.0 copy-start.6
  55.6 5.6 %remap_upper.1 = (f32[2,160,128]{2,1,0:T(8,128)S(1)}, f32[2,160,128]{2,1,0:T(8,128)S(1)}, f32[2,160,128]{2,1,0:T(8,128)S(1)}, f32[2,160,128]{2,1,0:T(8,128)S(1)}) custom-call(f32[2,2,144,128]{3,2,1,0:T(8,128)S(1)} %get-tuple-element.52.refs_0_, f32[2,2,144,128]{3,2,1,0:T(8,128)S(1)} %collective-permute-done.6.refs_1_, ...), custom_call_target="tpu_custom_call" | custom-call | flops 3520000000 | bytes 11520000 | tf_op jit(solution)/shard_map/remap_upper/pallas_call | solution.py:513
  61.2 0.0 copy-start
  61.2 3.5 %collective-permute-start.8 = (f32[2,160,128]{2,1,0:T(8,128)S(1)}, f32[2,160,128]{2,1,0:T(8,128)S(1)}, u32[]{:S(2)}, u32[]{:S(2)}) collective-permute-start(f32[2,160,128]{2,1,0:T(8,128)S(1)} %get-tuple-element.58), channel_id=1, source_target_pairs={{0,1},{1,2},{2,3},{3,0},{4,5},{5,6},{6,7},{7,4},{8,9},{9,10},{10,1... | collective-permute-start | bytes 491528 | tf_op jit(solution)/shard_map/ppermute | solution.py:442
  64.7 1.5 %collective-permute-start.9 = (f32[2,160,128]{2,1,0:T(8,128)S(1)}, f32[2,160,128]{2,1,0:T(8,128)S(1)}, u32[]{:S(2)}, u32[]{:S(2)}) collective-permute-start(f32[2,160,128]{2,1,0:T(8,128)S(1)} %get-tuple-element.59), channel_id=1, source_target_pairs={{0,2},{1,3},{2,0},{3,1},{4,6},{5,7},{6,4},{7,5},{8,10},{9,11},{10,... | collective-permute-start | bytes 491528 | tf_op jit(solution)/shard_map/ppermute | solution.py:442
  66.2 0.0 collective-permute-done.3.refs_1_
  66.2 0.7 collective-permute-start.10
  66.9 0.0 copy-done.7
  66.9 0.0 copy-done.8
  66.9 0.0 copy-done.9
  66.9 0.1 add_select_fusion.refs_7_.refs_10_
  67.0 0.0 collective-permute-done.4.refs_2_
  67.0 0.0 collective-permute-done.5.refs_3_
  67.0 2.7 %remap_lower.1 = (f32[1,160,128]{2,1,0:T(8,128)S(1)}, f32[1,160,128]{2,1,0:T(8,128)S(1)}, f32[1,160,128]{2,1,0:T(8,128)S(1)}, f32[1,160,128]{2,1,0:T(8,128)S(1)}) custom-call(f32[1,2,144,128]{3,2,1,0:T(8,128)S(1)} %get-tuple-element.48.refs_4_.refs_0_, f32[1,2,144,128]{3,2,1,0:T(8,128)S(1)} %collective-permute-done.3.refs_1_, ...), custom_call_target="tpu_custom_call" | custom-call | flops 220000000 | bytes 720000 | tf_op jit(solution)/shard_map/remap_lower/pallas_call | solution.py:513
  69.7 3.0 %collective-permute-start.12 = (f32[1,160,128]{2,1,0:T(8,128)S(1)}, f32[1,160,128]{2,1,0:T(8,128)S(1)}, u32[]{:S(2)}, u32[]{:S(2)}) collective-permute-start(f32[1,160,128]{2,1,0:T(8,128)S(1)} %get-tuple-element.66), channel_id=1, source_target_pairs={{0,1},{1,2},{2,3},{3,0},{4,5},{5,6},{6,7},{7,4},{8,9},{9,10},{10,1... | collective-permute-start | bytes 245768 | tf_op jit(solution)/shard_map/ppermute | solution.py:442
  72.7 3.9 %collective-permute-start.13 = (f32[1,160,128]{2,1,0:T(8,128)S(1)}, f32[1,160,128]{2,1,0:T(8,128)S(1)}, u32[]{:S(2)}, u32[]{:S(2)}) collective-permute-start(f32[1,160,128]{2,1,0:T(8,128)S(1)} %get-tuple-element.67), channel_id=1, source_target_pairs={{0,2},{1,3},{2,0},{3,1},{4,6},{5,7},{6,4},{7,5},{8,10},{9,11},{10,... | collective-permute-start | bytes 245768 | tf_op jit(solution)/shard_map/ppermute | solution.py:442
  76.6 3.9 %collective-permute-done.8.refs_3_ = f32[2,160,128]{2,1,0:T(8,128)S(1)} collective-permute-done((f32[2,160,128]{2,1,0:T(8,128)S(1)}, f32[2,160,128]{2,1,0:T(8,128)S(1)}, u32[]{:S(2)}, u32[]{:S(2)}) %collective-permute-start.8) | collective-permute-done | bytes 163872 | tf_op jit(solution)/shard_map/ppermute | solution.py:442
  80.5 0.0 collective-permute-start.14
  80.5 0.0 collective-permute-done.9.refs_4_
  80.5 0.3 collective-permute-done.10.refs_5_
  80.8 0.0 copy-start.2
  80.8 11.2 %collective-permute-start.11 = (f32[1,160,128]{2,1,0:T(8,128)S(1)}, f32[1,160,128]{2,1,0:T(8,128)S(1)}, u32[]{:S(2)}, u32[]{:S(2)}) collective-permute-start(f32[1,160,128]{2,1,0:T(8,128)S(1)} %select_select_fusion), channel_id=1, source_target_pairs={{0,4},{4,8},{8,12},{12,16},{16,20},{20,24},{24,28},{28,32},{32,36}... | collective-permute-start | bytes 245768 | tf_op jit(solution)/shard_map/ppermute | solution.py:538
  92.1 0.0 copy-done.1
  92.1 0.0 copy-done.3
  92.1 0.0 copy-done.4
  92.1 0.0 copy-done.5
  92.1 0.0 copy-done.6
  92.1 0.0 copy-done
  92.1 0.0 copy-done.2
  92.1 6.9 %final_upper.1 = (f32[12,32,576]{2,1,0:T(8,128)}, f32[12,32,576]{2,1,0:T(8,128)}, f32[12,32,576]{2,1,0:T(8,128)}, f32[12,32,576]{2,1,0:T(8,128)}, f32[3,32,576]{2,1,0:T(8,128)S(1)}) custom-call(s32[1]{0:T(128)} %bitcast.refs_0_, f32[13]{0:T(128)S(1)} %multiply_sine_fusion.1.refs_1_, f32[2,160,128]{2,1,0:T(8,128)S(1)} %get-tuple-element.64.refs_4_.refs_2_, ...), custom_call_target="tpu_custom_call" | custom-call | flops 7699999744 | bytes 25200000 | tf_op jit(solution)/shard_map/final_upper/pallas_call | solution.py:545
  99.0 0.0 collective-permute-done.12.refs_6_
  99.0 0.0 collective-permute-done.13.refs_7_
  99.0 0.0 collective-permute-done.14.refs_8_
  99.0 0.0 collective-permute-done.11.refs_2_
  99.0 4.4 %final_lower.1 = (f32[12,32,576]{2,1,0:T(8,128)}, f32[12,32,576]{2,1,0:T(8,128)}, f32[12,32,576]{2,1,0:T(8,128)}, f32[12,32,576]{2,1,0:T(8,128)}) custom-call(s32[1]{0:T(128)} %bitcast.refs_0_, f32[13]{0:T(128)S(1)} %multiply_sine_fusion.1.refs_1_, ...), custom_call_target="tpu_custom_call", output_to_operand_aliasing={{0}: (17, {}), {1}: (18, {}), {2}: (19, {}), {3}: (20, {})} | custom-call | flops 6600000000 | bytes 21600000 | tf_op jit(solution)/shard_map/final_lower/pallas_call | solution.py:561
  (5 shorter events, 0.1 us)
Async XLA Ops:
  1.8 22.8 %collective-permute-start.2 = (f32[72,576]{1,0:T(8,128)S(1)}, f32[72,576]{1,0:T(8,128)S(1)}, u32[]{:S(2)}, u32[]{:S(2)}) collective-permute-start(f32[72,576]{1,0:T(8,128)S(1)} %get-tuple-element.43), channel_id=1, source_target_pairs={{0,4},{4,8},{8,12},{12,16},{16,20},{20,24},{24,28},{28,32},{32,36}... | collective-permute-start | bytes 497672 | tf_op jit(solution)/shard_map/ppermute | solution.py:488
  5.1 8.4 %collective-permute-start = (f32[96,576]{1,0:T(8,128)S(1)}, f32[96,576]{1,0:T(8,128)S(1)}, u32[]{:S(2)}, u32[]{:S(2)}) collective-permute-start(f32[96,576]{1,0:T(8,128)S(1)} %get-tuple-element.41), channel_id=1, source_target_pairs={{4,0},{8,4},{12,8},{16,12},{20,16},{24,20},{28,24},{32,28},{36,32}... | collective-permute-start | bytes 663560 | tf_op jit(solution)/shard_map/ppermute | solution.py:487
  7.1 0.7 copy-start.10
  17.0 16.6 %collective-permute-start.1 = (f32[2,2,144,128]{3,2,1,0:T(8,128)S(1)}, f32[2,2,144,128]{3,2,1,0:T(8,128)S(1)}, u32[]{:S(2)}, u32[]{:S(2)}) collective-permute-start(f32[2,2,144,128]{3,2,1,0:T(8,128)S(1)} %get-tuple-element.42), channel_id=1, source_target_pairs={{0,2},{1,3},{2,0},{3,1},{4,6},{5,7},{6,4},{7,5},{8,10},{9,11},{10,... | collective-permute-start | bytes 884744 | tf_op jit(solution)/shard_map/ppermute | solution.py:442
  22.2 33.3 %collective-permute-start.6 = (f32[2,2,144,128]{3,2,1,0:T(8,128)S(1)}, f32[2,2,144,128]{3,2,1,0:T(8,128)S(1)}, u32[]{:S(2)}, u32[]{:S(2)}) collective-permute-start(f32[2,2,144,128]{3,2,1,0:T(8,128)S(1)} %get-tuple-element.53), channel_id=1, source_target_pairs={{0,1},{1,2},{2,3},{3,0},{4,5},{5,6},{6,7},{7,4},{8,9},{9,10},{10,1... | collective-permute-start | bytes 884744 | tf_op jit(solution)/shard_map/ppermute | solution.py:442
  22.2 33.3 %collective-permute-start.7 = (f32[2,2,144,128]{3,2,1,0:T(8,128)S(1)}, f32[2,2,144,128]{3,2,1,0:T(8,128)S(1)}, u32[]{:S(2)}, u32[]{:S(2)}) collective-permute-start(f32[2,2,144,128]{3,2,1,0:T(8,128)S(1)} %get-tuple-element.55), channel_id=1, source_target_pairs={{0,3},{1,0},{2,1},{3,2},{4,7},{5,4},{6,5},{7,6},{8,11},{9,8},{10,9... | collective-permute-start | bytes 884744 | tf_op jit(solution)/shard_map/ppermute | solution.py:442
  33.7 32.6 %collective-permute-start.3 = (f32[1,2,144,128]{3,2,1,0:T(8,128)S(1)}, f32[1,2,144,128]{3,2,1,0:T(8,128)S(1)}, u32[]{:S(2)}, u32[]{:S(2)}) collective-permute-start(f32[1,2,144,128]{3,2,1,0:T(8,128)S(1)} %get-tuple-element.49), channel_id=1, source_target_pairs={{0,1},{1,2},{2,3},{3,0},{4,5},{5,6},{6,7},{7,4},{8,9},{9,10},{10,1... | collective-permute-start | bytes 442376 | tf_op jit(solution)/shard_map/ppermute | solution.py:442
  40.2 26.8 %collective-permute-start.4 = (f32[1,2,144,128]{3,2,1,0:T(8,128)S(1)}, f32[1,2,144,128]{3,2,1,0:T(8,128)S(1)}, u32[]{:S(2)}, u32[]{:S(2)}) collective-permute-start(f32[1,2,144,128]{3,2,1,0:T(8,128)S(1)} %get-tuple-element.50), channel_id=1, source_target_pairs={{0,2},{1,3},{2,0},{3,1},{4,6},{5,7},{6,4},{7,5},{8,10},{9,11},{10,... | collective-permute-start | bytes 442376 | tf_op jit(solution)/shard_map/ppermute | solution.py:442
  40.4 26.6 %collective-permute-start.5 = (f32[1,2,144,128]{3,2,1,0:T(8,128)S(1)}, f32[1,2,144,128]{3,2,1,0:T(8,128)S(1)}, u32[]{:S(2)}, u32[]{:S(2)}) collective-permute-start(f32[1,2,144,128]{3,2,1,0:T(8,128)S(1)} %get-tuple-element.51), channel_id=1, source_target_pairs={{0,3},{1,0},{2,1},{3,2},{4,7},{5,4},{6,5},{7,6},{8,11},{9,8},{10,9... | collective-permute-start | bytes 442376 | tf_op jit(solution)/shard_map/ppermute | solution.py:442
  55.5 11.4 %copy-start.7 = (f32[12,576]{1,0:T(8,128)S(1)}, f32[12,576]{1,0:T(8,128)}, u32[]{:S(2)}) copy-start(f32[12,576]{1,0:T(8,128)} %param.20) | copy-start | bytes 82948
  55.5 11.4 %copy-start.8 = (s32[576]{0:T(1024)S(1)}, s32[576]{0:T(1024)}, u32[]{:S(2)}) copy-start(s32[576]{0:T(1024)} %constant.61.clone) | copy-start | bytes 6916
  55.5 11.4 %copy-start.9 = (s32[12]{0:T(128)S(1)}, s32[12]{0:T(128)}, u32[]{:S(2)}) copy-start(s32[12]{0:T(128)} %param.19) | copy-start | bytes 148
  55.5 36.5 %copy-start.1 = (f32[12,32,576]{2,1,0:T(8,128)S(1)}, f32[12,32,576]{2,1,0:T(8,128)}, u32[]{:S(2)}) copy-start(f32[12,32,576]{2,1,0:T(8,128)} %refs_11_.2) | copy-start | bytes 2654212
  55.5 36.5 %copy-start.3 = (bf16[576,576]{1,0:T(8,128)(2,1)S(1)}, bf16[576,576]{1,0:T(8,128)(2,1)}, u32[]{:S(2)}) copy-start(bf16[576,576]{1,0:T(8,128)(2,1)} %constant.65.clone.refs_13_.refs_16_) | copy-start | bytes 1990660
  55.6 36.5 %copy-start.4 = (bf16[576,576]{1,0:T(8,128)(2,1)S(1)}, bf16[576,576]{1,0:T(8,128)(2,1)}, u32[]{:S(2)}) copy-start(bf16[576,576]{1,0:T(8,128)(2,1)} %constant.64.clone.refs_12_.refs_15_) | copy-start | bytes 1990660
  55.6 36.5 %copy-start.5 = (bf16[576,576]{1,0:T(8,128)(2,1)S(1)}, bf16[576,576]{1,0:T(8,128)(2,1)}, u32[]{:S(2)}) copy-start(bf16[576,576]{1,0:T(8,128)(2,1)} %constant.63.clone.refs_11_.refs_14_) | copy-start | bytes 1990660
  55.6 36.5 %copy-start.6 = (bf16[576,576]{1,0:T(8,128)(2,1)S(1)}, bf16[576,576]{1,0:T(8,128)(2,1)}, u32[]{:S(2)}) copy-start(bf16[576,576]{1,0:T(8,128)(2,1)} %constant.62.clone.refs_10_.refs_13_) | copy-start | bytes 1990660
  61.2 30.9 %copy-start = (f32[12,32,576]{2,1,0:T(8,128)S(1)}, f32[12,32,576]{2,1,0:T(8,128)}, u32[]{:S(2)}) copy-start(f32[12,32,576]{2,1,0:T(8,128)} %refs_12_.2) | copy-start | bytes 2654212
  61.2 19.3 %collective-permute-start.8 = (f32[2,160,128]{2,1,0:T(8,128)S(1)}, f32[2,160,128]{2,1,0:T(8,128)S(1)}, u32[]{:S(2)}, u32[]{:S(2)}) collective-permute-start(f32[2,160,128]{2,1,0:T(8,128)S(1)} %get-tuple-element.58), channel_id=1, source_target_pairs={{0,1},{1,2},{2,3},{3,0},{4,5},{5,6},{6,7},{7,4},{8,9},{9,10},{10,1... | collective-permute-start | bytes 491528 | tf_op jit(solution)/shard_map/ppermute | solution.py:442
  64.7 15.8 %collective-permute-start.9 = (f32[2,160,128]{2,1,0:T(8,128)S(1)}, f32[2,160,128]{2,1,0:T(8,128)S(1)}, u32[]{:S(2)}, u32[]{:S(2)}) collective-permute-start(f32[2,160,128]{2,1,0:T(8,128)S(1)} %get-tuple-element.59), channel_id=1, source_target_pairs={{0,2},{1,3},{2,0},{3,1},{4,6},{5,7},{6,4},{7,5},{8,10},{9,11},{10,... | collective-permute-start | bytes 491528 | tf_op jit(solution)/shard_map/ppermute | solution.py:442
  66.2 14.6 %collective-permute-start.10 = (f32[2,160,128]{2,1,0:T(8,128)S(1)}, f32[2,160,128]{2,1,0:T(8,128)S(1)}, u32[]{:S(2)}, u32[]{:S(2)}) collective-permute-start(f32[2,160,128]{2,1,0:T(8,128)S(1)} %get-tuple-element.60), channel_id=1, source_target_pairs={{0,3},{1,0},{2,1},{3,2},{4,7},{5,4},{6,5},{7,6},{8,11},{9,8},{10,9... | collective-permute-start | bytes 491528 | tf_op jit(solution)/shard_map/ppermute | solution.py:442
  69.7 29.3 %collective-permute-start.12 = (f32[1,160,128]{2,1,0:T(8,128)S(1)}, f32[1,160,128]{2,1,0:T(8,128)S(1)}, u32[]{:S(2)}, u32[]{:S(2)}) collective-permute-start(f32[1,160,128]{2,1,0:T(8,128)S(1)} %get-tuple-element.66), channel_id=1, source_target_pairs={{0,1},{1,2},{2,3},{3,0},{4,5},{5,6},{6,7},{7,4},{8,9},{9,10},{10,1... | collective-permute-start | bytes 245768 | tf_op jit(solution)/shard_map/ppermute | solution.py:442
  72.7 26.3 %collective-permute-start.13 = (f32[1,160,128]{2,1,0:T(8,128)S(1)}, f32[1,160,128]{2,1,0:T(8,128)S(1)}, u32[]{:S(2)}, u32[]{:S(2)}) collective-permute-start(f32[1,160,128]{2,1,0:T(8,128)S(1)} %get-tuple-element.67), channel_id=1, source_target_pairs={{0,2},{1,3},{2,0},{3,1},{4,6},{5,7},{6,4},{7,5},{8,10},{9,11},{10,... | collective-permute-start | bytes 245768 | tf_op jit(solution)/shard_map/ppermute | solution.py:442
  80.5 18.5 %collective-permute-start.14 = (f32[1,160,128]{2,1,0:T(8,128)S(1)}, f32[1,160,128]{2,1,0:T(8,128)S(1)}, u32[]{:S(2)}, u32[]{:S(2)}) collective-permute-start(f32[1,160,128]{2,1,0:T(8,128)S(1)} %get-tuple-element.68), channel_id=1, source_target_pairs={{0,3},{1,0},{2,1},{3,2},{4,7},{5,4},{6,5},{7,6},{8,11},{9,8},{10,9... | collective-permute-start | bytes 245768 | tf_op jit(solution)/shard_map/ppermute | solution.py:442
  80.8 11.3 %copy-start.2 = (f32[12,576]{1,0:T(8,128)S(1)}, f32[12,576]{1,0:T(8,128)}, u32[]{:S(2)}) copy-start(f32[12,576]{1,0:T(8,128)} %refs_9_.3) | copy-start | bytes 82948
  80.8 18.2 %collective-permute-start.11 = (f32[1,160,128]{2,1,0:T(8,128)S(1)}, f32[1,160,128]{2,1,0:T(8,128)S(1)}, u32[]{:S(2)}, u32[]{:S(2)}) collective-permute-start(f32[1,160,128]{2,1,0:T(8,128)S(1)} %select_select_fusion), channel_id=1, source_target_pairs={{0,4},{4,8},{8,12},{12,16},{16,20},{20,24},{24,28},{28,32},{32,36}... | collective-permute-start | bytes 245768 | tf_op jit(solution)/shard_map/ppermute | solution.py:538

commit v9 on v7

--- a/solution.py
+++ b/solution.py
@@ -296,17 +296,33 @@
     return (geopot - geopot_b) + 0.5 * (theta + theta_b) * (exner_mid - exner_b)
 
 
-def filtered(value, table, high, low, high_t, low_t, block):
-    def product(x, b_high, b_low):
-        x_high = x.astype(BF16)
-        x_low = (x - x_high.astype(F32)).astype(BF16)
-        dot = lambda a, b: jnp.dot(a, b, preferred_element_type=F32)
-        return dot(x_high, b_high) + (dot(x_low, b_high) + dot(x_high, b_low))
-
-    spectral = product(value, high, low)
+def filtered(value, table, basis, basis_t, split, block):
     rows, width = value.shape
+    span = tile_count(width) * LANES
+
+    def product(x, stacked):
+        high = x.astype(BF16)
+        low = (x - high.astype(F32)).astype(BF16)
+        for i, part in enumerate((high, low, high)):
+            split[pl.ds(0, rows), pl.ds(i * span, width)] = part
+        return jnp.dot(split[pl.ds(0, rows), :], stacked[...], preferred_element_type=F32)
+
+    spectral = product(value, basis)
     spectral = (spectral.reshape(rows // block, block, width) * table[:, None, :]).reshape(rows, width)
-    return value + product(spectral, high_t, low_t)
+    return value + product(spectral, basis_t)
+
+
+def clear_gaps(split, width):
+    span = tile_count(width) * LANES
+    last = width // LANES * LANES
+    for i in range(split.shape[1] // span):
+        split[:, pl.ds(i * span + last, span - last)] = jnp.zeros((split.shape[0], span - last), BF16)
+
+
+def stacked_tables(high, low):
+    rows, width = high.shape
+    gap = np.zeros((tile_count(rows) * LANES - rows, width), high.dtype)
+    return jnp.asarray(np.concatenate([high, gap, high, gap, low, gap]))
 
 
 def gather_messages(me, parts, order):
@@ -332,7 +348,7 @@
 def filter_rows(ref, count, table, tables, block):
     width = ref.shape[-1]
     value = ref[pl.ds(0, count)].reshape(count * block, width)
-    value = filtered(value, table, *(t[...] for t in tables), block)
+    value = filtered(value, table, *tables, block)
     ref[pl.ds(0, count)] = value.reshape(count, block, width)
 
 
@@ -341,9 +357,9 @@
 
 
 def upper_final_kernel(
-    levels, first, flag, faces, p0, p1, p2, p3, ground, table, zonal, merid, b0, b1, b2, b3, after,
+    levels, first, flag, faces, p0, p1, p2, p3, ground, table, zonal, merid, basis, basis_t, after,
     zonal_out, merid_out, thick_out, theta_out, edge_state,
-    order, zonal_s, merid_s, thick_s, theta_s, carried, sems,
+    order, zonal_s, merid_s, thick_s, theta_s, carried, split, sems,
 ):
     del after
     lat_rows, block, width = zonal.shape
@@ -378,14 +394,15 @@
 
     @pl.when(flag[0] != 0)
     def _():
-        tables = (b0, b1, b2, b3)
+        tables = (basis, basis_t, split)
+        clear_gaps(split, width)
         filter_rows(zonal_s, count, table[rows, :], tables, block)
 
     early += copy_all([(zonal_s, zonal_out.at[rows])], sems, 2)
 
     @pl.when(flag[0] != 0)
     def _():
-        tables = (b0, b1, b2, b3)
+        tables = (basis, basis_t, split)
         filter_rows(merid_s, count - 1, table[pl.ds(first + 1, count - 1), :], tables, block)
 
     late = copy_all([(merid_s.at[pl.ds(0, count - 1)], merid_out.at[pl.ds(first + 1, count - 1)])], sems, 3)
@@ -393,10 +410,10 @@
 
 
 def lower_final_kernel(
-    levels, flag, faces, south, halo_s, edge_state, p0, p1, p2, p3, ground, table, zonal, merid, b0, b1, b2, b3,
+    levels, flag, faces, south, halo_s, edge_state, p0, p1, p2, p3, ground, table, zonal, merid, basis, basis_t,
     zonal_in, merid_in, thick_in, theta_in,
     zonal_out, merid_out, thick_out, theta_out,
-    order, winds_s, thick_s, theta_s, sems,
+    order, winds_s, thick_s, theta_s, split, sems,
 ):
     del zonal_in, merid_in, thick_in, theta_in
     count = order.shape[0]
@@ -423,7 +440,8 @@
     @pl.when(flag[0] != 0)
     def _():
         picked = jnp.concatenate([table[rows, :], table[pl.ds(0, count + 1), :]], axis=0)
-        filter_rows(winds_s, 2 * count + 1, picked, (b0, b1, b2, b3), block)
+        clear_gaps(split, width)
+        filter_rows(winds_s, 2 * count + 1, picked, (basis, basis_t, split), block)
 
     late = copy_all(
         [
@@ -539,16 +557,17 @@
     high, low, wave = fourier_tables(width)
     active = (jnp.asarray(wave)[None, :] >= cutoff[:, None]) & (polar_mask[:, None] != 0)
     table = jnp.where(active, damping - 1.0, 0.0)
-    tables = [jnp.asarray(x) for x in (high, low, np.ascontiguousarray(high.T), np.ascontiguousarray(low.T))]
+    tables = [stacked_tables(high, low), stacked_tables(high.T, low.T)]
+    split_of = lambda rows: pltpu.VMEM((rows * block, 3 * tile_count(width) * LANES), BF16)
 
     *partial, edge_state = pl.pallas_call(
         lambda *refs: upper_final_kernel(levels, first, *refs),
         out_shape=[field] * 4 + [shape(3, block, width)],
-        in_specs=[SMEM] * 2 + [VMEM] * (peers + 8) + [pl.BlockSpec(memory_space=pl.ANY)],
+        in_specs=[SMEM] * 2 + [VMEM] * (peers + 6) + [pl.BlockSpec(memory_space=pl.ANY)],
         out_specs=[hbm] * 4 + [VMEM],
         scratch_shapes=[pltpu.VMEM((upper, message_rows, LANES), F32)]
         + [rows_of(upper)] * 4
-        + [rows_of(3), dma(4)],
+        + [rows_of(3), split_of(upper), dma(4)],
         compiler_params=params(18),
         cost_estimate=cost(7),
         name="final_upper",
@@ -560,11 +579,11 @@
         pl.pallas_call(
             lambda *refs: lower_final_kernel(levels, *refs),
             out_shape=[field] * 4,
-            in_specs=[SMEM] * 2 + [VMEM] * (peers + 11) + [hbm] * 4,
+            in_specs=[SMEM] * 2 + [VMEM] * (peers + 9) + [hbm] * 4,
             out_specs=[hbm] * 4,
             scratch_shapes=[pltpu.VMEM((first, message_rows, LANES), F32)]
-            + [rows_of(2 * first + 1), rows_of(first), rows_of(first), dma(4)],
-            input_output_aliases={peers + 13 + i: i for i in range(4)},
+            + [rows_of(2 * first + 1), rows_of(first), rows_of(first), split_of(2 * first + 1), dma(4)],
+            input_output_aliases={peers + 11 + i: i for i in range(4)},
             compiler_params=params(16),
             cost_estimate=cost(6),
             name="final_lower",

time: 103 us -> 102 us (level)
  no operation moved by 1% of the time
where the time goes in v9:
time: 102 us
  starting transfers between devices  56.4 us (55%)
  Pallas kernels  27.3 us (27%)
  waiting for transfers between devices  15.6 us (15%)
  between operations  1.71 us (2%)
    ppermute x12, starting transfers between devices, exchanged(): lax.ppermute(parts[step], 'lev', [(i, (i + step) % peers) for i in range(...  35.7 us
    ppermute x1, starting transfers between devices, body(): south = lax.ppermute(last_message, 'lat', northward)  13.9 us
    ppermute x12, waiting for transfers between devices, exchanged(): lax.ppermute(parts[step], 'lev', [(i, (i + step) % peers) for i in range(...  11.6 us
    pallas_call x2, Pallas kernels, remap(): pl.pallas_call(lambda *refs: remap_kernel(width, block, peers, *refs), ou...  8.33 us
    pallas_call x2, Pallas kernels, advect(): pl.pallas_call(lambda *refs: advect_kernel(start, each, peers, *refs), ou...  6.6 us
    pallas_call x1, Pallas kernels, body(): pl.pallas_call(lambda *refs: upper_final_kernel(levels, first, *refs), ou...  6.56 us
    ppermute x1, starting transfers between devices, body(): halo_s = lax.ppermute(to_north, 'lat', northward)  4.94 us
    pallas_call x1, Pallas kernels, body(): pl.pallas_call(lambda *refs: lower_final_kernel(levels, *refs), out_shape...  4.65 us
  transfers between devices with their start and end apart: 15, of which 6 were waited for; matrix products, arithmetic and copies ran while one was open for 1% of the time, Pallas kernels for 21%

profile of v9, /device:TPU:1, one launch (start us, length us, event | category | flops | bytes accessed | tf_op | source)
XLA Modules:
  0.0 102.0 jit_solution(17723913284334336532)
XLA Ops:
  0.6 0.0 copy-start.8
  0.6 1.1 %edges.1 = (f32[72,576]{1,0:T(8,128)S(1)}, f32[96,576]{1,0:T(8,128)S(1)}) custom-call(f32[12,32,576]{2,1,0:T(8,128)} %refs_12_.1, f32[12,32,576]{2,1,0:T(8,128)} %refs_4_.3, f32[12,32,576]{2,1,0:T(8,128)} %refs_5_.3, f32[12,576]{1,0:T(8,128)} %refs_9_.3), custom_call_target="tpu_custom_call" | custom-call | flops 1100000000 | bytes 3600000 | tf_op jit(solution)/shard_map/edges/pallas_call | solution.py:495
  1.8 4.9 %collective-permute-start.2 = (f32[72,576]{1,0:T(8,128)S(1)}, f32[72,576]{1,0:T(8,128)S(1)}, u32[]{:S(2)}, u32[]{:S(2)}) collective-permute-start(f32[72,576]{1,0:T(8,128)S(1)} %get-tuple-element.43), channel_id=1, source_target_pairs={{0,4},{4,8},{8,12},{12,16},{16,20},{20,24},{24,28},{28,32},{32,36}... | collective-permute-start | bytes 497672 | tf_op jit(solution)/shard_map/ppermute | solution.py:506
  6.7 1.9 %collective-permute-start = (f32[96,576]{1,0:T(8,128)S(1)}, f32[96,576]{1,0:T(8,128)S(1)}, u32[]{:S(2)}, u32[]{:S(2)}) collective-permute-start(f32[96,576]{1,0:T(8,128)S(1)} %get-tuple-element.41), channel_id=1, source_target_pairs={{4,0},{8,4},{12,8},{16,12},{20,16},{24,20},{28,24},{32,28},{36,32}... | collective-permute-start | bytes 663560 | tf_op jit(solution)/shard_map/ppermute | solution.py:505
  8.8 0.1 slice_bitcast_fusion.1
  8.8 0.0 copy-done.8
  8.9 0.6 broadcast_compare_fusion
  10.2 4.1 %collective-permute-done.refs_1_ = f32[96,576]{1,0:T(8,128)S(1)} collective-permute-done((f32[96,576]{1,0:T(8,128)S(1)}, f32[96,576]{1,0:T(8,128)S(1)}, u32[]{:S(2)}, u32[]{:S(2)}) %collective-permute-start) | collective-permute-done | bytes 221216 | tf_op jit(solution)/shard_map/ppermute | solution.py:505
  14.2 3.5 %advect_upper.1 = (f32[2,2,144,128]{3,2,1,0:T(8,128)S(1)}, f32[2,2,144,128]{3,2,1,0:T(8,128)S(1)}, f32[2,2,144,128]{3,2,1,0:T(8,128)S(1)}, f32[2,2,144,128]{3,2,1,0:T(8,128)S(1)}) custom-call(f32[2,12]{1,0:T(2,128)S(1)} %fusion.refs_0_, f32[96,576]{1,0:T(8,128)S(1)} %collective-permute-done.refs_1_, f32[12,32,576]{2,1,0:T(8,128)} %refs_11_.2, ...), custom_call_target="tpu_custom_call" | custom-call | flops 5500000256 | bytes 18000000 | tf_op jit(solution)/shard_map/advect_upper/pallas_call | solution.py:509
  17.8 3.1 %collective-permute-start.1 = (f32[2,2,144,128]{3,2,1,0:T(8,128)S(1)}, f32[2,2,144,128]{3,2,1,0:T(8,128)S(1)}, u32[]{:S(2)}, u32[]{:S(2)}) collective-permute-start(f32[2,2,144,128]{3,2,1,0:T(8,128)S(1)} %get-tuple-element.42), channel_id=1, source_target_pairs={{0,1},{1,2},{2,3},{3,0},{4,5},{5,6},{6,7},{7,4},{8,9},{9,10},{10,1... | collective-permute-start | bytes 884744 | tf_op jit(solution)/shard_map/ppermute | solution.py:460
  20.8 4.2 %collective-permute-start.6 = (f32[2,2,144,128]{3,2,1,0:T(8,128)S(1)}, f32[2,2,144,128]{3,2,1,0:T(8,128)S(1)}, u32[]{:S(2)}, u32[]{:S(2)}) collective-permute-start(f32[2,2,144,128]{3,2,1,0:T(8,128)S(1)} %get-tuple-element.54), channel_id=1, source_target_pairs={{0,2},{1,3},{2,0},{3,1},{4,6},{5,7},{6,4},{7,5},{8,10},{9,11},{10,... | collective-permute-start | bytes 884744 | tf_op jit(solution)/shard_map/ppermute | solution.py:460
  25.0 2.4 %collective-permute-start.7 = (f32[2,2,144,128]{3,2,1,0:T(8,128)S(1)}, f32[2,2,144,128]{3,2,1,0:T(8,128)S(1)}, u32[]{:S(2)}, u32[]{:S(2)}) collective-permute-start(f32[2,2,144,128]{3,2,1,0:T(8,128)S(1)} %get-tuple-element.55), channel_id=1, source_target_pairs={{0,3},{1,0},{2,1},{3,2},{4,7},{5,4},{6,5},{7,6},{8,11},{9,8},{10,9... | collective-permute-start | bytes 884744 | tf_op jit(solution)/shard_map/ppermute | solution.py:460
  27.4 0.0 collective-permute-done.2.refs_1_.refs_3_
  27.4 3.1 %advect_lower.1 = (f32[1,2,144,128]{3,2,1,0:T(8,128)S(1)}, f32[1,2,144,128]{3,2,1,0:T(8,128)S(1)}, f32[1,2,144,128]{3,2,1,0:T(8,128)S(1)}, f32[1,2,144,128]{3,2,1,0:T(8,128)S(1)}) custom-call(f32[2,12]{1,0:T(2,128)S(1)} %fusion.refs_0_, f32[72,576]{1,0:T(8,128)S(1)} %collective-permute-done.2.refs_1_.refs_3_, f32[12,32,576]{2,1,0:T(8,128)} %refs_11_.2, ...), custom_call_target="tpu_custom_call" | custom-call | flops 3300000000 | bytes 10800000 | tf_op jit(solution)/shard_map/advect_lower/pallas_call | solution.py:509
  30.5 3.7 %collective-permute-done.1.refs_1_ = f32[2,2,144,128]{3,2,1,0:T(8,128)S(1)} collective-permute-done((f32[2,2,144,128]{3,2,1,0:T(8,128)S(1)}, f32[2,2,144,128]{3,2,1,0:T(8,128)S(1)}, u32[]{:S(2)}, u32[]{:S(2)}) %collective-permute-start.1) | collective-permute-done | bytes 294944 | tf_op jit(solution)/shard_map/ppermute | solution.py:460
  34.2 3.0 %collective-permute-start.3 = (f32[1,2,144,128]{3,2,1,0:T(8,128)S(1)}, f32[1,2,144,128]{3,2,1,0:T(8,128)S(1)}, u32[]{:S(2)}, u32[]{:S(2)}) collective-permute-start(f32[1,2,144,128]{3,2,1,0:T(8,128)S(1)} %get-tuple-element.49), channel_id=1, source_target_pairs={{0,1},{1,2},{2,3},{3,0},{4,5},{5,6},{6,7},{7,4},{8,9},{9,10},{10,1... | collective-permute-start | bytes 442376 | tf_op jit(solution)/shard_map/ppermute | solution.py:460
  37.3 4.0 %collective-permute-start.4 = (f32[1,2,144,128]{3,2,1,0:T(8,128)S(1)}, f32[1,2,144,128]{3,2,1,0:T(8,128)S(1)}, u32[]{:S(2)}, u32[]{:S(2)}) collective-permute-start(f32[1,2,144,128]{3,2,1,0:T(8,128)S(1)} %get-tuple-element.50), channel_id=1, source_target_pairs={{0,2},{1,3},{2,0},{3,1},{4,6},{5,7},{6,4},{7,5},{8,10},{9,11},{10,... | collective-permute-start | bytes 442376 | tf_op jit(solution)/shard_map/ppermute | solution.py:460
  41.2 3.6 %collective-permute-start.5 = (f32[1,2,144,128]{3,2,1,0:T(8,128)S(1)}, f32[1,2,144,128]{3,2,1,0:T(8,128)S(1)}, u32[]{:S(2)}, u32[]{:S(2)}) collective-permute-start(f32[1,2,144,128]{3,2,1,0:T(8,128)S(1)} %get-tuple-element.51), channel_id=1, source_target_pairs={{0,3},{1,0},{2,1},{3,2},{4,7},{5,4},{6,5},{7,6},{8,11},{9,8},{10,9... | collective-permute-start | bytes 442376 | tf_op jit(solution)/shard_map/ppermute | solution.py:460
  44.8 1.3 %collective-permute-done.6.refs_2_ = f32[2,2,144,128]{3,2,1,0:T(8,128)S(1)} collective-permute-done((f32[2,2,144,128]{3,2,1,0:T(8,128)S(1)}, f32[2,2,144,128]{3,2,1,0:T(8,128)S(1)}, u32[]{:S(2)}, u32[]{:S(2)}) %collective-permute-start.6) | collective-permute-done | bytes 294944 | tf_op jit(solution)/shard_map/ppermute | solution.py:460
  46.1 4.2 %collective-permute-done.7.refs_3_ = f32[2,2,144,128]{3,2,1,0:T(8,128)S(1)} collective-permute-done((f32[2,2,144,128]{3,2,1,0:T(8,128)S(1)}, f32[2,2,144,128]{3,2,1,0:T(8,128)S(1)}, u32[]{:S(2)}, u32[]{:S(2)}) %collective-permute-start.7) | collective-permute-done | bytes 294944 | tf_op jit(solution)/shard_map/ppermute | solution.py:460
  50.3 0.0 copy-start.5
  50.3 0.0 copy-start.6
  50.3 0.0 copy-start.7
  50.3 0.0 copy-start
  50.3 0.0 copy-start.1
  50.3 0.0 copy-start.2
  50.3 0.0 copy-start.3
  50.3 0.0 copy-start.4
  50.3 5.6 %remap_upper.1 = (f32[2,160,128]{2,1,0:T(8,128)S(1)}, f32[2,160,128]{2,1,0:T(8,128)S(1)}, f32[2,160,128]{2,1,0:T(8,128)S(1)}, f32[2,160,128]{2,1,0:T(8,128)S(1)}) custom-call(f32[2,2,144,128]{3,2,1,0:T(8,128)S(1)} %get-tuple-element.52.refs_0_, f32[2,2,144,128]{3,2,1,0:T(8,128)S(1)} %collective-permute-done.1.refs_1_, ...), custom_call_target="tpu_custom_call" | custom-call | flops 3520000000 | bytes 11520000 | tf_op jit(solution)/shard_map/remap_upper/pallas_call | solution.py:530
  56.0 0.3 collective-permute-start.8
  56.2 6.5 %collective-permute-start.9 = (f32[2,160,128]{2,1,0:T(8,128)S(1)}, f32[2,160,128]{2,1,0:T(8,128)S(1)}, u32[]{:S(2)}, u32[]{:S(2)}) collective-permute-start(f32[2,160,128]{2,1,0:T(8,128)S(1)} %get-tuple-element.59), channel_id=1, source_target_pairs={{0,2},{1,3},{2,0},{3,1},{4,6},{5,7},{6,4},{7,5},{8,10},{9,11},{10,... | collective-permute-start | bytes 491528 | tf_op jit(solution)/shard_map/ppermute | solution.py:460
  62.8 0.0 collective-permute-done.3.refs_1_
  62.8 0.0 collective-permute-start.10
  62.8 0.0 copy-done.5
  62.8 0.0 copy-done.6
  62.8 0.0 copy-done.7
  62.8 0.1 add_select_fusion.refs_7_.refs_10_
  62.9 0.0 collective-permute-done.4.refs_2_
  62.9 0.0 collective-permute-done.5.refs_3_
  62.9 2.7 %remap_lower.1 = (f32[1,160,128]{2,1,0:T(8,128)S(1)}, f32[1,160,128]{2,1,0:T(8,128)S(1)}, f32[1,160,128]{2,1,0:T(8,128)S(1)}, f32[1,160,128]{2,1,0:T(8,128)S(1)}) custom-call(f32[1,2,144,128]{3,2,1,0:T(8,128)S(1)} %get-tuple-element.48.refs_4_.refs_0_, f32[1,2,144,128]{3,2,1,0:T(8,128)S(1)} %collective-permute-done.3.refs_1_, ...), custom_call_target="tpu_custom_call" | custom-call | flops 220000000 | bytes 720000 | tf_op jit(solution)/shard_map/remap_lower/pallas_call | solution.py:530
  65.6 2.4 %collective-permute-start.12 = (f32[1,160,128]{2,1,0:T(8,128)S(1)}, f32[1,160,128]{2,1,0:T(8,128)S(1)}, u32[]{:S(2)}, u32[]{:S(2)}) collective-permute-start(f32[1,160,128]{2,1,0:T(8,128)S(1)} %get-tuple-element.66), channel_id=1, source_target_pairs={{0,1},{1,2},{2,3},{3,0},{4,5},{5,6},{6,7},{7,4},{8,9},{9,10},{10,1... | collective-permute-start | bytes 245768 | tf_op jit(solution)/shard_map/ppermute | solution.py:460
  68.0 2.0 %collective-permute-start.13 = (f32[1,160,128]{2,1,0:T(8,128)S(1)}, f32[1,160,128]{2,1,0:T(8,128)S(1)}, u32[]{:S(2)}, u32[]{:S(2)}) collective-permute-start(f32[1,160,128]{2,1,0:T(8,128)S(1)} %get-tuple-element.67), channel_id=1, source_target_pairs={{0,2},{1,3},{2,0},{3,1},{4,6},{5,7},{6,4},{7,5},{8,10},{9,11},{10,... | collective-permute-start | bytes 245768 | tf_op jit(solution)/shard_map/ppermute | solution.py:460
  70.1 0.0 collective-permute-done.8.refs_3_
  70.1 4.2 %collective-permute-start.14 = (f32[1,160,128]{2,1,0:T(8,128)S(1)}, f32[1,160,128]{2,1,0:T(8,128)S(1)}, u32[]{:S(2)}, u32[]{:S(2)}) collective-permute-start(f32[1,160,128]{2,1,0:T(8,128)S(1)} %get-tuple-element.68), channel_id=1, source_target_pairs={{0,3},{1,0},{2,1},{3,2},{4,7},{5,4},{6,5},{7,6},{8,11},{9,8},{10,9... | collective-permute-start | bytes 245768 | tf_op jit(solution)/shard_map/ppermute | solution.py:460
  74.3 1.5 %collective-permute-done.9.refs_4_ = f32[2,160,128]{2,1,0:T(8,128)S(1)} collective-permute-done((f32[2,160,128]{2,1,0:T(8,128)S(1)}, f32[2,160,128]{2,1,0:T(8,128)S(1)}, u32[]{:S(2)}, u32[]{:S(2)}) %collective-permute-start.9) | collective-permute-done | bytes 163872 | tf_op jit(solution)/shard_map/ppermute | solution.py:460
  75.8 0.8 collective-permute-done.10.refs_5_
  76.7 13.9 %collective-permute-start.11 = (f32[1,160,128]{2,1,0:T(8,128)S(1)}, f32[1,160,128]{2,1,0:T(8,128)S(1)}, u32[]{:S(2)}, u32[]{:S(2)}) collective-permute-start(f32[1,160,128]{2,1,0:T(8,128)S(1)} %select_select_fusion), channel_id=1, source_target_pairs={{0,4},{4,8},{8,12},{12,16},{16,20},{20,24},{24,28},{28,32},{32,36}... | collective-permute-start | bytes 245768 | tf_op jit(solution)/shard_map/ppermute | solution.py:555
  90.6 0.0 copy-done
  90.6 0.0 copy-done.1
  90.6 0.0 copy-done.2
  90.6 0.0 copy-done.3
  90.6 0.0 copy-done.4
  90.6 6.6 %final_upper.1 = (f32[12,32,576]{2,1,0:T(8,128)}, f32[12,32,576]{2,1,0:T(8,128)}, f32[12,32,576]{2,1,0:T(8,128)}, f32[12,32,576]{2,1,0:T(8,128)}, f32[3,32,576]{2,1,0:T(8,128)S(1)}) custom-call(s32[1]{0:T(128)} %bitcast.refs_0_, f32[13]{0:T(128)S(1)} %multiply_sine_fusion.1.refs_1_, f32[2,160,128]{2,1,0:T(8,128)S(1)} %get-tuple-element.64.refs_4_.refs_2_, ...), custom_call_target="tpu_custom_call" | custom-call | flops 7699999744 | bytes 25200000 | tf_op jit(solution)/shard_map/final_upper/pallas_call | solution.py:563
  97.2 0.0 collective-permute-done.12.refs_6_
  97.2 0.0 collective-permute-done.13.refs_7_
  97.2 0.0 collective-permute-done.14.refs_8_
  97.2 0.0 collective-permute-done.11.refs_2_
  97.2 4.6 %final_lower.1 = (f32[12,32,576]{2,1,0:T(8,128)}, f32[12,32,576]{2,1,0:T(8,128)}, f32[12,32,576]{2,1,0:T(8,128)}, f32[12,32,576]{2,1,0:T(8,128)}) custom-call(s32[1]{0:T(128)} %bitcast.refs_0_, f32[13]{0:T(128)S(1)} %multiply_sine_fusion.1.refs_1_, ...), custom_call_target="tpu_custom_call", output_to_operand_aliasing={{0}: (15, {}), {1}: (16, {}), {2}: (17, {}), {3}: (18, {})} | custom-call | flops 6600000000 | bytes 21600000 | tf_op jit(solution)/shard_map/final_lower/pallas_call | solution.py:579
  (5 shorter events, 0.1 us)
Async XLA Ops:
  0.6 8.2 %copy-start.8 = (s32[12]{0:T(128)S(1)}, s32[12]{0:T(128)}, u32[]{:S(2)}) copy-start(s32[12]{0:T(128)} %param.16) | copy-start | bytes 148
  1.8 25.6 %collective-permute-start.2 = (f32[72,576]{1,0:T(8,128)S(1)}, f32[72,576]{1,0:T(8,128)S(1)}, u32[]{:S(2)}, u32[]{:S(2)}) collective-permute-start(f32[72,576]{1,0:T(8,128)S(1)} %get-tuple-element.43), channel_id=1, source_target_pairs={{0,4},{4,8},{8,12},{12,16},{16,20},{20,24},{24,28},{28,32},{32,36}... | collective-permute-start | bytes 497672 | tf_op jit(solution)/shard_map/ppermute | solution.py:506
  6.7 7.5 %collective-permute-start = (f32[96,576]{1,0:T(8,128)S(1)}, f32[96,576]{1,0:T(8,128)S(1)}, u32[]{:S(2)}, u32[]{:S(2)}) collective-permute-start(f32[96,576]{1,0:T(8,128)S(1)} %get-tuple-element.41), channel_id=1, source_target_pairs={{4,0},{8,4},{12,8},{16,12},{20,16},{24,20},{28,24},{32,28},{36,32}... | collective-permute-start | bytes 663560 | tf_op jit(solution)/shard_map/ppermute | solution.py:505
  17.8 16.5 %collective-permute-start.1 = (f32[2,2,144,128]{3,2,1,0:T(8,128)S(1)}, f32[2,2,144,128]{3,2,1,0:T(8,128)S(1)}, u32[]{:S(2)}, u32[]{:S(2)}) collective-permute-start(f32[2,2,144,128]{3,2,1,0:T(8,128)S(1)} %get-tuple-element.42), channel_id=1, source_target_pairs={{0,1},{1,2},{2,3},{3,0},{4,5},{5,6},{6,7},{7,4},{8,9},{9,10},{10,1... | collective-permute-start | bytes 884744 | tf_op jit(solution)/shard_map/ppermute | solution.py:460
  20.8 25.3 %collective-permute-start.6 = (f32[2,2,144,128]{3,2,1,0:T(8,128)S(1)}, f32[2,2,144,128]{3,2,1,0:T(8,128)S(1)}, u32[]{:S(2)}, u32[]{:S(2)}) collective-permute-start(f32[2,2,144,128]{3,2,1,0:T(8,128)S(1)} %get-tuple-element.54), channel_id=1, source_target_pairs={{0,2},{1,3},{2,0},{3,1},{4,6},{5,7},{6,4},{7,5},{8,10},{9,11},{10,... | collective-permute-start | bytes 884744 | tf_op jit(solution)/shard_map/ppermute | solution.py:460
  25.0 25.3 %collective-permute-start.7 = (f32[2,2,144,128]{3,2,1,0:T(8,128)S(1)}, f32[2,2,144,128]{3,2,1,0:T(8,128)S(1)}, u32[]{:S(2)}, u32[]{:S(2)}) collective-permute-start(f32[2,2,144,128]{3,2,1,0:T(8,128)S(1)} %get-tuple-element.55), channel_id=1, source_target_pairs={{0,3},{1,0},{2,1},{3,2},{4,7},{5,4},{6,5},{7,6},{8,11},{9,8},{10,9... | collective-permute-start | bytes 884744 | tf_op jit(solution)/shard_map/ppermute | solution.py:460
  34.2 28.5 %collective-permute-start.3 = (f32[1,2,144,128]{3,2,1,0:T(8,128)S(1)}, f32[1,2,144,128]{3,2,1,0:T(8,128)S(1)}, u32[]{:S(2)}, u32[]{:S(2)}) collective-permute-start(f32[1,2,144,128]{3,2,1,0:T(8,128)S(1)} %get-tuple-element.49), channel_id=1, source_target_pairs={{0,1},{1,2},{2,3},{3,0},{4,5},{5,6},{6,7},{7,4},{8,9},{9,10},{10,1... | collective-permute-start | bytes 442376 | tf_op jit(solution)/shard_map/ppermute | solution.py:460
  37.3 25.6 %collective-permute-start.4 = (f32[1,2,144,128]{3,2,1,0:T(8,128)S(1)}, f32[1,2,144,128]{3,2,1,0:T(8,128)S(1)}, u32[]{:S(2)}, u32[]{:S(2)}) collective-permute-start(f32[1,2,144,128]{3,2,1,0:T(8,128)S(1)} %get-tuple-element.50), channel_id=1, source_target_pairs={{0,2},{1,3},{2,0},{3,1},{4,6},{5,7},{6,4},{7,5},{8,10},{9,11},{10,... | collective-permute-start | bytes 442376 | tf_op jit(solution)/shard_map/ppermute | solution.py:460
  41.2 21.7 %collective-permute-start.5 = (f32[1,2,144,128]{3,2,1,0:T(8,128)S(1)}, f32[1,2,144,128]{3,2,1,0:T(8,128)S(1)}, u32[]{:S(2)}, u32[]{:S(2)}) collective-permute-start(f32[1,2,144,128]{3,2,1,0:T(8,128)S(1)} %get-tuple-element.51), channel_id=1, source_target_pairs={{0,3},{1,0},{2,1},{3,2},{4,7},{5,4},{6,5},{7,6},{8,11},{9,8},{10,9... | collective-permute-start | bytes 442376 | tf_op jit(solution)/shard_map/ppermute | solution.py:460
  50.3 12.5 %copy-start.5 = (f32[12,576]{1,0:T(8,128)S(1)}, f32[12,576]{1,0:T(8,128)}, u32[]{:S(2)}) copy-start(f32[12,576]{1,0:T(8,128)} %param.18) | copy-start | bytes 82948
  50.3 12.5 %copy-start.6 = (s32[576]{0:T(1024)S(1)}, s32[576]{0:T(1024)}, u32[]{:S(2)}) copy-start(s32[576]{0:T(1024)} %constant.57.clone) | copy-start | bytes 6916
  50.3 12.5 %copy-start.7 = (s32[12]{0:T(128)S(1)}, s32[12]{0:T(128)}, u32[]{:S(2)}) copy-start(s32[12]{0:T(128)} %param.17) | copy-start | bytes 148
  50.3 40.3 %copy-start = (f32[12,32,576]{2,1,0:T(8,128)S(1)}, f32[12,32,576]{2,1,0:T(8,128)}, u32[]{:S(2)}) copy-start(f32[12,32,576]{2,1,0:T(8,128)} %refs_12_.1) | copy-start | bytes 2654212
  50.3 40.3 %copy-start.1 = (f32[12,32,576]{2,1,0:T(8,128)S(1)}, f32[12,32,576]{2,1,0:T(8,128)}, u32[]{:S(2)}) copy-start(f32[12,32,576]{2,1,0:T(8,128)} %refs_11_.2) | copy-start | bytes 2654212
  50.3 40.3 %copy-start.2 = (f32[12,576]{1,0:T(8,128)S(1)}, f32[12,576]{1,0:T(8,128)}, u32[]{:S(2)}) copy-start(f32[12,576]{1,0:T(8,128)} %refs_9_.3) | copy-start | bytes 82948
  50.3 40.3 %copy-start.3 = (bf16[1920,576]{1,0:T(8,128)(2,1)S(1)}, bf16[1920,576]{1,0:T(8,128)(2,1)}, u32[]{:S(2)}) copy-start(bf16[1920,576]{1,0:T(8,128)(2,1)} %constant.59.clone.refs_11_.refs_14_) | copy-start | bytes 6635524
  50.3 40.3 %copy-start.4 = (bf16[1920,576]{1,0:T(8,128)(2,1)S(1)}, bf16[1920,576]{1,0:T(8,128)(2,1)}, u32[]{:S(2)}) copy-start(bf16[1920,576]{1,0:T(8,128)(2,1)} %constant.58.clone.refs_10_.refs_13_) | copy-start | bytes 6635524
  56.0 14.1 %collective-permute-start.8 = (f32[2,160,128]{2,1,0:T(8,128)S(1)}, f32[2,160,128]{2,1,0:T(8,128)S(1)}, u32[]{:S(2)}, u32[]{:S(2)}) collective-permute-start(f32[2,160,128]{2,1,0:T(8,128)S(1)} %get-tuple-element.58), channel_id=1, source_target_pairs={{0,1},{1,2},{2,3},{3,0},{4,5},{5,6},{6,7},{7,4},{8,9},{9,10},{10,1... | collective-permute-start | bytes 491528 | tf_op jit(solution)/shard_map/ppermute | solution.py:460
  56.2 19.6 %collective-permute-start.9 = (f32[2,160,128]{2,1,0:T(8,128)S(1)}, f32[2,160,128]{2,1,0:T(8,128)S(1)}, u32[]{:S(2)}, u32[]{:S(2)}) collective-permute-start(f32[2,160,128]{2,1,0:T(8,128)S(1)} %get-tuple-element.59), channel_id=1, source_target_pairs={{0,2},{1,3},{2,0},{3,1},{4,6},{5,7},{6,4},{7,5},{8,10},{9,11},{10,... | collective-permute-start | bytes 491528 | tf_op jit(solution)/shard_map/ppermute | solution.py:460
  62.8 13.9 %collective-permute-start.10 = (f32[2,160,128]{2,1,0:T(8,128)S(1)}, f32[2,160,128]{2,1,0:T(8,128)S(1)}, u32[]{:S(2)}, u32[]{:S(2)}) collective-permute-start(f32[2,160,128]{2,1,0:T(8,128)S(1)} %get-tuple-element.60), channel_id=1, source_target_pairs={{0,3},{1,0},{2,1},{3,2},{4,7},{5,4},{6,5},{7,6},{8,11},{9,8},{10,9... | collective-permute-start | bytes 491528 | tf_op jit(solution)/shard_map/ppermute | solution.py:460
  65.6 31.6 %collective-permute-start.12 = (f32[1,160,128]{2,1,0:T(8,128)S(1)}, f32[1,160,128]{2,1,0:T(8,128)S(1)}, u32[]{:S(2)}, u32[]{:S(2)}) collective-permute-start(f32[1,160,128]{2,1,0:T(8,128)S(1)} %get-tuple-element.66), channel_id=1, source_target_pairs={{0,1},{1,2},{2,3},{3,0},{4,5},{5,6},{6,7},{7,4},{8,9},{9,10},{10,1... | collective-permute-start | bytes 245768 | tf_op jit(solution)/shard_map/ppermute | solution.py:460
  68.0 29.1 %collective-permute-start.13 = (f32[1,160,128]{2,1,0:T(8,128)S(1)}, f32[1,160,128]{2,1,0:T(8,128)S(1)}, u32[]{:S(2)}, u32[]{:S(2)}) collective-permute-start(f32[1,160,128]{2,1,0:T(8,128)S(1)} %get-tuple-element.67), channel_id=1, source_target_pairs={{0,2},{1,3},{2,0},{3,1},{4,6},{5,7},{6,4},{7,5},{8,10},{9,11},{10,... | collective-permute-start | bytes 245768 | tf_op jit(solution)/shard_map/ppermute | solution.py:460
  70.1 27.1 %collective-permute-start.14 = (f32[1,160,128]{2,1,0:T(8,128)S(1)}, f32[1,160,128]{2,1,0:T(8,128)S(1)}, u32[]{:S(2)}, u32[]{:S(2)}) collective-permute-start(f32[1,160,128]{2,1,0:T(8,128)S(1)} %get-tuple-element.68), channel_id=1, source_target_pairs={{0,3},{1,0},{2,1},{3,2},{4,7},{5,4},{6,5},{7,6},{8,11},{9,8},{10,9... | collective-permute-start | bytes 245768 | tf_op jit(solution)/shard_map/ppermute | solution.py:460
  76.7 20.5 %collective-permute-start.11 = (f32[1,160,128]{2,1,0:T(8,128)S(1)}, f32[1,160,128]{2,1,0:T(8,128)S(1)}, u32[]{:S(2)}, u32[]{:S(2)}) collective-permute-start(f32[1,160,128]{2,1,0:T(8,128)S(1)} %select_select_fusion), channel_id=1, source_target_pairs={{0,4},{4,8},{8,12},{12,16},{16,20},{20,24},{24,28},{28,32},{32,36}... | collective-permute-start | bytes 245768 | tf_op jit(solution)/shard_map/ppermute | solution.py:555

commit v10 on v9

--- a/solution.py
+++ b/solution.py
@@ -476,7 +476,6 @@
     coef = jnp.stack([faces[:-1], faces[1:]]) * (0.5 * COURANT) / centres
     northward = [(i, i + 1) for i in range(lat_count - 1)]
     southward = [(i + 1, i) for i in range(lat_count - 1)]
-    flag = jnp.any(polar_mask != 0).astype(jnp.int32).reshape(1)
     shape = lambda *dims: jax.ShapeDtypeStruct(dims, F32)
     hbm = pl.BlockSpec(memory_space=pltpu.HBM)
     rows_of = lambda n: pltpu.VMEM((n, block, width), F32)
@@ -503,7 +502,6 @@
         name="edges",
     )(*fields[1:], *stay(surface_geo))
     halo_n = lax.ppermute(to_south, "lat", southward)
-    halo_s = lax.ppermute(to_north, "lat", northward)
 
     def advect(start, each, halo, name):
         return pl.pallas_call(
@@ -520,9 +518,13 @@
             name=name,
         )(coef, halo, *fields)
 
-    upper_columns = exchanged(advect(first, upper_each, halo_n, "advect_upper"))
+    upper_sent = advect(first, upper_each, halo_n, "advect_upper")
+    to_north, *upper_sent = lax.optimization_barrier((to_north, *upper_sent))
+    upper_columns = exchanged(upper_sent)
+    halo_s = lax.ppermute(to_north, "lat", northward)
     lower_sent = advect(0, lower_each, halo_s, "advect_lower")
-    upper_columns[1], *lower_sent = lax.optimization_barrier((upper_columns[1], *lower_sent))
+    upper_columns[1], polar_mask, *lower_sent = lax.optimization_barrier((upper_columns[1], polar_mask, *lower_sent))
+    flag = jnp.any(polar_mask != 0).astype(jnp.int32).reshape(1)
     lower_columns = exchanged(lower_sent)
 
     def remap(columns, each, name, after):

time: 102 us -> 101 us (level)
  the two profiles are of different devices: /device:TPU:1 before, /device:TPU:25 now
where the time goes in v10:
time: 101 us
  starting transfers between devices  48.9 us (48%)
  Pallas kernels  27.3 us (27%)
  waiting for transfers between devices  22.3 us (22%)
  between operations  1.74 us (2%)
    ppermute x12, starting transfers between devices, exchanged(): lax.ppermute(parts[step], 'lev', [(i, (i + step) % peers) for i in range(...  32.4 us
    ppermute x12, waiting for transfers between devices, exchanged(): lax.ppermute(parts[step], 'lev', [(i, (i + step) % peers) for i in range(...  17.1 us
    ppermute x1, starting transfers between devices, body(): south = lax.ppermute(last_message, 'lat', northward)  12 us
    pallas_call x2, Pallas kernels, remap(): pl.pallas_call(lambda *refs: remap_kernel(width, block, peers, *refs), ou...  8.33 us
    pallas_call x2, Pallas kernels, advect(): pl.pallas_call(lambda *refs: advect_kernel(start, each, peers, *refs), ou...  6.59 us
    pallas_call x1, Pallas kernels, body(): pl.pallas_call(lambda *refs: upper_final_kernel(levels, first, *refs), ou...  6.56 us
    ppermute x1, waiting for transfers between devices, body(): halo_n = lax.ppermute(to_south, 'lat', southward)  5.19 us
    pallas_call x1, Pallas kernels, body(): pl.pallas_call(lambda *refs: lower_final_kernel(levels, *refs), out_shape...  4.65 us
  transfers between devices with their start and end apart: 15, of which 3 were waited for; matrix products, arithmetic and copies ran while one was open for 1% of the time, Pallas kernels for 18%

profile of v10, /device:TPU:25, one launch (start us, length us, event | category | flops | bytes accessed | tf_op | source)
XLA Modules:
  0.0 101.2 jit_solution(8888847287719684581)
XLA Ops:
  0.6 1.1 %edges.1 = (f32[72,576]{1,0:T(8,128)S(1)}, f32[96,576]{1,0:T(8,128)S(1)}) custom-call(f32[12,32,576]{2,1,0:T(8,128)} %refs_12_.1, f32[12,32,576]{2,1,0:T(8,128)} %refs_4_.3, f32[12,32,576]{2,1,0:T(8,128)} %refs_5_.3, f32[12,576]{1,0:T(8,128)} %refs_9_.3), custom_call_target="tpu_custom_call" | custom-call | flops 1100000000 | bytes 3600000 | tf_op jit(solution)/shard_map/edges/pallas_call | solution.py:494
  1.8 2.6 %collective-permute-start = (f32[96,576]{1,0:T(8,128)S(1)}, f32[96,576]{1,0:T(8,128)S(1)}, u32[]{:S(2)}, u32[]{:S(2)}) collective-permute-start(f32[96,576]{1,0:T(8,128)S(1)} %get-tuple-element.48), channel_id=1, source_target_pairs={{4,0},{8,4},{12,8},{16,12},{20,16},{24,20},{28,24},{32,28},{36,32}... | collective-permute-start | bytes 663560 | tf_op jit(solution)/shard_map/ppermute | solution.py:504
  4.5 0.1 slice_bitcast_fusion.1
  4.6 5.2 %collective-permute-done.refs_1_ = f32[96,576]{1,0:T(8,128)S(1)} collective-permute-done((f32[96,576]{1,0:T(8,128)S(1)}, f32[96,576]{1,0:T(8,128)S(1)}, u32[]{:S(2)}, u32[]{:S(2)}) %collective-permute-start) | collective-permute-done | bytes 221216 | tf_op jit(solution)/shard_map/ppermute | solution.py:504
  9.7 3.5 %advect_upper.1 = (f32[2,2,144,128]{3,2,1,0:T(8,128)S(1)}, f32[2,2,144,128]{3,2,1,0:T(8,128)S(1)}, f32[2,2,144,128]{3,2,1,0:T(8,128)S(1)}, f32[2,2,144,128]{3,2,1,0:T(8,128)S(1)}) custom-call(f32[2,12]{1,0:T(2,128)S(1)} %fusion.refs_0_, f32[96,576]{1,0:T(8,128)S(1)} %collective-permute-done.refs_1_, f32[12,32,576]{2,1,0:T(8,128)} %refs_11_.2, ...), custom_call_target="tpu_custom_call" | custom-call | flops 5500000256 | bytes 18000000 | tf_op jit(solution)/shard_map/advect_upper/pallas_call | solution.py:507
  13.3 1.9 %collective-permute-start.2 = (f32[72,576]{1,0:T(8,128)S(1)}, f32[72,576]{1,0:T(8,128)S(1)}, u32[]{:S(2)}, u32[]{:S(2)}) collective-permute-start(f32[72,576]{1,0:T(8,128)S(1)} %get-tuple-element.54), channel_id=1, source_target_pairs={{0,4},{4,8},{8,12},{12,16},{16,20},{20,24},{24,28},{28,32},{32,36}... | collective-permute-start | bytes 497672 | tf_op jit(solution)/shard_map/ppermute | solution.py:524
  15.2 0.0 copy-start.8
  15.2 3.1 %collective-permute-start.1 = (f32[2,2,144,128]{3,2,1,0:T(8,128)S(1)}, f32[2,2,144,128]{3,2,1,0:T(8,128)S(1)}, u32[]{:S(2)}, u32[]{:S(2)}) collective-permute-start(f32[2,2,144,128]{3,2,1,0:T(8,128)S(1)} %get-tuple-element.53), channel_id=1, source_target_pairs={{0,1},{1,2},{2,3},{3,0},{4,5},{5,6},{6,7},{7,4},{8,9},{9,10},{10,1... | collective-permute-start | bytes 884744 | tf_op jit(solution)/shard_map/ppermute | solution.py:460
  18.3 4.6 %collective-permute-start.6 = (f32[2,2,144,128]{3,2,1,0:T(8,128)S(1)}, f32[2,2,144,128]{3,2,1,0:T(8,128)S(1)}, u32[]{:S(2)}, u32[]{:S(2)}) collective-permute-start(f32[2,2,144,128]{3,2,1,0:T(8,128)S(1)} %get-tuple-element.66), channel_id=1, source_target_pairs={{0,2},{1,3},{2,0},{3,1},{4,6},{5,7},{6,4},{7,5},{8,10},{9,11},{10,... | collective-permute-start | bytes 884744 | tf_op jit(solution)/shard_map/ppermute | solution.py:460
  22.9 2.4 %collective-permute-start.7 = (f32[2,2,144,128]{3,2,1,0:T(8,128)S(1)}, f32[2,2,144,128]{3,2,1,0:T(8,128)S(1)}, u32[]{:S(2)}, u32[]{:S(2)}) collective-permute-start(f32[2,2,144,128]{3,2,1,0:T(8,128)S(1)} %get-tuple-element.67), channel_id=1, source_target_pairs={{0,3},{1,0},{2,1},{3,2},{4,7},{5,4},{6,5},{7,6},{8,11},{9,8},{10,9... | collective-permute-start | bytes 884744 | tf_op jit(solution)/shard_map/ppermute | solution.py:460
  25.3 0.0 collective-permute-done.2.refs_1_.refs_3_
  25.3 3.1 %advect_lower.1 = (f32[1,2,144,128]{3,2,1,0:T(8,128)S(1)}, f32[1,2,144,128]{3,2,1,0:T(8,128)S(1)}, f32[1,2,144,128]{3,2,1,0:T(8,128)S(1)}, f32[1,2,144,128]{3,2,1,0:T(8,128)S(1)}) custom-call(f32[2,12]{1,0:T(2,128)S(1)} %fusion.refs_0_, f32[72,576]{1,0:T(8,128)S(1)} %collective-permute-done.2.refs_1_.refs_3_, f32[12,32,576]{2,1,0:T(8,128)} %refs_11_.2, ...), custom_call_target="tpu_custom_call" | custom-call | flops 3300000000 | bytes 10800000 | tf_op jit(solution)/shard_map/advect_lower/pallas_call | solution.py:507
  28.4 10.0 %collective-permute-done.1.refs_1_ = f32[2,2,144,128]{3,2,1,0:T(8,128)S(1)} collective-permute-done((f32[2,2,144,128]{3,2,1,0:T(8,128)S(1)}, f32[2,2,144,128]{3,2,1,0:T(8,128)S(1)}, u32[]{:S(2)}, u32[]{:S(2)}) %collective-permute-start.1) | collective-permute-done | bytes 294944 | tf_op jit(solution)/shard_map/ppermute | solution.py:460
  38.4 0.0 copy-done.8
  38.4 0.6 broadcast_compare_fusion
  39.7 0.0 copy-start.5
  39.7 0.0 copy-start.6
  39.8 0.0 copy-start.7
  39.8 0.0 copy-start
  39.8 0.0 copy-start.1
  39.8 0.0 copy-start.2
  39.8 0.0 copy-start.3
  39.8 0.0 copy-start.4
  39.8 0.1 collective-permute-start.3
  39.9 0.1 collective-permute-start.4
  40.0 3.5 %collective-permute-start.5 = (f32[1,2,144,128]{3,2,1,0:T(8,128)S(1)}, f32[1,2,144,128]{3,2,1,0:T(8,128)S(1)}, u32[]{:S(2)}, u32[]{:S(2)}) collective-permute-start(f32[1,2,144,128]{3,2,1,0:T(8,128)S(1)} %get-tuple-element.63), channel_id=1, source_target_pairs={{0,3},{1,0},{2,1},{3,2},{4,7},{5,4},{6,5},{7,6},{8,11},{9,8},{10,9... | collective-permute-start | bytes 442376 | tf_op jit(solution)/shard_map/ppermute | solution.py:460
  43.5 0.0 collective-permute-done.6.refs_2_
  43.5 0.0 collective-permute-done.7.refs_3_
  43.5 5.6 %remap_upper.1 = (f32[2,160,128]{2,1,0:T(8,128)S(1)}, f32[2,160,128]{2,1,0:T(8,128)S(1)}, f32[2,160,128]{2,1,0:T(8,128)S(1)}, f32[2,160,128]{2,1,0:T(8,128)S(1)}) custom-call(f32[2,2,144,128]{3,2,1,0:T(8,128)S(1)} %get-tuple-element.64.refs_0_, f32[2,2,144,128]{3,2,1,0:T(8,128)S(1)} %collective-permute-done.1.refs_1_, ...), custom_call_target="tpu_custom_call" | custom-call | flops 3520000000 | bytes 11520000 | tf_op jit(solution)/shard_map/remap_upper/pallas_call | solution.py:532
  49.1 9.1 %collective-permute-start.8 = (f32[2,160,128]{2,1,0:T(8,128)S(1)}, f32[2,160,128]{2,1,0:T(8,128)S(1)}, u32[]{:S(2)}, u32[]{:S(2)}) collective-permute-start(f32[2,160,128]{2,1,0:T(8,128)S(1)} %get-tuple-element.70), channel_id=1, source_target_pairs={{0,1},{1,2},{2,3},{3,0},{4,5},{5,6},{6,7},{7,4},{8,9},{9,10},{10,1... | collective-permute-start | bytes 491528 | tf_op jit(solution)/shard_map/ppermute | solution.py:460
  58.2 0.7 collective-permute-start.9
  58.9 0.0 collective-permute-done.3.refs_1_
  58.9 2.7 %collective-permute-start.10 = (f32[2,160,128]{2,1,0:T(8,128)S(1)}, f32[2,160,128]{2,1,0:T(8,128)S(1)}, u32[]{:S(2)}, u32[]{:S(2)}) collective-permute-start(f32[2,160,128]{2,1,0:T(8,128)S(1)} %get-tuple-element.72), channel_id=1, source_target_pairs={{0,3},{1,0},{2,1},{3,2},{4,7},{5,4},{6,5},{7,6},{8,11},{9,8},{10,9... | collective-permute-start | bytes 491528 | tf_op jit(solution)/shard_map/ppermute | solution.py:460
  61.6 0.0 copy-done.5
  61.6 0.0 copy-done.6
  61.6 0.0 copy-done.7
  61.6 0.1 add_select_fusion.refs_7_.refs_10_
  61.7 0.0 collective-permute-done.4.refs_2_
  61.7 0.0 collective-permute-done.5.refs_3_
  61.7 2.7 %remap_lower.1 = (f32[1,160,128]{2,1,0:T(8,128)S(1)}, f32[1,160,128]{2,1,0:T(8,128)S(1)}, f32[1,160,128]{2,1,0:T(8,128)S(1)}, f32[1,160,128]{2,1,0:T(8,128)S(1)}) custom-call(f32[1,2,144,128]{3,2,1,0:T(8,128)S(1)} %get-tuple-element.60.refs_4_.refs_0_, f32[1,2,144,128]{3,2,1,0:T(8,128)S(1)} %collective-permute-done.3.refs_1_, ...), custom_call_target="tpu_custom_call" | custom-call | flops 220000000 | bytes 720000 | tf_op jit(solution)/shard_map/remap_lower/pallas_call | solution.py:532
  64.5 0.1 collective-permute-start.12
  64.5 4.3 %collective-permute-start.13 = (f32[1,160,128]{2,1,0:T(8,128)S(1)}, f32[1,160,128]{2,1,0:T(8,128)S(1)}, u32[]{:S(2)}, u32[]{:S(2)}) collective-permute-start(f32[1,160,128]{2,1,0:T(8,128)S(1)} %get-tuple-element.79), channel_id=1, source_target_pairs={{0,2},{1,3},{2,0},{3,1},{4,6},{5,7},{6,4},{7,5},{8,10},{9,11},{10,... | collective-permute-start | bytes 245768 | tf_op jit(solution)/shard_map/ppermute | solution.py:460
  68.9 0.0 collective-permute-done.8.refs_3_
  68.9 1.7 %collective-permute-start.14 = (f32[1,160,128]{2,1,0:T(8,128)S(1)}, f32[1,160,128]{2,1,0:T(8,128)S(1)}, u32[]{:S(2)}, u32[]{:S(2)}) collective-permute-start(f32[1,160,128]{2,1,0:T(8,128)S(1)} %get-tuple-element.80), channel_id=1, source_target_pairs={{0,3},{1,0},{2,1},{3,2},{4,7},{5,4},{6,5},{7,6},{8,11},{9,8},{10,9... | collective-permute-start | bytes 245768 | tf_op jit(solution)/shard_map/ppermute | solution.py:460
  70.6 0.0 collective-permute-done.9.refs_4_
  70.6 7.0 %collective-permute-done.10.refs_5_ = f32[2,160,128]{2,1,0:T(8,128)S(1)} collective-permute-done((f32[2,160,128]{2,1,0:T(8,128)S(1)}, f32[2,160,128]{2,1,0:T(8,128)S(1)}, u32[]{:S(2)}, u32[]{:S(2)}) %collective-permute-start.10) | collective-permute-done | bytes 163872 | tf_op jit(solution)/shard_map/ppermute | solution.py:460
  77.6 12.0 %collective-permute-start.11 = (f32[1,160,128]{2,1,0:T(8,128)S(1)}, f32[1,160,128]{2,1,0:T(8,128)S(1)}, u32[]{:S(2)}, u32[]{:S(2)}) collective-permute-start(f32[1,160,128]{2,1,0:T(8,128)S(1)} %select_select_fusion), channel_id=1, source_target_pairs={{0,4},{4,8},{8,12},{12,16},{16,20},{20,24},{24,28},{28,32},{32,36}... | collective-permute-start | bytes 245768 | tf_op jit(solution)/shard_map/ppermute | solution.py:557
  89.7 0.0 copy-done
  89.7 0.0 copy-done.1
  89.7 0.0 copy-done.2
  89.7 0.0 copy-done.3
  89.7 0.0 copy-done.4
  89.7 6.6 %final_upper.1 = (f32[12,32,576]{2,1,0:T(8,128)}, f32[12,32,576]{2,1,0:T(8,128)}, f32[12,32,576]{2,1,0:T(8,128)}, f32[12,32,576]{2,1,0:T(8,128)}, f32[3,32,576]{2,1,0:T(8,128)S(1)}) custom-call(s32[1]{0:T(128)} %bitcast.2.refs_0_, f32[13]{0:T(128)S(1)} %multiply_sine_fusion.1.refs_1_, f32[2,160,128]{2,1,0:T(8,128)S(1)} %get-tuple-element.76.refs_4_.refs_2_, ...), custom_call_target="tpu_custom_call" | custom-call | flops 7699999744 | bytes 25200000 | tf_op jit(solution)/shard_map/final_upper/pallas_call | solution.py:565
  96.3 0.0 collective-permute-done.12.refs_6_
  96.3 0.0 collective-permute-done.13.refs_7_
  96.3 0.0 collective-permute-done.14.refs_8_
  96.3 0.0 collective-permute-done.11.refs_2_
  96.4 4.6 %final_lower.1 = (f32[12,32,576]{2,1,0:T(8,128)}, f32[12,32,576]{2,1,0:T(8,128)}, f32[12,32,576]{2,1,0:T(8,128)}, f32[12,32,576]{2,1,0:T(8,128)}) custom-call(s32[1]{0:T(128)} %bitcast.2.refs_0_, f32[13]{0:T(128)S(1)} %multiply_sine_fusion.1.refs_1_, ...), custom_call_target="tpu_custom_call", output_to_operand_aliasing={{0}: (15, {}), {1}: (16, {}), {2}: (17, {}), {3}: (18, {})} | custom-call | flops 6600000000 | bytes 21600000 | tf_op jit(solution)/shard_map/final_lower/pallas_call | solution.py:581
  (5 shorter events, 0.1 us)
Async XLA Ops:
  1.8 8.0 %collective-permute-start = (f32[96,576]{1,0:T(8,128)S(1)}, f32[96,576]{1,0:T(8,128)S(1)}, u32[]{:S(2)}, u32[]{:S(2)}) collective-permute-start(f32[96,576]{1,0:T(8,128)S(1)} %get-tuple-element.48), channel_id=1, source_target_pairs={{4,0},{8,4},{12,8},{16,12},{20,16},{24,20},{28,24},{32,28},{36,32}... | collective-permute-start | bytes 663560 | tf_op jit(solution)/shard_map/ppermute | solution.py:504
  13.3 12.1 %collective-permute-start.2 = (f32[72,576]{1,0:T(8,128)S(1)}, f32[72,576]{1,0:T(8,128)S(1)}, u32[]{:S(2)}, u32[]{:S(2)}) collective-permute-start(f32[72,576]{1,0:T(8,128)S(1)} %get-tuple-element.54), channel_id=1, source_target_pairs={{0,4},{4,8},{8,12},{12,16},{16,20},{20,24},{24,28},{28,32},{32,36}... | collective-permute-start | bytes 497672 | tf_op jit(solution)/shard_map/ppermute | solution.py:524
  15.2 23.2 %copy-start.8 = (s32[12]{0:T(128)S(1)}, s32[12]{0:T(128)}, u32[]{:S(2)}) copy-start(s32[12]{0:T(128)} %param.16) | copy-start | bytes 148
  15.2 23.2 %collective-permute-start.1 = (f32[2,2,144,128]{3,2,1,0:T(8,128)S(1)}, f32[2,2,144,128]{3,2,1,0:T(8,128)S(1)}, u32[]{:S(2)}, u32[]{:S(2)}) collective-permute-start(f32[2,2,144,128]{3,2,1,0:T(8,128)S(1)} %get-tuple-element.53), channel_id=1, source_target_pairs={{0,1},{1,2},{2,3},{3,0},{4,5},{5,6},{6,7},{7,4},{8,9},{9,10},{10,1... | collective-permute-start | bytes 884744 | tf_op jit(solution)/shard_map/ppermute | solution.py:460
  18.3 25.2 %collective-permute-start.6 = (f32[2,2,144,128]{3,2,1,0:T(8,128)S(1)}, f32[2,2,144,128]{3,2,1,0:T(8,128)S(1)}, u32[]{:S(2)}, u32[]{:S(2)}) collective-permute-start(f32[2,2,144,128]{3,2,1,0:T(8,128)S(1)} %get-tuple-element.66), channel_id=1, source_target_pairs={{0,2},{1,3},{2,0},{3,1},{4,6},{5,7},{6,4},{7,5},{8,10},{9,11},{10,... | collective-permute-start | bytes 884744 | tf_op jit(solution)/shard_map/ppermute | solution.py:460
  22.9 20.6 %collective-permute-start.7 = (f32[2,2,144,128]{3,2,1,0:T(8,128)S(1)}, f32[2,2,144,128]{3,2,1,0:T(8,128)S(1)}, u32[]{:S(2)}, u32[]{:S(2)}) collective-permute-start(f32[2,2,144,128]{3,2,1,0:T(8,128)S(1)} %get-tuple-element.67), channel_id=1, source_target_pairs={{0,3},{1,0},{2,1},{3,2},{4,7},{5,4},{6,5},{7,6},{8,11},{9,8},{10,9... | collective-permute-start | bytes 884744 | tf_op jit(solution)/shard_map/ppermute | solution.py:460
  39.7 21.9 %copy-start.5 = (f32[12,576]{1,0:T(8,128)S(1)}, f32[12,576]{1,0:T(8,128)}, u32[]{:S(2)}) copy-start(f32[12,576]{1,0:T(8,128)} %param.18) | copy-start | bytes 82948
  39.7 21.9 %copy-start.6 = (s32[576]{0:T(1024)S(1)}, s32[576]{0:T(1024)}, u32[]{:S(2)}) copy-start(s32[576]{0:T(1024)} %constant.57.clone) | copy-start | bytes 6916
  39.8 21.9 %copy-start.7 = (s32[12]{0:T(128)S(1)}, s32[12]{0:T(128)}, u32[]{:S(2)}) copy-start(s32[12]{0:T(128)} %param.17) | copy-start | bytes 148
  39.8 49.9 %copy-start = (f32[12,32,576]{2,1,0:T(8,128)S(1)}, f32[12,32,576]{2,1,0:T(8,128)}, u32[]{:S(2)}) copy-start(f32[12,32,576]{2,1,0:T(8,128)} %refs_12_.1) | copy-start | bytes 2654212
  39.8 49.9 %copy-start.1 = (f32[12,32,576]{2,1,0:T(8,128)S(1)}, f32[12,32,576]{2,1,0:T(8,128)}, u32[]{:S(2)}) copy-start(f32[12,32,576]{2,1,0:T(8,128)} %refs_11_.2) | copy-start | bytes 2654212
  39.8 49.9 %copy-start.2 = (f32[12,576]{1,0:T(8,128)S(1)}, f32[12,576]{1,0:T(8,128)}, u32[]{:S(2)}) copy-start(f32[12,576]{1,0:T(8,128)} %refs_9_.3) | copy-start | bytes 82948
  39.8 49.9 %copy-start.3 = (bf16[1920,576]{1,0:T(8,128)(2,1)S(1)}, bf16[1920,576]{1,0:T(8,128)(2,1)}, u32[]{:S(2)}) copy-start(bf16[1920,576]{1,0:T(8,128)(2,1)} %constant.59.clone.refs_11_.refs_14_) | copy-start | bytes 6635524
  39.8 49.9 %copy-start.4 = (bf16[1920,576]{1,0:T(8,128)(2,1)S(1)}, bf16[1920,576]{1,0:T(8,128)(2,1)}, u32[]{:S(2)}) copy-start(bf16[1920,576]{1,0:T(8,128)(2,1)} %constant.58.clone.refs_10_.refs_13_) | copy-start | bytes 6635524
  39.8 19.1 %collective-permute-start.3 = (f32[1,2,144,128]{3,2,1,0:T(8,128)S(1)}, f32[1,2,144,128]{3,2,1,0:T(8,128)S(1)}, u32[]{:S(2)}, u32[]{:S(2)}) collective-permute-start(f32[1,2,144,128]{3,2,1,0:T(8,128)S(1)} %get-tuple-element.61), channel_id=1, source_target_pairs={{0,1},{1,2},{2,3},{3,0},{4,5},{5,6},{6,7},{7,4},{8,9},{9,10},{10,1... | collective-permute-start | bytes 442376 | tf_op jit(solution)/shard_map/ppermute | solution.py:460
  39.9 21.8 %collective-permute-start.4 = (f32[1,2,144,128]{3,2,1,0:T(8,128)S(1)}, f32[1,2,144,128]{3,2,1,0:T(8,128)S(1)}, u32[]{:S(2)}, u32[]{:S(2)}) collective-permute-start(f32[1,2,144,128]{3,2,1,0:T(8,128)S(1)} %get-tuple-element.62), channel_id=1, source_target_pairs={{0,2},{1,3},{2,0},{3,1},{4,6},{5,7},{6,4},{7,5},{8,10},{9,11},{10,... | collective-permute-start | bytes 442376 | tf_op jit(solution)/shard_map/ppermute | solution.py:460
  40.0 21.7 %collective-permute-start.5 = (f32[1,2,144,128]{3,2,1,0:T(8,128)S(1)}, f32[1,2,144,128]{3,2,1,0:T(8,128)S(1)}, u32[]{:S(2)}, u32[]{:S(2)}) collective-permute-start(f32[1,2,144,128]{3,2,1,0:T(8,128)S(1)} %get-tuple-element.63), channel_id=1, source_target_pairs={{0,3},{1,0},{2,1},{3,2},{4,7},{5,4},{6,5},{7,6},{8,11},{9,8},{10,9... | collective-permute-start | bytes 442376 | tf_op jit(solution)/shard_map/ppermute | solution.py:460
  49.1 19.8 %collective-permute-start.8 = (f32[2,160,128]{2,1,0:T(8,128)S(1)}, f32[2,160,128]{2,1,0:T(8,128)S(1)}, u32[]{:S(2)}, u32[]{:S(2)}) collective-permute-start(f32[2,160,128]{2,1,0:T(8,128)S(1)} %get-tuple-element.70), channel_id=1, source_target_pairs={{0,1},{1,2},{2,3},{3,0},{4,5},{5,6},{6,7},{7,4},{8,9},{9,10},{10,1... | collective-permute-start | bytes 491528 | tf_op jit(solution)/shard_map/ppermute | solution.py:460
  58.2 12.3 %collective-permute-start.9 = (f32[2,160,128]{2,1,0:T(8,128)S(1)}, f32[2,160,128]{2,1,0:T(8,128)S(1)}, u32[]{:S(2)}, u32[]{:S(2)}) collective-permute-start(f32[2,160,128]{2,1,0:T(8,128)S(1)} %get-tuple-element.71), channel_id=1, source_target_pairs={{0,2},{1,3},{2,0},{3,1},{4,6},{5,7},{6,4},{7,5},{8,10},{9,11},{10,... | collective-permute-start | bytes 491528 | tf_op jit(solution)/shard_map/ppermute | solution.py:460
  58.9 18.7 %collective-permute-start.10 = (f32[2,160,128]{2,1,0:T(8,128)S(1)}, f32[2,160,128]{2,1,0:T(8,128)S(1)}, u32[]{:S(2)}, u32[]{:S(2)}) collective-permute-start(f32[2,160,128]{2,1,0:T(8,128)S(1)} %get-tuple-element.72), channel_id=1, source_target_pairs={{0,3},{1,0},{2,1},{3,2},{4,7},{5,4},{6,5},{7,6},{8,11},{9,8},{10,9... | collective-permute-start | bytes 491528 | tf_op jit(solution)/shard_map/ppermute | solution.py:460
  64.5 31.9 %collective-permute-start.12 = (f32[1,160,128]{2,1,0:T(8,128)S(1)}, f32[1,160,128]{2,1,0:T(8,128)S(1)}, u32[]{:S(2)}, u32[]{:S(2)}) collective-permute-start(f32[1,160,128]{2,1,0:T(8,128)S(1)} %get-tuple-element.78), channel_id=1, source_target_pairs={{0,1},{1,2},{2,3},{3,0},{4,5},{5,6},{6,7},{7,4},{8,9},{9,10},{10,1... | collective-permute-start | bytes 245768 | tf_op jit(solution)/shard_map/ppermute | solution.py:460
  64.5 31.8 %collective-permute-start.13 = (f32[1,160,128]{2,1,0:T(8,128)S(1)}, f32[1,160,128]{2,1,0:T(8,128)S(1)}, u32[]{:S(2)}, u32[]{:S(2)}) collective-permute-start(f32[1,160,128]{2,1,0:T(8,128)S(1)} %get-tuple-element.79), channel_id=1, source_target_pairs={{0,2},{1,3},{2,0},{3,1},{4,6},{5,7},{6,4},{7,5},{8,10},{9,11},{10,... | collective-permute-start | bytes 245768 | tf_op jit(solution)/shard_map/ppermute | solution.py:460
  68.9 27.5 %collective-permute-start.14 = (f32[1,160,128]{2,1,0:T(8,128)S(1)}, f32[1,160,128]{2,1,0:T(8,128)S(1)}, u32[]{:S(2)}, u32[]{:S(2)}) collective-permute-start(f32[1,160,128]{2,1,0:T(8,128)S(1)} %get-tuple-element.80), channel_id=1, source_target_pairs={{0,3},{1,0},{2,1},{3,2},{4,7},{5,4},{6,5},{7,6},{8,11},{9,8},{10,9... | collective-permute-start | bytes 245768 | tf_op jit(solution)/shard_map/ppermute | solution.py:460
  77.6 18.7 %collective-permute-start.11 = (f32[1,160,128]{2,1,0:T(8,128)S(1)}, f32[1,160,128]{2,1,0:T(8,128)S(1)}, u32[]{:S(2)}, u32[]{:S(2)}) collective-permute-start(f32[1,160,128]{2,1,0:T(8,128)S(1)} %select_select_fusion), channel_id=1, source_target_pairs={{0,4},{4,8},{8,12},{12,16},{16,20},{20,24},{24,28},{28,32},{32,36}... | collective-permute-start | bytes 245768 | tf_op jit(solution)/shard_map/ppermute | solution.py:557

commit v11 on v10

--- a/solution.py
+++ b/solution.py
@@ -86,19 +86,23 @@
         yield x - (jnp.roll(flux, -1, axis=1) - flux) - (w_n * (x_n + x) - w_s * (x + x_s))
 
 
-def edges_kernel(merid, thick, theta, ground, to_north, to_south, thick_s, theta_s, merid_s, ground_s, sems):
-    lat_rows, levels, _ = thick.shape
-    top = lat_rows - 1
-    copies = []
-    for source, target in ((thick, thick_s), (theta, theta_s)):
-        copies += [(source.at[pl.ds(0, 1)], target.at[pl.ds(0, 1)]), (source.at[pl.ds(top, 1)], target.at[pl.ds(1, 1)])]
-    wait_all(copy_all([*copies, (merid.at[pl.ds(0, 1)], merid_s), (ground, ground_s)], sems))
-    to_north[pl.ds(0, levels), :] = thick_s[1]
-    to_north[pl.ds(levels, levels), :] = theta_s[1] * thick_s[1]
-    to_north[pl.ds(2 * levels, 1), :] = ground_s[pl.ds(top, 1), :]
+def south_edge_kernel(merid, thick, theta, to_south, thick_s, theta_s, sems):
+    levels = thick.shape[1]
+    first = pl.ds(0, 1)
+    copies = [(thick.at[first], thick_s), (theta.at[first], theta_s)]
+    wait_all(copy_all([*copies, (merid.at[0], to_south.at[pl.ds(2 * levels, levels)])], sems))
     to_south[pl.ds(0, levels), :] = thick_s[0]
     to_south[pl.ds(levels, levels), :] = theta_s[0] * thick_s[0]
-    to_south[pl.ds(2 * levels, levels), :] = merid_s[0]
+
+
+def north_edge_kernel(thick, theta, ground, after, to_north, thick_s, theta_s, ground_s, sems):
+    del after
+    lat_rows, levels, _ = thick.shape
+    last = pl.ds(lat_rows - 1, 1)
+    wait_all(copy_all([(thick.at[last], thick_s), (theta.at[last], theta_s), (ground, ground_s)], sems))
+    to_north[pl.ds(0, levels), :] = thick_s[0]
+    to_north[pl.ds(levels, levels), :] = theta_s[0] * thick_s[0]
+    to_north[pl.ds(2 * levels, 1), :] = ground_s[pl.ds(lat_rows - 1, 1), :]
 
 
 def advect_kernel(first, rows_each, peers, coef, halo, *refs):
@@ -312,6 +316,22 @@
     return value + product(spectral, basis_t)
 
 
+def filtered_by_parts(value, table, basis, basis_t, block):
+    rows, width = value.shape
+    span = tile_count(width) * LANES
+
+    def product(x, stacked):
+        x_high = x.astype(BF16)
+        x_low = (x - x_high.astype(F32)).astype(BF16)
+        high, low = stacked[pl.ds(0, width), :], stacked[pl.ds(2 * span, width), :]
+        dot = lambda a, b: jnp.dot(a, b, preferred_element_type=F32)
+        return dot(x_high, high) + (dot(x_low, high) + dot(x_high, low))
+
+    spectral = product(value, basis)
+    spectral = (spectral.reshape(rows // block, block, width) * table[:, None, :]).reshape(rows, width)
+    return value + product(spectral, basis_t)
+
+
 def clear_gaps(split, width):
     span = tile_count(width) * LANES
     last = width // LANES * LANES
@@ -348,7 +368,7 @@
 def filter_rows(ref, count, table, tables, block):
     width = ref.shape[-1]
     value = ref[pl.ds(0, count)].reshape(count * block, width)
-    value = filtered(value, table, *tables, block)
+    value = (filtered if len(tables) == 3 else filtered_by_parts)(value, table, *tables, block)
     ref[pl.ds(0, count)] = value.reshape(count, block, width)
 
 
@@ -413,7 +433,7 @@
     levels, flag, faces, south, halo_s, edge_state, p0, p1, p2, p3, ground, table, zonal, merid, basis, basis_t,
     zonal_in, merid_in, thick_in, theta_in,
     zonal_out, merid_out, thick_out, theta_out,
-    order, winds_s, thick_s, theta_s, split, sems,
+    order, winds_s, thick_s, theta_s, sems,
 ):
     del zonal_in, merid_in, thick_in, theta_in
     count = order.shape[0]
@@ -440,8 +460,7 @@
     @pl.when(flag[0] != 0)
     def _():
         picked = jnp.concatenate([table[rows, :], table[pl.ds(0, count + 1), :]], axis=0)
-        clear_gaps(split, width)
-        filter_rows(winds_s, 2 * count + 1, picked, (basis, basis_t, split), block)
+        filter_rows(winds_s, 2 * count + 1, picked, (basis, basis_t), block)
 
     late = copy_all(
         [
@@ -491,17 +510,27 @@
     field = shape(lat_rows, block, width)
 
     fields = stay(zonal_wind, meridional_wind, thickness, potential_temp)
-    to_north, to_south = pl.pallas_call(
-        edges_kernel,
-        out_shape=[shape(2 * block + 8, width), shape(3 * block, width)],
-        in_specs=[hbm] * 4,
-        out_specs=[VMEM] * 2,
-        scratch_shapes=[rows_of(2), rows_of(2), rows_of(1), pltpu.VMEM((lat_rows, width), F32), dma(6)],
+    to_south = pl.pallas_call(
+        south_edge_kernel,
+        out_shape=shape(3 * block, width),
+        in_specs=[hbm] * 3,
+        out_specs=VMEM,
+        scratch_shapes=[rows_of(1), rows_of(1), dma(3)],
         compiler_params=params(8),
         cost_estimate=cost(1),
-        name="edges",
-    )(*fields[1:], *stay(surface_geo))
+        name="south_edge",
+    )(*fields[1:])
     halo_n = lax.ppermute(to_south, "lat", southward)
+    to_north = pl.pallas_call(
+        north_edge_kernel,
+        out_shape=shape(2 * block + 8, width),
+        in_specs=[hbm] * 3 + [pl.BlockSpec(memory_space=pl.ANY)],
+        out_specs=VMEM,
+        scratch_shapes=[rows_of(1), rows_of(1), pltpu.VMEM((lat_rows, width), F32), dma(3)],
+        compiler_params=params(8),
+        cost_estimate=cost(1),
+        name="north_edge",
+    )(*fields[2:], *stay(surface_geo), to_south)
 
     def advect(start, each, halo, name):
         return pl.pallas_call(
@@ -584,7 +613,7 @@
             in_specs=[SMEM] * 2 + [VMEM] * (peers + 9) + [hbm] * 4,
             out_specs=[hbm] * 4,
             scratch_shapes=[pltpu.VMEM((first, message_rows, LANES), F32)]
-            + [rows_of(2 * first + 1), rows_of(first), rows_of(first), split_of(2 * first + 1), dma(4)],
+            + [rows_of(2 * first + 1), rows_of(first), rows_of(first), dma(4)],
             input_output_aliases={peers + 11 + i: i for i in range(4)},
             compiler_params=params(16),
             cost_estimate=cost(6),

time: 101 us -> 99 us (0.980); the launches traced: 101 us -> 101 us
  transfers between devices with their start and end apart: 15 -> 15, of which waited for: 3 -> 3; matrix products, arithmetic and copies ran while one was open for 1% -> 1% of each run, Pallas kernels for 18% -> 19%
where the time goes in v11:
time: 99 us; the launch traced here: 101 us
  starting transfers between devices  48.9 us (49%)
  Pallas kernels  27.8 us (28%)
  waiting for transfers between devices  21.3 us (22%)
  between operations  1.75 us (2%)
    ppermute x12, starting transfers between devices, exchanged(): lax.ppermute(parts[step], 'lev', [(i, (i + step) % peers) for i in range(...  32.4 us
    ppermute x12, waiting for transfers between devices, exchanged(): lax.ppermute(parts[step], 'lev', [(i, (i + step) % peers) for i in range(...  17.1 us
    ppermute x1, starting transfers between devices, body(): south = lax.ppermute(last_message, 'lat', northward)  12 us
    pallas_call x2, Pallas kernels, remap(): pl.pallas_call(lambda *refs: remap_kernel(width, block, peers, *refs), ou...  8.33 us
    pallas_call x2, Pallas kernels, advect(): pl.pallas_call(lambda *refs: advect_kernel(start, each, peers, *refs), ou...  6.59 us
    pallas_call x1, Pallas kernels, body(): pl.pallas_call(lambda *refs: upper_final_kernel(levels, first, *refs), ou...  6.56 us
    pallas_call x1, Pallas kernels, body(): pl.pallas_call(lambda *refs: lower_final_kernel(levels, *refs), out_shape...  4.4 us
    ppermute x1, waiting for transfers between devices, body(): halo_n = lax.ppermute(to_south, 'lat', southward)  4.21 us
  transfers between devices with their start and end apart: 15, of which 3 were waited for; matrix products, arithmetic and copies ran while one was open for 1% of the time, Pallas kernels for 19%

profile of v11, /device:TPU:25, one launch (start us, length us, event | category | flops | bytes accessed | tf_op | source)
XLA Modules:
  0.0 100.8 jit_solution(7542865115606430267)
XLA Ops:
  0.6 1.0 south_edge.1.after
  1.6 2.6 %collective-permute-start = (f32[96,576]{1,0:T(8,128)S(1)}, f32[96,576]{1,0:T(8,128)S(1)}, u32[]{:S(2)}, u32[]{:S(2)}) collective-permute-start(f32[96,576]{1,0:T(8,128)S(1)} %south_edge.1.after), channel_id=1, source_target_pairs={{4,0},{8,4},{12,8},{16,12},{20,16},{24,20},{28,24},{32,28},{36,32}... | collective-permute-start | bytes 663560 | tf_op jit(solution)/shard_map/ppermute | solution.py:523
  4.3 0.1 slice_bitcast_fusion.1
  4.4 1.0 north_edge.1
  5.4 4.2 %collective-permute-done.refs_1_ = f32[96,576]{1,0:T(8,128)S(1)} collective-permute-done((f32[96,576]{1,0:T(8,128)S(1)}, f32[96,576]{1,0:T(8,128)S(1)}, u32[]{:S(2)}, u32[]{:S(2)}) %collective-permute-start) | collective-permute-done | bytes 221216 | tf_op jit(solution)/shard_map/ppermute | solution.py:523
  9.6 3.5 %advect_upper.1 = (f32[2,2,144,128]{3,2,1,0:T(8,128)S(1)}, f32[2,2,144,128]{3,2,1,0:T(8,128)S(1)}, f32[2,2,144,128]{3,2,1,0:T(8,128)S(1)}, f32[2,2,144,128]{3,2,1,0:T(8,128)S(1)}) custom-call(f32[2,12]{1,0:T(2,128)S(1)} %fusion.refs_0_, f32[96,576]{1,0:T(8,128)S(1)} %collective-permute-done.refs_1_, f32[12,32,576]{2,1,0:T(8,128)} %refs_11_.2, ...), custom_call_target="tpu_custom_call" | custom-call | flops 5500000256 | bytes 18000000 | tf_op jit(solution)/shard_map/advect_upper/pallas_call | solution.py:536
  13.1 1.9 %collective-permute-start.2 = (f32[72,576]{1,0:T(8,128)S(1)}, f32[72,576]{1,0:T(8,128)S(1)}, u32[]{:S(2)}, u32[]{:S(2)}) collective-permute-start(f32[72,576]{1,0:T(8,128)S(1)} %north_edge.1), channel_id=1, source_target_pairs={{0,4},{4,8},{8,12},{12,16},{16,20},{20,24},{24,28},{28,32},{32,36}... | collective-permute-start | bytes 497672 | tf_op jit(solution)/shard_map/ppermute | solution.py:553
  15.1 0.0 copy-start.8
  15.1 3.1 %collective-permute-start.1 = (f32[2,2,144,128]{3,2,1,0:T(8,128)S(1)}, f32[2,2,144,128]{3,2,1,0:T(8,128)S(1)}, u32[]{:S(2)}, u32[]{:S(2)}) collective-permute-start(f32[2,2,144,128]{3,2,1,0:T(8,128)S(1)} %get-tuple-element.49), channel_id=1, source_target_pairs={{0,1},{1,2},{2,3},{3,0},{4,5},{5,6},{6,7},{7,4},{8,9},{9,10},{10,1... | collective-permute-start | bytes 884744 | tf_op jit(solution)/shard_map/ppermute | solution.py:479
  18.2 4.6 %collective-permute-start.6 = (f32[2,2,144,128]{3,2,1,0:T(8,128)S(1)}, f32[2,2,144,128]{3,2,1,0:T(8,128)S(1)}, u32[]{:S(2)}, u32[]{:S(2)}) collective-permute-start(f32[2,2,144,128]{3,2,1,0:T(8,128)S(1)} %get-tuple-element.62), channel_id=1, source_target_pairs={{0,2},{1,3},{2,0},{3,1},{4,6},{5,7},{6,4},{7,5},{8,10},{9,11},{10,... | collective-permute-start | bytes 884744 | tf_op jit(solution)/shard_map/ppermute | solution.py:479
  22.8 2.4 %collective-permute-start.7 = (f32[2,2,144,128]{3,2,1,0:T(8,128)S(1)}, f32[2,2,144,128]{3,2,1,0:T(8,128)S(1)}, u32[]{:S(2)}, u32[]{:S(2)}) collective-permute-start(f32[2,2,144,128]{3,2,1,0:T(8,128)S(1)} %get-tuple-element.63), channel_id=1, source_target_pairs={{0,3},{1,0},{2,1},{3,2},{4,7},{5,4},{6,5},{7,6},{8,11},{9,8},{10,9... | collective-permute-start | bytes 884744 | tf_op jit(solution)/shard_map/ppermute | solution.py:479
  25.2 0.0 collective-permute-done.2.refs_1_.refs_3_
  25.2 3.1 %advect_lower.1 = (f32[1,2,144,128]{3,2,1,0:T(8,128)S(1)}, f32[1,2,144,128]{3,2,1,0:T(8,128)S(1)}, f32[1,2,144,128]{3,2,1,0:T(8,128)S(1)}, f32[1,2,144,128]{3,2,1,0:T(8,128)S(1)}) custom-call(f32[2,12]{1,0:T(2,128)S(1)} %fusion.refs_0_, f32[72,576]{1,0:T(8,128)S(1)} %collective-permute-done.2.refs_1_.refs_3_, f32[12,32,576]{2,1,0:T(8,128)} %refs_11_.2, ...), custom_call_target="tpu_custom_call" | custom-call | flops 3300000000 | bytes 10800000 | tf_op jit(solution)/shard_map/advect_lower/pallas_call | solution.py:536
  28.3 10.0 %collective-permute-done.1.refs_1_ = f32[2,2,144,128]{3,2,1,0:T(8,128)S(1)} collective-permute-done((f32[2,2,144,128]{3,2,1,0:T(8,128)S(1)}, f32[2,2,144,128]{3,2,1,0:T(8,128)S(1)}, u32[]{:S(2)}, u32[]{:S(2)}) %collective-permute-start.1) | collective-permute-done | bytes 294944 | tf_op jit(solution)/shard_map/ppermute | solution.py:479
  38.3 0.0 copy-done.8
  38.3 0.6 broadcast_compare_fusion
  39.6 0.0 copy-start.5
  39.6 0.0 copy-start.6
  39.6 0.0 copy-start.7
  39.6 0.0 copy-start
  39.7 0.0 copy-start.1
  39.7 0.0 copy-start.2
  39.7 0.0 copy-start.3
  39.7 0.0 copy-start.4
  39.7 0.1 collective-permute-start.3
  39.8 0.1 collective-permute-start.4
  39.9 3.5 %collective-permute-start.5 = (f32[1,2,144,128]{3,2,1,0:T(8,128)S(1)}, f32[1,2,144,128]{3,2,1,0:T(8,128)S(1)}, u32[]{:S(2)}, u32[]{:S(2)}) collective-permute-start(f32[1,2,144,128]{3,2,1,0:T(8,128)S(1)} %get-tuple-element.59), channel_id=1, source_target_pairs={{0,3},{1,0},{2,1},{3,2},{4,7},{5,4},{6,5},{7,6},{8,11},{9,8},{10,9... | collective-permute-start | bytes 442376 | tf_op jit(solution)/shard_map/ppermute | solution.py:479
  43.4 0.0 collective-permute-done.6.refs_2_
  43.4 0.0 collective-permute-done.7.refs_3_
  43.4 5.6 %remap_upper.1 = (f32[2,160,128]{2,1,0:T(8,128)S(1)}, f32[2,160,128]{2,1,0:T(8,128)S(1)}, f32[2,160,128]{2,1,0:T(8,128)S(1)}, f32[2,160,128]{2,1,0:T(8,128)S(1)}) custom-call(f32[2,2,144,128]{3,2,1,0:T(8,128)S(1)} %get-tuple-element.60.refs_0_, f32[2,2,144,128]{3,2,1,0:T(8,128)S(1)} %collective-permute-done.1.refs_1_, ...), custom_call_target="tpu_custom_call" | custom-call | flops 3520000000 | bytes 11520000 | tf_op jit(solution)/shard_map/remap_upper/pallas_call | solution.py:561
  49.0 9.1 %collective-permute-start.8 = (f32[2,160,128]{2,1,0:T(8,128)S(1)}, f32[2,160,128]{2,1,0:T(8,128)S(1)}, u32[]{:S(2)}, u32[]{:S(2)}) collective-permute-start(f32[2,160,128]{2,1,0:T(8,128)S(1)} %get-tuple-element.66), channel_id=1, source_target_pairs={{0,1},{1,2},{2,3},{3,0},{4,5},{5,6},{6,7},{7,4},{8,9},{9,10},{10,1... | collective-permute-start | bytes 491528 | tf_op jit(solution)/shard_map/ppermute | solution.py:479
  58.1 0.7 collective-permute-start.9
  58.8 0.0 collective-permute-done.3.refs_1_
  58.8 2.7 %collective-permute-start.10 = (f32[2,160,128]{2,1,0:T(8,128)S(1)}, f32[2,160,128]{2,1,0:T(8,128)S(1)}, u32[]{:S(2)}, u32[]{:S(2)}) collective-permute-start(f32[2,160,128]{2,1,0:T(8,128)S(1)} %get-tuple-element.68), channel_id=1, source_target_pairs={{0,3},{1,0},{2,1},{3,2},{4,7},{5,4},{6,5},{7,6},{8,11},{9,8},{10,9... | collective-permute-start | bytes 491528 | tf_op jit(solution)/shard_map/ppermute | solution.py:479
  61.5 0.0 copy-done.5
  61.5 0.0 copy-done.6
  61.5 0.0 copy-done.7
  61.5 0.1 add_select_fusion.refs_7_.refs_10_
  61.6 0.0 collective-permute-done.4.refs_2_
  61.6 0.0 collective-permute-done.5.refs_3_
  61.6 2.7 %remap_lower.1 = (f32[1,160,128]{2,1,0:T(8,128)S(1)}, f32[1,160,128]{2,1,0:T(8,128)S(1)}, f32[1,160,128]{2,1,0:T(8,128)S(1)}, f32[1,160,128]{2,1,0:T(8,128)S(1)}) custom-call(f32[1,2,144,128]{3,2,1,0:T(8,128)S(1)} %get-tuple-element.56.refs_4_.refs_0_, f32[1,2,144,128]{3,2,1,0:T(8,128)S(1)} %collective-permute-done.3.refs_1_, ...), custom_call_target="tpu_custom_call" | custom-call | flops 220000000 | bytes 720000 | tf_op jit(solution)/shard_map/remap_lower/pallas_call | solution.py:561
  64.3 0.1 collective-permute-start.12
  64.4 4.3 %collective-permute-start.13 = (f32[1,160,128]{2,1,0:T(8,128)S(1)}, f32[1,160,128]{2,1,0:T(8,128)S(1)}, u32[]{:S(2)}, u32[]{:S(2)}) collective-permute-start(f32[1,160,128]{2,1,0:T(8,128)S(1)} %get-tuple-element.75), channel_id=1, source_target_pairs={{0,2},{1,3},{2,0},{3,1},{4,6},{5,7},{6,4},{7,5},{8,10},{9,11},{10,... | collective-permute-start | bytes 245768 | tf_op jit(solution)/shard_map/ppermute | solution.py:479
  68.8 0.0 collective-permute-done.8.refs_3_
  68.8 1.7 %collective-permute-start.14 = (f32[1,160,128]{2,1,0:T(8,128)S(1)}, f32[1,160,128]{2,1,0:T(8,128)S(1)}, u32[]{:S(2)}, u32[]{:S(2)}) collective-permute-start(f32[1,160,128]{2,1,0:T(8,128)S(1)} %get-tuple-element.76), channel_id=1, source_target_pairs={{0,3},{1,0},{2,1},{3,2},{4,7},{5,4},{6,5},{7,6},{8,11},{9,8},{10,9... | collective-permute-start | bytes 245768 | tf_op jit(solution)/shard_map/ppermute | solution.py:479
  70.4 0.0 collective-permute-done.9.refs_4_
  70.5 7.0 %collective-permute-done.10.refs_5_ = f32[2,160,128]{2,1,0:T(8,128)S(1)} collective-permute-done((f32[2,160,128]{2,1,0:T(8,128)S(1)}, f32[2,160,128]{2,1,0:T(8,128)S(1)}, u32[]{:S(2)}, u32[]{:S(2)}) %collective-permute-start.10) | collective-permute-done | bytes 163872 | tf_op jit(solution)/shard_map/ppermute | solution.py:479
  77.5 12.0 %collective-permute-start.11 = (f32[1,160,128]{2,1,0:T(8,128)S(1)}, f32[1,160,128]{2,1,0:T(8,128)S(1)}, u32[]{:S(2)}, u32[]{:S(2)}) collective-permute-start(f32[1,160,128]{2,1,0:T(8,128)S(1)} %select_select_fusion), channel_id=1, source_target_pairs={{0,4},{4,8},{8,12},{12,16},{16,20},{20,24},{24,28},{28,32},{32,36}... | collective-permute-start | bytes 245768 | tf_op jit(solution)/shard_map/ppermute | solution.py:586
  89.6 0.0 copy-done
  89.6 0.0 copy-done.1
  89.6 0.0 copy-done.2
  89.6 0.0 copy-done.3
  89.6 0.0 copy-done.4
  89.6 6.6 %final_upper.1 = (f32[12,32,576]{2,1,0:T(8,128)}, f32[12,32,576]{2,1,0:T(8,128)}, f32[12,32,576]{2,1,0:T(8,128)}, f32[12,32,576]{2,1,0:T(8,128)}, f32[3,32,576]{2,1,0:T(8,128)S(1)}) custom-call(s32[1]{0:T(128)} %bitcast.2.refs_0_, f32[13]{0:T(128)S(1)} %multiply_sine_fusion.1.refs_1_, f32[2,160,128]{2,1,0:T(8,128)S(1)} %get-tuple-element.72.refs_4_.refs_2_, ...), custom_call_target="tpu_custom_call" | custom-call | flops 7699999744 | bytes 25200000 | tf_op jit(solution)/shard_map/final_upper/pallas_call | solution.py:594
  96.2 0.0 collective-permute-done.12.refs_6_
  96.2 0.0 collective-permute-done.13.refs_7_
  96.2 0.0 collective-permute-done.14.refs_8_
  96.2 0.0 collective-permute-done.11.refs_2_
  96.2 4.4 %final_lower.1 = (f32[12,32,576]{2,1,0:T(8,128)}, f32[12,32,576]{2,1,0:T(8,128)}, f32[12,32,576]{2,1,0:T(8,128)}, f32[12,32,576]{2,1,0:T(8,128)}) custom-call(s32[1]{0:T(128)} %bitcast.2.refs_0_, f32[13]{0:T(128)S(1)} %multiply_sine_fusion.1.refs_1_, ...), custom_call_target="tpu_custom_call", output_to_operand_aliasing={{0}: (15, {}), {1}: (16, {}), {2}: (17, {}), {3}: (18, {})} | custom-call | flops 6600000000 | bytes 21600000 | tf_op jit(solution)/shard_map/final_lower/pallas_call | solution.py:610
  (5 shorter events, 0.1 us)
Async XLA Ops:
  1.6 8.0 %collective-permute-start = (f32[96,576]{1,0:T(8,128)S(1)}, f32[96,576]{1,0:T(8,128)S(1)}, u32[]{:S(2)}, u32[]{:S(2)}) collective-permute-start(f32[96,576]{1,0:T(8,128)S(1)} %south_edge.1.after), channel_id=1, source_target_pairs={{4,0},{8,4},{12,8},{16,12},{20,16},{24,20},{28,24},{32,28},{36,32}... | collective-permute-start | bytes 663560 | tf_op jit(solution)/shard_map/ppermute | solution.py:523
  13.1 12.1 %collective-permute-start.2 = (f32[72,576]{1,0:T(8,128)S(1)}, f32[72,576]{1,0:T(8,128)S(1)}, u32[]{:S(2)}, u32[]{:S(2)}) collective-permute-start(f32[72,576]{1,0:T(8,128)S(1)} %north_edge.1), channel_id=1, source_target_pairs={{0,4},{4,8},{8,12},{12,16},{16,20},{20,24},{24,28},{28,32},{32,36}... | collective-permute-start | bytes 497672 | tf_op jit(solution)/shard_map/ppermute | solution.py:553
  15.1 23.2 %copy-start.8 = (s32[12]{0:T(128)S(1)}, s32[12]{0:T(128)}, u32[]{:S(2)}) copy-start(s32[12]{0:T(128)} %param.16) | copy-start | bytes 148
  15.1 23.2 %collective-permute-start.1 = (f32[2,2,144,128]{3,2,1,0:T(8,128)S(1)}, f32[2,2,144,128]{3,2,1,0:T(8,128)S(1)}, u32[]{:S(2)}, u32[]{:S(2)}) collective-permute-start(f32[2,2,144,128]{3,2,1,0:T(8,128)S(1)} %get-tuple-element.49), channel_id=1, source_target_pairs={{0,1},{1,2},{2,3},{3,0},{4,5},{5,6},{6,7},{7,4},{8,9},{9,10},{10,1... | collective-permute-start | bytes 884744 | tf_op jit(solution)/shard_map/ppermute | solution.py:479
  18.2 25.2 %collective-permute-start.6 = (f32[2,2,144,128]{3,2,1,0:T(8,128)S(1)}, f32[2,2,144,128]{3,2,1,0:T(8,128)S(1)}, u32[]{:S(2)}, u32[]{:S(2)}) collective-permute-start(f32[2,2,144,128]{3,2,1,0:T(8,128)S(1)} %get-tuple-element.62), channel_id=1, source_target_pairs={{0,2},{1,3},{2,0},{3,1},{4,6},{5,7},{6,4},{7,5},{8,10},{9,11},{10,... | collective-permute-start | bytes 884744 | tf_op jit(solution)/shard_map/ppermute | solution.py:479
  22.8 20.6 %collective-permute-start.7 = (f32[2,2,144,128]{3,2,1,0:T(8,128)S(1)}, f32[2,2,144,128]{3,2,1,0:T(8,128)S(1)}, u32[]{:S(2)}, u32[]{:S(2)}) collective-permute-start(f32[2,2,144,128]{3,2,1,0:T(8,128)S(1)} %get-tuple-element.63), channel_id=1, source_target_pairs={{0,3},{1,0},{2,1},{3,2},{4,7},{5,4},{6,5},{7,6},{8,11},{9,8},{10,9... | collective-permute-start | bytes 884744 | tf_op jit(solution)/shard_map/ppermute | solution.py:479
  39.6 21.9 %copy-start.5 = (f32[12,576]{1,0:T(8,128)S(1)}, f32[12,576]{1,0:T(8,128)}, u32[]{:S(2)}) copy-start(f32[12,576]{1,0:T(8,128)} %param.18) | copy-start | bytes 82948
  39.6 21.9 %copy-start.6 = (s32[576]{0:T(1024)S(1)}, s32[576]{0:T(1024)}, u32[]{:S(2)}) copy-start(s32[576]{0:T(1024)} %constant.57.clone) | copy-start | bytes 6916
  39.6 21.9 %copy-start.7 = (s32[12]{0:T(128)S(1)}, s32[12]{0:T(128)}, u32[]{:S(2)}) copy-start(s32[12]{0:T(128)} %param.17) | copy-start | bytes 148
  39.6 49.9 %copy-start = (f32[12,32,576]{2,1,0:T(8,128)S(1)}, f32[12,32,576]{2,1,0:T(8,128)}, u32[]{:S(2)}) copy-start(f32[12,32,576]{2,1,0:T(8,128)} %refs_12_.1) | copy-start | bytes 2654212
  39.7 49.9 %copy-start.1 = (f32[12,32,576]{2,1,0:T(8,128)S(1)}, f32[12,32,576]{2,1,0:T(8,128)}, u32[]{:S(2)}) copy-start(f32[12,32,576]{2,1,0:T(8,128)} %refs_11_.2) | copy-start | bytes 2654212
  39.7 49.9 %copy-start.2 = (f32[12,576]{1,0:T(8,128)S(1)}, f32[12,576]{1,0:T(8,128)}, u32[]{:S(2)}) copy-start(f32[12,576]{1,0:T(8,128)} %refs_9_.3) | copy-start | bytes 82948
  39.7 49.9 %copy-start.3 = (bf16[1920,576]{1,0:T(8,128)(2,1)S(1)}, bf16[1920,576]{1,0:T(8,128)(2,1)}, u32[]{:S(2)}) copy-start(bf16[1920,576]{1,0:T(8,128)(2,1)} %constant.59.clone.refs_11_.refs_14_) | copy-start | bytes 6635524
  39.7 49.9 %copy-start.4 = (bf16[1920,576]{1,0:T(8,128)(2,1)S(1)}, bf16[1920,576]{1,0:T(8,128)(2,1)}, u32[]{:S(2)}) copy-start(bf16[1920,576]{1,0:T(8,128)(2,1)} %constant.58.clone.refs_10_.refs_13_) | copy-start | bytes 6635524
  39.7 19.1 %collective-permute-start.3 = (f32[1,2,144,128]{3,2,1,0:T(8,128)S(1)}, f32[1,2,144,128]{3,2,1,0:T(8,128)S(1)}, u32[]{:S(2)}, u32[]{:S(2)}) collective-permute-start(f32[1,2,144,128]{3,2,1,0:T(8,128)S(1)} %get-tuple-element.57), channel_id=1, source_target_pairs={{0,1},{1,2},{2,3},{3,0},{4,5},{5,6},{6,7},{7,4},{8,9},{9,10},{10,1... | collective-permute-start | bytes 442376 | tf_op jit(solution)/shard_map/ppermute | solution.py:479
  39.8 21.8 %collective-permute-start.4 = (f32[1,2,144,128]{3,2,1,0:T(8,128)S(1)}, f32[1,2,144,128]{3,2,1,0:T(8,128)S(1)}, u32[]{:S(2)}, u32[]{:S(2)}) collective-permute-start(f32[1,2,144,128]{3,2,1,0:T(8,128)S(1)} %get-tuple-element.58), channel_id=1, source_target_pairs={{0,2},{1,3},{2,0},{3,1},{4,6},{5,7},{6,4},{7,5},{8,10},{9,11},{10,... | collective-permute-start | bytes 442376 | tf_op jit(solution)/shard_map/ppermute | solution.py:479
  39.9 21.7 %collective-permute-start.5 = (f32[1,2,144,128]{3,2,1,0:T(8,128)S(1)}, f32[1,2,144,128]{3,2,1,0:T(8,128)S(1)}, u32[]{:S(2)}, u32[]{:S(2)}) collective-permute-start(f32[1,2,144,128]{3,2,1,0:T(8,128)S(1)} %get-tuple-element.59), channel_id=1, source_target_pairs={{0,3},{1,0},{2,1},{3,2},{4,7},{5,4},{6,5},{7,6},{8,11},{9,8},{10,9... | collective-permute-start | bytes 442376 | tf_op jit(solution)/shard_map/ppermute | solution.py:479
  49.0 19.8 %collective-permute-start.8 = (f32[2,160,128]{2,1,0:T(8,128)S(1)}, f32[2,160,128]{2,1,0:T(8,128)S(1)}, u32[]{:S(2)}, u32[]{:S(2)}) collective-permute-start(f32[2,160,128]{2,1,0:T(8,128)S(1)} %get-tuple-element.66), channel_id=1, source_target_pairs={{0,1},{1,2},{2,3},{3,0},{4,5},{5,6},{6,7},{7,4},{8,9},{9,10},{10,1... | collective-permute-start | bytes 491528 | tf_op jit(solution)/shard_map/ppermute | solution.py:479
  58.1 12.3 %collective-permute-start.9 = (f32[2,160,128]{2,1,0:T(8,128)S(1)}, f32[2,160,128]{2,1,0:T(8,128)S(1)}, u32[]{:S(2)}, u32[]{:S(2)}) collective-permute-start(f32[2,160,128]{2,1,0:T(8,128)S(1)} %get-tuple-element.67), channel_id=1, source_target_pairs={{0,2},{1,3},{2,0},{3,1},{4,6},{5,7},{6,4},{7,5},{8,10},{9,11},{10,... | collective-permute-start | bytes 491528 | tf_op jit(solution)/shard_map/ppermute | solution.py:479
  58.8 18.7 %collective-permute-start.10 = (f32[2,160,128]{2,1,0:T(8,128)S(1)}, f32[2,160,128]{2,1,0:T(8,128)S(1)}, u32[]{:S(2)}, u32[]{:S(2)}) collective-permute-start(f32[2,160,128]{2,1,0:T(8,128)S(1)} %get-tuple-element.68), channel_id=1, source_target_pairs={{0,3},{1,0},{2,1},{3,2},{4,7},{5,4},{6,5},{7,6},{8,11},{9,8},{10,9... | collective-permute-start | bytes 491528 | tf_op jit(solution)/shard_map/ppermute | solution.py:479
  64.3 31.9 %collective-permute-start.12 = (f32[1,160,128]{2,1,0:T(8,128)S(1)}, f32[1,160,128]{2,1,0:T(8,128)S(1)}, u32[]{:S(2)}, u32[]{:S(2)}) collective-permute-start(f32[1,160,128]{2,1,0:T(8,128)S(1)} %get-tuple-element.74), channel_id=1, source_target_pairs={{0,1},{1,2},{2,3},{3,0},{4,5},{5,6},{6,7},{7,4},{8,9},{9,10},{10,1... | collective-permute-start | bytes 245768 | tf_op jit(solution)/shard_map/ppermute | solution.py:479
  64.4 31.8 %collective-permute-start.13 = (f32[1,160,128]{2,1,0:T(8,128)S(1)}, f32[1,160,128]{2,1,0:T(8,128)S(1)}, u32[]{:S(2)}, u32[]{:S(2)}) collective-permute-start(f32[1,160,128]{2,1,0:T(8,128)S(1)} %get-tuple-element.75), channel_id=1, source_target_pairs={{0,2},{1,3},{2,0},{3,1},{4,6},{5,7},{6,4},{7,5},{8,10},{9,11},{10,... | collective-permute-start | bytes 245768 | tf_op jit(solution)/shard_map/ppermute | solution.py:479
  68.8 27.5 %collective-permute-start.14 = (f32[1,160,128]{2,1,0:T(8,128)S(1)}, f32[1,160,128]{2,1,0:T(8,128)S(1)}, u32[]{:S(2)}, u32[]{:S(2)}) collective-permute-start(f32[1,160,128]{2,1,0:T(8,128)S(1)} %get-tuple-element.76), channel_id=1, source_target_pairs={{0,3},{1,0},{2,1},{3,2},{4,7},{5,4},{6,5},{7,6},{8,11},{9,8},{10,9... | collective-permute-start | bytes 245768 | tf_op jit(solution)/shard_map/ppermute | solution.py:479
  77.5 18.7 %collective-permute-start.11 = (f32[1,160,128]{2,1,0:T(8,128)S(1)}, f32[1,160,128]{2,1,0:T(8,128)S(1)}, u32[]{:S(2)}, u32[]{:S(2)}) collective-permute-start(f32[1,160,128]{2,1,0:T(8,128)S(1)} %select_select_fusion), channel_id=1, source_target_pairs={{0,4},{4,8},{8,12},{12,16},{16,20},{20,24},{24,28},{28,32},{32,36}... | collective-permute-start | bytes 245768 | tf_op jit(solution)/shard_map/ppermute | solution.py:586
